TPU v7x, 128 devices: a whole 4x4x4 slice. The times are simulated.
128 devices in a mesh: cons: 4 (over y_lo, core), prod: 32 (over y_hi, z, x).
Axes of the slice: x: 4, y: 4 (y_hi: 2, y_lo: 2; y = y_hi * 2 + y_lo), z: 4, core: 2. Of those that a mesh axis runs over, the one named last changes fastest.
Arguments:
- tastes: bfloat16 [16384, 128], P('cons'), may hold values from -128 to 128
- price_coef: float32 [16384], P('cons'), may hold values from 0.5 to 5
- characteristics: bfloat16 [65536, 128], P('prod'), may hold values from -6 to 6
- mean_utility: float32 [65536], P('prod'), may hold values from -4 to 4
- panel_cols: int32 [256], replicated, may hold values from 0 to 65535
- firm_map: int32 [65536], P('prod'), may hold values from 0 to 65535, as said below
- inverses: float32 [512, 128, 128], P('prod'), may hold values from -0.5 to 0.5
Outputs:
- shares: float32 [65536], P('prod')
- markup: float32 [65536], P('prod')
- response: float32 [65536, 256], P('prod')
Inputs may be any that keep to these rules, and one draw needn't show every extreme that they name: `firm_map`: a permutation of the products; the rows of firm order held by each index of prod name exactly 64 products held by each index of prod.
All inputs are finite; a program needn't handle non-finite values.
Results may differ from a plain program's by a relative error of at most 0.002.
The roundings to bfloat16 on the way count: a program that leaves them out, or rounds other values in their place, can miss the bound.
Values may be sent and summed in bfloat16 or wider, within the bound.
No kernel may reach another device: no remote copies, remote signals or barrier semaphores. Data moves between devices by JAX's collectives and lax.ppermute only.
A program may use at most 64 MiB of HBM per device.

v0:
```python
import jax
import jax.numpy as jnp
from jax import lax
from jax.sharding import PartitionSpec as P


def utilities(taste_block, characteristics, mean_utility):
    return (
        jnp.einsum("ik,jk->ij", taste_block, characteristics, preferred_element_type=jnp.float32)
        + mean_utility[None, :]
    )


def request_order(firm_map):
    local_count = firm_map.shape[0]
    holders = lax.axis_size("prod")
    per_pair = local_count // holders
    source = firm_map // local_count
    order = jnp.argsort(source, stable=True)
    wanted = firm_map[order].reshape(holders, per_pair)
    return (order, wanted)


def regroup(jacobian, shares, firm_map):
    local_count = jacobian.shape[0]
    order, wanted = request_order(firm_map)
    base = lax.axis_index("prod") * local_count
    local_ids = lax.all_to_all(wanted, "prod", split_axis=0, concat_axis=0, tiled=True) - base
    rows_out = jnp.take(jacobian, local_ids, axis=0)
    values_out = jnp.take(shares, local_ids, axis=0)
    rows_back = lax.all_to_all(rows_out, "prod", split_axis=0, concat_axis=0, tiled=True)
    values_back = lax.all_to_all(values_out, "prod", split_axis=0, concat_axis=0, tiled=True)
    flat_rows = rows_back.reshape(local_count, jacobian.shape[1])
    flat_values = values_back.reshape(local_count)
    placed_rows = jnp.zeros_like(flat_rows).at[order].set(flat_rows)
    placed_values = jnp.zeros_like(flat_values).at[order].set(flat_values)
    return (placed_rows, placed_values)


def apply_blocks(inverses, placed_rows, placed_values):
    firm_count, block_size = (inverses.shape[0], inverses.shape[1])
    ordered = placed_rows.reshape(firm_count, block_size, placed_rows.shape[1])
    response = jnp.einsum(
        "fab,fbc->fac", inverses, ordered, precision=lax.Precision.HIGHEST
    ).reshape(placed_rows.shape)
    markup = jnp.einsum(
        "fab,fb->fa",
        inverses,
        placed_values.reshape(firm_count, block_size),
        precision=lax.Precision.HIGHEST,
    ).reshape(placed_values.shape)
    return (response, markup)


def body(tastes, price_coef, characteristics, mean_utility, panel_cols, firm_map, inverses):
    local_products = characteristics.shape[0]
    local_consumers = tastes.shape[0]
    col_count = panel_cols.shape[0]
    count_products = local_products * lax.axis_size("prod")
    count_consumers = local_consumers * lax.axis_size("cons")
    product_ids = lax.axis_index("prod") * local_products + lax.iota(jnp.int32, local_products)
    hits = product_ids[None, :] == panel_cols[:, None]
    part_chars = jnp.dot(
        hits.astype(jnp.bfloat16), characteristics, preferred_element_type=jnp.float32
    )
    part_means = jnp.dot(hits.astype(jnp.float32), mean_utility, precision=lax.Precision.HIGHEST)
    col_chars, col_means = lax.psum((part_chars, part_means), "prod")
    used_chars, used_means, used_ids = (characteristics, mean_utility, product_ids)
    block_rows = min(512, local_consumers)
    block_count = local_consumers // block_rows
    taste_blocks = tastes.reshape(block_count, block_rows, tastes.shape[1])
    coef_blocks = price_coef.reshape(block_count, block_rows)

    def local_peak(taste_block):
        utility = utilities(taste_block, used_chars, used_means)
        return jnp.maximum(jnp.max(utility, axis=1), 0.0)

    highest = lax.pmax(lax.map(local_peak, taste_blocks).reshape(local_consumers), "prod")

    def local_sum(inputs):
        taste_block, peak_block = inputs
        utility = utilities(taste_block, used_chars, used_means)
        return jnp.sum(jnp.exp(utility - peak_block[:, None]), axis=1)

    partial_total = lax.map(local_sum, (taste_blocks, highest.reshape(block_count, block_rows)))
    total = lax.psum(partial_total.reshape(local_consumers), "prod")
    denominator = jnp.exp(-highest) + total

    def consume(state_now, inputs):
        panel_sum, share_sum, diag_sum = state_now
        taste_block, coef_block, peak_block, denom_block = inputs
        utility = utilities(taste_block, used_chars, used_means)
        scaled = count_products * jnp.exp(utility - peak_block[:, None]) / denom_block[:, None]
        share_sum = share_sum + jnp.sum(scaled, axis=0)
        diag_sum = diag_sum + jnp.dot(coef_block, scaled, precision=lax.Precision.HIGHEST)
        col_util = (
            jnp.dot(taste_block.astype(jnp.float32), col_chars.T, precision=lax.Precision.HIGHEST)
            + col_means[None, :]
        )
        col_scaled = count_products * jnp.exp(col_util - peak_block[:, None]) / denom_block[:, None]
        weighted = (coef_block[:, None] * col_scaled).astype(jnp.bfloat16)
        panel_sum = panel_sum + lax.dot_general(
            scaled.astype(jnp.bfloat16),
            weighted,
            (((0,), (0,)), ((), ())),
            preferred_element_type=jnp.float32,
        )
        return ((panel_sum, share_sum, diag_sum), None)

    start_state = (
        jnp.zeros((local_products, col_count), jnp.float32),
        jnp.zeros((local_products,), jnp.float32),
        jnp.zeros((local_products,), jnp.float32),
    )
    scan_inputs = (
        taste_blocks,
        coef_blocks,
        highest.reshape(block_count, block_rows),
        denominator.reshape(block_count, block_rows),
    )
    (panel_sum, share_sum, diag_sum), _ = lax.scan(consume, start_state, scan_inputs)
    marks = (used_ids[:, None] == panel_cols[None, :]).astype(jnp.float32)
    panel_all, share_all, diag_all = lax.psum((panel_sum, share_sum, diag_sum), "cons")
    local_shares = share_all / count_consumers
    diagonal = diag_all / count_consumers
    jacobian = panel_all / count_consumers - diagonal[:, None] * marks
    placed_rows, placed_values = regroup(jacobian, local_shares, firm_map)
    response, markup = apply_blocks(inverses, placed_rows, placed_values)
    return (local_shares, markup, response)


def solution(mesh):
    return jax.shard_map(
        body,
        mesh=mesh,
        in_specs=(
            P("cons", None),
            P("cons"),
            P("prod", None),
            P("prod"),
            P(),
            P("prod"),
            P("prod", None, None),
        ),
        out_specs=(P("prod"), P("prod"), P("prod", None)),
        check_vma=False,
    )
```

profile of v0, /device:TPU:1, one launch (start us, length us, event | category | flops | bytes accessed | tf_op | source)
XLA Modules:
  0.0 614.1 jit_solution(9384950392548161168)
XLA Ops:
  7.2 2.3 fusion.23
  9.6 15.6 %while.35 = (s32[]{:T(128)}, f32[8,512]{1,0:T(8,128)S(1)}, bf16[8,512,128]{2,1,0:T(8,128)(2,1)}, bf16[2048,128]{1,0:T(8,128)(2,1)}, f32[2048]{0:T(1024)}, /*index=5*/s32[]{:T(128)}, s32[]{:T(128)}) while((s32[]{:T(128)}, f32[8,512]{1,0:T(8,128)S(1)}, bf16[8,512,128]{2,1,0:T(8,128)(2,1)}, bf16[2048,128]{1,0:T(8,128)(2,1)}, f32[2048]{0:T(1024)}, ...), condition=%wide.region_2.3_spmd, body=%wide.region_0.2_spmd.sunk | while | flops 270532608 | bytes 674385 | solution.py:78
  9.6 1.9 add_reduce_fusion.2
  11.6 1.9 add_reduce_fusion.2
  13.5 1.9 add_reduce_fusion.2
  15.5 1.9 add_reduce_fusion.2
  17.4 1.9 add_reduce_fusion.2
  19.4 1.9 add_reduce_fusion.2
  21.3 1.9 add_reduce_fusion.2
  23.3 1.9 add_reduce_fusion.2
  25.3 159.6 %pmax.7 = f32[4096]{0:T(1024)S(1)} all-reduce(f32[4096]{0:T(1024)S(1)} %bitcast.112), channel_id=1, replica_groups=mesh['cons'=4,'prod'=32] {'prod'}, use_global_device_ids=true, to_apply=%region_3.0 | all-reduce | flops 4096 | bytes 32768 | tf_op jit(solution)/shard_map/pmax | solution.py:78
  184.8 16.8 %while.36 = (s32[]{:T(128)}, f32[8,512]{1,0:T(8,128)S(1)}, bf16[8,512,128]{2,1,0:T(8,128)(2,1)}, bf16[2048,128]{1,0:T(8,128)(2,1)}, f32[2048]{0:T(1024)}, /*index=5*/f32[8,512]{1,0:T(8,128)S(1)}, s32[]{:T(128)}, s32[]{:T(128)}) while((s32[]{:T(128)}, f32[8,512]{1,0:T(8,128)S(1)}, bf16[8,512,128]{2,1,0:T(8,128)(2,1)}, ...), condition=%wide.region_6.7_spmd, body=%wide.region_4.6_spmd.sunk | while | flops 271580672 | bytes 676445 | solution.py:85
  184.9 2.0 exponential_reduce_fusion.2
  187.0 2.0 exponential_reduce_fusion.2
  189.1 2.0 exponential_reduce_fusion.2
  191.2 2.0 exponential_reduce_fusion.2
  193.3 2.0 exponential_reduce_fusion.2
  195.4 2.0 exponential_reduce_fusion.2
  197.5 2.0 exponential_reduce_fusion.2
  199.6 2.0 exponential_reduce_fusion.2
  201.7 1.7 fusion.21
  203.4 150.8 %all-reduce = (f32[4096]{0:T(1024)S(1)}, f32[256]{0:T(256)S(1)}) all-reduce(f32[4096]{0:T(1024)S(1)} %bitcast.111, f32[256]{0:T(256)S(1)} %bitcast.121), channel_id=1, replica_groups=mesh['cons'=4,'prod'=32] {'prod'}, use_global_device_ids=true, to_apply=%region_7.8 | all-reduce | flops 4352 | bytes 34816 | tf_op jit(solution)/shard_map/psum | solution.py:86
  354.3 78.8 %while.37 = (s32[]{:T(128)}, f32[2048,256]{1,0:T(8,128)S(1)}, f32[2048]{0:T(1024)S(1)}, f32[2048]{0:T(1024)S(1)}, bf16[8,512,128]{2,1,0:T(8,128)(2,1)}, /*index=...) while((s32[]{:T(128)}, f32[2048,256]{1,0:T(8,128)S(1)}, ...), condition=%wide.region_12.13_spmd.clone, body=%wide.region_10.12_spmd.clone.sunk | while | flops 1027348480 | bytes 35621072 | solution.py:121
  354.4 2.3 fusion.76
  356.7 2.1 fusion.77
  360.2 4.0 convolution_add_fusion.3
  364.2 2.3 fusion.76
  366.6 2.1 fusion.77
  370.0 4.0 convolution_add_fusion.3
  374.1 2.3 fusion.76
  376.4 2.1 fusion.77
  378.5 1.4 fusion.75
  379.9 4.0 convolution_add_fusion.3
  383.9 2.3 fusion.76
  386.2 2.1 fusion.77
  388.3 1.4 fusion.75
  389.7 4.0 convolution_add_fusion.3
  393.8 2.3 fusion.76
  396.1 2.1 fusion.77
  399.6 4.0 convolution_add_fusion.3
  403.6 2.3 fusion.76
  405.9 2.1 fusion.77
  409.4 4.0 convolution_add_fusion.3
  413.5 2.3 fusion.76
  415.8 2.1 fusion.77
  419.2 4.0 convolution_add_fusion.3
  423.3 2.3 fusion.76
  425.6 2.1 fusion.77
  429.1 4.0 convolution_add_fusion.3
  434.5 5.0 sort.17
  439.5 11.8 %gather_fusion = s32[2048]{0:T(1024)S(1)} fusion(s32[2048]{0:T(1024)S(1)} %copy-done.2, s32[2048]{0:T(1024)S(1)} %get-tuple-element.226), kind=kCustom, calls=%fused_computation | custom fusion | bytes 24576 | tf_op jit(solution)/shard_map/gather | solution.py:20
  451.4 12.7 %all_to_all.20 = s32[32,1,64]{2,1,0:T(1,128)S(1)} all-to-all(s32[32,1,64]{2,1,0:T(1,128)S(1)} %all_to_all.13), channel_id=1, replica_groups=mesh['cons'=4,'prod'=32] {'prod'}, dimensions={0} | all-to-all | bytes 16384 | tf_op jit(solution)/shard_map/all_to_all | solution.py:28
  464.2 60.9 %all-reduce.1 = (f32[2048]{0:T(1024)S(1)}, f32[2048]{0:T(1024)S(1)}) all-reduce(f32[2048]{0:T(1024)S(1)} %get-tuple-element.129, f32[2048]{0:T(1024)S(1)} %get-tuple-element.132), channel_id=1, replica_groups=mesh['cons'=4,'prod'=32] {'cons'}, use_global_device_ids=true, to_apply=%region_13.14 | all-reduce | flops 4096 | bytes 32768 | tf_op jit(solution)/shard_map/psum | solution.py:123
  525.1 11.8 %gather_fusion.1 = f32[2048]{0:T(1024)S(1)} fusion(f32[2048]{0:T(1024)S(1)} %broadcast_multiply_fusion.1, s32[2048]{0:T(1024)S(1)} %broadcast_clamp_fusion), kind=kCustom, calls=%fused_computation.1 | custom fusion | bytes 24576 | tf_op jit(solution)/shard_map/jit(_take)/gather | solution.py:30
  537.6 4.0 all-to-all-start.1
  541.7 1.9 select_subtract_fusion
  543.6 8.6 %gather_fusion.2 = f32[2048,256]{1,0:T(8,128)} fusion(f32[2048,256]{1,0:T(8,128)S(1)} %select_subtract_fusion, s32[2048]{0:T(1024)S(1)} %broadcast_clamp_fusion), kind=kCustom, calls=%fused_computation.2 | custom fusion | bytes 4202496 | tf_op jit(solution)/shard_map/jit(_take)/gather | solution.py:29
  552.2 3.2 broadcast_select_fusion
  555.5 9.3 %all-to-all-start.2 = ((f32[32,64,256]{2,1,0:T(8,128)}), f32[32,64,256]{2,1,0:T(8,128)S(1)}, u32[]{:S(2)}, u32[]{:S(2)}) async-start(f32[32,64,256]{2,1,0:T(8,128)} %broadcast_select_fusion), calls=%async_computation.2 | async-start | bytes 4194304 | tf_op jit(solution)/shard_map/all_to_all | solution.py:31
  566.0 8.0 %scatter_custom_fusion = f32[2048]{0:T(1024)S(1)} fusion(s32[2048]{0:T(1024)S(1)} %get-tuple-element.227, f32[2048]{0:T(1024)S(1)} %reshape.152, f32[]{:T(128)} %constant.89.clone.1), kind=kCustom, calls=%fused_computation.70 | custom fusion | bytes 8196 | tf_op jit(solution)/shard_map/scatter | solution.py:36
  574.1 2.3 fusion.36
  576.4 16.2 %all-to-all-done.2 = f32[32,64,256]{2,1,0:T(8,128)S(1)} async-done(((f32[32,64,256]{2,1,0:T(8,128)}), f32[32,64,256]{2,1,0:T(8,128)S(1)}, u32[]{:S(2)}, u32[]{:S(2)}) %all-to-all-start.2) | async-done | bytes 2097184 | tf_op jit(solution)/shard_map/all_to_all | solution.py:31
  594.0 10.0 %scatter_custom_fusion.1 = f32[2048,256]{1,0:T(8,128)S(1)} fusion(s32[2048]{0:T(1024)S(1)} %get-tuple-element.227, f32[2048,256]{1,0:T(8,128)} %bitcast.101, f32[]{:T(128)} %constant.89.clone.1), kind=kCustom, calls=%fused_computation.46 | custom fusion | bytes 2097664 | tf_op jit(solution)/shard_map/scatter | solution.py:35
  603.9 3.3 fusion.37
  (151 shorter events, 14.6 us)
Async XLA Ops:
  7.2 566.9 %copy-start = (f32[16,128,128]{2,1,0:T(8,128)S(1)}, f32[16,128,128]{2,1,0:T(8,128)}, u32[]{:S(2)}) copy-start(f32[16,128,128]{2,1,0:T(8,128)} %param.19) | copy-start | bytes 3145732
  7.2 347.2 %all-reduce.5.cloned.1.call-start = ((), (), s32[]{:S(2)}) async-start(), calls=%async_computation.3 | async-start | bytes 262144 | tf_op jit(solution)/shard_map/psum | solution.py:67
  9.5 532.1 %all-reduce.7.cloned.1.call-start = ((), (), s32[]{:S(2)}) async-start(), calls=%async_computation.4 | async-start | bytes 4194304 | tf_op jit(solution)/shard_map/psum | solution.py:123
  184.8 16.9 %copy-start.7 = (s32[256]{0:T(256)S(1)}, s32[256]{0:T(256)}, u32[]{:S(2)}) copy-start(s32[256]{0:T(256)} %param.17) | copy-start | bytes 3076
  184.8 169.5 %copy-start.6 = (f32[4096]{0:T(1024)S(1)}, f32[4096]{0:T(1024)}, u32[]{:S(2)}) copy-start(f32[4096]{0:T(1024)} %param.14) | copy-start | bytes 49156
  356.7 2.1 copy-start.3
  356.7 2.1 copy-start.8
  366.5 2.1 copy-start.3
  366.5 2.1 copy-start.8
  376.4 2.1 copy-start.3
  376.4 2.1 copy-start.8
  386.2 2.1 copy-start.3
  386.2 2.1 copy-start.8
  396.1 2.1 copy-start.3
  396.1 2.1 copy-start.8
  405.9 2.1 copy-start.3
  405.9 2.1 copy-start.8
  415.7 2.1 copy-start.3
  415.8 2.1 copy-start.8
  425.6 2.1 copy-start.3
  425.6 2.1 copy-start.8
  433.1 1.3 copy-start.4
  433.1 1.3 copy-start.2
  525.1 11.8 %copy-start.1 = (f32[2048]{0:T(1024)}, f32[2048]{0:T(1024)S(1)}, u32[]{:S(2)}) copy-start(f32[2048]{0:T(1024)S(1)} %broadcast_multiply_fusion.1) | copy-start | bytes 24580
  537.6 17.8 %all-to-all-start.1 = ((f32[32,1,64]{2,1,0:T(1,128)}), f32[32,1,64]{2,1,0:T(1,128)S(1)}, u32[]{:S(2)}, u32[]{:S(2)}) async-start(f32[32,1,64]{2,1,0:T(1,128)} %and_select_fusion), calls=%async_computation.1 | async-start | bytes 32768 | tf_op jit(solution)/shard_map/all_to_all | solution.py:32
  555.5 37.2 %all-to-all-start.2 = ((f32[32,64,256]{2,1,0:T(8,128)}), f32[32,64,256]{2,1,0:T(8,128)S(1)}, u32[]{:S(2)}, u32[]{:S(2)}) async-start(f32[32,64,256]{2,1,0:T(8,128)} %broadcast_select_fusion), calls=%async_computation.2 | async-start | bytes 4194304 | tf_op jit(solution)/shard_map/all_to_all | solution.py:31
  592.6 1.3 copy-start.5
Sparse Core Ops, SparseCore 0:
  11.1 311.2 all-reduce.4
  434.6 103.9 all-reduce.6
where the time goes:
time: 617 us; the launch traced here: 614 us
  blocking collectives  384 us (62%)
  matrix products  118 us (19%)
  local copies, waits for them, and re-layouts  55 us (9%)
  waiting for transfers between devices  16.3 us (3%)
  between operations  14.3 us (2%)
  starting transfers between devices  13.3 us (2%)
  other arithmetic  11.7 us (2%)
    pmax x1, blocking collectives, body(): lax.pmax(lax.map(local_peak, taste_blocks).reshape(local_consumers), 'prod')  160 us
    psum x1, blocking collectives, body(): total = lax.psum(partial_total.reshape(local_consumers), 'prod')  151 us
    psum x1, blocking collectives, body(): lax.psum((panel_sum, share_sum, diag_sum), 'cons')  60.9 us
    dot_general x24, matrix products, utilities(): jnp.einsum('ik,jk->ij', taste_block, characteristics, preferred_element_t...  49.2 us
    dot_general x8, matrix products, consume(): lax.dot_general(scaled.astype(jnp.bfloat16), weighted, (((0,), (0,)), (()...  32 us
    dot_general x8, matrix products, consume(): jnp.dot(coef_block, scaled, precision=lax.Precision.HIGHEST)  16.6 us
    all_to_all x1, waiting for transfers between devices, regroup(): lax.all_to_all(rows_out, 'prod', split_axis=0, concat_axis=0, tiled=True)  16.2 us
    all_to_all x1, blocking collectives, regroup(): lax.all_to_all(wanted, 'prod', split_axis=0, concat_axis=0, tiled=True)  12.7 us
  transfers between devices with their start and end apart: 4, of which 1 were waited for; matrix products, arithmetic and copies ran while one was open for 14% of the time, Pallas kernels for 0%

commit v1 on v0

v1 whole, which is shorter than its diff:
```python
import jax
import jax.numpy as jnp
from jax import lax
from jax.experimental import pallas as pl
from jax.experimental.pallas import tpu as pltpu
from jax.sharding import PartitionSpec as P

NT = (((1,), (1,)), ((), ()))
VMEM_BYTES = 56 * 1024 * 1024


def dot_nt(left, right):
    return lax.dot_general(left, right, NT, preferred_element_type=jnp.float32)


def split3(values):
    high = lax.reduce_precision(values, 8, 7)
    middle = lax.reduce_precision(values - high, 8, 7)
    low = lax.reduce_precision(values - high - middle, 8, 7)
    high, middle, low = (piece.astype(jnp.bfloat16) for piece in (high, middle, low))
    return high, middle, low


def stats_kernel(block, chunk, chars_ref, tastes_ref, stat_ref, expo_ref, util_ref):
    rows = chars_ref.shape[0]
    tastes = tastes_ref[...]
    peak = jnp.full((8, block), -jnp.inf, jnp.float32)
    for start in range(0, rows, chunk):
        util = dot_nt(chars_ref[start : start + chunk, :], tastes)
        util_ref[start : start + chunk, :] = util
        peak = jnp.maximum(peak, jnp.max(util.reshape(chunk // 8, 8, block), axis=0))
    peak = jnp.max(peak, axis=0, keepdims=True)
    total = jnp.zeros((8, block), jnp.float32)
    for start in range(0, rows, chunk):
        expo = jnp.exp(util_ref[start : start + chunk, :] - peak)
        total = total + jnp.sum(expo.reshape(chunk // 8, 8, block), axis=0)
        expo_ref[start : start + chunk, :] = expo.astype(jnp.bfloat16)
    stat_ref[0:1, :] = peak
    stat_ref[1:2, :] = jnp.sum(total, axis=0, keepdims=True)


def stats(chars, tastes):
    rows, depth = chars.shape
    consumers = tastes.shape[0]
    block, chunk = 256, 256

    def kernel(*refs):
        stats_kernel(block, chunk, *refs)

    return pl.pallas_call(
        kernel,
        grid=(consumers // block,),
        in_specs=[
            pl.BlockSpec((rows, depth), lambda i: (0, 0)),
            pl.BlockSpec((block, depth), lambda i: (i, 0)),
        ],
        out_specs=[
            pl.BlockSpec((2, block), lambda i: (0, i)),
            pl.BlockSpec((rows, block), lambda i: (0, i)),
        ],
        out_shape=[
            jax.ShapeDtypeStruct((2, consumers), jnp.float32),
            jax.ShapeDtypeStruct((rows, consumers), jnp.bfloat16),
        ],
        scratch_shapes=[pltpu.VMEM((rows, block), jnp.float32)],
        compiler_params=pltpu.CompilerParams(vmem_limit_bytes=VMEM_BYTES),
        cost_estimate=pl.CostEstimate(
            flops=2 * rows * consumers * depth, bytes_accessed=rows * consumers * 2, transcendentals=rows * consumers
        ),
        name="stats",
    )(chars, tastes)


def pick_rows(ids_t, chars):
    per_pair, holders = ids_t.shape
    rows, depth = chars.shape
    group = max(1, 256 // per_pair)

    def kernel(ids_ref, chars_ref, out_ref):
        lanes = lax.broadcasted_iota(jnp.int32, (per_pair, rows), 1)
        table = chars_ref[...]
        for start in range(0, holders, group):
            marks = [
                jnp.where(ids_ref[:, q : q + 1] == lanes, 1.0, 0.0).astype(jnp.bfloat16)
                for q in range(start, min(start + group, holders))
            ]
            hot = jnp.concatenate(marks, axis=0)
            picked = jnp.dot(hot, table, preferred_element_type=jnp.float32)
            out_ref[start * per_pair : start * per_pair + hot.shape[0], :] = picked.astype(jnp.bfloat16)

    return pl.pallas_call(
        kernel,
        out_shape=jax.ShapeDtypeStruct((per_pair * holders, depth), jnp.bfloat16),
        compiler_params=pltpu.CompilerParams(vmem_limit_bytes=VMEM_BYTES),
        cost_estimate=pl.CostEstimate(flops=2 * rows * rows * depth, bytes_accessed=rows * depth * 4, transcendentals=0),
        name="pick_rows",
    )(ids_t, chars)


def place_rows(order, received):
    rows, depth = received.shape
    chunk = 256

    def kernel(order_ref, received_ref, out_ref):
        order_row = order_ref[...]
        table = received_ref[...]
        for start in range(0, rows, chunk):
            ids = start + lax.broadcasted_iota(jnp.int32, (chunk, rows), 0)
            hot = jnp.where(ids == order_row, 1.0, 0.0).astype(jnp.bfloat16)
            placed = jnp.dot(hot, table, preferred_element_type=jnp.float32)
            out_ref[start : start + chunk, :] = placed.astype(jnp.bfloat16)

    return pl.pallas_call(
        kernel,
        out_shape=jax.ShapeDtypeStruct((rows, depth), jnp.bfloat16),
        compiler_params=pltpu.CompilerParams(vmem_limit_bytes=VMEM_BYTES),
        cost_estimate=pl.CostEstimate(flops=2 * rows * rows * depth, bytes_accessed=rows * depth * 4, transcendentals=0),
        name="place_rows",
    )(order, received)


def lane_groups(values):
    total = values[:, 0:128]
    for start in range(128, values.shape[1], 128):
        total = total + values[:, start : start + 128]
    return total


def weights(tastes, row_values, col_chars):
    consumers, depth = tastes.shape
    cols = col_chars.shape[0]
    block = 1024

    def kernel(tastes_ref, rows_ref, cols_ref, weight_ref, diag_ref):
        @pl.when(pl.program_id(0) == 0)
        def _():
            diag_ref[...] = jnp.zeros_like(diag_ref)

        expo = jnp.exp(dot_nt(cols_ref[...], tastes_ref[...]) - rows_ref[0:1, :])
        weighted = rows_ref[2:3, :] * (expo * rows_ref[1:2, :])
        diag_ref[...] += lane_groups(weighted)
        weight_ref[...] = weighted.astype(jnp.bfloat16)

    return pl.pallas_call(
        kernel,
        grid=(consumers // block,),
        in_specs=[
            pl.BlockSpec((block, depth), lambda i: (i, 0)),
            pl.BlockSpec((3, block), lambda i: (0, i)),
            pl.BlockSpec((cols, depth), lambda i: (0, 0)),
        ],
        out_specs=[
            pl.BlockSpec((cols, block), lambda i: (0, i)),
            pl.BlockSpec((cols, 128), lambda i: (0, 0)),
        ],
        out_shape=[
            jax.ShapeDtypeStruct((cols, consumers), jnp.bfloat16),
            jax.ShapeDtypeStruct((cols, 128), jnp.float32),
        ],
        compiler_params=pltpu.CompilerParams(vmem_limit_bytes=VMEM_BYTES),
        cost_estimate=pl.CostEstimate(
            flops=2 * cols * consumers * depth, bytes_accessed=cols * consumers * 2, transcendentals=cols * consumers
        ),
        name="weights",
    )(tastes, row_values, col_chars)


def panel(chars, tastes, row_values, weighted):
    rows, depth = chars.shape
    consumers = tastes.shape[0]
    cols = weighted.shape[0]
    block, chunk = 1024, 256

    def kernel(chars_ref, tastes_ref, rows_ref, weight_ref, panel_ref, share_ref):
        @pl.when(pl.program_id(0) == 0)
        def _():
            panel_ref[...] = jnp.zeros_like(panel_ref)
            share_ref[...] = jnp.zeros_like(share_ref)

        people, weight = tastes_ref[...], weight_ref[...]
        peak, ratio = rows_ref[0:1, :], rows_ref[1:2, :]
        for start in range(0, rows, chunk):
            scaled = jnp.exp(dot_nt(chars_ref[start : start + chunk, :], people) - peak) * ratio
            share_ref[start : start + chunk, :] += lane_groups(scaled)
            panel_ref[start : start + chunk, :] += dot_nt(scaled.astype(jnp.bfloat16), weight)

    return pl.pallas_call(
        kernel,
        grid=(consumers // block,),
        in_specs=[
            pl.BlockSpec((rows, depth), lambda i: (0, 0)),
            pl.BlockSpec((block, depth), lambda i: (i, 0)),
            pl.BlockSpec((3, block), lambda i: (0, i)),
            pl.BlockSpec((cols, block), lambda i: (0, i)),
        ],
        out_specs=[
            pl.BlockSpec((rows, cols), lambda i: (0, 0)),
            pl.BlockSpec((rows, 128), lambda i: (0, 0)),
        ],
        out_shape=[
            jax.ShapeDtypeStruct((rows, cols), jnp.float32),
            jax.ShapeDtypeStruct((rows, 128), jnp.float32),
        ],
        compiler_params=pltpu.CompilerParams(vmem_limit_bytes=VMEM_BYTES),
        cost_estimate=pl.CostEstimate(
            flops=2 * rows * consumers * (depth + cols), bytes_accessed=rows * cols * 8, transcendentals=rows * consumers
        ),
        name="panel",
    )(chars, tastes, row_values, weighted)


def share_sums(expo, factors):
    rows, consumers = expo.shape
    block = 1024

    def kernel(expo_ref, factor_ref, out_ref):
        @pl.when(pl.program_id(0) == 0)
        def _():
            out_ref[...] = jnp.zeros_like(out_ref)

        out_ref[...] += dot_nt(factor_ref[...], expo_ref[...])

    return pl.pallas_call(
        kernel,
        grid=(consumers // block,),
        in_specs=[
            pl.BlockSpec((rows, block), lambda i: (0, i)),
            pl.BlockSpec((16, block), lambda i: (0, i)),
        ],
        out_specs=pl.BlockSpec((16, rows), lambda i: (0, 0)),
        out_shape=jax.ShapeDtypeStruct((16, rows), jnp.float32),
        compiler_params=pltpu.CompilerParams(vmem_limit_bytes=VMEM_BYTES),
        cost_estimate=pl.CostEstimate(flops=2 * rows * consumers * 128, bytes_accessed=rows * consumers * 2, transcendentals=0),
        name="share_sums",
    )(expo, factors)


def swap(value, axis, mask):
    size = lax.axis_size(axis)
    return lax.ppermute(value, axis, [(i, i ^ mask) for i in range(size)])


def butterfly_masks(size):
    masks, step = [], 1
    while step < size:
        masks.append(step)
        if step * 2 < size:
            masks.append(step * 3)
        step *= 4
    return masks


def body(tastes, price_coef, characteristics, mean_utility, panel_cols, firm_map, inverses):
    products, depth = characteristics.shape
    consumers = tastes.shape[0]
    cols = panel_cols.shape[0]
    holders = lax.axis_size("prod")
    per_pair = products // holders
    count_products = products * holders
    count_consumers = consumers * lax.axis_size("cons")
    base = lax.axis_index("prod") * products
    core = lax.axis_index("cons") % 2

    wanted, order = lax.sort((firm_map, lax.iota(jnp.int32, products)), num_keys=1)
    ids = lax.all_to_all(wanted.reshape(holders, per_pair), "prod", split_axis=0, concat_axis=0, tiled=True) - base

    pieces = jnp.stack(split3(mean_utility), axis=1)
    chars = jnp.concatenate([characteristics, jnp.pad(pieces, ((0, 0), (0, depth - 3)))], axis=1)
    beside = jnp.broadcast_to(lax.iota(jnp.int32, depth)[None, :] < 3, (consumers, depth)).astype(jnp.bfloat16)
    people = jnp.concatenate([tastes, beside], axis=1)

    product_ids = base + lax.iota(jnp.int32, products)
    hits = (panel_cols[:, None] == product_ids[None, :]).astype(jnp.bfloat16)
    col_chars = jnp.dot(hits, chars, preferred_element_type=jnp.float32).astype(jnp.bfloat16)

    stat, expo = stats(chars, people)

    sent = pick_rows(ids.T, chars).reshape(holders, per_pair, 2 * depth)
    received = lax.all_to_all(sent, "prod", split_axis=0, concat_axis=0, tiled=True).reshape(products, 2 * depth)
    firm_chars = place_rows(order.reshape(1, products), received)

    masks = butterfly_masks(holders)
    for mask in masks:
        col_chars = col_chars + swap(col_chars, "prod", mask)

    local_peak = stat[0]
    for mask in masks:
        other = swap(stat, "prod", mask)
        joint = jnp.maximum(stat[0], other[0])
        total = stat[1] * jnp.exp(stat[0] - joint) + other[1] * jnp.exp(other[0] - joint)
        stat = jnp.stack([joint, total])
    peak = jnp.maximum(stat[0], 0.0)
    denom = jnp.exp(-peak) + stat[1] * jnp.exp(stat[0] - peak)
    ratio = count_products / denom

    row_values = jnp.stack([peak, ratio, price_coef])
    weighted, diag_part = weights(people, row_values, col_chars)
    diagonal = jnp.sum(diag_part, axis=1)
    for mask in (1, 2):
        diagonal = diagonal + swap(diagonal, "cons", mask)
    room = 32768.0 / (count_products * jnp.maximum(diagonal, 1e-25))
    panel_part, share_part = panel(firm_chars, people, row_values, weighted)

    half = products // 2
    kept = lax.dynamic_slice_in_dim(panel_part, core * half, half, 0)
    given = lax.dynamic_slice_in_dim(panel_part, (1 - core) * half, half, 0)
    chip_sum = lax.optimization_barrier(((kept + swap(given, "cons", 1)) * room[None, :]).astype(jnp.float16))
    other_sum = swap(chip_sum, "cons", 2)

    factors = jnp.stack(split3(jnp.exp(local_peak - peak) * ratio), axis=0)
    own_shares = jnp.sum(share_sums(expo, jnp.pad(factors, ((0, 13), (0, 0)))), axis=0)
    sums = lax.psum(jnp.concatenate([own_shares, jnp.sum(share_part, axis=1)]), "cons") / count_consumers
    shares, firm_shares = sums[:products], sums[products:]

    firm_count, block_size = inverses.shape[0], inverses.shape[1]
    firm_ids = lax.dynamic_slice_in_dim(firm_map, core * half, half, 0)
    marks = firm_ids[:, None] == panel_cols[None, :]
    cross = (chip_sum.astype(jnp.float32) + other_sum.astype(jnp.float32)) / (room[None, :] * count_consumers)
    jacobian = cross - jnp.where(marks, diagonal[None, :] / count_consumers, 0.0)
    own_inverses = lax.dynamic_slice_in_dim(inverses, core * (firm_count // 2), firm_count // 2, 0)
    response = jnp.einsum(
        "fab,fbc->fac",
        own_inverses,
        jacobian.reshape(firm_count // 2, block_size, cols),
        precision=lax.Precision.HIGHEST,
    ).reshape(half, cols)
    other_response = swap(response, "cons", 1)
    response = jnp.where(
        core == 0,
        jnp.concatenate([response, other_response], axis=0),
        jnp.concatenate([other_response, response], axis=0),
    )
    markup = jnp.sum(inverses * firm_shares.reshape(firm_count, 1, block_size), axis=2).reshape(products)
    return (shares, markup, response)


def solution(mesh):
    return jax.shard_map(
        body,
        mesh=mesh,
        in_specs=(
            P("cons", None),
            P("cons"),
            P("prod", None),
            P("prod"),
            P(),
            P("prod"),
            P("prod", None, None),
        ),
        out_specs=(P("prod"), P("prod"), P("prod", None)),
        check_vma=False,
    )
```

time: 617 us -> 172 us (0.28)
  blocking collectives: 384 us -> 9.45 us
  matrix products: 118 us -> 1.5 us
  Pallas kernels: 0 us -> 54.7 us
  local copies, waits for them, and re-layouts: 55 us -> 4.15 us
  starting transfers between devices: 13.3 us -> 48.5 us
  between operations: 14.3 us -> 0.92 us
  waiting for transfers between devices: 16.3 us -> 29.6 us
  other arithmetic: 11.7 us -> 20.8 us
    psum x2 -> x1, blocking collectives: 212 us -> 9.45 us  [body(): lax.psum(jnp.concatenate([own_shares, jnp.sum(share_part, axis=1)]), 'cons')]
    pmax x1 -> x0, blocking collectives: 160 us -> none  [body(): lax.pmax(lax.map(local_peak, taste_blocks).reshape(local_consumers), 'prod')]
    dot_general x52 -> x2, matrix products: 118 us -> 1.5 us  [the longest x1 1.02 us: body(): jnp.einsum('fab,fbc->fac', own_inverses, jacobian.reshape(firm_count // 2...]
    pallas_call x0 -> x6, Pallas kernels: none -> 54.7 us  [the longest x1 18.4 us: stats(): pl.pallas_call(kernel, grid=(consumers // block,), in_specs=[pl.BlockSpec...]
    gather x4 -> x0, local copies, waits for them, and re-layouts: 32.2 us -> none  [the longest x2 11.9 us: regroup(): values_out = jnp.take(shares, local_ids, axis=0)]
    ppermute x0 -> x15, starting transfers between devices: none -> 29.9 us  [swap(): return lax.ppermute(value, axis, [(i, i ^ mask) for i in range(size)])]
    ppermute x0 -> x15, waiting for transfers between devices: none -> 28.5 us  [swap(): return lax.ppermute(value, axis, [(i, i ^ mask) for i in range(size)])]
    scatter x2 -> x0, local copies, waits for them, and re-layouts: 18 us -> none  [the longest x1 9.97 us: regroup(): placed_rows = jnp.zeros_like(flat_rows).at[order].set(flat_rows)]
  transfers between devices with their start and end apart: 4 -> 17, of which waited for: 1 -> 8; matrix products, arithmetic and copies ran while one was open for 14% -> 8% of each run, Pallas kernels for 0% -> 11%
where the time goes in v1:
time: 172 us; the launch traced here: 170 us
  Pallas kernels  54.7 us (32%)
  starting transfers between devices  48.5 us (28%)
  waiting for transfers between devices  29.6 us (17%)
  other arithmetic  20.8 us (12%)
  blocking collectives  9.45 us (5%)
  local copies, waits for them, and re-layouts  4.15 us (2%)
    ppermute x15, starting transfers between devices, swap(): return lax.ppermute(value, axis, [(i, i ^ mask) for i in range(size)])  29.9 us
    ppermute x15, waiting for transfers between devices, swap(): return lax.ppermute(value, axis, [(i, i ^ mask) for i in range(size)])  28.5 us
    pallas_call x1, Pallas kernels, stats(): pl.pallas_call(kernel, grid=(consumers // block,), in_specs=[pl.BlockSpec...  18.4 us
    pallas_call x1, Pallas kernels, panel(): pl.pallas_call(kernel, grid=(consumers // block,), in_specs=[pl.BlockSpec...  13.4 us
    all_to_all x1, starting transfers between devices, body(): lax.all_to_all(wanted.reshape(holders, per_pair), 'prod', split_axis=0, c...  10.2 us
    psum x1, blocking collectives, body(): lax.psum(jnp.concatenate([own_shares, jnp.sum(share_part, axis=1)]), 'cons')  9.45 us
    pallas_call x1, Pallas kernels, share_sums(): pl.pallas_call(kernel, grid=(consumers // block,), in_specs=[pl.BlockSpec...  8.97 us
    all_to_all x1, starting transfers between devices, body(): lax.all_to_all(sent, 'prod', split_axis=0, concat_axis=0, tiled=True)  8.35 us
  transfers between devices with their start and end apart: 17, of which 8 were waited for; matrix products, arithmetic and copies ran while one was open for 8% of the time, Pallas kernels for 11%

profile of v1, /device:TPU:1, one launch (start us, length us, event | category | flops | bytes accessed | tf_op | source)
XLA Modules:
  0.0 169.6 jit_solution(3507192243208894481)
XLA Ops:
  0.7 0.8 reduce-precision_convert_fusion.3
  1.5 0.3 copy.14
  1.9 2.2 %fusion.6.refs_0_.chars_ref = bf16[2048,256]{1,0:T(8,128)(2,1)} fusion(bf16[2048,3]{1,0:T(8,128)(2,1)S(1)} %copy.14, bf16[2048,128]{1,0:T(8,128)(2,1)} %param.9), kind=kLoop, calls=%fused_computation.7 | loop fusion | flops 3145728 | bytes 1585152 | tf_op jit(solution)/shard_map/concatenate | solution.py:268
  4.1 1.6 pad_maximum_fusion.refs_1_.tastes_ref
  5.7 18.4 %stats.1 = (f32[2,4096]{1,0:T(2,128)}, bf16[2048,4096]{1,0:T(8,128)(2,1)}) custom-call(bf16[2048,256]{1,0:T(8,128)(2,1)} %fusion.6.refs_0_.chars_ref, bf16[4096,256]{1,0:T(8,128)(2,1)} %pad_maximum_fusion.refs_1_.tastes_ref), custom_call_target="tpu_custom_call" | custom-call | flops 4294967296 | bytes 16777216 | tf_op jit(solution)/shard_map/stats/pallas_call | solution.py:50
  24.1 2.1 %collective-permute-start = (f32[2,4096]{1,0:T(2,128)}, f32[2,4096]{1,0:T(2,128)S(1)}, u32[]{:S(2)}, u32[]{:S(2)}) collective-permute-start(f32[2,4096]{1,0:T(2,128)} %get-tuple-element.12), channel_id=1, source_target_pairs={{0,1},{1,0},{2,3},{3,2},{4,5},{5,4},{6,7},{7,6},{8,9},{9,8},{10,11... | collective-permute-start | bytes 98312 | tf_op jit(solution)/shard_map/ppermute | solution.py:240
  26.1 5.0 %sort.15 = (s32[2048]{0:T(1024)S(1)}, s32[2048]{0:T(1024)}) sort(s32[2048]{0:T(1024)S(1)} %copy-done.7, s32[2048]{0:T(1024)S(1)} %iota.14), dimensions={0}, to_apply=%region_1.2 | sort | flops 22528 | bytes 32768 | tf_op jit(solution)/shard_map/sort | solution.py:264
  31.2 0.7 all_to_all.9
  31.8 10.2 %all-to-all-start = ((s32[32,1,64]{2,1,0:T(1,128)}), s32[32,1,64]{2,1,0:T(1,128)S(1)}, u32[]{:S(2)}, u32[]{:S(2)}) async-start(s32[32,1,64]{2,1,0:T(1,128)} %bitcast.1), calls=%async_computation | async-start | bytes 32768 | tf_op jit(solution)/shard_map/all_to_all | solution.py:265
  42.1 0.0 collective-permute-done
  42.1 0.9 fusion.23
  43.0 2.5 %collective-permute-start.1 = (f32[2,4096]{1,0:T(2,128)S(1)}, f32[2,4096]{1,0:T(2,128)S(1)}, u32[]{:S(2)}, u32[]{:S(2)}) collective-permute-start(f32[2,4096]{1,0:T(2,128)S(1)} %pad_maximum_fusion.2), channel_id=1, source_target_pairs={{0,3},{1,2},{2,1},{3,0},{4,7},{5,6},{6,5},{7,4},{8,11},{9,10},{10,... | collective-permute-start | bytes 98312 | tf_op jit(solution)/shard_map/ppermute | solution.py:240
  45.6 1.8 %collective-permute-done.1 = f32[2,4096]{1,0:T(2,128)S(1)} collective-permute-done((f32[2,4096]{1,0:T(2,128)S(1)}, f32[2,4096]{1,0:T(2,128)S(1)}, u32[]{:S(2)}, u32[]{:S(2)}) %collective-permute-start.1) | collective-permute-done | bytes 32800 | tf_op jit(solution)/shard_map/ppermute | solution.py:240
  47.4 0.1 fusion.22
  47.5 1.3 collective-permute-start.2
  48.8 0.5 fusion.3
  49.3 0.1 collective-permute-start.5
  49.4 1.1 all-to-all-done
  50.5 0.1 copy.16
  50.6 0.0 collective-permute-done.2
  50.6 0.1 fusion.21
  50.7 2.5 %collective-permute-start.3 = (f32[2,4096]{1,0:T(2,128)S(1)}, f32[2,4096]{1,0:T(2,128)S(1)}, u32[]{:S(2)}, u32[]{:S(2)}) collective-permute-start(f32[2,4096]{1,0:T(2,128)S(1)} %pad_maximum_fusion.4), channel_id=1, source_target_pairs={{0,12},{1,13},{2,14},{3,15},{4,8},{5,9},{6,10},{7,11},{8,4},{9,5},... | collective-permute-start | bytes 98312 | tf_op jit(solution)/shard_map/ppermute | solution.py:240
  53.3 0.6 subtract_bitcast_fusion.ids_ref
  53.9 2.2 %collective-permute-start.6 = (bf16[256,256]{1,0:T(8,128)(2,1)S(1)}, bf16[256,256]{1,0:T(8,128)(2,1)S(1)}, u32[]{:S(2)}, u32[]{:S(2)}) collective-permute-start(bf16[256,256]{1,0:T(8,128)(2,1)S(1)} %add.117), channel_id=1, source_target_pairs={{0,3},{1,2},{2,1},{3,0},{4,7},{5,6},{6,5},{7,4},{8,11},{9,10},{10,... | collective-permute-start | bytes 393224 | tf_op jit(solution)/shard_map/ppermute | solution.py:240
  56.1 0.0 collective-permute-done.3
  56.1 0.1 fusion.20
  56.2 2.7 %collective-permute-start.4 = (f32[2,4096]{1,0:T(2,128)S(1)}, f32[2,4096]{1,0:T(2,128)S(1)}, u32[]{:S(2)}, u32[]{:S(2)}) collective-permute-start(f32[2,4096]{1,0:T(2,128)S(1)} %pad_maximum_fusion.5), channel_id=1, source_target_pairs={{0,16},{1,17},{2,18},{3,19},{4,20},{5,21},{6,22},{7,23},{8,24},{9,... | collective-permute-start | bytes 98312 | tf_op jit(solution)/shard_map/ppermute | solution.py:240
  58.9 0.1 collective-permute-done.6
  59.1 0.1 collective-permute-start.7
  59.2 4.6 %pick_rows.1 = bf16[2048,256]{1,0:T(8,128)(2,1)} custom-call(s32[64,32]{1,0:T(8,128)} %subtract_bitcast_fusion.ids_ref, bf16[2048,256]{1,0:T(8,128)(2,1)} %fusion.6.refs_0_.chars_ref), custom_call_target="tpu_custom_call" | custom-call | flops 2147483648 | bytes 2097152 | tf_op jit(solution)/shard_map/pick_rows/pallas_call | solution.py:91
  63.8 8.3 %all-to-all-start.1 = ((bf16[32,64,256]{2,1,0:T(8,128)(2,1)}), bf16[32,64,256]{2,1,0:T(8,128)(2,1)S(1)}, u32[]{:S(2)}, u32[]{:S(2)}) async-start(bf16[32,64,256]{2,1,0:T(8,128)(2,1)} %bitcast.20), calls=%async_computation.1 | async-start | bytes 2097152 | tf_op jit(solution)/shard_map/all_to_all | solution.py:279
  72.2 2.5 %collective-permute-start.8 = (bf16[256,256]{1,0:T(8,128)(2,1)S(1)}, bf16[256,256]{1,0:T(8,128)(2,1)S(1)}, u32[]{:S(2)}, u32[]{:S(2)}) collective-permute-start(bf16[256,256]{1,0:T(8,128)(2,1)S(1)} %add.119), channel_id=1, source_target_pairs={{0,12},{1,13},{2,14},{3,15},{4,8},{5,9},{6,10},{7,11},{8,4},{9,5},... | collective-permute-start | bytes 393224 | tf_op jit(solution)/shard_map/ppermute | solution.py:240
  74.7 0.1 reduce-precision_convert_fusion.1
  74.8 3.9 %collective-permute-done.8 = bf16[256,256]{1,0:T(8,128)(2,1)S(1)} collective-permute-done((bf16[256,256]{1,0:T(8,128)(2,1)S(1)}, bf16[256,256]{1,0:T(8,128)(2,1)S(1)}, u32[]{:S(2)}, u32[]{:S(2)}) %collective-permute-start.8) | collective-permute-done | bytes 131104 | tf_op jit(solution)/shard_map/ppermute | solution.py:240
  78.8 4.3 %collective-permute-start.9 = (bf16[256,256]{1,0:T(8,128)(2,1)S(1)}, bf16[256,256]{1,0:T(8,128)(2,1)S(1)}, u32[]{:S(2)}, u32[]{:S(2)}) collective-permute-start(bf16[256,256]{1,0:T(8,128)(2,1)S(1)} %add.120), channel_id=1, source_target_pairs={{0,16},{1,17},{2,18},{3,19},{4,20},{5,21},{6,22},{7,23},{8,24},{9,... | collective-permute-start | bytes 393224 | tf_op jit(solution)/shard_map/ppermute | solution.py:240
  83.1 0.7 pad_maximum_fusion.1.rows_ref
  83.8 7.1 %collective-permute-done.9 = bf16[256,256]{1,0:T(8,128)(2,1)S(1)} collective-permute-done((bf16[256,256]{1,0:T(8,128)(2,1)S(1)}, bf16[256,256]{1,0:T(8,128)(2,1)S(1)}, u32[]{:S(2)}, u32[]{:S(2)}) %collective-permute-start.9) | collective-permute-done | bytes 131104 | tf_op jit(solution)/shard_map/ppermute | solution.py:240
  90.9 0.7 add.121.cols_ref
  91.6 4.7 %weights.1 = (bf16[256,4096]{1,0:T(8,128)(2,1)}, f32[256,128]{1,0:T(8,128)}) custom-call(bf16[4096,256]{1,0:T(8,128)(2,1)} %pad_maximum_fusion.refs_1_.tastes_ref, f32[3,4096]{1,0:T(4,128)} %pad_maximum_fusion.1.rows_ref, bf16[256,256]{1,0:T(8,128)(2,1)} %add.121.cols_ref), custom_call_target="tpu_custom_call" | custom-call | flops 536870912 | bytes 2097152 | tf_op jit(solution)/shard_map/weights/pallas_call | solution.py:144
  96.3 1.0 copy-done.4
  97.2 4.6 %place_rows.1.chars_ref = bf16[2048,256]{1,0:T(8,128)(2,1)} custom-call(s32[1,2048]{1,0:T(1,128)} %bitcast.23, bf16[2048,256]{1,0:T(8,128)(2,1)} %bitcast.19), custom_call_target="tpu_custom_call" | custom-call | flops 2147483648 | bytes 2097152 | tf_op jit(solution)/shard_map/place_rows/pallas_call | solution.py:113
  101.8 13.4 %panel.1 = (f32[2048,256]{1,0:T(8,128)}, f32[2048,128]{1,0:T(8,128)}) custom-call(bf16[2048,256]{1,0:T(8,128)(2,1)} %place_rows.1.chars_ref, bf16[4096,256]{1,0:T(8,128)(2,1)} %pad_maximum_fusion.refs_1_.tastes_ref, f32[3,4096]{1,0:T(4,128)} %pad_maximum_fusion.1.rows_ref, bf16[256,4096]{1,0:T(8,128)(2,1)} %get-tuple-element.15.weight_ref), custom_call_target="tpu_custom_call" | custom-call | flops 8589934592 | bytes 4194304 | tf_op jit(solution)/shard_map/panel/pallas_call | solution.py:187
  115.3 1.4 constant_dynamic-slice_fusion
  116.7 6.1 %collective-permute-start.10 = (f32[1024,256]{1,0:T(8,128)S(1)}, f32[1024,256]{1,0:T(8,128)}, u32[]{:S(2)}, u32[]{:S(2)}) collective-permute-start(f32[1024,256]{1,0:T(8,128)S(1)} %constant_dynamic-slice_fusion), channel_id=1, source_target_pairs={{0,32},{32,0},{64,96},{96,64},{1,33},{33,1},{65,97},{97,65},{2,34}... | collective-permute-start | bytes 3145736 | tf_op jit(solution)/shard_map/ppermute | solution.py:240
  122.8 0.1 reduce_sum.39
  122.9 0.1 collective-permute-start.11
  123.0 2.1 %collective-permute-done.11 = f32[256]{0:T(256)S(1)} collective-permute-done((f32[256]{0:T(256)S(1)}, f32[256]{0:T(256)S(1)}, u32[]{:S(2)}, u32[]{:S(2)}) %collective-permute-start.11) | collective-permute-done | bytes 1056 | tf_op jit(solution)/shard_map/ppermute | solution.py:240
  125.1 0.4 collective-permute-start.12
  125.5 2.0 %collective-permute-done.12 = f32[256]{0:T(256)S(1)} collective-permute-done((f32[256]{0:T(256)S(1)}, f32[256]{0:T(256)S(1)}, u32[]{:S(2)}, u32[]{:S(2)}) %collective-permute-start.12) | collective-permute-done | bytes 1056 | tf_op jit(solution)/shard_map/ppermute | solution.py:240
  127.5 0.0 copy-start
  127.6 1.5 multiply_convert_fusion
  129.0 0.5 collective-permute-start.13
  129.6 11.5 %collective-permute-done.13 = f16[1024,256]{1,0:T(8,128)(2,1)S(1)} collective-permute-done((f16[1024,256]{1,0:T(8,128)(2,1)S(1)}, f16[1024,256]{1,0:T(8,128)(2,1)S(1)}, u32[]{:S(2)}, u32[]{:S(2)}) %collective-permute-start.13) | collective-permute-done | bytes 524320 | tf_op jit(solution)/shard_map/ppermute | solution.py:240
  141.0 0.2 select_subtract_fusion
  141.3 1.0 fusion.9
  142.3 2.5 %collective-permute-start.14 = (f32[1024,256]{1,0:T(8,128)S(1)}, f32[1024,256]{1,0:T(8,128)S(1)}, u32[]{:S(2)}, u32[]{:S(2)}) collective-permute-start(f32[1024,256]{1,0:T(8,128)S(1)} %bitcast.16), channel_id=1, source_target_pairs={{0,32},{32,0},{64,96},{96,64},{1,33},{33,1},{65,97},{97,65},{2,34}... | collective-permute-start | bytes 3145736 | tf_op jit(solution)/shard_map/ppermute | solution.py:240
  144.8 0.7 fusion.15.factor_ref
  145.5 9.0 %share_sums.1 = f32[16,2048]{1,0:T(8,128)} custom-call(bf16[2048,4096]{1,0:T(8,128)(2,1)} %get-tuple-element.11.expo_ref, bf16[16,4096]{1,0:T(8,128)(2,1)} %fusion.15.factor_ref), custom_call_target="tpu_custom_call" | custom-call | flops 2147483648 | bytes 16777216 | tf_op jit(solution)/shard_map/share_sums/pallas_call | solution.py:223
  154.5 0.9 reduce_sum.36
  155.4 1.6 reduce_sum.37
  157.0 9.5 %psum.7 = f32[4096]{0:T(1024)S(1)} all-reduce(f32[4096]{0:T(1024)S(1)} %pad_maximum_fusion.7), channel_id=1, replica_groups=mesh['cons'=4,'prod'=32] {'cons'}, use_global_device_ids=true, to_apply=%region_3.4 | all-reduce | flops 4096 | bytes 32768 | tf_op jit(solution)/shard_map/psum | solution.py:312
  166.5 0.6 slice_bitcast_fusion
  167.1 0.9 multiply_reduce_fusion
  168.0 1.6 maximum_select_fusion
  (47 shorter events, 0.5 us)
Async XLA Ops:
  0.6 3.5 %copy-start.2 = (bf16[4096,128]{1,0:T(8,128)(2,1)S(1)}, bf16[4096,128]{1,0:T(8,128)(2,1)}, u32[]{:S(2)}) copy-start(bf16[4096,128]{1,0:T(8,128)(2,1)} %param.7) | copy-start | bytes 3145732
  5.7 20.4 %copy-start.7 = (s32[2048]{0:T(1024)S(1)}, s32[2048]{0:T(1024)}, u32[]{:S(2)}) copy-start(s32[2048]{0:T(1024)} %param.12) | copy-start | bytes 24580
  5.7 43.1 %copy-start.3 = (bf16[2048,256]{1,0:T(8,128)(2,1)S(1)}, bf16[2048,256]{1,0:T(8,128)(2,1)}, u32[]{:S(2)}) copy-start(bf16[2048,256]{1,0:T(8,128)(2,1)} %fusion.6.refs_0_.chars_ref) | copy-start | bytes 3145732
  5.7 43.1 %copy-start.9 = (s32[256]{0:T(256)S(1)}, s32[256]{0:T(256)}, u32[]{:S(2)}) copy-start(s32[256]{0:T(256)} %param.11) | copy-start | bytes 3076
  24.1 18.0 %collective-permute-start = (f32[2,4096]{1,0:T(2,128)}, f32[2,4096]{1,0:T(2,128)S(1)}, u32[]{:S(2)}, u32[]{:S(2)}) collective-permute-start(f32[2,4096]{1,0:T(2,128)} %get-tuple-element.12), channel_id=1, source_target_pairs={{0,1},{1,0},{2,3},{3,2},{4,5},{5,4},{6,7},{7,6},{8,9},{9,8},{10,11... | collective-permute-start | bytes 98312 | tf_op jit(solution)/shard_map/ppermute | solution.py:240
  31.8 18.7 %all-to-all-start = ((s32[32,1,64]{2,1,0:T(1,128)}), s32[32,1,64]{2,1,0:T(1,128)S(1)}, u32[]{:S(2)}, u32[]{:S(2)}) async-start(s32[32,1,64]{2,1,0:T(1,128)} %bitcast.1), calls=%async_computation | async-start | bytes 32768 | tf_op jit(solution)/shard_map/all_to_all | solution.py:265
  43.0 4.3 %collective-permute-start.1 = (f32[2,4096]{1,0:T(2,128)S(1)}, f32[2,4096]{1,0:T(2,128)S(1)}, u32[]{:S(2)}, u32[]{:S(2)}) collective-permute-start(f32[2,4096]{1,0:T(2,128)S(1)} %pad_maximum_fusion.2), channel_id=1, source_target_pairs={{0,3},{1,2},{2,1},{3,0},{4,7},{5,6},{6,5},{7,4},{8,11},{9,10},{10,... | collective-permute-start | bytes 98312 | tf_op jit(solution)/shard_map/ppermute | solution.py:240
  47.5 3.1 %collective-permute-start.2 = (f32[2,4096]{1,0:T(2,128)S(1)}, f32[2,4096]{1,0:T(2,128)S(1)}, u32[]{:S(2)}, u32[]{:S(2)}) collective-permute-start(f32[2,4096]{1,0:T(2,128)S(1)} %pad_maximum_fusion.3), channel_id=1, source_target_pairs={{0,4},{1,5},{2,6},{3,7},{4,0},{5,1},{6,2},{7,3},{8,12},{9,13},{10,... | collective-permute-start | bytes 98312 | tf_op jit(solution)/shard_map/ppermute | solution.py:240
  49.3 4.6 %collective-permute-start.5 = (bf16[256,256]{1,0:T(8,128)(2,1)S(1)}, bf16[256,256]{1,0:T(8,128)(2,1)S(1)}, u32[]{:S(2)}, u32[]{:S(2)}) collective-permute-start(bf16[256,256]{1,0:T(8,128)(2,1)S(1)} %fusion.3), channel_id=1, source_target_pairs={{0,1},{1,0},{2,3},{3,2},{4,5},{5,4},{6,7},{7,6},{8,9},{9,8},{10,11... | collective-permute-start | bytes 393224 | tf_op jit(solution)/shard_map/ppermute | solution.py:240
  50.7 5.3 %collective-permute-start.3 = (f32[2,4096]{1,0:T(2,128)S(1)}, f32[2,4096]{1,0:T(2,128)S(1)}, u32[]{:S(2)}, u32[]{:S(2)}) collective-permute-start(f32[2,4096]{1,0:T(2,128)S(1)} %pad_maximum_fusion.4), channel_id=1, source_target_pairs={{0,12},{1,13},{2,14},{3,15},{4,8},{5,9},{6,10},{7,11},{8,4},{9,5},... | collective-permute-start | bytes 98312 | tf_op jit(solution)/shard_map/ppermute | solution.py:240
  53.9 5.1 %collective-permute-start.6 = (bf16[256,256]{1,0:T(8,128)(2,1)S(1)}, bf16[256,256]{1,0:T(8,128)(2,1)S(1)}, u32[]{:S(2)}, u32[]{:S(2)}) collective-permute-start(bf16[256,256]{1,0:T(8,128)(2,1)S(1)} %add.117), channel_id=1, source_target_pairs={{0,3},{1,2},{2,1},{3,0},{4,7},{5,6},{6,5},{7,4},{8,11},{9,10},{10,... | collective-permute-start | bytes 393224 | tf_op jit(solution)/shard_map/ppermute | solution.py:240
  56.2 18.5 %collective-permute-start.4 = (f32[2,4096]{1,0:T(2,128)S(1)}, f32[2,4096]{1,0:T(2,128)S(1)}, u32[]{:S(2)}, u32[]{:S(2)}) collective-permute-start(f32[2,4096]{1,0:T(2,128)S(1)} %pad_maximum_fusion.5), channel_id=1, source_target_pairs={{0,16},{1,17},{2,18},{3,19},{4,20},{5,21},{6,22},{7,23},{8,24},{9,... | collective-permute-start | bytes 98312 | tf_op jit(solution)/shard_map/ppermute | solution.py:240
  59.1 13.1 %collective-permute-start.7 = (bf16[256,256]{1,0:T(8,128)(2,1)S(1)}, bf16[256,256]{1,0:T(8,128)(2,1)S(1)}, u32[]{:S(2)}, u32[]{:S(2)}) collective-permute-start(bf16[256,256]{1,0:T(8,128)(2,1)S(1)} %add.118), channel_id=1, source_target_pairs={{0,4},{1,5},{2,6},{3,7},{4,0},{5,1},{6,2},{7,3},{8,12},{9,13},{10,... | collective-permute-start | bytes 393224 | tf_op jit(solution)/shard_map/ppermute | solution.py:240
  63.8 10.9 %copy-start.6 = (f32[2,4096]{1,0:T(2,128)S(1)}, f32[2,4096]{1,0:T(2,128)}, u32[]{:S(2)}) copy-start(f32[2,4096]{1,0:T(2,128)} %get-tuple-element.12) | copy-start | bytes 98308
  63.8 19.3 %copy-start.8 = (f32[4096]{0:T(1024)S(1)}, f32[4096]{0:T(1024)}, u32[]{:S(2)}) copy-start(f32[4096]{0:T(1024)} %param.8) | copy-start | bytes 49156
  63.8 32.5 %all-to-all-start.1 = ((bf16[32,64,256]{2,1,0:T(8,128)(2,1)}), bf16[32,64,256]{2,1,0:T(8,128)(2,1)S(1)}, u32[]{:S(2)}, u32[]{:S(2)}) async-start(bf16[32,64,256]{2,1,0:T(8,128)(2,1)} %bitcast.20), calls=%async_computation.1 | async-start | bytes 2097152 | tf_op jit(solution)/shard_map/all_to_all | solution.py:279
  72.2 6.5 %collective-permute-start.8 = (bf16[256,256]{1,0:T(8,128)(2,1)S(1)}, bf16[256,256]{1,0:T(8,128)(2,1)S(1)}, u32[]{:S(2)}, u32[]{:S(2)}) collective-permute-start(bf16[256,256]{1,0:T(8,128)(2,1)S(1)} %add.119), channel_id=1, source_target_pairs={{0,12},{1,13},{2,14},{3,15},{4,8},{5,9},{6,10},{7,11},{8,4},{9,5},... | collective-permute-start | bytes 393224 | tf_op jit(solution)/shard_map/ppermute | solution.py:240
  78.8 12.1 %collective-permute-start.9 = (bf16[256,256]{1,0:T(8,128)(2,1)S(1)}, bf16[256,256]{1,0:T(8,128)(2,1)S(1)}, u32[]{:S(2)}, u32[]{:S(2)}) collective-permute-start(bf16[256,256]{1,0:T(8,128)(2,1)S(1)} %add.120), channel_id=1, source_target_pairs={{0,16},{1,17},{2,18},{3,19},{4,20},{5,21},{6,22},{7,23},{8,24},{9,... | collective-permute-start | bytes 393224 | tf_op jit(solution)/shard_map/ppermute | solution.py:240
  96.3 1.0 copy-start.4
  101.8 21.0 %copy-start.5 = (f32[256,128]{1,0:T(8,128)S(1)}, f32[256,128]{1,0:T(8,128)}, u32[]{:S(2)}) copy-start(f32[256,128]{1,0:T(8,128)} %get-tuple-element.18) | copy-start | bytes 393220
  115.3 12.3 %copy-start.1 = (f32[2048,256]{1,0:T(8,128)S(1)}, f32[2048,256]{1,0:T(8,128)}, u32[]{:S(2)}) copy-start(f32[2048,256]{1,0:T(8,128)} %get-tuple-element.17) | copy-start | bytes 6291460
  116.7 10.8 %collective-permute-start.10 = (f32[1024,256]{1,0:T(8,128)S(1)}, f32[1024,256]{1,0:T(8,128)}, u32[]{:S(2)}, u32[]{:S(2)}) collective-permute-start(f32[1024,256]{1,0:T(8,128)S(1)} %constant_dynamic-slice_fusion), channel_id=1, source_target_pairs={{0,32},{32,0},{64,96},{96,64},{1,33},{33,1},{65,97},{97,65},{2,34}... | collective-permute-start | bytes 3145736 | tf_op jit(solution)/shard_map/ppermute | solution.py:240
  122.9 2.2 %collective-permute-start.11 = (f32[256]{0:T(256)S(1)}, f32[256]{0:T(256)S(1)}, u32[]{:S(2)}, u32[]{:S(2)}) collective-permute-start(f32[256]{0:T(256)S(1)} %reduce_sum.39), channel_id=1, source_target_pairs={{0,32},{32,0},{64,96},{96,64},{1,33},{33,1},{65,97},{97,65},{2,34}... | collective-permute-start | bytes 3080 | tf_op jit(solution)/shard_map/ppermute | solution.py:240
  125.1 2.4 %collective-permute-start.12 = (f32[256]{0:T(256)S(1)}, f32[256]{0:T(256)S(1)}, u32[]{:S(2)}, u32[]{:S(2)}) collective-permute-start(f32[256]{0:T(256)S(1)} %add.127), channel_id=1, source_target_pairs={{0,64},{32,96},{64,0},{96,32},{1,65},{33,97},{65,1},{97,33},{2,66}... | collective-permute-start | bytes 3080 | tf_op jit(solution)/shard_map/ppermute | solution.py:240
  125.5 15.5 %dynamic-slice-start = ((s32[2048]{0:T(1024)}, s32[]{:T(128)}), s32[1024]{0:T(1024)S(1)}, s32[]{:S(2)}) async-start(s32[2048]{0:T(1024)} %param.12, s32[]{:T(128)} %select_n.32), calls=%async_computation.2 | async-start | bytes 8704 | tf_op jit(solution)/shard_map/dynamic_slice | solution.py:316
  127.5 13.7 %copy-start = (f32[16,128,128]{2,1,0:T(8,128)S(1)}, f32[16,128,128]{2,1,0:T(8,128)}, u32[]{:S(2)}) copy-start(f32[16,128,128]{2,1,0:T(8,128)} %param.13) | copy-start | bytes 3145732
  129.0 12.0 %collective-permute-start.13 = (f16[1024,256]{1,0:T(8,128)(2,1)S(1)}, f16[1024,256]{1,0:T(8,128)(2,1)S(1)}, u32[]{:S(2)}, u32[]{:S(2)}) collective-permute-start(f16[1024,256]{1,0:T(8,128)(2,1)S(1)} %multiply_convert_fusion), channel_id=1, source_target_pairs={{0,64},{32,96},{64,0},{96,32},{1,65},{33,97},{65,1},{97,33},{2,66}... | collective-permute-start | bytes 1572872 | tf_op jit(solution)/shard_map/ppermute | solution.py:240
  142.3 25.7 %collective-permute-start.14 = (f32[1024,256]{1,0:T(8,128)S(1)}, f32[1024,256]{1,0:T(8,128)S(1)}, u32[]{:S(2)}, u32[]{:S(2)}) collective-permute-start(f32[1024,256]{1,0:T(8,128)S(1)} %bitcast.16), channel_id=1, source_target_pairs={{0,32},{32,0},{64,96},{96,64},{1,33},{33,1},{65,97},{97,65},{2,34}... | collective-permute-start | bytes 3145736 | tf_op jit(solution)/shard_map/ppermute | solution.py:240

commit v2 on v1

--- a/solution.py
+++ b/solution.py
@@ -21,9 +21,14 @@
     return high, middle, low
 
 
+def beside_ones(tastes):
+    ones = lax.broadcasted_iota(jnp.int32, tastes.shape, 1) < 3
+    return jnp.concatenate([tastes, jnp.where(ones, 1.0, 0.0).astype(tastes.dtype)], axis=1)
+
+
 def stats_kernel(block, chunk, chars_ref, tastes_ref, stat_ref, expo_ref, util_ref):
     rows = chars_ref.shape[0]
-    tastes = tastes_ref[...]
+    tastes = beside_ones(tastes_ref[...])
     peak = jnp.full((8, block), -jnp.inf, jnp.float32)
     for start in range(0, rows, chunk):
         util = dot_nt(chars_ref[start : start + chunk, :], tastes)
@@ -52,7 +57,7 @@
         grid=(consumers // block,),
         in_specs=[
             pl.BlockSpec((rows, depth), lambda i: (0, 0)),
-            pl.BlockSpec((block, depth), lambda i: (i, 0)),
+            pl.BlockSpec((block, tastes.shape[1]), lambda i: (i, 0)),
         ],
         out_specs=[
             pl.BlockSpec((2, block), lambda i: (0, i)),
@@ -71,39 +76,43 @@
     )(chars, tastes)
 
 
-def pick_rows(ids_t, chars):
+def pick_rows(ids_t, chars, tail):
     per_pair, holders = ids_t.shape
     rows, depth = chars.shape
+    extra = tail.shape[0]
+    each = per_pair + extra
     group = max(1, 256 // per_pair)
 
-    def kernel(ids_ref, chars_ref, out_ref):
+    def kernel(ids_ref, chars_ref, tail_ref, out_ref):
         lanes = lax.broadcasted_iota(jnp.int32, (per_pair, rows), 1)
         table = chars_ref[...]
         for start in range(0, holders, group):
-            marks = [
-                jnp.where(ids_ref[:, q : q + 1] == lanes, 1.0, 0.0).astype(jnp.bfloat16)
-                for q in range(start, min(start + group, holders))
-            ]
-            hot = jnp.concatenate(marks, axis=0)
-            picked = jnp.dot(hot, table, preferred_element_type=jnp.float32)
-            out_ref[start * per_pair : start * per_pair + hot.shape[0], :] = picked.astype(jnp.bfloat16)
-
-    return pl.pallas_call(
-        kernel,
-        out_shape=jax.ShapeDtypeStruct((per_pair * holders, depth), jnp.bfloat16),
+            span = range(start, min(start + group, holders))
+            marks = [jnp.where(ids_ref[:, q : q + 1] == lanes, 1.0, 0.0).astype(jnp.bfloat16) for q in span]
+            picked = jnp.dot(jnp.concatenate(marks, axis=0), table, preferred_element_type=jnp.float32)
+            for place, q in enumerate(span):
+                mine = picked[place * per_pair : (place + 1) * per_pair, :]
+                out_ref[q * each : q * each + per_pair, :] = mine.astype(jnp.bfloat16)
+                out_ref[q * each + per_pair : (q + 1) * each, :] = tail_ref[...]
+
+    return pl.pallas_call(
+        kernel,
+        out_shape=jax.ShapeDtypeStruct((each * holders, depth), jnp.bfloat16),
         compiler_params=pltpu.CompilerParams(vmem_limit_bytes=VMEM_BYTES),
         cost_estimate=pl.CostEstimate(flops=2 * rows * rows * depth, bytes_accessed=rows * depth * 4, transcendentals=0),
         name="pick_rows",
-    )(ids_t, chars)
-
-
-def place_rows(order, received):
-    rows, depth = received.shape
+    )(ids_t, chars, tail)
+
+
+def place_rows(order, received, holders):
+    rows = order.shape[1]
+    total, depth = received.shape
+    per_pair, each = rows // holders, total // holders
     chunk = 256
 
     def kernel(order_ref, received_ref, out_ref):
         order_row = order_ref[...]
-        table = received_ref[...]
+        table = jnp.concatenate([received_ref[q * each : q * each + per_pair, :] for q in range(holders)], axis=0)
         for start in range(0, rows, chunk):
             ids = start + lax.broadcasted_iota(jnp.int32, (chunk, rows), 0)
             hot = jnp.where(ids == order_row, 1.0, 0.0).astype(jnp.bfloat16)
@@ -127,8 +136,8 @@
 
 
 def weights(tastes, row_values, col_chars):
-    consumers, depth = tastes.shape
-    cols = col_chars.shape[0]
+    consumers = tastes.shape[0]
+    cols, depth = col_chars.shape
     block = 1024
 
     def kernel(tastes_ref, rows_ref, cols_ref, weight_ref, diag_ref):
@@ -136,7 +145,7 @@
         def _():
             diag_ref[...] = jnp.zeros_like(diag_ref)
 
-        expo = jnp.exp(dot_nt(cols_ref[...], tastes_ref[...]) - rows_ref[0:1, :])
+        expo = jnp.exp(dot_nt(cols_ref[...], beside_ones(tastes_ref[...])) - rows_ref[0:1, :])
         weighted = rows_ref[2:3, :] * (expo * rows_ref[1:2, :])
         diag_ref[...] += lane_groups(weighted)
         weight_ref[...] = weighted.astype(jnp.bfloat16)
@@ -145,7 +154,7 @@
         kernel,
         grid=(consumers // block,),
         in_specs=[
-            pl.BlockSpec((block, depth), lambda i: (i, 0)),
+            pl.BlockSpec((block, tastes.shape[1]), lambda i: (i, 0)),
             pl.BlockSpec((3, block), lambda i: (0, i)),
             pl.BlockSpec((cols, depth), lambda i: (0, 0)),
         ],
@@ -165,8 +174,8 @@
     )(tastes, row_values, col_chars)
 
 
-def panel(chars, tastes, row_values, weighted):
-    rows, depth = chars.shape
+def panel(chars, part, parts, tastes, row_values, weighted):
+    rows, depth = chars.shape[0] // parts, chars.shape[1]
     consumers = tastes.shape[0]
     cols = weighted.shape[0]
     block, chunk = 1024, 256
@@ -177,7 +186,7 @@
             panel_ref[...] = jnp.zeros_like(panel_ref)
             share_ref[...] = jnp.zeros_like(share_ref)
 
-        people, weight = tastes_ref[...], weight_ref[...]
+        people, weight = beside_ones(tastes_ref[...]), weight_ref[...]
         peak, ratio = rows_ref[0:1, :], rows_ref[1:2, :]
         for start in range(0, rows, chunk):
             scaled = jnp.exp(dot_nt(chars_ref[start : start + chunk, :], people) - peak) * ratio
@@ -188,8 +197,8 @@
         kernel,
         grid=(consumers // block,),
         in_specs=[
-            pl.BlockSpec((rows, depth), lambda i: (0, 0)),
-            pl.BlockSpec((block, depth), lambda i: (i, 0)),
+            pl.BlockSpec((rows, depth), lambda i: (part, 0)),
+            pl.BlockSpec((block, tastes.shape[1]), lambda i: (i, 0)),
             pl.BlockSpec((3, block), lambda i: (0, i)),
             pl.BlockSpec((cols, block), lambda i: (0, i)),
         ],
@@ -218,17 +227,17 @@
         def _():
             out_ref[...] = jnp.zeros_like(out_ref)
 
-        out_ref[...] += dot_nt(factor_ref[...], expo_ref[...])
+        out_ref[...] += dot_nt(expo_ref[...], factor_ref[...])
 
     return pl.pallas_call(
         kernel,
         grid=(consumers // block,),
         in_specs=[
             pl.BlockSpec((rows, block), lambda i: (0, i)),
-            pl.BlockSpec((16, block), lambda i: (0, i)),
-        ],
-        out_specs=pl.BlockSpec((16, rows), lambda i: (0, 0)),
-        out_shape=jax.ShapeDtypeStruct((16, rows), jnp.float32),
+            pl.BlockSpec((128, block), lambda i: (0, i)),
+        ],
+        out_specs=pl.BlockSpec((rows, 128), lambda i: (0, 0)),
+        out_shape=jax.ShapeDtypeStruct((rows, 128), jnp.float32),
         compiler_params=pltpu.CompilerParams(vmem_limit_bytes=VMEM_BYTES),
         cost_estimate=pl.CostEstimate(flops=2 * rows * consumers * 128, bytes_accessed=rows * consumers * 2, transcendentals=0),
         name="share_sums",
@@ -261,30 +270,39 @@
     base = lax.axis_index("prod") * products
     core = lax.axis_index("cons") % 2
 
-    wanted, order = lax.sort((firm_map, lax.iota(jnp.int32, products)), num_keys=1)
-    ids = lax.all_to_all(wanted.reshape(holders, per_pair), "prod", split_axis=0, concat_axis=0, tiled=True) - base
-
     pieces = jnp.stack(split3(mean_utility), axis=1)
     chars = jnp.concatenate([characteristics, jnp.pad(pieces, ((0, 0), (0, depth - 3)))], axis=1)
-    beside = jnp.broadcast_to(lax.iota(jnp.int32, depth)[None, :] < 3, (consumers, depth)).astype(jnp.bfloat16)
-    people = jnp.concatenate([tastes, beside], axis=1)
-
+    width = 2 * depth
+
+    wanted, order = lax.sort((firm_map, lax.iota(jnp.int32, products)), num_keys=1)
+    wanted = (wanted % products).reshape(holders, per_pair)
+    digits = jnp.concatenate([wanted // 256, wanted % 256], axis=1).astype(jnp.bfloat16)
+    digits = jnp.pad(digits, ((0, 0), (0, width - 2 * per_pair)))[:, None, :]
     product_ids = base + lax.iota(jnp.int32, products)
     hits = (panel_cols[:, None] == product_ids[None, :]).astype(jnp.bfloat16)
-    col_chars = jnp.dot(hits, chars, preferred_element_type=jnp.float32).astype(jnp.bfloat16)
-
-    stat, expo = stats(chars, people)
-
-    sent = pick_rows(ids.T, chars).reshape(holders, per_pair, 2 * depth)
-    received = lax.all_to_all(sent, "prod", split_axis=0, concat_axis=0, tiled=True).reshape(products, 2 * depth)
-    firm_chars = place_rows(order.reshape(1, products), received)
-
-    masks = butterfly_masks(holders)
-    for mask in masks:
-        col_chars = col_chars + swap(col_chars, "prod", mask)
-
+    col_part = jnp.dot(hits, chars, preferred_element_type=jnp.float32).astype(jnp.bfloat16)
+    share_cols = cols // holders
+    message = jnp.concatenate([col_part.reshape(holders, share_cols, width), digits], axis=1)
+    message = jnp.pad(message, ((0, 0), (0, -(share_cols + 1) % 16), (0, 0)))
+    first = lax.all_to_all(message, "prod", split_axis=0, concat_axis=0, tiled=True)
+
+    stat, expo = stats(chars, tastes)
     local_peak = stat[0]
-    for mask in masks:
+
+    asked = first[:, share_cols, : 2 * per_pair].astype(jnp.int32)
+    ids = asked[:, :per_pair] * 256 + asked[:, per_pair:]
+    collected = jnp.sum(first[:, :share_cols, :].astype(jnp.float32), axis=0).astype(jnp.bfloat16)
+    collected = jnp.pad(collected, ((0, -share_cols % 16), (0, 0)))
+    each = per_pair + collected.shape[0]
+    sent = pick_rows(ids.T, chars, collected).reshape(holders, each, width)
+    second = lax.all_to_all(sent, "prod", split_axis=0, concat_axis=0, tiled=True)
+    col_chars = second[:, per_pair : per_pair + share_cols, :].reshape(cols, width)
+    half, quarter = products // 2, products // 4
+    kept_row = (order // half == core).astype(jnp.int32)
+    place = (order // quarter % 2) * half + kept_row * quarter + order % quarter
+    firm_chars = place_rows(place.reshape(1, products), second.reshape(holders * each, width), holders)
+
+    for mask in butterfly_masks(holders):
         other = swap(stat, "prod", mask)
         joint = jnp.maximum(stat[0], other[0])
         total = stat[1] * jnp.exp(stat[0] - joint) + other[1] * jnp.exp(other[0] - joint)
@@ -294,42 +312,55 @@
     ratio = count_products / denom
 
     row_values = jnp.stack([peak, ratio, price_coef])
-    weighted, diag_part = weights(people, row_values, col_chars)
+    weighted, diag_part = weights(tastes, row_values, col_chars)
     diagonal = jnp.sum(diag_part, axis=1)
     for mask in (1, 2):
         diagonal = diagonal + swap(diagonal, "cons", mask)
     room = 32768.0 / (count_products * jnp.maximum(diagonal, 1e-25))
-    panel_part, share_part = panel(firm_chars, people, row_values, weighted)
-
-    half = products // 2
-    kept = lax.dynamic_slice_in_dim(panel_part, core * half, half, 0)
-    given = lax.dynamic_slice_in_dim(panel_part, (1 - core) * half, half, 0)
-    chip_sum = lax.optimization_barrier(((kept + swap(given, "cons", 1)) * room[None, :]).astype(jnp.float16))
-    other_sum = swap(chip_sum, "cons", 2)
-
+
+    firm_count, block_size = inverses.shape[0], inverses.shape[1]
+    own_inverses = lax.dynamic_slice_in_dim(inverses, core * (firm_count // 2), firm_count // 2, 0)
+    firm_ids = lax.dynamic_slice_in_dim(firm_map, core * half, half, 0)
+    chip_sums, other_sums, share_parts = [], [], []
+    for part in (0, 1):
+        given, given_share = panel(firm_chars, 2 * part, 4, tastes, row_values, weighted)
+        got = swap(given, "cons", 1)
+        kept, kept_share = panel(firm_chars, 2 * part + 1, 4, tastes, row_values, weighted)
+        chip_sum = lax.optimization_barrier(((kept + got) * room[None, :]).astype(jnp.float16))
+        chip_sums.append(chip_sum)
+        other_sums.append(swap(chip_sum, "cons", 2))
+        share_parts.append((given_share, kept_share))
+
+    given_share = jnp.sum(jnp.concatenate([share_parts[0][0], share_parts[1][0]]), axis=1)
+    kept_share = jnp.sum(jnp.concatenate([share_parts[0][1], share_parts[1][1]]), axis=1)
+    first_half = jnp.where(core == 0, kept_share, given_share)
+    second_half = jnp.where(core == 0, given_share, kept_share)
     factors = jnp.stack(split3(jnp.exp(local_peak - peak) * ratio), axis=0)
-    own_shares = jnp.sum(share_sums(expo, jnp.pad(factors, ((0, 13), (0, 0)))), axis=0)
-    sums = lax.psum(jnp.concatenate([own_shares, jnp.sum(share_part, axis=1)]), "cons") / count_consumers
+    own_shares = jnp.sum(share_sums(expo, jnp.pad(factors, ((0, 125), (0, 0)))), axis=1)
+    sums = jnp.concatenate([own_shares, first_half, second_half])
+    for mask in (1, 2):
+        sums = sums + swap(sums, "cons", mask)
+    sums = sums / count_consumers
+    other_sums[1], sums = lax.optimization_barrier((other_sums[1], sums))
     shares, firm_shares = sums[:products], sums[products:]
 
-    firm_count, block_size = inverses.shape[0], inverses.shape[1]
-    firm_ids = lax.dynamic_slice_in_dim(firm_map, core * half, half, 0)
-    marks = firm_ids[:, None] == panel_cols[None, :]
-    cross = (chip_sum.astype(jnp.float32) + other_sum.astype(jnp.float32)) / (room[None, :] * count_consumers)
-    jacobian = cross - jnp.where(marks, diagonal[None, :] / count_consumers, 0.0)
-    own_inverses = lax.dynamic_slice_in_dim(inverses, core * (firm_count // 2), firm_count // 2, 0)
-    response = jnp.einsum(
-        "fab,fbc->fac",
-        own_inverses,
-        jacobian.reshape(firm_count // 2, block_size, cols),
-        precision=lax.Precision.HIGHEST,
-    ).reshape(half, cols)
-    other_response = swap(response, "cons", 1)
-    response = jnp.where(
-        core == 0,
-        jnp.concatenate([response, other_response], axis=0),
-        jnp.concatenate([other_response, response], axis=0),
-    )
+    responses = []
+    for part in (0, 1):
+        both = chip_sums[part].astype(jnp.float32) + other_sums[part].astype(jnp.float32)
+        part_ids = firm_ids[part * quarter : (part + 1) * quarter]
+        marks = part_ids[:, None] == panel_cols[None, :]
+        jacobian = both / (room[None, :] * count_consumers) - jnp.where(marks, diagonal[None, :] / count_consumers, 0.0)
+        blocks = firm_count // 4
+        response = jnp.einsum(
+            "fab,fbc->fac",
+            own_inverses[part * blocks : (part + 1) * blocks],
+            jacobian.reshape(blocks, block_size, cols),
+            precision=lax.Precision.HIGHEST,
+        ).reshape(quarter, cols)
+        responses.append((response, swap(response, "cons", 1)))
+    mine = [pair[0] for pair in responses]
+    theirs = [pair[1] for pair in responses]
+    response = jnp.where(core == 0, jnp.concatenate(mine + theirs, axis=0), jnp.concatenate(theirs + mine, axis=0))
     markup = jnp.sum(inverses * firm_shares.reshape(firm_count, 1, block_size), axis=2).reshape(products)
     return (shares, markup, response)
 

time: 172 us -> 150 us (0.87)
  starting transfers between devices: 48.5 us -> 35.7 us
  Pallas kernels: 54.7 us -> 64.9 us
  blocking collectives: 9.45 us -> 0 us
  waiting for transfers between devices: 29.6 us -> 22.8 us
    ppermute x15, waiting for transfers between devices: 28.5 us -> 16.2 us  [swap(): return lax.ppermute(value, axis, [(i, i ^ mask) for i in range(size)])]
    pallas_call x1 -> x4, Pallas kernels: 13.4 us -> 23.8 us  [panel(): pl.pallas_call(kernel, grid=(consumers // block,), in_specs=[pl.BlockSpec...]
    psum x1 -> x0, blocking collectives: 9.45 us -> none  [body(): lax.psum(jnp.concatenate([own_shares, jnp.sum(share_part, axis=1)]), 'cons')]
    ppermute x15, starting transfers between devices: 29.9 us -> 24.8 us  [swap(): return lax.ppermute(value, axis, [(i, i ^ mask) for i in range(size)])]
    all_to_all x1, starting transfers between devices: 10.2 us -> 6.11 us  [body(): lax.all_to_all(message, 'prod', split_axis=0, concat_axis=0, tiled=True)]
    all_to_all x1, waiting for transfers between devices: 1.12 us -> 4.63 us  [body(): lax.all_to_all(message, 'prod', split_axis=0, concat_axis=0, tiled=True)]
    all_to_all x1, starting transfers between devices: 8.35 us -> 4.85 us  [body(): lax.all_to_all(sent, 'prod', split_axis=0, concat_axis=0, tiled=True)]
    all_to_all x1, waiting for transfers between devices: 0.01 us -> 2 us  [body(): lax.all_to_all(sent, 'prod', split_axis=0, concat_axis=0, tiled=True)]
  transfers between devices with their start and end apart: 17 -> 17, of which waited for: 8 -> 9; matrix products, arithmetic and copies ran while one was open for 8% -> 10% of each run, Pallas kernels for 11% -> 6%
where the time goes in v2:
time: 150 us; the launch traced here: 149 us
  Pallas kernels  64.9 us (43%)
  starting transfers between devices  35.7 us (24%)
  waiting for transfers between devices  22.8 us (15%)
  other arithmetic  20 us (13%)
  local copies, waits for them, and re-layouts  2.8 us (2%)
  matrix products  1.66 us (1%)
    ppermute x15, starting transfers between devices, swap(): return lax.ppermute(value, axis, [(i, i ^ mask) for i in range(size)])  24.8 us
    pallas_call x4, Pallas kernels, panel(): pl.pallas_call(kernel, grid=(consumers // block,), in_specs=[pl.BlockSpec...  23.8 us
    pallas_call x1, Pallas kernels, stats(): pl.pallas_call(kernel, grid=(consumers // block,), in_specs=[pl.BlockSpec...  17.8 us
    ppermute x15, waiting for transfers between devices, swap(): return lax.ppermute(value, axis, [(i, i ^ mask) for i in range(size)])  16.2 us
    pallas_call x1, Pallas kernels, share_sums(): pl.pallas_call(kernel, grid=(consumers // block,), in_specs=[pl.BlockSpec...  9.52 us
    all_to_all x1, starting transfers between devices, body(): lax.all_to_all(message, 'prod', split_axis=0, concat_axis=0, tiled=True)  6.11 us
    all_to_all x1, starting transfers between devices, body(): lax.all_to_all(sent, 'prod', split_axis=0, concat_axis=0, tiled=True)  4.85 us
    pallas_call x1, Pallas kernels, pick_rows(): pl.pallas_call(kernel, out_shape=jax.ShapeDtypeStruct((each * holders, de...  4.67 us
  transfers between devices with their start and end apart: 17, of which 9 were waited for; matrix products, arithmetic and copies ran while one was open for 10% of the time, Pallas kernels for 6%

profile of v2, /device:TPU:1, one launch (start us, length us, event | category | flops | bytes accessed | tf_op | source)
XLA Modules:
  0.0 148.9 jit_solution(9598219873489770624)
XLA Ops:
  0.6 0.7 reduce-precision_convert_fusion.3
  1.4 0.3 copy.45
  1.7 2.2 %fusion.12.chars_ref.refs_0_ = bf16[2048,256]{1,0:T(8,128)(2,1)} fusion(bf16[2048,3]{1,0:T(8,128)(2,1)S(1)} %copy.45, bf16[2048,128]{1,0:T(8,128)(2,1)} %param.9), kind=kLoop, calls=%fused_computation.11 | loop fusion | flops 3145728 | bytes 1585152 | tf_op jit(solution)/shard_map/concatenate | solution.py:274
  4.0 17.8 %stats.1 = (f32[2,4096]{1,0:T(2,128)}, bf16[2048,4096]{1,0:T(8,128)(2,1)}) custom-call(bf16[2048,256]{1,0:T(8,128)(2,1)} %fusion.12.chars_ref.refs_0_, bf16[4096,128]{1,0:T(8,128)(2,1)} %tastes_ref.9), custom_call_target="tpu_custom_call" | custom-call | flops 4294967296 | bytes 16777216 | tf_op jit(solution)/shard_map/stats/pallas_call | solution.py:55
  21.8 2.0 %collective-permute-start = (f32[2,4096]{1,0:T(2,128)}, f32[2,4096]{1,0:T(2,128)S(1)}, u32[]{:S(2)}, u32[]{:S(2)}) collective-permute-start(f32[2,4096]{1,0:T(2,128)} %get-tuple-element.21), channel_id=1, source_target_pairs={{0,1},{1,0},{2,3},{3,2},{4,5},{5,4},{6,7},{7,6},{8,9},{9,8},{10,11... | collective-permute-start | bytes 98312 | tf_op jit(solution)/shard_map/ppermute | solution.py:249
  23.9 4.4 %sort.15 = (s32[2048]{0:T(1024)S(1)}, s32[2048]{0:T(1024)S(1)}) sort(s32[2048]{0:T(1024)S(1)} %copy-done.9, s32[2048]{0:T(1024)S(1)} %iota.8), dimensions={0}, to_apply=%region_0.1 | sort | flops 22528 | bytes 32768 | tf_op jit(solution)/shard_map/sort | solution.py:277
  28.4 0.1 copy.46
  28.6 0.9 fusion.40
  29.5 1.9 %collective-permute-start.1 = (f32[2,4096]{1,0:T(2,128)S(1)}, f32[2,4096]{1,0:T(2,128)S(1)}, u32[]{:S(2)}, u32[]{:S(2)}) collective-permute-start(f32[2,4096]{1,0:T(2,128)S(1)} %pad_maximum_fusion.1), channel_id=1, source_target_pairs={{0,3},{1,2},{2,1},{3,0},{4,7},{5,6},{6,5},{7,4},{8,11},{9,10},{10,... | collective-permute-start | bytes 98312 | tf_op jit(solution)/shard_map/ppermute | solution.py:249
  31.4 0.5 fusion.9
  31.9 0.1 copy.50
  32.1 1.5 %collective-permute-done.1 = f32[2,4096]{1,0:T(2,128)S(1)} collective-permute-done((f32[2,4096]{1,0:T(2,128)S(1)}, f32[2,4096]{1,0:T(2,128)S(1)}, u32[]{:S(2)}, u32[]{:S(2)}) %collective-permute-start.1) | collective-permute-done | bytes 32800 | tf_op jit(solution)/shard_map/ppermute | solution.py:249
  33.7 1.7 %collective-permute-start.2 = (f32[2,4096]{1,0:T(2,128)S(1)}, f32[2,4096]{1,0:T(2,128)S(1)}, u32[]{:S(2)}, u32[]{:S(2)}) collective-permute-start(f32[2,4096]{1,0:T(2,128)S(1)} %pad_maximum_fusion.2), channel_id=1, source_target_pairs={{0,4},{1,5},{2,6},{3,7},{4,0},{5,1},{6,2},{7,3},{8,12},{9,13},{10,... | collective-permute-start | bytes 98312 | tf_op jit(solution)/shard_map/ppermute | solution.py:249
  35.4 0.1 fusion.34
  35.5 1.2 collective-permute-done.2
  36.8 3.7 %collective-permute-start.3 = (f32[2,4096]{1,0:T(2,128)S(1)}, f32[2,4096]{1,0:T(2,128)S(1)}, u32[]{:S(2)}, u32[]{:S(2)}) collective-permute-start(f32[2,4096]{1,0:T(2,128)S(1)} %pad_maximum_fusion.3), channel_id=1, source_target_pairs={{0,12},{1,13},{2,14},{3,15},{4,8},{5,9},{6,10},{7,11},{8,4},{9,5},... | collective-permute-start | bytes 98312 | tf_op jit(solution)/shard_map/ppermute | solution.py:249
  40.5 0.8 fusion.23
  41.2 6.1 %all-to-all-start = ((bf16[32,16,256]{2,1,0:T(8,128)(2,1)}), bf16[32,16,256]{2,1,0:T(8,128)(2,1)S(1)}, u32[]{:S(2)}, u32[]{:S(2)}) async-start(bf16[32,16,256]{2,1,0:T(8,128)(2,1)} %fusion.23), calls=%async_computation | async-start | bytes 524288 | tf_op jit(solution)/shard_map/all_to_all | solution.py:287
  47.5 2.8 %collective-permute-start.4 = (f32[2,4096]{1,0:T(2,128)S(1)}, f32[2,4096]{1,0:T(2,128)S(1)}, u32[]{:S(2)}, u32[]{:S(2)}) collective-permute-start(f32[2,4096]{1,0:T(2,128)S(1)} %pad_maximum_fusion.4), channel_id=1, source_target_pairs={{0,16},{1,17},{2,18},{3,19},{4,20},{5,21},{6,22},{7,23},{8,24},{9,... | collective-permute-start | bytes 98312 | tf_op jit(solution)/shard_map/ppermute | solution.py:249
  50.3 0.6 fusion.46
  50.9 0.9 collective-permute-done.4
  51.8 0.1 reduce-precision_convert_fusion.1
  52.0 4.6 %all-to-all-done = bf16[32,16,256]{2,1,0:T(8,128)(2,1)S(1)} async-done(((bf16[32,16,256]{2,1,0:T(8,128)(2,1)}), bf16[32,16,256]{2,1,0:T(8,128)(2,1)S(1)}, u32[]{:S(2)}, u32[]{:S(2)}) %all-to-all-start) | async-done | bytes 262176 | tf_op jit(solution)/shard_map/all_to_all | solution.py:287
  56.6 0.1 copy.54
  56.7 0.6 fusion.26.ids_ref
  57.4 0.6 pad.23.tail_ref
  58.0 4.7 %pick_rows.1 = bf16[2560,256]{1,0:T(8,128)(2,1)} custom-call(s32[64,32]{1,0:T(8,128)} %fusion.26.ids_ref, bf16[2048,256]{1,0:T(8,128)(2,1)} %fusion.12.chars_ref.refs_0_, bf16[16,256]{1,0:T(8,128)(2,1)} %pad.23.tail_ref), custom_call_target="tpu_custom_call" | custom-call | flops 2147483648 | bytes 2097152 | tf_op jit(solution)/shard_map/pick_rows/pallas_call | solution.py:98
  62.7 4.8 %all-to-all-start.1 = ((bf16[32,80,256]{2,1,0:T(8,128)(2,1)}), bf16[32,80,256]{2,1,0:T(8,128)(2,1)S(1)}, u32[]{:S(2)}, u32[]{:S(2)}) async-start(bf16[32,80,256]{2,1,0:T(8,128)(2,1)} %bitcast.32), calls=%async_computation.1 | async-start | bytes 2621440 | tf_op jit(solution)/shard_map/all_to_all | solution.py:298
  67.6 1.2 fusion.14.factor_ref
  68.7 9.5 %share_sums.1 = f32[2048,128]{1,0:T(8,128)} custom-call(bf16[2048,4096]{1,0:T(8,128)(2,1)} %get-tuple-element.26.expo_ref, bf16[128,4096]{1,0:T(8,128)(2,1)} %fusion.14.factor_ref), custom_call_target="tpu_custom_call" | custom-call | flops 2147483648 | bytes 16777216 | tf_op jit(solution)/shard_map/share_sums/pallas_call | solution.py:232
  78.2 1.6 %reduce_sum.59 = f32[2048]{0:T(1024)S(1)} reduce(f32[2048,128]{1,0:T(8,128)} %share_sums.1, f32[]{:T(128)} %constant.121.clone.1), dimensions={1}, to_apply=%region_3.4 | reduce | flops 260096 | bytes 1056772 | tf_op jit(solution)/shard_map/reduce_sum | solution.py:339
  79.8 0.7 pad_maximum_fusion.rows_ref
  80.5 2.0 %all-to-all-done.1 = bf16[32,80,256]{2,1,0:T(8,128)(2,1)S(1)} async-done(((bf16[32,80,256]{2,1,0:T(8,128)(2,1)}), bf16[32,80,256]{2,1,0:T(8,128)(2,1)S(1)}, u32[]{:S(2)}, u32[]{:S(2)}) %all-to-all-start.1) | async-done | bytes 1310752 | tf_op jit(solution)/shard_map/all_to_all | solution.py:298
  82.5 0.7 slice_bitcast_fusion.cols_ref
  83.3 4.5 %weights.1 = (bf16[256,4096]{1,0:T(8,128)(2,1)}, f32[256,128]{1,0:T(8,128)}) custom-call(bf16[4096,128]{1,0:T(8,128)(2,1)} %tastes_ref.9, f32[3,4096]{1,0:T(4,128)} %pad_maximum_fusion.rows_ref, bf16[256,256]{1,0:T(8,128)(2,1)} %slice_bitcast_fusion.cols_ref), custom_call_target="tpu_custom_call" | custom-call | flops 536870912 | bytes 2097152 | tf_op jit(solution)/shard_map/weights/pallas_call | solution.py:153
  87.7 4.7 %place_rows.1.chars_ref = bf16[2048,256]{1,0:T(8,128)(2,1)} custom-call(s32[1,2048]{1,0:T(1,128)} %bitcast.35, bf16[2560,256]{1,0:T(8,128)(2,1)} %bitcast.31), custom_call_target="tpu_custom_call" | custom-call | flops 2147483648 | bytes 2097152 | tf_op jit(solution)/shard_map/place_rows/pallas_call | solution.py:122
  92.4 5.9 %panel.5 = (f32[512,256]{1,0:T(8,128)}, f32[512,128]{1,0:T(8,128)}) custom-call(bf16[2048,256]{1,0:T(8,128)(2,1)} %place_rows.1.chars_ref, bf16[4096,128]{1,0:T(8,128)(2,1)} %tastes_ref.9, f32[3,4096]{1,0:T(4,128)} %pad_maximum_fusion.rows_ref, bf16[256,4096]{1,0:T(8,128)(2,1)} %get-tuple-element.22.weight_ref), custom_call_target="tpu_custom_call" | custom-call | flops 2147483648 | bytes 1048576 | tf_op jit(solution)/shard_map/panel/pallas_call | solution.py:196
  98.3 5.9 %panel.7 = (f32[512,256]{1,0:T(8,128)}, f32[512,128]{1,0:T(8,128)}) custom-call(bf16[2048,256]{1,0:T(8,128)(2,1)} %place_rows.1.chars_ref, bf16[4096,128]{1,0:T(8,128)(2,1)} %tastes_ref.9, f32[3,4096]{1,0:T(4,128)} %pad_maximum_fusion.rows_ref, bf16[256,4096]{1,0:T(8,128)(2,1)} %get-tuple-element.22.weight_ref), custom_call_target="tpu_custom_call" | custom-call | flops 2147483648 | bytes 1048576 | tf_op jit(solution)/shard_map/panel/pallas_call | solution.py:196
  104.2 5.9 %panel.4 = (f32[512,256]{1,0:T(8,128)}, f32[512,128]{1,0:T(8,128)}) custom-call(bf16[2048,256]{1,0:T(8,128)(2,1)} %place_rows.1.chars_ref, bf16[4096,128]{1,0:T(8,128)(2,1)} %tastes_ref.9, f32[3,4096]{1,0:T(4,128)} %pad_maximum_fusion.rows_ref, bf16[256,4096]{1,0:T(8,128)(2,1)} %get-tuple-element.22.weight_ref), custom_call_target="tpu_custom_call" | custom-call | flops 2147483648 | bytes 1048576 | tf_op jit(solution)/shard_map/panel/pallas_call | solution.py:196
  110.1 6.0 %panel.6 = (f32[512,256]{1,0:T(8,128)}, f32[512,128]{1,0:T(8,128)}) custom-call(bf16[2048,256]{1,0:T(8,128)(2,1)} %place_rows.1.chars_ref, bf16[4096,128]{1,0:T(8,128)(2,1)} %tastes_ref.9, f32[3,4096]{1,0:T(4,128)} %pad_maximum_fusion.rows_ref, bf16[256,4096]{1,0:T(8,128)(2,1)} %get-tuple-element.22.weight_ref), custom_call_target="tpu_custom_call" | custom-call | flops 2147483648 | bytes 1048576 | tf_op jit(solution)/shard_map/panel/pallas_call | solution.py:196
  116.2 6.6 %collective-permute-start.5 = (f32[512,256]{1,0:T(8,128)}, f32[512,256]{1,0:T(8,128)S(1)}, u32[]{:S(2)}, u32[]{:S(2)}) collective-permute-start(f32[512,256]{1,0:T(8,128)} %get-tuple-element.24), channel_id=1, source_target_pairs={{0,32},{32,0},{64,96},{96,64},{1,33},{33,1},{65,97},{97,65},{2,34}... | collective-permute-start | bytes 1572872 | tf_op jit(solution)/shard_map/ppermute | solution.py:249
  122.8 0.1 reduce_sum.58
  122.9 0.1 collective-permute-start.6
  123.0 0.5 collective-permute-start.11
  123.5 0.2 maximum_reduce_fusion.1
  123.8 1.2 maximum_reduce_fusion
  125.0 0.5 collective-permute-start.7
  125.5 0.4 collective-permute-start.9
  125.8 1.7 %collective-permute-done.7 = f32[256]{0:T(256)S(1)} collective-permute-done((f32[256]{0:T(256)S(1)}, f32[256]{0:T(256)S(1)}, u32[]{:S(2)}, u32[]{:S(2)}) %collective-permute-start.7) | collective-permute-done | bytes 1056 | tf_op jit(solution)/shard_map/ppermute | solution.py:249
  127.5 0.5 collective-permute-start.10
  128.0 1.3 multiply_convert_fusion
  129.3 1.1 collective-permute-start.8
  130.4 0.4 collective-permute-start.12
  130.9 4.9 %collective-permute-done.8 = f16[512,256]{1,0:T(8,128)(2,1)S(1)} collective-permute-done((f16[512,256]{1,0:T(8,128)(2,1)S(1)}, f16[512,256]{1,0:T(8,128)(2,1)S(1)}, u32[]{:S(2)}, u32[]{:S(2)}) %collective-permute-start.8) | collective-permute-done | bytes 262176 | tf_op jit(solution)/shard_map/ppermute | solution.py:249
  135.8 5.6 %collective-permute-done.12 = f16[512,256]{1,0:T(8,128)(2,1)S(1)} collective-permute-done((f16[512,256]{1,0:T(8,128)(2,1)S(1)}, f16[512,256]{1,0:T(8,128)(2,1)S(1)}, u32[]{:S(2)}, u32[]{:S(2)}) %collective-permute-start.12) | collective-permute-done | bytes 262176 | tf_op jit(solution)/shard_map/ppermute | solution.py:249
  141.4 0.2 select_subtract_fusion.1
  141.7 0.6 fusion.21
  142.3 2.4 %collective-permute-start.13 = (f32[512,256]{1,0:T(8,128)S(1)}, f32[512,256]{1,0:T(8,128)S(1)}, u32[]{:S(2)}, u32[]{:S(2)}) collective-permute-start(f32[512,256]{1,0:T(8,128)S(1)} %bitcast.25), channel_id=1, source_target_pairs={{0,32},{32,0},{64,96},{96,64},{1,33},{33,1},{65,97},{97,65},{2,34}... | collective-permute-start | bytes 1572872 | tf_op jit(solution)/shard_map/ppermute | solution.py:249
  144.7 0.6 fusion.19
  145.3 0.1 collective-permute-start.14
  145.4 0.6 slice_bitcast_fusion.1
  146.0 0.9 multiply_reduce_fusion
  147.0 0.3 collective-permute-done.14
  147.3 1.6 %maximum_select_fusion = f32[2048,256]{1,0:T(8,128)} fusion(f32[512,256]{1,0:T(8,128)S(1)} %collective-permute-done.14, f32[512,256]{1,0:T(8,128)S(1)} %collective-permute-done.13, f32[512,256]{1,0:T(8,128)S(1)} %bitcast.28, f32[512,256]{1,0:T(8,128)S(1)} %bitcast.26, pred[]{:T(512)S(6)} %eq.61), kind=kLoop, calls=%fused_computation.5 | loop fusion | flops 3670016 | bytes 4194305 | tf_op jit(solution)/shard_map/jit(_where)/select_n | solution.py:363
  (65 shorter events, 0.8 us)
Async XLA Ops:
  4.0 19.9 %copy-start.9 = (s32[2048]{0:T(1024)S(1)}, s32[2048]{0:T(1024)}, u32[]{:S(2)}) copy-start(s32[2048]{0:T(1024)} %param.12) | copy-start | bytes 24580
  4.0 27.4 %copy-start.2 = (bf16[2048,256]{1,0:T(8,128)(2,1)S(1)}, bf16[2048,256]{1,0:T(8,128)(2,1)}, u32[]{:S(2)}) copy-start(bf16[2048,256]{1,0:T(8,128)(2,1)} %fusion.12.chars_ref.refs_0_) | copy-start | bytes 3145732
  4.0 27.4 %copy-start.11 = (s32[256]{0:T(256)S(1)}, s32[256]{0:T(256)}, u32[]{:S(2)}) copy-start(s32[256]{0:T(256)} %param.11) | copy-start | bytes 3076
  21.8 30.0 %copy-start.8 = (f32[2,4096]{1,0:T(2,128)S(1)}, f32[2,4096]{1,0:T(2,128)}, u32[]{:S(2)}) copy-start(f32[2,4096]{1,0:T(2,128)} %get-tuple-element.21) | copy-start | bytes 98308
  21.8 6.7 %collective-permute-start = (f32[2,4096]{1,0:T(2,128)}, f32[2,4096]{1,0:T(2,128)S(1)}, u32[]{:S(2)}, u32[]{:S(2)}) collective-permute-start(f32[2,4096]{1,0:T(2,128)} %get-tuple-element.21), channel_id=1, source_target_pairs={{0,1},{1,0},{2,3},{3,2},{4,5},{5,4},{6,7},{7,6},{8,9},{9,8},{10,11... | collective-permute-start | bytes 98312 | tf_op jit(solution)/shard_map/ppermute | solution.py:249
  29.5 4.1 %collective-permute-start.1 = (f32[2,4096]{1,0:T(2,128)S(1)}, f32[2,4096]{1,0:T(2,128)S(1)}, u32[]{:S(2)}, u32[]{:S(2)}) collective-permute-start(f32[2,4096]{1,0:T(2,128)S(1)} %pad_maximum_fusion.1), channel_id=1, source_target_pairs={{0,3},{1,2},{2,1},{3,0},{4,7},{5,6},{6,5},{7,4},{8,11},{9,10},{10,... | collective-permute-start | bytes 98312 | tf_op jit(solution)/shard_map/ppermute | solution.py:249
  33.7 3.0 %collective-permute-start.2 = (f32[2,4096]{1,0:T(2,128)S(1)}, f32[2,4096]{1,0:T(2,128)S(1)}, u32[]{:S(2)}, u32[]{:S(2)}) collective-permute-start(f32[2,4096]{1,0:T(2,128)S(1)} %pad_maximum_fusion.2), channel_id=1, source_target_pairs={{0,4},{1,5},{2,6},{3,7},{4,0},{5,1},{6,2},{7,3},{8,12},{9,13},{10,... | collective-permute-start | bytes 98312 | tf_op jit(solution)/shard_map/ppermute | solution.py:249
  36.8 10.5 %collective-permute-start.3 = (f32[2,4096]{1,0:T(2,128)S(1)}, f32[2,4096]{1,0:T(2,128)S(1)}, u32[]{:S(2)}, u32[]{:S(2)}) collective-permute-start(f32[2,4096]{1,0:T(2,128)S(1)} %pad_maximum_fusion.3), channel_id=1, source_target_pairs={{0,12},{1,13},{2,14},{3,15},{4,8},{5,9},{6,10},{7,11},{8,4},{9,5},... | collective-permute-start | bytes 98312 | tf_op jit(solution)/shard_map/ppermute | solution.py:249
  41.2 15.4 %all-to-all-start = ((bf16[32,16,256]{2,1,0:T(8,128)(2,1)}), bf16[32,16,256]{2,1,0:T(8,128)(2,1)S(1)}, u32[]{:S(2)}, u32[]{:S(2)}) async-start(bf16[32,16,256]{2,1,0:T(8,128)(2,1)} %fusion.23), calls=%async_computation | async-start | bytes 524288 | tf_op jit(solution)/shard_map/all_to_all | solution.py:287
  47.5 4.4 %collective-permute-start.4 = (f32[2,4096]{1,0:T(2,128)S(1)}, f32[2,4096]{1,0:T(2,128)S(1)}, u32[]{:S(2)}, u32[]{:S(2)}) collective-permute-start(f32[2,4096]{1,0:T(2,128)S(1)} %pad_maximum_fusion.4), channel_id=1, source_target_pairs={{0,16},{1,17},{2,18},{3,19},{4,20},{5,21},{6,22},{7,23},{8,24},{9,... | collective-permute-start | bytes 98312 | tf_op jit(solution)/shard_map/ppermute | solution.py:249
  62.7 19.8 %all-to-all-start.1 = ((bf16[32,80,256]{2,1,0:T(8,128)(2,1)}), bf16[32,80,256]{2,1,0:T(8,128)(2,1)S(1)}, u32[]{:S(2)}, u32[]{:S(2)}) async-start(bf16[32,80,256]{2,1,0:T(8,128)(2,1)} %bitcast.32), calls=%async_computation.1 | async-start | bytes 2621440 | tf_op jit(solution)/shard_map/all_to_all | solution.py:298
  68.7 11.1 %copy-start.10 = (f32[4096]{0:T(1024)S(1)}, f32[4096]{0:T(1024)}, u32[]{:S(2)}) copy-start(f32[4096]{0:T(1024)} %param.8) | copy-start | bytes 49156
  82.5 5.2 %copy-start.1 = (bf16[32,80,256]{2,1,0:T(8,128)(2,1)}, bf16[32,80,256]{2,1,0:T(8,128)(2,1)S(1)}, u32[]{:S(2)}) copy-start(bf16[32,80,256]{2,1,0:T(8,128)(2,1)S(1)} %all-to-all-done.1) | copy-start | bytes 3932164
  110.1 12.7 %copy-start.7 = (f32[256,128]{1,0:T(8,128)S(1)}, f32[256,128]{1,0:T(8,128)}, u32[]{:S(2)}) copy-start(f32[256,128]{1,0:T(8,128)} %get-tuple-element.25) | copy-start | bytes 393220
  110.1 12.9 %copy-start.12 = (f32[512,256]{1,0:T(8,128)S(1)}, f32[512,256]{1,0:T(8,128)}, u32[]{:S(2)}) copy-start(f32[512,256]{1,0:T(8,128)} %get-tuple-element.33) | copy-start | bytes 1572868
  110.1 13.4 %copy-start.4 = (f32[512,128]{1,0:T(8,128)S(1)}, f32[512,128]{1,0:T(8,128)}, u32[]{:S(2)}) copy-start(f32[512,128]{1,0:T(8,128)} %get-tuple-element.30) | copy-start | bytes 786436
  110.1 13.4 %copy-start.5 = (f32[512,128]{1,0:T(8,128)S(1)}, f32[512,128]{1,0:T(8,128)}, u32[]{:S(2)}) copy-start(f32[512,128]{1,0:T(8,128)} %get-tuple-element.29) | copy-start | bytes 786436
  110.1 13.6 %copy-start.6 = (f32[512,128]{1,0:T(8,128)S(1)}, f32[512,128]{1,0:T(8,128)}, u32[]{:S(2)}) copy-start(f32[512,128]{1,0:T(8,128)} %get-tuple-element.28) | copy-start | bytes 786436
  110.1 17.9 %copy-start.3 = (f32[512,256]{1,0:T(8,128)S(1)}, f32[512,256]{1,0:T(8,128)}, u32[]{:S(2)}) copy-start(f32[512,256]{1,0:T(8,128)} %get-tuple-element.23) | copy-start | bytes 1572868
  116.2 14.7 %dynamic-slice-start = ((s32[2048]{0:T(1024)}, s32[]{:T(128)}), s32[1024]{0:T(1024)S(1)}, s32[]{:S(2)}) async-start(s32[2048]{0:T(1024)} %param.12, s32[]{:T(128)} %select_n.86), calls=%async_computation.2 | async-start | bytes 8704 | tf_op jit(solution)/shard_map/dynamic_slice | solution.py:323
  116.2 11.8 %collective-permute-start.5 = (f32[512,256]{1,0:T(8,128)}, f32[512,256]{1,0:T(8,128)S(1)}, u32[]{:S(2)}, u32[]{:S(2)}) collective-permute-start(f32[512,256]{1,0:T(8,128)} %get-tuple-element.24), channel_id=1, source_target_pairs={{0,32},{32,0},{64,96},{96,64},{1,33},{33,1},{65,97},{97,65},{2,34}... | collective-permute-start | bytes 1572872 | tf_op jit(solution)/shard_map/ppermute | solution.py:249
  122.9 2.0 %collective-permute-start.6 = (f32[256]{0:T(256)S(1)}, f32[256]{0:T(256)S(1)}, u32[]{:S(2)}, u32[]{:S(2)}) collective-permute-start(f32[256]{0:T(256)S(1)} %reduce_sum.58), channel_id=1, source_target_pairs={{0,32},{32,0},{64,96},{96,64},{1,33},{33,1},{65,97},{97,65},{2,34}... | collective-permute-start | bytes 3080 | tf_op jit(solution)/shard_map/ppermute | solution.py:249
  123.0 5.0 %collective-permute-start.11 = (f32[512,256]{1,0:T(8,128)S(1)}, f32[512,256]{1,0:T(8,128)S(1)}, u32[]{:S(2)}, u32[]{:S(2)}) collective-permute-start(f32[512,256]{1,0:T(8,128)S(1)} %copy-done.12), channel_id=1, source_target_pairs={{0,32},{32,0},{64,96},{96,64},{1,33},{33,1},{65,97},{97,65},{2,34}... | collective-permute-start | bytes 1572872 | tf_op jit(solution)/shard_map/ppermute | solution.py:249
  125.0 2.5 %collective-permute-start.7 = (f32[256]{0:T(256)S(1)}, f32[256]{0:T(256)S(1)}, u32[]{:S(2)}, u32[]{:S(2)}) collective-permute-start(f32[256]{0:T(256)S(1)} %add.155), channel_id=1, source_target_pairs={{0,64},{32,96},{64,0},{96,32},{1,65},{33,97},{65,1},{97,33},{2,66}... | collective-permute-start | bytes 3080 | tf_op jit(solution)/shard_map/ppermute | solution.py:249
  125.5 2.0 %collective-permute-start.9 = (f32[4096]{0:T(1024)S(1)}, f32[4096]{0:T(1024)S(1)}, u32[]{:S(2)}, u32[]{:S(2)}) collective-permute-start(f32[4096]{0:T(1024)S(1)} %pad_maximum_fusion.6), channel_id=1, source_target_pairs={{0,32},{32,0},{64,96},{96,64},{1,33},{33,1},{65,97},{97,65},{2,34}... | collective-permute-start | bytes 49160 | tf_op jit(solution)/shard_map/ppermute | solution.py:249
  127.5 3.4 %collective-permute-start.10 = (f32[4096]{0:T(1024)S(1)}, f32[4096]{0:T(1024)S(1)}, u32[]{:S(2)}, u32[]{:S(2)}) collective-permute-start(f32[4096]{0:T(1024)S(1)} %fusion.54), channel_id=1, source_target_pairs={{0,64},{32,96},{64,0},{96,32},{1,65},{33,97},{65,1},{97,33},{2,66}... | collective-permute-start | bytes 49160 | tf_op jit(solution)/shard_map/ppermute | solution.py:249
  128.0 13.7 %copy-start = (f32[16,128,128]{2,1,0:T(8,128)S(1)}, f32[16,128,128]{2,1,0:T(8,128)}, u32[]{:S(2)}) copy-start(f32[16,128,128]{2,1,0:T(8,128)} %param.13) | copy-start | bytes 3145732
  129.3 6.5 %collective-permute-start.8 = (f16[512,256]{1,0:T(8,128)(2,1)S(1)}, f16[512,256]{1,0:T(8,128)(2,1)S(1)}, u32[]{:S(2)}, u32[]{:S(2)}) collective-permute-start(f16[512,256]{1,0:T(8,128)(2,1)S(1)} %get-tuple-element.66), channel_id=1, source_target_pairs={{0,64},{32,96},{64,0},{96,32},{1,65},{33,97},{65,1},{97,33},{2,66}... | collective-permute-start | bytes 786440 | tf_op jit(solution)/shard_map/ppermute | solution.py:249
  130.4 11.0 %collective-permute-start.12 = (f16[512,256]{1,0:T(8,128)(2,1)S(1)}, f16[512,256]{1,0:T(8,128)(2,1)S(1)}, u32[]{:S(2)}, u32[]{:S(2)}) collective-permute-start(f16[512,256]{1,0:T(8,128)(2,1)S(1)} %get-tuple-element.65), channel_id=1, source_target_pairs={{0,64},{32,96},{64,0},{96,32},{1,65},{33,97},{65,1},{97,33},{2,66}... | collective-permute-start | bytes 786440 | tf_op jit(solution)/shard_map/ppermute | solution.py:249
  142.3 4.7 %collective-permute-start.13 = (f32[512,256]{1,0:T(8,128)S(1)}, f32[512,256]{1,0:T(8,128)S(1)}, u32[]{:S(2)}, u32[]{:S(2)}) collective-permute-start(f32[512,256]{1,0:T(8,128)S(1)} %bitcast.25), channel_id=1, source_target_pairs={{0,32},{32,0},{64,96},{96,64},{1,33},{33,1},{65,97},{97,65},{2,34}... | collective-permute-start | bytes 1572872 | tf_op jit(solution)/shard_map/ppermute | solution.py:249
  145.3 2.0 %collective-permute-start.14 = (f32[512,256]{1,0:T(8,128)S(1)}, f32[512,256]{1,0:T(8,128)S(1)}, u32[]{:S(2)}, u32[]{:S(2)}) collective-permute-start(f32[512,256]{1,0:T(8,128)S(1)} %bitcast.27), channel_id=1, source_target_pairs={{0,32},{32,0},{64,96},{96,64},{1,33},{33,1},{65,97},{97,65},{2,34}... | collective-permute-start | bytes 1572872 | tf_op jit(solution)/shard_map/ppermute | solution.py:249

commit v3 on v2

v3 whole, which is shorter than its diff:
```python
import jax
import jax.numpy as jnp
from jax import lax
from jax.experimental import pallas as pl
from jax.experimental.pallas import tpu as pltpu
from jax.sharding import PartitionSpec as P

NT = (((1,), (1,)), ((), ()))
VMEM_BYTES = 24 * 1024 * 1024


def dot_nt(left, right):
    return lax.dot_general(left, right, NT, preferred_element_type=jnp.float32)


def split3(values):
    high = lax.reduce_precision(values, 8, 7)
    middle = lax.reduce_precision(values - high, 8, 7)
    low = lax.reduce_precision(values - high - middle, 8, 7)
    high, middle, low = (piece.astype(jnp.bfloat16) for piece in (high, middle, low))
    return high, middle, low


def beside_ones(tastes):
    ones = lax.broadcasted_iota(jnp.int32, tastes.shape, 1) < 3
    return jnp.concatenate([tastes, jnp.where(ones, 1.0, 0.0).astype(tastes.dtype)], axis=1)


def stats(chars, tastes, gate):
    rows, depth = chars.shape
    consumers = tastes.shape[0]
    block, sub, chunk = 2048, 256, 256
    count = block // sub

    def kernel(chars_ref, tastes_ref, gate_ref, stat_ref, util_ref):
        people = [beside_ones(tastes_ref[k * sub : (k + 1) * sub, :]) for k in range(count)]
        before = None
        for k in range(count + 1):
            peak = jnp.full((8, sub), -jnp.inf, jnp.float32)
            total = jnp.zeros((8, sub), jnp.float32)
            for start in range(0, rows, chunk):
                if k < count:
                    util = dot_nt(chars_ref[start : start + chunk, :], people[k])
                    util_ref[k % 2, start : start + chunk, :] = util
                    peak = jnp.maximum(peak, jnp.max(util.reshape(chunk // 8, 8, sub), axis=0))
                if k > 0:
                    expo = jnp.exp(util_ref[(k - 1) % 2, start : start + chunk, :] - before)
                    total = total + jnp.sum(expo.reshape(chunk // 8, 8, sub), axis=0)
            if k > 0:
                stat_ref[0:1, (k - 1) * sub : k * sub] = before
                stat_ref[1:2, (k - 1) * sub : k * sub] = jnp.sum(total, axis=0, keepdims=True)
            before = jnp.max(peak, axis=0, keepdims=True)

    return pl.pallas_call(
        kernel,
        grid=(consumers // block,),
        in_specs=[
            pl.BlockSpec((rows, depth), lambda i: (0, 0)),
            pl.BlockSpec((block, tastes.shape[1]), lambda i: (i, 0)),
            pl.BlockSpec(memory_space=pl.ANY),
        ],
        out_specs=pl.BlockSpec((2, block), lambda i: (0, i)),
        out_shape=jax.ShapeDtypeStruct((2, consumers), jnp.float32),
        scratch_shapes=[pltpu.VMEM((2, rows, sub), jnp.float32)],
        compiler_params=pltpu.CompilerParams(vmem_limit_bytes=VMEM_BYTES),
        name="stats",
    )(chars, tastes, gate)


def pick_rows(ids_t, chars, tail, stat):
    per_pair, holders = ids_t.shape
    rows, depth = chars.shape
    extra = tail.shape[0]
    each = per_pair + extra
    group = max(1, 256 // per_pair)

    def kernel(ids_ref, chars_ref, tail_ref, stat_ref, out_ref, stat_out_ref):
        stat_out_ref[...] = stat_ref[...]
        lanes = lax.broadcasted_iota(jnp.int32, (per_pair, rows), 1)
        table = chars_ref[...]
        for start in range(0, holders, group):
            span = range(start, min(start + group, holders))
            marks = [jnp.where(ids_ref[:, q : q + 1] == lanes, 1.0, 0.0).astype(jnp.bfloat16) for q in span]
            picked = jnp.dot(jnp.concatenate(marks, axis=0), table, preferred_element_type=jnp.float32)
            for place, q in enumerate(span):
                mine = picked[place * per_pair : (place + 1) * per_pair, :]
                out_ref[q * each : q * each + per_pair, :] = mine.astype(jnp.bfloat16)
                out_ref[q * each + per_pair : (q + 1) * each, :] = tail_ref[...]

    return pl.pallas_call(
        kernel,
        out_shape=[jax.ShapeDtypeStruct((each * holders, depth), jnp.bfloat16), jax.ShapeDtypeStruct(stat.shape, stat.dtype)],
        compiler_params=pltpu.CompilerParams(vmem_limit_bytes=VMEM_BYTES),
        name="pick_rows",
    )(ids_t, chars, tail, stat)


def place_rows(order, received, holders, stat):
    rows = order.shape[1]
    total, depth = received.shape
    per_pair, each = rows // holders, total // holders
    chunk = 256

    def kernel(order_ref, received_ref, stat_ref, out_ref, stat_out_ref):
        stat_out_ref[...] = stat_ref[...]
        order_row = order_ref[...]
        table = jnp.concatenate([received_ref[q * each : q * each + per_pair, :] for q in range(holders)], axis=0)
        for start in range(0, rows, chunk):
            ids = start + lax.broadcasted_iota(jnp.int32, (chunk, rows), 0)
            hot = jnp.where(ids == order_row, 1.0, 0.0).astype(jnp.bfloat16)
            placed = jnp.dot(hot, table, preferred_element_type=jnp.float32)
            out_ref[start : start + chunk, :] = placed.astype(jnp.bfloat16)

    return pl.pallas_call(
        kernel,
        out_shape=[jax.ShapeDtypeStruct((rows, depth), jnp.bfloat16), jax.ShapeDtypeStruct(stat.shape, stat.dtype)],
        compiler_params=pltpu.CompilerParams(vmem_limit_bytes=VMEM_BYTES),
        name="place_rows",
    )(order, received, stat)


def lane_groups(values):
    total = values[:, 0:128]
    for start in range(128, values.shape[1], 128):
        total = total + values[:, start : start + 128]
    return total


def first_panel(chars, parts, tastes, row_values, col_chars):
    rows, depth = chars.shape[0] // parts, chars.shape[1]
    consumers = tastes.shape[0]
    cols = col_chars.shape[0]
    block, chunk = 1024, 256

    def kernel(chars_ref, tastes_ref, rows_ref, cols_ref, panel_ref, share_ref, weight_ref, diag_ref):
        @pl.when(pl.program_id(0) == 0)
        def _():
            panel_ref[...] = jnp.zeros_like(panel_ref)
            share_ref[...] = jnp.zeros_like(share_ref)
            diag_ref[...] = jnp.zeros_like(diag_ref)

        people = beside_ones(tastes_ref[...])
        peak, ratio = rows_ref[0:1, :], rows_ref[1:2, :]
        weighted = rows_ref[2:3, :] * (jnp.exp(dot_nt(cols_ref[...], people) - peak) * ratio)
        diag_ref[...] += lane_groups(weighted)
        weight = weighted.astype(jnp.bfloat16)
        weight_ref[...] = weight
        for start in range(0, rows, chunk):
            scaled = jnp.exp(dot_nt(chars_ref[start : start + chunk, :], people) - peak) * ratio
            share_ref[start : start + chunk, :] += lane_groups(scaled)
            panel_ref[start : start + chunk, :] += dot_nt(scaled.astype(jnp.bfloat16), weight)

    return pl.pallas_call(
        kernel,
        grid=(consumers // block,),
        in_specs=[
            pl.BlockSpec((rows, depth), lambda i: (0, 0)),
            pl.BlockSpec((block, tastes.shape[1]), lambda i: (i, 0)),
            pl.BlockSpec((3, block), lambda i: (0, i)),
            pl.BlockSpec((cols, depth), lambda i: (0, 0)),
        ],
        out_specs=[
            pl.BlockSpec((rows, cols), lambda i: (0, 0)),
            pl.BlockSpec((rows, 128), lambda i: (0, 0)),
            pl.BlockSpec((cols, block), lambda i: (0, i)),
            pl.BlockSpec((cols, 128), lambda i: (0, 0)),
        ],
        out_shape=[
            jax.ShapeDtypeStruct((rows, cols), jnp.float32),
            jax.ShapeDtypeStruct((rows, 128), jnp.float32),
            jax.ShapeDtypeStruct((cols, consumers), jnp.bfloat16),
            jax.ShapeDtypeStruct((cols, 128), jnp.float32),
        ],
        compiler_params=pltpu.CompilerParams(vmem_limit_bytes=VMEM_BYTES),
        cost_estimate=pl.CostEstimate(
            flops=2 * rows * consumers * (depth + cols), bytes_accessed=rows * cols * 8, transcendentals=rows * consumers
        ),
        name="first_panel",
    )(chars, tastes, row_values, col_chars)


def panel(chars, part, parts, tastes, row_values, weighted, gate):
    rows, depth = chars.shape[0] // parts, chars.shape[1]
    consumers = tastes.shape[0]
    cols = weighted.shape[0]
    chunk = 256

    def kernel(chars_ref, tastes_ref, rows_ref, weight_ref, gate_ref, panel_ref, share_ref):
        people, weight = beside_ones(tastes_ref[...]), weight_ref[...]
        peak, ratio = rows_ref[0:1, :], rows_ref[1:2, :]
        for start in range(0, rows, chunk):
            scaled = jnp.exp(dot_nt(chars_ref[start : start + chunk, :], people) - peak) * ratio
            share_ref[start : start + chunk, :] = lane_groups(scaled)
            panel_ref[start : start + chunk, :] = dot_nt(scaled.astype(jnp.bfloat16), weight)

    return pl.pallas_call(
        kernel,
        grid=(1,),
        in_specs=[
            pl.BlockSpec((rows, depth), lambda i: (part, 0)),
            pl.BlockSpec(tastes.shape, lambda i: (0, 0)),
            pl.BlockSpec((3, consumers), lambda i: (0, 0)),
            pl.BlockSpec((cols, consumers), lambda i: (0, 0)),
            pl.BlockSpec(memory_space=pl.ANY),
        ],
        out_specs=[
            pl.BlockSpec((rows, cols), lambda i: (0, 0)),
            pl.BlockSpec((rows, 128), lambda i: (0, 0)),
        ],
        out_shape=[
            jax.ShapeDtypeStruct((rows, cols), jnp.float32),
            jax.ShapeDtypeStruct((rows, 128), jnp.float32),
        ],
        compiler_params=pltpu.CompilerParams(vmem_limit_bytes=VMEM_BYTES),
        cost_estimate=pl.CostEstimate(
            flops=2 * rows * consumers * (depth + cols), bytes_accessed=rows * cols * 8, transcendentals=rows * consumers
        ),
        name="panel",
    )(chars, tastes, row_values, weighted, gate)


def share_sums(chars, tastes, row_values, gate):
    rows, depth = chars.shape
    consumers = tastes.shape[0]
    block, chunk = 1024, 256

    def kernel(chars_ref, tastes_ref, rows_ref, gate_ref, share_ref):
        @pl.when(pl.program_id(0) == 0)
        def _():
            share_ref[...] = jnp.zeros_like(share_ref)

        people = beside_ones(tastes_ref[...])
        peak, ratio = rows_ref[0:1, :], rows_ref[1:2, :]
        for start in range(0, rows, chunk):
            scaled = jnp.exp(dot_nt(chars_ref[start : start + chunk, :], people) - peak) * ratio
            share_ref[start : start + chunk, :] += lane_groups(scaled)

    return pl.pallas_call(
        kernel,
        grid=(consumers // block,),
        in_specs=[
            pl.BlockSpec((rows, depth), lambda i: (0, 0)),
            pl.BlockSpec((block, tastes.shape[1]), lambda i: (i, 0)),
            pl.BlockSpec((3, block), lambda i: (0, i)),
            pl.BlockSpec(memory_space=pl.ANY),
        ],
        out_specs=pl.BlockSpec((rows, 128), lambda i: (0, 0)),
        out_shape=jax.ShapeDtypeStruct((rows, 128), jnp.float32),
        compiler_params=pltpu.CompilerParams(vmem_limit_bytes=VMEM_BYTES),
        name="share_sums",
    )(chars, tastes, row_values, gate)


def swap(value, axis, mask):
    size = lax.axis_size(axis)
    return lax.ppermute(value, axis, [(i, i ^ mask) for i in range(size)])


def butterfly_masks(size):
    masks, step = [], 1
    while step < size:
        masks.append(step)
        if step * 2 < size:
            masks.append(step * 3)
        step *= 4
    return masks


def body(tastes, price_coef, characteristics, mean_utility, panel_cols, firm_map, inverses):
    products, depth = characteristics.shape
    consumers = tastes.shape[0]
    cols = panel_cols.shape[0]
    holders = lax.axis_size("prod")
    per_pair = products // holders
    count_products = products * holders
    count_consumers = consumers * lax.axis_size("cons")
    base = lax.axis_index("prod") * products
    core = lax.axis_index("cons") % 2

    pieces = jnp.stack(split3(mean_utility), axis=1)
    chars = jnp.concatenate([characteristics, jnp.pad(pieces, ((0, 0), (0, depth - 3)))], axis=1)
    width = 2 * depth

    wanted, order = lax.sort((firm_map, lax.iota(jnp.int32, products)), num_keys=1)
    wanted = (wanted % products).reshape(holders, per_pair)
    digits = jnp.concatenate([wanted // 256, wanted % 256], axis=1).astype(jnp.bfloat16)
    digits = jnp.pad(digits, ((0, 0), (0, width - 2 * per_pair)))[:, None, :]
    product_ids = base + lax.iota(jnp.int32, products)
    hits = (panel_cols[:, None] == product_ids[None, :]).astype(jnp.bfloat16)
    col_part = jnp.dot(hits, chars, preferred_element_type=jnp.float32).astype(jnp.bfloat16)
    share_cols = cols // holders
    message = jnp.concatenate([col_part.reshape(holders, share_cols, width), digits], axis=1)
    message = jnp.pad(message, ((0, 0), (0, -(share_cols + 1) % 16), (0, 0)))
    first = lax.all_to_all(message, "prod", split_axis=0, concat_axis=0, tiled=True)

    stat = stats(chars, tastes, message)

    asked = first[:, share_cols, : 2 * per_pair].astype(jnp.int32)
    ids = asked[:, :per_pair] * 256 + asked[:, per_pair:]
    collected = jnp.sum(first[:, :share_cols, :].astype(jnp.float32), axis=0).astype(jnp.bfloat16)
    collected = jnp.pad(collected, ((0, -share_cols % 16), (0, 0)))
    each = per_pair + collected.shape[0]
    sent, stat = pick_rows(ids.T, chars, collected, stat)
    second = lax.all_to_all(sent.reshape(holders, each, width), "prod", split_axis=0, concat_axis=0, tiled=True)
    col_chars = second[:, per_pair : per_pair + share_cols, :].reshape(cols, width)
    half, quarter = products // 2, products // 4
    kept_row = (order // half == core).astype(jnp.int32)
    place = (order // quarter % 2) * half + kept_row * quarter + order % quarter
    for hop, mask in enumerate(butterfly_masks(holders)):
        if hop == 1:
            firm_chars, stat = place_rows(place.reshape(1, products), second.reshape(holders * each, width), holders, stat)
        other = swap(stat, "prod", mask)
        joint = jnp.maximum(stat[0], other[0])
        total = stat[1] * jnp.exp(stat[0] - joint) + other[1] * jnp.exp(other[0] - joint)
        stat = jnp.stack([joint, total])
    peak = jnp.maximum(stat[0], 0.0)
    denom = jnp.exp(-peak) + stat[1] * jnp.exp(stat[0] - peak)
    ratio = count_products / denom

    row_values = jnp.stack([peak, ratio, price_coef])
    given, given_share, weighted, diag_part = first_panel(firm_chars, 4, tastes, row_values, col_chars)
    diagonal = jnp.sum(diag_part, axis=1)
    for mask in (1, 2):
        diagonal = diagonal + swap(diagonal, "cons", mask)
    room = 32768.0 / (count_products * jnp.maximum(diagonal, 1e-25))

    firm_count, block_size = inverses.shape[0], inverses.shape[1]
    own_inverses = lax.dynamic_slice_in_dim(inverses, core * (firm_count // 2), firm_count // 2, 0)
    firm_ids = lax.dynamic_slice_in_dim(firm_map, core * half, half, 0)
    blocks = firm_count // 4
    chip_sums, share_parts, responses = [], [], []

    def respond(part, chip_sum, other_sum):
        both = chip_sum.astype(jnp.float32) + other_sum.astype(jnp.float32)
        part_ids = firm_ids[part * quarter : (part + 1) * quarter]
        marks = part_ids[:, None] == panel_cols[None, :]
        jacobian = both / (room[None, :] * count_consumers) - jnp.where(marks, diagonal[None, :] / count_consumers, 0.0)
        response = jnp.einsum(
            "fab,fbc->fac",
            own_inverses[part * blocks : (part + 1) * blocks],
            jacobian.reshape(blocks, block_size, cols),
            precision=lax.Precision.HIGHEST,
        ).reshape(quarter, cols)
        responses.append((response, swap(response, "cons", 1)))

    for part in (0, 1):
        if part:
            given, given_share = panel(firm_chars, 2 * part, 4, tastes, row_values, weighted, gate)
        got = swap(given, "cons", 1)
        kept, kept_share = panel(firm_chars, 2 * part + 1, 4, tastes, row_values, weighted, given)
        fitted = (kept + got) * room[None, :]
        chip_sum, gate = lax.optimization_barrier((fitted.astype(jnp.float16), jnp.max(fitted, axis=0, keepdims=True)))
        chip_sums.append((chip_sum, swap(chip_sum, "cons", 2)))
        share_parts.append((given_share, kept_share))
    respond(0, *chip_sums[0])
    gate = gate + responses[0][0][:8]

    given_share = jnp.sum(jnp.concatenate([share_parts[0][0], share_parts[1][0]]), axis=1)
    kept_share = jnp.sum(jnp.concatenate([share_parts[0][1], share_parts[1][1]]), axis=1)
    first_half = jnp.where(core == 0, kept_share, given_share)
    second_half = jnp.where(core == 0, given_share, kept_share)
    own_shares = jnp.sum(share_sums(chars, tastes, row_values, gate), axis=1)
    sums = jnp.concatenate([own_shares, first_half, second_half])
    for mask in (1, 2):
        sums = sums + swap(sums, "cons", mask)
    sums = sums / count_consumers
    shares, firm_shares = sums[:products], sums[products:]

    respond(1, *chip_sums[1])
    mine = [pair[0] for pair in responses]
    theirs = [pair[1] for pair in responses]
    response = jnp.where(core == 0, jnp.concatenate(mine + theirs, axis=0), jnp.concatenate(theirs + mine, axis=0))
    markup = jnp.sum(inverses * firm_shares.reshape(firm_count, 1, block_size), axis=2).reshape(products)
    return (shares, markup, response)


def solution(mesh):
    return jax.shard_map(
        body,
        mesh=mesh,
        in_specs=(
            P("cons", None),
            P("cons"),
            P("prod", None),
            P("prod"),
            P(),
            P("prod"),
            P("prod", None, None),
        ),
        out_specs=(P("prod"), P("prod"), P("prod", None)),
        check_vma=False,
    )
```

time: 150 us -> 144 us (0.960)
  Pallas kernels: 64.9 us -> 34.3 us
  waiting for transfers between devices: 22.8 us -> 40.8 us
  local copies, waits for them, and re-layouts: 2.8 us -> 10.3 us
  other arithmetic: 20 us -> 17.3 us
    pallas_call x7 -> x6, Pallas kernels: 37.5 us -> 17.6 us  [the longest x3 8.28 us: panel(): pl.pallas_call(kernel, grid=(1,), in_specs=[pl.BlockSpec((rows, depth), l...]
    all_to_all x1, waiting for transfers between devices: 2 us -> 18.6 us  [body(): lax.all_to_all(sent.reshape(holders, each, width), 'prod', split_axis=0,...]
    ppermute x15, starting transfers between devices: 24.8 us -> 15.9 us  [swap(): return lax.ppermute(value, axis, [(i, i ^ mask) for i in range(size)])]
    unnamed x27 -> x29, local copies, waits for them, and re-layouts: 0.17 us -> 8.94 us
    pallas_call x1, Pallas kernels: 17.8 us -> 9.48 us  [stats(): pl.pallas_call(kernel, grid=(consumers // block,), in_specs=[pl.BlockSpec...]
    ppermute x15, waiting for transfers between devices: 16.2 us -> 22.2 us  [swap(): return lax.ppermute(value, axis, [(i, i ^ mask) for i in range(size)])]
    all_to_all x1, starting transfers between devices: 6.11 us -> 11.3 us  [body(): lax.all_to_all(message, 'prod', split_axis=0, concat_axis=0, tiled=True)]
    all_to_all x1, waiting for transfers between devices: 4.63 us -> 0.01 us  [body(): lax.all_to_all(message, 'prod', split_axis=0, concat_axis=0, tiled=True)]
  transfers between devices with their start and end apart: 17 -> 17, of which waited for: 9 -> 8; matrix products, arithmetic and copies ran while one was open for 10% -> 4% of each run, Pallas kernels for 6% -> 10%
where the time goes in v3:
time: 144 us; the launch traced here: 143 us
  waiting for transfers between devices  40.8 us (28%)
  starting transfers between devices  36.4 us (25%)
  Pallas kernels  34.3 us (24%)
  other arithmetic  17.3 us (12%)
  local copies, waits for them, and re-layouts  10.3 us (7%)
  matrix products  2.78 us (2%)
    ppermute x15, waiting for transfers between devices, swap(): return lax.ppermute(value, axis, [(i, i ^ mask) for i in range(size)])  22.2 us
    all_to_all x1, waiting for transfers between devices, body(): lax.all_to_all(sent.reshape(holders, each, width), 'prod', split_axis=0,...  18.6 us
    ppermute x15, starting transfers between devices, swap(): return lax.ppermute(value, axis, [(i, i ^ mask) for i in range(size)])  15.9 us
    all_to_all x1, starting transfers between devices, body(): lax.all_to_all(message, 'prod', split_axis=0, concat_axis=0, tiled=True)  11.3 us
    pallas_call x1, Pallas kernels, stats(): pl.pallas_call(kernel, grid=(consumers // block,), in_specs=[pl.BlockSpec...  9.48 us
    all_to_all x1, starting transfers between devices, body(): lax.all_to_all(sent.reshape(holders, each, width), 'prod', split_axis=0,...  9.12 us
    unnamed x29, local copies, waits for them, and re-layouts  8.94 us
    pallas_call x3, Pallas kernels, panel(): pl.pallas_call(kernel, grid=(1,), in_specs=[pl.BlockSpec((rows, depth), l...  8.28 us
  transfers between devices with their start and end apart: 17, of which 8 were waited for; matrix products, arithmetic and copies ran while one was open for 4% of the time, Pallas kernels for 10%

profile of v3, /device:TPU:1, one launch (start us, length us, event | category | flops | bytes accessed | tf_op | source)
XLA Modules:
  0.0 142.9 jit_solution(4766789842015988916)
XLA Ops:
  0.6 0.7 reduce-precision_convert_fusion.1
  1.4 0.3 copy.47
  1.8 5.1 %sort.15 = (s32[2048]{0:T(1024)S(1)}, s32[2048]{0:T(1024)S(1)}) sort(s32[2048]{0:T(1024)} %param.12, s32[2048]{0:T(1024)S(1)} %iota.8), dimensions={0}, to_apply=%region_0.1 | sort | flops 22528 | bytes 32768 | tf_op jit(solution)/shard_map/sort | solution.py:284
  7.0 0.1 copy.48
  7.1 0.1 copy.52
  7.2 0.1 copy.53
  7.3 0.1 fusion.31
  7.4 1.3 fusion.9.chars_ref
  8.8 0.5 fusion.6
  9.3 0.8 fusion.18.gate_ref
  10.0 11.3 %all-to-all-start = ((bf16[32,16,256]{2,1,0:T(8,128)(2,1)}), bf16[32,16,256]{2,1,0:T(8,128)(2,1)S(1)}, u32[]{:S(2)}, u32[]{:S(2)}) async-start(bf16[32,16,256]{2,1,0:T(8,128)(2,1)} %fusion.18.gate_ref), calls=%async_computation | async-start | bytes 524288 | tf_op jit(solution)/shard_map/all_to_all | solution.py:294
  21.4 9.5 %stats.1.stat_ref = f32[2,4096]{1,0:T(2,128)S(1)} custom-call(bf16[2048,256]{1,0:T(8,128)(2,1)S(1)} %fusion.9.chars_ref, bf16[4096,128]{1,0:T(8,128)(2,1)S(1)} %copy-done, bf16[32,16,256]{2,1,0:T(8,128)(2,1)} %fusion.18.gate_ref), custom_call_target="tpu_custom_call" | custom-call | tf_op jit(solution)/shard_map/stats/pallas_call | solution.py:54
  30.9 0.1 copy.56
  31.1 2.4 %pick_rows.1 = (bf16[2560,256]{1,0:T(8,128)(2,1)S(1)}, f32[2,4096]{1,0:T(2,128)S(1)}) custom-call(s32[64,32]{1,0:T(8,128)S(1)} %fusion.25.ids_ref, bf16[2048,256]{1,0:T(8,128)(2,1)S(1)} %fusion.9.chars_ref, bf16[16,256]{1,0:T(8,128)(2,1)S(1)} %pad.19.tail_ref, f32[2,4096]{1,0:T(2,128)S(1)} %stats.1.stat_ref), custom_call_target="tpu_custom_call" | custom-call | tf_op jit(solution)/shard_map/pick_rows/pallas_call | solution.py:90
  33.5 1.0 copy-done.1
  34.6 1.2 collective-permute-start
  35.8 9.1 %all-to-all-start.1 = ((bf16[32,80,256]{2,1,0:T(8,128)(2,1)}), bf16[32,80,256]{2,1,0:T(8,128)(2,1)S(1)}, u32[]{:S(2)}, u32[]{:S(2)}) async-start(bf16[32,80,256]{2,1,0:T(8,128)(2,1)} %bitcast.29), calls=%async_computation.1 | async-start | bytes 2621440 | tf_op jit(solution)/shard_map/all_to_all | solution.py:304
  45.1 18.6 %all-to-all-done.1 = bf16[32,80,256]{2,1,0:T(8,128)(2,1)S(1)} async-done(((bf16[32,80,256]{2,1,0:T(8,128)(2,1)}), bf16[32,80,256]{2,1,0:T(8,128)(2,1)S(1)}, u32[]{:S(2)}, u32[]{:S(2)}) %all-to-all-start.1) | async-done | bytes 1310752 | tf_op jit(solution)/shard_map/all_to_all | solution.py:304
  63.7 2.3 %place_rows.1 = (bf16[2048,256]{1,0:T(8,128)(2,1)S(1)}, f32[2,4096]{1,0:T(2,128)S(1)}) custom-call(s32[1,2048]{1,0:T(1,128)S(1)} %bitcast.30, bf16[2560,256]{1,0:T(8,128)(2,1)S(1)} %bitcast.28, f32[2,4096]{1,0:T(2,128)S(1)} %pad_maximum_fusion.1.stat_ref), custom_call_target="tpu_custom_call" | custom-call | tf_op jit(solution)/shard_map/place_rows/pallas_call | solution.py:114
  66.0 0.1 collective-permute-start.1
  66.1 4.0 %collective-permute-done.1 = f32[2,4096]{1,0:T(2,128)S(1)} collective-permute-done((f32[2,4096]{1,0:T(2,128)S(1)}, f32[2,4096]{1,0:T(2,128)S(1)}, u32[]{:S(2)}, u32[]{:S(2)}) %collective-permute-start.1) | collective-permute-done | bytes 32800 | tf_op jit(solution)/shard_map/ppermute | solution.py:256
  70.2 0.1 collective-permute-start.2
  70.3 3.0 %collective-permute-done.2 = f32[2,4096]{1,0:T(2,128)S(1)} collective-permute-done((f32[2,4096]{1,0:T(2,128)S(1)}, f32[2,4096]{1,0:T(2,128)S(1)}, u32[]{:S(2)}, u32[]{:S(2)}) %collective-permute-start.2) | collective-permute-done | bytes 32800 | tf_op jit(solution)/shard_map/ppermute | solution.py:256
  73.4 1.3 collective-permute-start.3
  74.8 2.7 %collective-permute-done.3 = f32[2,4096]{1,0:T(2,128)S(1)} collective-permute-done((f32[2,4096]{1,0:T(2,128)S(1)}, f32[2,4096]{1,0:T(2,128)S(1)}, u32[]{:S(2)}, u32[]{:S(2)}) %collective-permute-start.3) | collective-permute-done | bytes 32800 | tf_op jit(solution)/shard_map/ppermute | solution.py:256
  77.6 1.0 collective-permute-start.4
  78.6 3.3 %collective-permute-done.4 = f32[2,4096]{1,0:T(2,128)S(1)} collective-permute-done((f32[2,4096]{1,0:T(2,128)S(1)}, f32[2,4096]{1,0:T(2,128)S(1)}, u32[]{:S(2)}, u32[]{:S(2)}) %collective-permute-start.4) | collective-permute-done | bytes 32800 | tf_op jit(solution)/shard_map/ppermute | solution.py:256
  81.9 0.1 maximum_maximum_fusion
  82.1 4.6 %first_panel.1 = (f32[512,256]{1,0:T(8,128)S(1)}, f32[512,128]{1,0:T(8,128)S(1)}, bf16[256,4096]{1,0:T(8,128)(2,1)S(1)}, f32[256,128]{1,0:T(8,128)S(1)}) custom-call(bf16[2048,256]{1,0:T(8,128)(2,1)S(1)} %get-tuple-element.28.chars_ref, bf16[4096,128]{1,0:T(8,128)(2,1)S(1)} %copy-done, f32[3,4096]{1,0:T(4,128)S(1)} %pad_maximum_fusion.rows_ref, ...), custom_call_target="tpu_custom_call" | custom-call | flops 2147483648 | bytes 1048576 | tf_op jit(solution)/shard_map/first_panel/pallas_call | solution.py:153
  86.8 1.3 copy-done.5
  88.1 7.2 %collective-permute-start.5 = (f32[512,256]{1,0:T(8,128)S(1)}, f32[512,256]{1,0:T(8,128)}, u32[]{:S(2)}, u32[]{:S(2)}) collective-permute-start(f32[512,256]{1,0:T(8,128)S(1)} %get-tuple-element.30.gate_ref), channel_id=1, source_target_pairs={{0,32},{32,0},{64,96},{96,64},{1,33},{33,1},{65,97},{97,65},{2,34}... | collective-permute-start | bytes 1572872 | tf_op jit(solution)/shard_map/ppermute | solution.py:256
  95.3 0.1 reduce_sum.58
  95.4 0.1 collective-permute-start.6
  95.5 1.3 collective-permute-done.6
  96.8 0.4 collective-permute-start.7
  97.2 1.2 copy-done.3
  98.5 1.6 %copy-done.6 = bf16[256,4096]{1,0:T(8,128)(2,1)S(1)} copy-done((bf16[256,4096]{1,0:T(8,128)(2,1)S(1)}, bf16[256,4096]{1,0:T(8,128)(2,1)}, u32[]{:S(2)}) %copy-start.6) | copy-done | bytes 2097176
  100.1 2.5 %panel.3 = (f32[512,256]{1,0:T(8,128)S(1)}, f32[512,128]{1,0:T(8,128)S(1)}) custom-call(bf16[2048,256]{1,0:T(8,128)(2,1)S(1)} %copy-done.3, bf16[4096,128]{1,0:T(8,128)(2,1)S(1)} %copy-done, f32[3,4096]{1,0:T(4,128)S(1)} %pad_maximum_fusion.rows_ref, bf16[256,4096]{1,0:T(8,128)(2,1)S(1)} %copy-done.6, f32[512,256]{1,0:T(8,128)S(1)} %get-tuple-element.30.gate_ref), custom_call_target="tpu_custom_call" | custom-call | flops 2147483648 | bytes 1048576 | tf_op jit(solution)/shard_map/panel/pallas_call | solution.py:196
  102.6 1.2 fusion.19
  103.7 3.3 %panel.4 = (f32[512,256]{1,0:T(8,128)}, f32[512,128]{1,0:T(8,128)S(1)}) custom-call(bf16[2048,256]{1,0:T(8,128)(2,1)S(1)} %copy-done.3, bf16[4096,128]{1,0:T(8,128)(2,1)S(1)} %copy-done, f32[3,4096]{1,0:T(4,128)S(1)} %pad_maximum_fusion.rows_ref, bf16[256,4096]{1,0:T(8,128)(2,1)S(1)} %copy-done.6, f32[1,256]{1,0:T(1,128)S(1)} %bitcast.31), custom_call_target="tpu_custom_call" | custom-call | flops 2147483648 | bytes 1048576 | tf_op jit(solution)/shard_map/panel/pallas_call | solution.py:196
  107.0 0.6 collective-permute-start.8
  107.7 1.1 collective-permute-start.9
  108.7 1.2 copy-done.4
  110.0 1.6 %copy-done.7 = bf16[256,4096]{1,0:T(8,128)(2,1)S(1)} copy-done((bf16[256,4096]{1,0:T(8,128)(2,1)S(1)}, bf16[256,4096]{1,0:T(8,128)(2,1)}, u32[]{:S(2)}) %copy-start.7) | copy-done | bytes 2097176
  111.6 2.5 %panel.5 = (f32[512,256]{1,0:T(8,128)S(1)}, f32[512,128]{1,0:T(8,128)S(1)}) custom-call(bf16[2048,256]{1,0:T(8,128)(2,1)S(1)} %copy-done.4, bf16[4096,128]{1,0:T(8,128)(2,1)S(1)} %copy-done, f32[3,4096]{1,0:T(4,128)S(1)} %pad_maximum_fusion.rows_ref, bf16[256,4096]{1,0:T(8,128)(2,1)S(1)} %copy-done.7, f32[512,256]{1,0:T(8,128)} %get-tuple-element.34.gate_ref), custom_call_target="tpu_custom_call" | custom-call | flops 2147483648 | bytes 1048576 | tf_op jit(solution)/shard_map/panel/pallas_call | solution.py:196
  114.1 1.8 %fusion.21 = (f32[256]{0:T(256)S(1)}, f16[512,256]{1,0:T(8,128)(2,1)}) fusion(f32[256]{0:T(256)S(1)} %get-tuple-element.44, f32[512,256]{1,0:T(8,128)S(1)} %get-tuple-element.35, f32[512,256]{1,0:T(8,128)} %collective-permute-done.8), kind=kLoop, calls=%fused_computation.27 | loop fusion | flops 524032 | bytes 1312768 | tf_op jit(solution)/shard_map/reduce_max | solution.py:352
  115.9 0.4 collective-permute-start.12
  116.3 0.2 maximum_reduce_fusion.1
  116.5 0.2 maximum_reduce_fusion
  116.8 7.1 %collective-permute-done.12 = f16[512,256]{1,0:T(8,128)(2,1)} collective-permute-done((f16[512,256]{1,0:T(8,128)(2,1)}, f16[512,256]{1,0:T(8,128)(2,1)}, u32[]{:S(2)}, u32[]{:S(2)}) %collective-permute-start.12) | collective-permute-done | bytes 262176 | tf_op jit(solution)/shard_map/ppermute | solution.py:256
  123.8 2.1 %select_subtract_fusion = (f32[512,256]{1,0:T(8,128)}, f32[512,256]{1,0:T(8,128)S(1)}) fusion(f16[512,256]{1,0:T(8,128)(2,1)} %collective-permute-done.12, f16[512,256]{1,0:T(8,128)(2,1)} %get-tuple-element.42, f32[256]{0:T(256)S(1)} %get-tuple-element.72, s32[256]{0:T(256)S(1)} %copy-done.13, f32[256]{0:T(256)S(1)} %get-tuple-element.43, ...), kind=kLoop, calls=%fused_computation.16 | loop fusion | flops 1835008 | bytes 2104320 | tf_op jit(solution)/shard_map/sub | solution.py:337
  125.9 0.6 fusion.16
  126.5 0.8 copy-done.10
  127.3 7.2 %share_sums.1 = f32[2048,128]{1,0:T(8,128)S(1)} custom-call(bf16[2048,256]{1,0:T(8,128)(2,1)S(1)} %fusion.9.chars_ref, bf16[4096,128]{1,0:T(8,128)(2,1)S(1)} %copy-done, f32[3,4096]{1,0:T(4,128)S(1)} %pad_maximum_fusion.rows_ref, f32[8,256]{1,0:T(8,128)S(1)} %slice_add_fusion.1.gate_ref), custom_call_target="tpu_custom_call" | custom-call | tf_op jit(solution)/shard_map/share_sums/pallas_call | solution.py:238
  134.5 0.3 reduce_sum.59
  134.9 1.2 collective-permute-start.10
  136.1 0.1 collective-permute-start.13
  136.2 0.7 collective-permute-done.10
  136.9 0.4 collective-permute-start.11
  137.3 1.7 %fusion.14 = f32[4,128,256]{2,1,0:T(8,128)S(1)} fusion(f32[4,128,256]{2,1,0:T(8,128)} %bitcast.35, f32[16,128,128]{2,1,0:T(8,128)} %param.13, s32[]{:T(128)S(6)} %select_n.81), kind=kOutput, calls=%fused_computation.20 | convolution fusion | flops 201326592 | bytes 1572868 | tf_op jit(solution)/shard_map/fab,fbc->fac/dot_general | solution.py:338
  139.0 0.7 collective-permute-start.14
  139.8 0.6 slice_bitcast_fusion.1
  140.4 0.9 multiply_reduce_fusion
  141.3 1.6 %maximum_select_fusion = f32[2048,256]{1,0:T(8,128)} fusion(f32[512,256]{1,0:T(8,128)S(1)} %collective-permute-done.14, f32[512,256]{1,0:T(8,128)S(1)} %collective-permute-done.13, f32[512,256]{1,0:T(8,128)S(1)} %bitcast.37, f32[512,256]{1,0:T(8,128)S(1)} %bitcast.34, pred[]{:T(512)S(6)} %eq.64), kind=kLoop, calls=%fused_computation.1 | loop fusion | flops 3670016 | bytes 4194305 | tf_op jit(solution)/shard_map/jit(_where)/select_n | solution.py:372
  (66 shorter events, 0.9 us)
Async XLA Ops:
  0.6 8.1 %copy-start.13 = (s32[256]{0:T(256)S(1)}, s32[256]{0:T(256)}, u32[]{:S(2)}) copy-start(s32[256]{0:T(256)} %param.11) | copy-start | bytes 3076
  7.4 14.0 %copy-start = (bf16[4096,128]{1,0:T(8,128)(2,1)S(1)}, bf16[4096,128]{1,0:T(8,128)(2,1)}, u32[]{:S(2)}) copy-start(bf16[4096,128]{1,0:T(8,128)(2,1)} %tastes_ref.11) | copy-start | bytes 3145732
  10.0 20.9 %all-to-all-start = ((bf16[32,16,256]{2,1,0:T(8,128)(2,1)}), bf16[32,16,256]{2,1,0:T(8,128)(2,1)S(1)}, u32[]{:S(2)}, u32[]{:S(2)}) async-start(bf16[32,16,256]{2,1,0:T(8,128)(2,1)} %fusion.18.gate_ref), calls=%async_computation | async-start | bytes 524288 | tf_op jit(solution)/shard_map/all_to_all | solution.py:294
  33.5 1.1 copy-start.1
  34.6 10.4 %collective-permute-start = (f32[2,4096]{1,0:T(2,128)S(1)}, f32[2,4096]{1,0:T(2,128)S(1)}, u32[]{:S(2)}, u32[]{:S(2)}) collective-permute-start(f32[2,4096]{1,0:T(2,128)S(1)} %get-tuple-element.26), channel_id=1, source_target_pairs={{0,1},{1,0},{2,3},{3,2},{4,5},{5,4},{6,7},{7,6},{8,9},{9,8},{10,11... | collective-permute-start | bytes 98312 | tf_op jit(solution)/shard_map/ppermute | solution.py:256
  35.8 46.2 %copy-start.12 = (f32[4096]{0:T(1024)S(1)}, f32[4096]{0:T(1024)}, u32[]{:S(2)}) copy-start(f32[4096]{0:T(1024)} %param.8) | copy-start | bytes 49156
  35.8 27.8 %all-to-all-start.1 = ((bf16[32,80,256]{2,1,0:T(8,128)(2,1)}), bf16[32,80,256]{2,1,0:T(8,128)(2,1)S(1)}, u32[]{:S(2)}, u32[]{:S(2)}) async-start(bf16[32,80,256]{2,1,0:T(8,128)(2,1)} %bitcast.29), calls=%async_computation.1 | async-start | bytes 2621440 | tf_op jit(solution)/shard_map/all_to_all | solution.py:304
  66.0 20.7 %copy-start.2 = (bf16[2048,256]{1,0:T(8,128)(2,1)}, bf16[2048,256]{1,0:T(8,128)(2,1)S(1)}, u32[]{:S(2)}) copy-start(bf16[2048,256]{1,0:T(8,128)(2,1)S(1)} %get-tuple-element.28.chars_ref) | copy-start | bytes 3145732
  66.0 4.1 %collective-permute-start.1 = (f32[2,4096]{1,0:T(2,128)S(1)}, f32[2,4096]{1,0:T(2,128)S(1)}, u32[]{:S(2)}, u32[]{:S(2)}) collective-permute-start(f32[2,4096]{1,0:T(2,128)S(1)} %get-tuple-element.27), channel_id=1, source_target_pairs={{0,3},{1,2},{2,1},{3,0},{4,7},{5,6},{6,5},{7,4},{8,11},{9,10},{10,... | collective-permute-start | bytes 98312 | tf_op jit(solution)/shard_map/ppermute | solution.py:256
  70.2 3.1 %collective-permute-start.2 = (f32[2,4096]{1,0:T(2,128)S(1)}, f32[2,4096]{1,0:T(2,128)S(1)}, u32[]{:S(2)}, u32[]{:S(2)}) collective-permute-start(f32[2,4096]{1,0:T(2,128)S(1)} %pad_maximum_fusion.2), channel_id=1, source_target_pairs={{0,4},{1,5},{2,6},{3,7},{4,0},{5,1},{6,2},{7,3},{8,12},{9,13},{10,... | collective-permute-start | bytes 98312 | tf_op jit(solution)/shard_map/ppermute | solution.py:256
  73.4 4.1 %collective-permute-start.3 = (f32[2,4096]{1,0:T(2,128)S(1)}, f32[2,4096]{1,0:T(2,128)S(1)}, u32[]{:S(2)}, u32[]{:S(2)}) collective-permute-start(f32[2,4096]{1,0:T(2,128)S(1)} %pad_maximum_fusion.3), channel_id=1, source_target_pairs={{0,12},{1,13},{2,14},{3,15},{4,8},{5,9},{6,10},{7,11},{8,4},{9,5},... | collective-permute-start | bytes 98312 | tf_op jit(solution)/shard_map/ppermute | solution.py:256
  77.6 4.3 %collective-permute-start.4 = (f32[2,4096]{1,0:T(2,128)S(1)}, f32[2,4096]{1,0:T(2,128)S(1)}, u32[]{:S(2)}, u32[]{:S(2)}) collective-permute-start(f32[2,4096]{1,0:T(2,128)S(1)} %pad_maximum_fusion.4), channel_id=1, source_target_pairs={{0,16},{1,17},{2,18},{3,19},{4,20},{5,21},{6,22},{7,23},{8,24},{9,... | collective-permute-start | bytes 98312 | tf_op jit(solution)/shard_map/ppermute | solution.py:256
  86.8 1.3 copy-start.5
  88.1 14.5 %collective-permute-start.5 = (f32[512,256]{1,0:T(8,128)S(1)}, f32[512,256]{1,0:T(8,128)}, u32[]{:S(2)}, u32[]{:S(2)}) collective-permute-start(f32[512,256]{1,0:T(8,128)S(1)} %get-tuple-element.30.gate_ref), channel_id=1, source_target_pairs={{0,32},{32,0},{64,96},{96,64},{1,33},{33,1},{65,97},{97,65},{2,34}... | collective-permute-start | bytes 1572872 | tf_op jit(solution)/shard_map/ppermute | solution.py:256
  95.4 1.4 collective-permute-start.6
  96.8 5.7 %collective-permute-start.7 = (f32[256]{0:T(256)S(1)}, f32[256]{0:T(256)S(1)}, u32[]{:S(2)}, u32[]{:S(2)}) collective-permute-start(f32[256]{0:T(256)S(1)} %add.141), channel_id=1, source_target_pairs={{0,64},{32,96},{64,0},{96,32},{1,65},{33,97},{65,1},{97,33},{2,66}... | collective-permute-start | bytes 3080 | tf_op jit(solution)/shard_map/ppermute | solution.py:256
  97.2 1.2 copy-start.3
  98.5 1.6 %copy-start.6 = (bf16[256,4096]{1,0:T(8,128)(2,1)S(1)}, bf16[256,4096]{1,0:T(8,128)(2,1)}, u32[]{:S(2)}) copy-start(bf16[256,4096]{1,0:T(8,128)(2,1)} %copy-done.5) | copy-start | bytes 6291460
  107.0 7.0 %collective-permute-start.8 = (f32[512,256]{1,0:T(8,128)}, f32[512,256]{1,0:T(8,128)}, u32[]{:S(2)}, u32[]{:S(2)}) collective-permute-start(f32[512,256]{1,0:T(8,128)} %get-tuple-element.34.gate_ref), channel_id=1, source_target_pairs={{0,32},{32,0},{64,96},{96,64},{1,33},{33,1},{65,97},{97,65},{2,34}... | collective-permute-start | bytes 1572872 | tf_op jit(solution)/shard_map/ppermute | solution.py:256
  107.7 9.1 %collective-permute-start.9 = (f16[512,256]{1,0:T(8,128)(2,1)S(1)}, f16[512,256]{1,0:T(8,128)(2,1)}, u32[]{:S(2)}, u32[]{:S(2)}) collective-permute-start(f16[512,256]{1,0:T(8,128)(2,1)S(1)} %get-tuple-element.37), channel_id=1, source_target_pairs={{0,64},{32,96},{64,0},{96,32},{1,65},{33,97},{65,1},{97,33},{2,66}... | collective-permute-start | bytes 786440 | tf_op jit(solution)/shard_map/ppermute | solution.py:256
  108.7 1.2 copy-start.4
  110.0 1.6 %copy-start.7 = (bf16[256,4096]{1,0:T(8,128)(2,1)S(1)}, bf16[256,4096]{1,0:T(8,128)(2,1)}, u32[]{:S(2)}) copy-start(bf16[256,4096]{1,0:T(8,128)(2,1)} %copy-done.5) | copy-start | bytes 6291460
  111.6 4.7 %dynamic-slice-start = ((s32[2048]{0:T(1024)}, s32[]{:T(128)}), s32[1024]{0:T(1024)S(1)}, s32[]{:S(2)}) async-start(s32[2048]{0:T(1024)} %param.12, s32[]{:T(128)} %select_n.82), calls=%async_computation.2 | async-start | bytes 8704 | tf_op jit(solution)/shard_map/dynamic_slice | solution.py:329
  115.9 7.9 %collective-permute-start.12 = (f16[512,256]{1,0:T(8,128)(2,1)}, f16[512,256]{1,0:T(8,128)(2,1)}, u32[]{:S(2)}, u32[]{:S(2)}) collective-permute-start(f16[512,256]{1,0:T(8,128)(2,1)} %get-tuple-element.42), channel_id=1, source_target_pairs={{0,64},{32,96},{64,0},{96,32},{1,65},{33,97},{65,1},{97,33},{2,66}... | collective-permute-start | bytes 786440 | tf_op jit(solution)/shard_map/ppermute | solution.py:256
  116.3 9.6 %copy-start.8 = (f32[16,128,128]{2,1,0:T(8,128)S(1)}, f32[16,128,128]{2,1,0:T(8,128)}, u32[]{:S(2)}) copy-start(f32[16,128,128]{2,1,0:T(8,128)} %param.13) | copy-start | bytes 3145732
  126.5 0.8 copy-start.10
  134.5 5.8 %copy-start.9 = (f32[16,128,128]{2,1,0:T(8,128)S(1)}, f32[16,128,128]{2,1,0:T(8,128)}, u32[]{:S(2)}) copy-start(f32[16,128,128]{2,1,0:T(8,128)} %param.13) | copy-start | bytes 3145732
  134.5 6.8 %copy-start.11 = (f32[4,128,256]{2,1,0:T(8,128)S(1)}, f32[4,128,256]{2,1,0:T(8,128)}, u32[]{:S(2)}) copy-start(f32[4,128,256]{2,1,0:T(8,128)} %copy-done.10) | copy-start | bytes 1572868
  134.9 2.0 %collective-permute-start.10 = (f32[4096]{0:T(1024)S(1)}, f32[4096]{0:T(1024)S(1)}, u32[]{:S(2)}, u32[]{:S(2)}) collective-permute-start(f32[4096]{0:T(1024)S(1)} %pad_maximum_fusion.6), channel_id=1, source_target_pairs={{0,32},{32,0},{64,96},{96,64},{1,33},{33,1},{65,97},{97,65},{2,34}... | collective-permute-start | bytes 49160 | tf_op jit(solution)/shard_map/ppermute | solution.py:256
  136.1 5.2 %collective-permute-start.13 = (f32[512,256]{1,0:T(8,128)}, f32[512,256]{1,0:T(8,128)S(1)}, u32[]{:S(2)}, u32[]{:S(2)}) collective-permute-start(f32[512,256]{1,0:T(8,128)} %bitcast.33), channel_id=1, source_target_pairs={{0,32},{32,0},{64,96},{96,64},{1,33},{33,1},{65,97},{97,65},{2,34}... | collective-permute-start | bytes 1572872 | tf_op jit(solution)/shard_map/ppermute | solution.py:256
  136.9 2.8 %collective-permute-start.11 = (f32[4096]{0:T(1024)S(1)}, f32[4096]{0:T(1024)S(1)}, u32[]{:S(2)}, u32[]{:S(2)}) collective-permute-start(f32[4096]{0:T(1024)S(1)} %fusion.51), channel_id=1, source_target_pairs={{0,64},{32,96},{64,0},{96,32},{1,65},{33,97},{65,1},{97,33},{2,66}... | collective-permute-start | bytes 49160 | tf_op jit(solution)/shard_map/ppermute | solution.py:256
  139.0 2.3 %collective-permute-start.14 = (f32[512,256]{1,0:T(8,128)S(1)}, f32[512,256]{1,0:T(8,128)S(1)}, u32[]{:S(2)}, u32[]{:S(2)}) collective-permute-start(f32[512,256]{1,0:T(8,128)S(1)} %bitcast.36), channel_id=1, source_target_pairs={{0,32},{32,0},{64,96},{96,64},{1,33},{33,1},{65,97},{97,65},{2,34}... | collective-permute-start | bytes 1572872 | tf_op jit(solution)/shard_map/ppermute | solution.py:256

commit v4 on v3

--- a/solution.py
+++ b/solution.py
@@ -306,13 +306,18 @@
     half, quarter = products // 2, products // 4
     kept_row = (order // half == core).astype(jnp.int32)
     place = (order // quarter % 2) * half + kept_row * quarter + order % quarter
-    for hop, mask in enumerate(butterfly_masks(holders)):
-        if hop == 1:
-            firm_chars, stat = place_rows(place.reshape(1, products), second.reshape(holders * each, width), holders, stat)
-        other = swap(stat, "prod", mask)
-        joint = jnp.maximum(stat[0], other[0])
-        total = stat[1] * jnp.exp(stat[0] - joint) + other[1] * jnp.exp(other[0] - joint)
-        stat = jnp.stack([joint, total])
+    def join(stat, masks):
+        for mask in masks:
+            other = swap(stat, "prod", mask)
+            joint = jnp.maximum(stat[0], other[0])
+            total = stat[1] * jnp.exp(stat[0] - joint) + other[1] * jnp.exp(other[0] - joint)
+            stat = jnp.stack([joint, total])
+        return stat
+
+    masks = butterfly_masks(holders)
+    stat = lax.cond(panel_cols[0] >= 0, lambda value: join(value, masks[:3]), lambda value: value, stat)
+    firm_chars, stat = place_rows(place.reshape(1, products), second.reshape(holders * each, width), holders, stat)
+    stat = join(stat, masks[3:])
     peak = jnp.maximum(stat[0], 0.0)
     denom = jnp.exp(-peak) + stat[1] * jnp.exp(stat[0] - peak)
     ratio = count_products / denom
@@ -352,8 +357,6 @@
         chip_sum, gate = lax.optimization_barrier((fitted.astype(jnp.float16), jnp.max(fitted, axis=0, keepdims=True)))
         chip_sums.append((chip_sum, swap(chip_sum, "cons", 2)))
         share_parts.append((given_share, kept_share))
-    respond(0, *chip_sums[0])
-    gate = gate + responses[0][0][:8]
 
     given_share = jnp.sum(jnp.concatenate([share_parts[0][0], share_parts[1][0]]), axis=1)
     kept_share = jnp.sum(jnp.concatenate([share_parts[0][1], share_parts[1][1]]), axis=1)
@@ -366,6 +369,7 @@
     sums = sums / count_consumers
     shares, firm_shares = sums[:products], sums[products:]
 
+    respond(0, *chip_sums[0])
     respond(1, *chip_sums[1])
     mine = [pair[0] for pair in responses]
     theirs = [pair[1] for pair in responses]

time: 144 us -> 130 us (0.903)
  waiting for transfers between devices: 40.8 us -> 22.5 us
  starting transfers between devices: 36.4 us -> 42.3 us
    all_to_all x1, waiting for transfers between devices: 18.6 us -> 0.01 us  [body(): lax.all_to_all(sent.reshape(holders, each, width), 'prod', split_axis=0,...]
    ppermute x15, starting transfers between devices: 15.9 us -> 21.5 us  [swap(): return lax.ppermute(value, axis, [(i, i ^ mask) for i in range(size)])]
    unnamed x29 -> x23, local copies, waits for them, and re-layouts: 8.94 us -> 8.13 us
  transfers between devices with their start and end apart: 17 -> 17, of which waited for: 8 -> 8; matrix products, arithmetic and copies ran while one was open for 4% -> 6% of each run, Pallas kernels for 10% -> 17%
where the time goes in v4:
time: 130 us; the launch traced here: 129 us
  starting transfers between devices  42.3 us (33%)
  Pallas kernels  34.3 us (26%)
  waiting for transfers between devices  22.5 us (17%)
  other arithmetic  16.5 us (13%)
  local copies, waits for them, and re-layouts  9.97 us (8%)
  between operations  1.75 us (1%)
  matrix products  1.66 us (1%)
    ppermute x15, waiting for transfers between devices, swap(): return lax.ppermute(value, axis, [(i, i ^ mask) for i in range(size)])  22.5 us
    ppermute x15, starting transfers between devices, swap(): return lax.ppermute(value, axis, [(i, i ^ mask) for i in range(size)])  21.5 us
    all_to_all x1, starting transfers between devices, body(): lax.all_to_all(message, 'prod', split_axis=0, concat_axis=0, tiled=True)  11.3 us
    pallas_call x1, Pallas kernels, stats(): pl.pallas_call(kernel, grid=(consumers // block,), in_specs=[pl.BlockSpec...  9.48 us
    all_to_all x1, starting transfers between devices, body(): lax.all_to_all(sent.reshape(holders, each, width), 'prod', split_axis=0,...  9.4 us
    pallas_call x3, Pallas kernels, panel(): pl.pallas_call(kernel, grid=(1,), in_specs=[pl.BlockSpec((rows, depth), l...  8.27 us
    unnamed x23, local copies, waits for them, and re-layouts  8.13 us
    pallas_call x1, Pallas kernels, share_sums(): pl.pallas_call(kernel, grid=(consumers // block,), in_specs=[pl.BlockSpec...  7.18 us
  transfers between devices with their start and end apart: 17, of which 8 were waited for; matrix products, arithmetic and copies ran while one was open for 6% of the time, Pallas kernels for 17%

profile of v4, /device:TPU:1, one launch (start us, length us, event | category | flops | bytes accessed | tf_op | source)
XLA Modules:
  0.0 129.1 jit_solution(17340043428396604494)
XLA Ops:
  0.6 0.7 reduce-precision_convert_fusion.1
  1.4 0.3 copy.47
  1.8 5.1 %sort.15 = (s32[2048]{0:T(1024)S(1)}, s32[2048]{0:T(1024)S(1)}) sort(s32[2048]{0:T(1024)} %param.14, s32[2048]{0:T(1024)S(1)} %iota.8), dimensions={0}, to_apply=%region_0.1 | sort | flops 22528 | bytes 32768 | tf_op jit(solution)/shard_map/sort | solution.py:284
  7.0 0.1 copy.48
  7.1 0.1 copy.52
  7.3 0.1 fusion.34
  7.4 1.3 %fusion.12.chars_ref = bf16[2048,256]{1,0:T(8,128)(2,1)S(1)} fusion(bf16[2048,3]{1,0:T(8,128)(2,1)S(1)} %copy.47, bf16[2048,128]{1,0:T(8,128)(2,1)} %param.11), kind=kLoop, calls=%fused_computation.19 | loop fusion | flops 3145728 | bytes 1585152 | tf_op jit(solution)/shard_map/concatenate | solution.py:281
  8.8 0.5 fusion.9
  9.3 0.8 fusion.21.gate_ref
  10.0 11.3 %all-to-all-start = ((bf16[32,16,256]{2,1,0:T(8,128)(2,1)}), bf16[32,16,256]{2,1,0:T(8,128)(2,1)S(1)}, u32[]{:S(2)}, u32[]{:S(2)}) async-start(bf16[32,16,256]{2,1,0:T(8,128)(2,1)} %fusion.21.gate_ref), calls=%async_computation | async-start | bytes 524288 | tf_op jit(solution)/shard_map/all_to_all | solution.py:294
  21.4 9.5 %stats.1.stat_ref = f32[2,4096]{1,0:T(2,128)S(1)} custom-call(bf16[2048,256]{1,0:T(8,128)(2,1)S(1)} %fusion.12.chars_ref, bf16[4096,128]{1,0:T(8,128)(2,1)S(1)} %copy-done, bf16[32,16,256]{2,1,0:T(8,128)(2,1)} %fusion.21.gate_ref), custom_call_target="tpu_custom_call" | custom-call | tf_op jit(solution)/shard_map/stats/pallas_call | solution.py:54
  30.9 0.1 copy.56
  31.1 2.4 %pick_rows.1 = (bf16[2560,256]{1,0:T(8,128)(2,1)S(1)}, f32[2,4096]{1,0:T(2,128)S(1)}) custom-call(s32[64,32]{1,0:T(8,128)S(1)} %fusion.28.ids_ref, bf16[2048,256]{1,0:T(8,128)(2,1)S(1)} %fusion.12.chars_ref, bf16[16,256]{1,0:T(8,128)(2,1)S(1)} %pad.19.tail_ref, f32[2,4096]{1,0:T(2,128)S(1)} %stats.1.stat_ref), custom_call_target="tpu_custom_call" | custom-call | tf_op jit(solution)/shard_map/pick_rows/pallas_call | solution.py:90
  33.5 1.0 copy-done.1
  34.6 9.4 %all-to-all-start.1 = ((bf16[32,80,256]{2,1,0:T(8,128)(2,1)}), bf16[32,80,256]{2,1,0:T(8,128)(2,1)S(1)}, u32[]{:S(2)}, u32[]{:S(2)}) async-start(bf16[32,80,256]{2,1,0:T(8,128)(2,1)} %bitcast.29), calls=%async_computation.1 | async-start | bytes 2621440 | tf_op jit(solution)/shard_map/all_to_all | solution.py:304
  44.0 0.5 slice.99
  45.2 21.8 %conditional.1 = (f32[2,4096]{1,0:T(2,128)S(1)}) conditional(s32[]{:T(128)} %bitcast.8, f32[2,4096]{1,0:T(2,128)S(1)} %get-tuple-element.31, f32[2,4096]{1,0:T(2,128)S(1)} %get-tuple-element.31), branch_computations={%region_2.3_spmd, %region_3.4_spmd} | conditional | flops 98304 | bytes 884864 | solution.py:318
  45.2 1.3 %collective-permute-start = (f32[2,4096]{1,0:T(2,128)S(1)}, f32[2,4096]{1,0:T(2,128)S(1)}, u32[]{:S(2)}, u32[]{:S(2)}) collective-permute-start(f32[2,4096]{1,0:T(2,128)S(1)} %param.1), channel_id=1, source_target_pairs={{0,1},{1,0},{2,3},{3,2},{4,5},{5,4},{6,7},{7,6},{8,9},{9,8},{10,11... | collective-permute-start | bytes 98312 | tf_op jit(solution)/shard_map/cond/branch_1_fun/ppermute | solution.py:256
  46.5 12.7 %collective-permute-done = f32[2,4096]{1,0:T(2,128)S(1)} collective-permute-done((f32[2,4096]{1,0:T(2,128)S(1)}, f32[2,4096]{1,0:T(2,128)S(1)}, u32[]{:S(2)}, u32[]{:S(2)}) %collective-permute-start) | collective-permute-done | bytes 32800 | tf_op jit(solution)/shard_map/cond/branch_1_fun/ppermute | solution.py:256
  59.4 1.9 %collective-permute-start.1 = (f32[2,4096]{1,0:T(2,128)S(1)}, f32[2,4096]{1,0:T(2,128)S(1)}, u32[]{:S(2)}, u32[]{:S(2)}) collective-permute-start(f32[2,4096]{1,0:T(2,128)S(1)} %pad_maximum_fusion), channel_id=1, source_target_pairs={{0,3},{1,2},{2,1},{3,0},{4,7},{5,6},{6,5},{7,4},{8,11},{9,10},{10,... | collective-permute-start | bytes 98312 | tf_op jit(solution)/shard_map/cond/branch_1_fun/ppermute | solution.py:256
  61.2 2.5 %collective-permute-done.1 = f32[2,4096]{1,0:T(2,128)S(1)} collective-permute-done((f32[2,4096]{1,0:T(2,128)S(1)}, f32[2,4096]{1,0:T(2,128)S(1)}, u32[]{:S(2)}, u32[]{:S(2)}) %collective-permute-start.1) | collective-permute-done | bytes 32800 | tf_op jit(solution)/shard_map/cond/branch_1_fun/ppermute | solution.py:256
  63.8 1.3 collective-permute-start.2
  65.1 1.6 %collective-permute-done.2 = f32[2,4096]{1,0:T(2,128)S(1)} collective-permute-done((f32[2,4096]{1,0:T(2,128)S(1)}, f32[2,4096]{1,0:T(2,128)S(1)}, u32[]{:S(2)}, u32[]{:S(2)}) %collective-permute-start.2) | collective-permute-done | bytes 32800 | tf_op jit(solution)/shard_map/cond/branch_1_fun/ppermute | solution.py:256
  67.0 2.3 %place_rows.1 = (bf16[2048,256]{1,0:T(8,128)(2,1)S(1)}, f32[2,4096]{1,0:T(2,128)S(1)}) custom-call(s32[1,2048]{1,0:T(1,128)S(1)} %bitcast.30, bf16[2560,256]{1,0:T(8,128)(2,1)S(1)} %bitcast.28, f32[2,4096]{1,0:T(2,128)S(1)} %get-tuple-element.78.stat_ref), custom_call_target="tpu_custom_call" | custom-call | tf_op jit(solution)/shard_map/place_rows/pallas_call | solution.py:114
  69.3 2.5 %collective-permute-start.3 = (f32[2,4096]{1,0:T(2,128)S(1)}, f32[2,4096]{1,0:T(2,128)S(1)}, u32[]{:S(2)}, u32[]{:S(2)}) collective-permute-start(f32[2,4096]{1,0:T(2,128)S(1)} %get-tuple-element.32), channel_id=1, source_target_pairs={{0,12},{1,13},{2,14},{3,15},{4,8},{5,9},{6,10},{7,11},{8,4},{9,5},... | collective-permute-start | bytes 98312 | tf_op jit(solution)/shard_map/ppermute | solution.py:256
  71.8 1.6 %collective-permute-done.3 = f32[2,4096]{1,0:T(2,128)S(1)} collective-permute-done((f32[2,4096]{1,0:T(2,128)S(1)}, f32[2,4096]{1,0:T(2,128)S(1)}, u32[]{:S(2)}, u32[]{:S(2)}) %collective-permute-start.3) | collective-permute-done | bytes 32800 | tf_op jit(solution)/shard_map/ppermute | solution.py:256
  73.5 2.8 %collective-permute-start.4 = (f32[2,4096]{1,0:T(2,128)S(1)}, f32[2,4096]{1,0:T(2,128)S(1)}, u32[]{:S(2)}, u32[]{:S(2)}) collective-permute-start(f32[2,4096]{1,0:T(2,128)S(1)} %pad_maximum_fusion.4), channel_id=1, source_target_pairs={{0,16},{1,17},{2,18},{3,19},{4,20},{5,21},{6,22},{7,23},{8,24},{9,... | collective-permute-start | bytes 98312 | tf_op jit(solution)/shard_map/ppermute | solution.py:256
  76.3 1.6 %collective-permute-done.4 = f32[2,4096]{1,0:T(2,128)S(1)} collective-permute-done((f32[2,4096]{1,0:T(2,128)S(1)}, f32[2,4096]{1,0:T(2,128)S(1)}, u32[]{:S(2)}, u32[]{:S(2)}) %collective-permute-start.4) | collective-permute-done | bytes 32800 | tf_op jit(solution)/shard_map/ppermute | solution.py:256
  77.8 0.1 maximum_maximum_fusion
  78.0 4.6 %first_panel.1 = (f32[512,256]{1,0:T(8,128)S(1)}, f32[512,128]{1,0:T(8,128)S(1)}, bf16[256,4096]{1,0:T(8,128)(2,1)S(1)}, f32[256,128]{1,0:T(8,128)S(1)}) custom-call(bf16[2048,256]{1,0:T(8,128)(2,1)S(1)} %get-tuple-element.33.chars_ref, bf16[4096,128]{1,0:T(8,128)(2,1)S(1)} %copy-done, f32[3,4096]{1,0:T(4,128)S(1)} %pad_maximum_fusion.3.rows_ref, ...), custom_call_target="tpu_custom_call" | custom-call | flops 2147483648 | bytes 1048576 | tf_op jit(solution)/shard_map/first_panel/pallas_call | solution.py:153
  82.7 1.3 %copy-done.5 = bf16[256,4096]{1,0:T(8,128)(2,1)} copy-done((bf16[256,4096]{1,0:T(8,128)(2,1)}, bf16[256,4096]{1,0:T(8,128)(2,1)S(1)}, u32[]{:S(2)}) %copy-start.5) | copy-done | bytes 2097176
  84.0 6.7 %collective-permute-start.5 = (f32[512,256]{1,0:T(8,128)S(1)}, f32[512,256]{1,0:T(8,128)}, u32[]{:S(2)}, u32[]{:S(2)}) collective-permute-start(f32[512,256]{1,0:T(8,128)S(1)} %get-tuple-element.35.gate_ref), channel_id=1, source_target_pairs={{0,32},{32,0},{64,96},{96,64},{1,33},{33,1},{65,97},{97,65},{2,34}... | collective-permute-start | bytes 1572872 | tf_op jit(solution)/shard_map/ppermute | solution.py:256
  90.7 0.1 reduce_sum.58
  90.8 0.1 collective-permute-start.6
  90.9 1.3 %collective-permute-done.6 = f32[256]{0:T(256)S(1)} collective-permute-done((f32[256]{0:T(256)S(1)}, f32[256]{0:T(256)S(1)}, u32[]{:S(2)}, u32[]{:S(2)}) %collective-permute-start.6) | collective-permute-done | bytes 1056 | tf_op jit(solution)/shard_map/ppermute | solution.py:256
  92.2 0.4 collective-permute-start.7
  92.6 1.2 copy-done.3
  93.9 1.6 %copy-done.6 = bf16[256,4096]{1,0:T(8,128)(2,1)S(1)} copy-done((bf16[256,4096]{1,0:T(8,128)(2,1)S(1)}, bf16[256,4096]{1,0:T(8,128)(2,1)}, u32[]{:S(2)}) %copy-start.6) | copy-done | bytes 2097176
  95.4 2.5 %panel.3 = (f32[512,256]{1,0:T(8,128)S(1)}, f32[512,128]{1,0:T(8,128)S(1)}) custom-call(bf16[2048,256]{1,0:T(8,128)(2,1)S(1)} %copy-done.3, bf16[4096,128]{1,0:T(8,128)(2,1)S(1)} %copy-done, f32[3,4096]{1,0:T(4,128)S(1)} %pad_maximum_fusion.3.rows_ref, bf16[256,4096]{1,0:T(8,128)(2,1)S(1)} %copy-done.6, f32[512,256]{1,0:T(8,128)S(1)} %get-tuple-element.35.gate_ref), custom_call_target="tpu_custom_call" | custom-call | flops 2147483648 | bytes 1048576 | tf_op jit(solution)/shard_map/panel/pallas_call | solution.py:196
  98.0 1.2 fusion.22
  99.1 3.3 %panel.4 = (f32[512,256]{1,0:T(8,128)}, f32[512,128]{1,0:T(8,128)S(1)}) custom-call(bf16[2048,256]{1,0:T(8,128)(2,1)S(1)} %copy-done.3, bf16[4096,128]{1,0:T(8,128)(2,1)S(1)} %copy-done, f32[3,4096]{1,0:T(4,128)S(1)} %pad_maximum_fusion.3.rows_ref, bf16[256,4096]{1,0:T(8,128)(2,1)S(1)} %copy-done.6, f32[1,256]{1,0:T(1,128)S(1)} %bitcast.32), custom_call_target="tpu_custom_call" | custom-call | flops 2147483648 | bytes 1048576 | tf_op jit(solution)/shard_map/panel/pallas_call | solution.py:196
  102.4 0.6 collective-permute-start.8
  103.1 1.1 collective-permute-start.11
  104.1 0.2 maximum_reduce_fusion.1
  104.3 1.2 copy-done.4
  105.6 1.6 %copy-done.7 = bf16[256,4096]{1,0:T(8,128)(2,1)S(1)} copy-done((bf16[256,4096]{1,0:T(8,128)(2,1)S(1)}, bf16[256,4096]{1,0:T(8,128)(2,1)}, u32[]{:S(2)}) %copy-start.7) | copy-done | bytes 2097176
  107.2 2.5 %panel.5 = (f32[512,256]{1,0:T(8,128)S(1)}, f32[512,128]{1,0:T(8,128)S(1)}) custom-call(bf16[2048,256]{1,0:T(8,128)(2,1)S(1)} %copy-done.4, bf16[4096,128]{1,0:T(8,128)(2,1)S(1)} %copy-done, f32[3,4096]{1,0:T(4,128)S(1)} %pad_maximum_fusion.3.rows_ref, bf16[256,4096]{1,0:T(8,128)(2,1)S(1)} %copy-done.7, f32[512,256]{1,0:T(8,128)} %get-tuple-element.39.gate_ref), custom_call_target="tpu_custom_call" | custom-call | flops 2147483648 | bytes 1048576 | tf_op jit(solution)/shard_map/panel/pallas_call | solution.py:196
  109.7 0.2 maximum_reduce_fusion
  109.9 1.8 %fusion.24 = (f32[256]{0:T(256)S(1)}, f16[512,256]{1,0:T(8,128)(2,1)}) fusion(f32[256]{0:T(256)S(1)} %get-tuple-element.53, f32[512,256]{1,0:T(8,128)S(1)} %get-tuple-element.40, f32[512,256]{1,0:T(8,128)} %collective-permute-done.8), kind=kLoop, calls=%fused_computation.39 | loop fusion | flops 524032 | bytes 1312768 | tf_op jit(solution)/shard_map/reduce_max | solution.py:357
  111.7 0.4 collective-permute-start.12
  112.1 7.2 %share_sums.1 = f32[2048,128]{1,0:T(8,128)S(1)} custom-call(bf16[2048,256]{1,0:T(8,128)(2,1)S(1)} %fusion.12.chars_ref, bf16[4096,128]{1,0:T(8,128)(2,1)S(1)} %copy-done, f32[3,4096]{1,0:T(4,128)S(1)} %pad_maximum_fusion.3.rows_ref, f32[1,256]{1,0:T(1,128)S(1)} %bitcast.31), custom_call_target="tpu_custom_call" | custom-call | tf_op jit(solution)/shard_map/share_sums/pallas_call | solution.py:238
  119.3 0.3 reduce_sum.59
  119.7 0.6 collective-permute-start.9
  120.3 0.8 collective-permute-done.9
  121.2 1.1 collective-permute-start.10
  122.2 1.4 %select_subtract_fusion.1 = (f32[512,256]{1,0:T(8,128)S(1)}, f32[512,256]{1,0:T(8,128)S(1)}) fusion(f16[512,256]{1,0:T(8,128)(2,1)} %collective-permute-done.11, f16[512,256]{1,0:T(8,128)(2,1)S(1)} %get-tuple-element.46, f32[256]{0:T(256)S(1)} %get-tuple-element.77, s32[256]{0:T(256)S(1)} %copy-done.10, f32[256]{0:T(256)S(1)} %get-tuple-element.52, ...), kind=kLoop, calls=%fused_computation.29 | loop fusion | flops 1835008 | bytes 2104320 | tf_op jit(solution)/shard_map/sub | solution.py:342
  123.6 0.6 fusion.19
  124.2 0.7 collective-permute-start.13
  124.9 0.6 fusion.17
  125.5 0.1 collective-permute-start.14
  125.6 0.6 slice_bitcast_fusion.1
  126.2 0.9 multiply_reduce_fusion
  127.2 0.3 collective-permute-done.14
  127.5 1.6 %maximum_select_fusion = f32[2048,256]{1,0:T(8,128)} fusion(f32[512,256]{1,0:T(8,128)S(1)} %collective-permute-done.14, f32[512,256]{1,0:T(8,128)S(1)} %collective-permute-done.13, f32[512,256]{1,0:T(8,128)S(1)} %bitcast.36, f32[512,256]{1,0:T(8,128)S(1)} %bitcast.34, pred[]{:T(512)S(6)} %eq.61), kind=kLoop, calls=%fused_computation.13 | loop fusion | flops 3670016 | bytes 4194305 | tf_op jit(solution)/shard_map/jit(_where)/select_n | solution.py:376
  (61 shorter events, 1.0 us)
Async XLA Ops:
  0.6 8.1 %copy-start.10 = (s32[256]{0:T(256)S(1)}, s32[256]{0:T(256)}, u32[]{:S(2)}) copy-start(s32[256]{0:T(256)} %param.13) | copy-start | bytes 3076
  7.4 14.0 %copy-start = (bf16[4096,128]{1,0:T(8,128)(2,1)S(1)}, bf16[4096,128]{1,0:T(8,128)(2,1)}, u32[]{:S(2)}) copy-start(bf16[4096,128]{1,0:T(8,128)(2,1)} %tastes_ref.11) | copy-start | bytes 3145732
  10.0 20.9 %all-to-all-start = ((bf16[32,16,256]{2,1,0:T(8,128)(2,1)}), bf16[32,16,256]{2,1,0:T(8,128)(2,1)S(1)}, u32[]{:S(2)}, u32[]{:S(2)}) async-start(bf16[32,16,256]{2,1,0:T(8,128)(2,1)} %fusion.21.gate_ref), calls=%async_computation | async-start | bytes 524288 | tf_op jit(solution)/shard_map/all_to_all | solution.py:294
  33.5 1.1 copy-start.1
  34.6 43.4 %copy-start.9 = (f32[4096]{0:T(1024)S(1)}, f32[4096]{0:T(1024)}, u32[]{:S(2)}) copy-start(f32[4096]{0:T(1024)} %param.10) | copy-start | bytes 49156
  34.6 32.4 %all-to-all-start.1 = ((bf16[32,80,256]{2,1,0:T(8,128)(2,1)}), bf16[32,80,256]{2,1,0:T(8,128)(2,1)S(1)}, u32[]{:S(2)}, u32[]{:S(2)}) async-start(bf16[32,80,256]{2,1,0:T(8,128)(2,1)} %bitcast.29), calls=%async_computation.1 | async-start | bytes 2621440 | tf_op jit(solution)/shard_map/all_to_all | solution.py:304
  45.2 14.1 %collective-permute-start = (f32[2,4096]{1,0:T(2,128)S(1)}, f32[2,4096]{1,0:T(2,128)S(1)}, u32[]{:S(2)}, u32[]{:S(2)}) collective-permute-start(f32[2,4096]{1,0:T(2,128)S(1)} %param.1), channel_id=1, source_target_pairs={{0,1},{1,0},{2,3},{3,2},{4,5},{5,4},{6,7},{7,6},{8,9},{9,8},{10,11... | collective-permute-start | bytes 98312 | tf_op jit(solution)/shard_map/cond/branch_1_fun/ppermute | solution.py:256
  59.4 4.3 %collective-permute-start.1 = (f32[2,4096]{1,0:T(2,128)S(1)}, f32[2,4096]{1,0:T(2,128)S(1)}, u32[]{:S(2)}, u32[]{:S(2)}) collective-permute-start(f32[2,4096]{1,0:T(2,128)S(1)} %pad_maximum_fusion), channel_id=1, source_target_pairs={{0,3},{1,2},{2,1},{3,0},{4,7},{5,6},{6,5},{7,4},{8,11},{9,10},{10,... | collective-permute-start | bytes 98312 | tf_op jit(solution)/shard_map/cond/branch_1_fun/ppermute | solution.py:256
  63.8 2.8 %collective-permute-start.2 = (f32[2,4096]{1,0:T(2,128)S(1)}, f32[2,4096]{1,0:T(2,128)S(1)}, u32[]{:S(2)}, u32[]{:S(2)}) collective-permute-start(f32[2,4096]{1,0:T(2,128)S(1)} %pad_maximum_fusion.1), channel_id=1, source_target_pairs={{0,4},{1,5},{2,6},{3,7},{4,0},{5,1},{6,2},{7,3},{8,12},{9,13},{10,... | collective-permute-start | bytes 98312 | tf_op jit(solution)/shard_map/cond/branch_1_fun/ppermute | solution.py:256
  69.3 13.3 %copy-start.2 = (bf16[2048,256]{1,0:T(8,128)(2,1)}, bf16[2048,256]{1,0:T(8,128)(2,1)S(1)}, u32[]{:S(2)}) copy-start(bf16[2048,256]{1,0:T(8,128)(2,1)S(1)} %get-tuple-element.33.chars_ref) | copy-start | bytes 3145732
  69.3 4.1 %collective-permute-start.3 = (f32[2,4096]{1,0:T(2,128)S(1)}, f32[2,4096]{1,0:T(2,128)S(1)}, u32[]{:S(2)}, u32[]{:S(2)}) collective-permute-start(f32[2,4096]{1,0:T(2,128)S(1)} %get-tuple-element.32), channel_id=1, source_target_pairs={{0,12},{1,13},{2,14},{3,15},{4,8},{5,9},{6,10},{7,11},{8,4},{9,5},... | collective-permute-start | bytes 98312 | tf_op jit(solution)/shard_map/ppermute | solution.py:256
  73.5 4.3 %collective-permute-start.4 = (f32[2,4096]{1,0:T(2,128)S(1)}, f32[2,4096]{1,0:T(2,128)S(1)}, u32[]{:S(2)}, u32[]{:S(2)}) collective-permute-start(f32[2,4096]{1,0:T(2,128)S(1)} %pad_maximum_fusion.4), channel_id=1, source_target_pairs={{0,16},{1,17},{2,18},{3,19},{4,20},{5,21},{6,22},{7,23},{8,24},{9,... | collective-permute-start | bytes 98312 | tf_op jit(solution)/shard_map/ppermute | solution.py:256
  82.6 1.3 %copy-start.5 = (bf16[256,4096]{1,0:T(8,128)(2,1)}, bf16[256,4096]{1,0:T(8,128)(2,1)S(1)}, u32[]{:S(2)}) copy-start(bf16[256,4096]{1,0:T(8,128)(2,1)S(1)} %get-tuple-element.34.weight_ref) | copy-start | bytes 6291460
  84.0 14.0 %collective-permute-start.5 = (f32[512,256]{1,0:T(8,128)S(1)}, f32[512,256]{1,0:T(8,128)}, u32[]{:S(2)}, u32[]{:S(2)}) collective-permute-start(f32[512,256]{1,0:T(8,128)S(1)} %get-tuple-element.35.gate_ref), channel_id=1, source_target_pairs={{0,32},{32,0},{64,96},{96,64},{1,33},{33,1},{65,97},{97,65},{2,34}... | collective-permute-start | bytes 1572872 | tf_op jit(solution)/shard_map/ppermute | solution.py:256
  90.8 1.4 %collective-permute-start.6 = (f32[256]{0:T(256)S(1)}, f32[256]{0:T(256)S(1)}, u32[]{:S(2)}, u32[]{:S(2)}) collective-permute-start(f32[256]{0:T(256)S(1)} %reduce_sum.58), channel_id=1, source_target_pairs={{0,32},{32,0},{64,96},{96,64},{1,33},{33,1},{65,97},{97,65},{2,34}... | collective-permute-start | bytes 3080 | tf_op jit(solution)/shard_map/ppermute | solution.py:256
  92.2 5.7 %collective-permute-start.7 = (f32[256]{0:T(256)S(1)}, f32[256]{0:T(256)S(1)}, u32[]{:S(2)}, u32[]{:S(2)}) collective-permute-start(f32[256]{0:T(256)S(1)} %add.126), channel_id=1, source_target_pairs={{0,64},{32,96},{64,0},{96,32},{1,65},{33,97},{65,1},{97,33},{2,66}... | collective-permute-start | bytes 3080 | tf_op jit(solution)/shard_map/ppermute | solution.py:256
  92.6 1.2 copy-start.3
  93.9 1.6 %copy-start.6 = (bf16[256,4096]{1,0:T(8,128)(2,1)S(1)}, bf16[256,4096]{1,0:T(8,128)(2,1)}, u32[]{:S(2)}) copy-start(bf16[256,4096]{1,0:T(8,128)(2,1)} %copy-done.5) | copy-start | bytes 6291460
  102.4 7.5 %collective-permute-start.8 = (f32[512,256]{1,0:T(8,128)}, f32[512,256]{1,0:T(8,128)}, u32[]{:S(2)}, u32[]{:S(2)}) collective-permute-start(f32[512,256]{1,0:T(8,128)} %get-tuple-element.39.gate_ref), channel_id=1, source_target_pairs={{0,32},{32,0},{64,96},{96,64},{1,33},{33,1},{65,97},{97,65},{2,34}... | collective-permute-start | bytes 1572872 | tf_op jit(solution)/shard_map/ppermute | solution.py:256
  103.1 19.2 %collective-permute-start.11 = (f16[512,256]{1,0:T(8,128)(2,1)S(1)}, f16[512,256]{1,0:T(8,128)(2,1)}, u32[]{:S(2)}, u32[]{:S(2)}) collective-permute-start(f16[512,256]{1,0:T(8,128)(2,1)S(1)} %get-tuple-element.46), channel_id=1, source_target_pairs={{0,64},{32,96},{64,0},{96,32},{1,65},{33,97},{65,1},{97,33},{2,66}... | collective-permute-start | bytes 786440 | tf_op jit(solution)/shard_map/ppermute | solution.py:256
  104.3 1.2 copy-start.4
  105.6 1.6 %copy-start.7 = (bf16[256,4096]{1,0:T(8,128)(2,1)S(1)}, bf16[256,4096]{1,0:T(8,128)(2,1)}, u32[]{:S(2)}) copy-start(bf16[256,4096]{1,0:T(8,128)(2,1)} %copy-done.5) | copy-start | bytes 6291460
  111.7 8.6 %dynamic-slice-start = ((s32[2048]{0:T(1024)}, s32[]{:T(128)}), s32[1024]{0:T(1024)S(1)}, s32[]{:S(2)}) async-start(s32[2048]{0:T(1024)} %param.14, s32[]{:T(128)} %select_n.86), calls=%async_computation.2 | async-start | bytes 8704 | tf_op jit(solution)/shard_map/dynamic_slice | solution.py:334
  111.7 10.5 %collective-permute-start.12 = (f16[512,256]{1,0:T(8,128)(2,1)}, f16[512,256]{1,0:T(8,128)(2,1)}, u32[]{:S(2)}, u32[]{:S(2)}) collective-permute-start(f16[512,256]{1,0:T(8,128)(2,1)} %get-tuple-element.47), channel_id=1, source_target_pairs={{0,64},{32,96},{64,0},{96,32},{1,65},{33,97},{65,1},{97,33},{2,66}... | collective-permute-start | bytes 786440 | tf_op jit(solution)/shard_map/ppermute | solution.py:256
  119.3 4.3 %copy-start.8 = (f32[16,128,128]{2,1,0:T(8,128)S(1)}, f32[16,128,128]{2,1,0:T(8,128)}, u32[]{:S(2)}) copy-start(f32[16,128,128]{2,1,0:T(8,128)} %param.15) | copy-start | bytes 3145732
  119.7 1.5 %collective-permute-start.9 = (f32[4096]{0:T(1024)S(1)}, f32[4096]{0:T(1024)S(1)}, u32[]{:S(2)}, u32[]{:S(2)}) collective-permute-start(f32[4096]{0:T(1024)S(1)} %pad_maximum_fusion.6), channel_id=1, source_target_pairs={{0,32},{32,0},{64,96},{96,64},{1,33},{33,1},{65,97},{97,65},{2,34}... | collective-permute-start | bytes 49160 | tf_op jit(solution)/shard_map/ppermute | solution.py:256
  121.2 4.4 %collective-permute-start.10 = (f32[4096]{0:T(1024)S(1)}, f32[4096]{0:T(1024)S(1)}, u32[]{:S(2)}, u32[]{:S(2)}) collective-permute-start(f32[4096]{0:T(1024)S(1)} %fusion.51), channel_id=1, source_target_pairs={{0,64},{32,96},{64,0},{96,32},{1,65},{33,97},{65,1},{97,33},{2,66}... | collective-permute-start | bytes 49160 | tf_op jit(solution)/shard_map/ppermute | solution.py:256
  124.2 3.0 %collective-permute-start.13 = (f32[512,256]{1,0:T(8,128)S(1)}, f32[512,256]{1,0:T(8,128)S(1)}, u32[]{:S(2)}, u32[]{:S(2)}) collective-permute-start(f32[512,256]{1,0:T(8,128)S(1)} %bitcast.33), channel_id=1, source_target_pairs={{0,32},{32,0},{64,96},{96,64},{1,33},{33,1},{65,97},{97,65},{2,34}... | collective-permute-start | bytes 1572872 | tf_op jit(solution)/shard_map/ppermute | solution.py:256
  125.5 2.0 %collective-permute-start.14 = (f32[512,256]{1,0:T(8,128)S(1)}, f32[512,256]{1,0:T(8,128)S(1)}, u32[]{:S(2)}, u32[]{:S(2)}) collective-permute-start(f32[512,256]{1,0:T(8,128)S(1)} %bitcast.35), channel_id=1, source_target_pairs={{0,32},{32,0},{64,96},{96,64},{1,33},{33,1},{65,97},{97,65},{2,34}... | collective-permute-start | bytes 1572872 | tf_op jit(solution)/shard_map/ppermute | solution.py:256

commit v5 on v4

--- a/solution.py
+++ b/solution.py
@@ -70,41 +70,52 @@
 def pick_rows(ids_t, chars, tail, stat):
     per_pair, holders = ids_t.shape
     rows, depth = chars.shape
-    extra = tail.shape[0]
-    each = per_pair + extra
-    group = max(1, 256 // per_pair)
+    each = per_pair + 16
+    group, pair = 256 // per_pair, 128 // per_pair
 
     def kernel(ids_ref, chars_ref, tail_ref, stat_ref, out_ref, stat_out_ref):
         stat_out_ref[...] = stat_ref[...]
         lanes = lax.broadcasted_iota(jnp.int32, (per_pair, rows), 1)
         table = chars_ref[...]
         for start in range(0, holders, group):
-            span = range(start, min(start + group, holders))
+            span = range(start, start + group)
             marks = [jnp.where(ids_ref[:, q : q + 1] == lanes, 1.0, 0.0).astype(jnp.bfloat16) for q in span]
             picked = jnp.dot(jnp.concatenate(marks, axis=0), table, preferred_element_type=jnp.float32)
             for place, q in enumerate(span):
-                mine = picked[place * per_pair : (place + 1) * per_pair, :]
+                if place % pair == 0:
+                    beside = picked[place * per_pair : (place + pair) * per_pair, 128:].T[:8, :]
+                    block = jnp.concatenate([beside + tail_ref[0:8, :], tail_ref[8:16, :]], axis=0).astype(jnp.bfloat16)
+                mine = picked[place * per_pair : (place + 1) * per_pair, :128]
                 out_ref[q * each : q * each + per_pair, :] = mine.astype(jnp.bfloat16)
-                out_ref[q * each + per_pair : (q + 1) * each, :] = tail_ref[...]
-
-    return pl.pallas_call(
-        kernel,
-        out_shape=[jax.ShapeDtypeStruct((each * holders, depth), jnp.bfloat16), jax.ShapeDtypeStruct(stat.shape, stat.dtype)],
+                out_ref[q * each + per_pair : (q + 1) * each, :] = block
+
+    return pl.pallas_call(
+        kernel,
+        out_shape=[
+            jax.ShapeDtypeStruct((each * holders, depth // 2), jnp.bfloat16),
+            jax.ShapeDtypeStruct(stat.shape, stat.dtype),
+        ],
         compiler_params=pltpu.CompilerParams(vmem_limit_bytes=VMEM_BYTES),
         name="pick_rows",
     )(ids_t, chars, tail, stat)
 
 
-def place_rows(order, received, holders, stat):
+def place_rows(order, received, beside, holders, stat):
     rows = order.shape[1]
     total, depth = received.shape
     per_pair, each = rows // holders, total // holders
     chunk = 256
 
-    def kernel(order_ref, received_ref, stat_ref, out_ref, stat_out_ref):
+    def kernel(order_ref, received_ref, beside_ref, stat_ref, out_ref, stat_out_ref):
         stat_out_ref[...] = stat_ref[...]
         order_row = order_ref[...]
         table = jnp.concatenate([received_ref[q * each : q * each + per_pair, :] for q in range(holders)], axis=0)
+        blank = jnp.zeros((120, 128), jnp.float32)
+        columns = [
+            jnp.concatenate([beside_ref[:, start : start + 128], blank], axis=0).T.astype(jnp.bfloat16)
+            for start in range(0, rows, 128)
+        ]
+        table = jnp.concatenate([table, jnp.concatenate(columns, axis=0)], axis=1)
         for start in range(0, rows, chunk):
             ids = start + lax.broadcasted_iota(jnp.int32, (chunk, rows), 0)
             hot = jnp.where(ids == order_row, 1.0, 0.0).astype(jnp.bfloat16)
@@ -113,10 +124,10 @@
 
     return pl.pallas_call(
         kernel,
-        out_shape=[jax.ShapeDtypeStruct((rows, depth), jnp.bfloat16), jax.ShapeDtypeStruct(stat.shape, stat.dtype)],
+        out_shape=[jax.ShapeDtypeStruct((rows, 2 * depth), jnp.bfloat16), jax.ShapeDtypeStruct(stat.shape, stat.dtype)],
         compiler_params=pltpu.CompilerParams(vmem_limit_bytes=VMEM_BYTES),
         name="place_rows",
-    )(order, received, stat)
+    )(order, received, beside, stat)
 
 
 def lane_groups(values):
@@ -133,7 +144,9 @@
     block, chunk = 1024, 256
 
     def kernel(chars_ref, tastes_ref, rows_ref, cols_ref, panel_ref, share_ref, weight_ref, diag_ref):
-        @pl.when(pl.program_id(0) == 0)
+        step = pl.program_id(0)
+
+        @pl.when(step == 0)
         def _():
             panel_ref[...] = jnp.zeros_like(panel_ref)
             share_ref[...] = jnp.zeros_like(share_ref)
@@ -150,6 +163,11 @@
             share_ref[start : start + chunk, :] += lane_groups(scaled)
             panel_ref[start : start + chunk, :] += dot_nt(scaled.astype(jnp.bfloat16), weight)
 
+        @pl.when(step == pl.num_programs(0) - 1)
+        def _():
+            total = jnp.sum(diag_ref[...].T, axis=0, keepdims=True)
+            panel_ref[rows:, :] = jnp.broadcast_to(total, (8, cols))
+
     return pl.pallas_call(
         kernel,
         grid=(consumers // block,),
@@ -160,16 +178,15 @@
             pl.BlockSpec((cols, depth), lambda i: (0, 0)),
         ],
         out_specs=[
-            pl.BlockSpec((rows, cols), lambda i: (0, 0)),
+            pl.BlockSpec((rows + 8, cols), lambda i: (0, 0)),
             pl.BlockSpec((rows, 128), lambda i: (0, 0)),
             pl.BlockSpec((cols, block), lambda i: (0, i)),
-            pl.BlockSpec((cols, 128), lambda i: (0, 0)),
-        ],
+        ],
+        scratch_shapes=[pltpu.VMEM((cols, 128), jnp.float32)],
         out_shape=[
-            jax.ShapeDtypeStruct((rows, cols), jnp.float32),
+            jax.ShapeDtypeStruct((rows + 8, cols), jnp.float32),
             jax.ShapeDtypeStruct((rows, 128), jnp.float32),
             jax.ShapeDtypeStruct((cols, consumers), jnp.bfloat16),
-            jax.ShapeDtypeStruct((cols, 128), jnp.float32),
         ],
         compiler_params=pltpu.CompilerParams(vmem_limit_bytes=VMEM_BYTES),
         cost_estimate=pl.CostEstimate(
@@ -279,33 +296,39 @@
 
     pieces = jnp.stack(split3(mean_utility), axis=1)
     chars = jnp.concatenate([characteristics, jnp.pad(pieces, ((0, 0), (0, depth - 3)))], axis=1)
-    width = 2 * depth
 
     wanted, order = lax.sort((firm_map, lax.iota(jnp.int32, products)), num_keys=1)
     wanted = (wanted % products).reshape(holders, per_pair)
-    digits = jnp.concatenate([wanted // 256, wanted % 256], axis=1).astype(jnp.bfloat16)
-    digits = jnp.pad(digits, ((0, 0), (0, width - 2 * per_pair)))[:, None, :]
+    digits = jnp.concatenate([wanted // 256, wanted % 256], axis=1).astype(jnp.bfloat16)[:, None, :]
     product_ids = base + lax.iota(jnp.int32, products)
     hits = (panel_cols[:, None] == product_ids[None, :]).astype(jnp.bfloat16)
     col_part = jnp.dot(hits, chars, preferred_element_type=jnp.float32).astype(jnp.bfloat16)
     share_cols = cols // holders
-    message = jnp.concatenate([col_part.reshape(holders, share_cols, width), digits], axis=1)
-    message = jnp.pad(message, ((0, 0), (0, -(share_cols + 1) % 16), (0, 0)))
+    col_pieces = col_part[:, depth : depth + 3].reshape(holders, share_cols, 3).transpose(0, 2, 1)
+    col_pieces = jnp.pad(col_pieces, ((0, 0), (0, 4), (0, depth - share_cols)))
+    message = jnp.concatenate([col_part[:, :depth].reshape(holders, share_cols, depth), digits, col_pieces], axis=1)
     first = lax.all_to_all(message, "prod", split_axis=0, concat_axis=0, tiled=True)
 
     stat = stats(chars, tastes, message)
 
-    asked = first[:, share_cols, : 2 * per_pair].astype(jnp.int32)
+    asked = first[:, share_cols, :].astype(jnp.int32)
     ids = asked[:, :per_pair] * 256 + asked[:, per_pair:]
-    collected = jnp.sum(first[:, :share_cols, :].astype(jnp.float32), axis=0).astype(jnp.bfloat16)
-    collected = jnp.pad(collected, ((0, -share_cols % 16), (0, 0)))
-    each = per_pair + collected.shape[0]
-    sent, stat = pick_rows(ids.T, chars, collected, stat)
-    second = lax.all_to_all(sent.reshape(holders, each, width), "prod", split_axis=0, concat_axis=0, tiled=True)
-    col_chars = second[:, per_pair : per_pair + share_cols, :].reshape(cols, width)
-    half, quarter = products // 2, products // 4
-    kept_row = (order // half == core).astype(jnp.int32)
-    place = (order // quarter % 2) * half + kept_row * quarter + order % quarter
+    summed = jnp.sum(first.astype(jnp.float32), axis=0)
+    zeros = jnp.zeros((3, depth), jnp.float32)
+    tail = jnp.concatenate([zeros, summed[share_cols + 1 : share_cols + 4], zeros[:2], summed[:share_cols]], axis=0)
+    each = per_pair + 16
+    sent, stat = pick_rows(ids.T, chars, tail, stat)
+    second = lax.all_to_all(sent.reshape(holders, each, depth), "prod", split_axis=0, concat_axis=0, tiled=True)
+    col_pieces = second[:, per_pair + 3 : per_pair + 6, :share_cols].transpose(0, 2, 1).reshape(cols, 3)
+    col_chars = second[:, per_pair + 8 :, :].reshape(cols, depth)
+    col_chars = jnp.concatenate([col_chars, jnp.pad(col_pieces, ((0, 0), (0, depth - 3)))], axis=1)
+    mean_rows = second[:, per_pair : per_pair + 8, :].astype(jnp.float32)
+    odd = lax.axis_index("prod") % 2 == 1
+    mean_rows = jnp.where(odd, mean_rows[:, :, per_pair:], mean_rows[:, :, :per_pair])
+    mean_rows = jnp.pad(mean_rows[:, :3], ((0, 0), (0, 5), (0, 0))).transpose(1, 0, 2).reshape(8, products)
+    half = products // 2
+    place = (order // half == core).astype(jnp.int32) * half + order % half
+
     def join(stat, masks):
         for mask in masks:
             other = swap(stat, "prod", mask)
@@ -316,64 +339,52 @@
 
     masks = butterfly_masks(holders)
     stat = lax.cond(panel_cols[0] >= 0, lambda value: join(value, masks[:3]), lambda value: value, stat)
-    firm_chars, stat = place_rows(place.reshape(1, products), second.reshape(holders * each, width), holders, stat)
+    firm_chars, stat = place_rows(
+        place.reshape(1, products), second.reshape(holders * each, depth), mean_rows, holders, stat
+    )
     stat = join(stat, masks[3:])
     peak = jnp.maximum(stat[0], 0.0)
     denom = jnp.exp(-peak) + stat[1] * jnp.exp(stat[0] - peak)
     ratio = count_products / denom
 
     row_values = jnp.stack([peak, ratio, price_coef])
-    given, given_share, weighted, diag_part = first_panel(firm_chars, 4, tastes, row_values, col_chars)
-    diagonal = jnp.sum(diag_part, axis=1)
-    for mask in (1, 2):
-        diagonal = diagonal + swap(diagonal, "cons", mask)
+    given, given_share, weighted = first_panel(firm_chars, 2, tastes, row_values, col_chars)
+    got = swap(given, "cons", 1)
+    kept, kept_share = panel(firm_chars, 1, 2, tastes, row_values, weighted, given)
+    diagonal = given[half] + got[half]
     room = 32768.0 / (count_products * jnp.maximum(diagonal, 1e-25))
-
-    firm_count, block_size = inverses.shape[0], inverses.shape[1]
-    own_inverses = lax.dynamic_slice_in_dim(inverses, core * (firm_count // 2), firm_count // 2, 0)
-    firm_ids = lax.dynamic_slice_in_dim(firm_map, core * half, half, 0)
-    blocks = firm_count // 4
-    chip_sums, share_parts, responses = [], [], []
-
-    def respond(part, chip_sum, other_sum):
-        both = chip_sum.astype(jnp.float32) + other_sum.astype(jnp.float32)
-        part_ids = firm_ids[part * quarter : (part + 1) * quarter]
-        marks = part_ids[:, None] == panel_cols[None, :]
-        jacobian = both / (room[None, :] * count_consumers) - jnp.where(marks, diagonal[None, :] / count_consumers, 0.0)
-        response = jnp.einsum(
-            "fab,fbc->fac",
-            own_inverses[part * blocks : (part + 1) * blocks],
-            jacobian.reshape(blocks, block_size, cols),
-            precision=lax.Precision.HIGHEST,
-        ).reshape(quarter, cols)
-        responses.append((response, swap(response, "cons", 1)))
-
-    for part in (0, 1):
-        if part:
-            given, given_share = panel(firm_chars, 2 * part, 4, tastes, row_values, weighted, gate)
-        got = swap(given, "cons", 1)
-        kept, kept_share = panel(firm_chars, 2 * part + 1, 4, tastes, row_values, weighted, given)
-        fitted = (kept + got) * room[None, :]
-        chip_sum, gate = lax.optimization_barrier((fitted.astype(jnp.float16), jnp.max(fitted, axis=0, keepdims=True)))
-        chip_sums.append((chip_sum, swap(chip_sum, "cons", 2)))
-        share_parts.append((given_share, kept_share))
-
-    given_share = jnp.sum(jnp.concatenate([share_parts[0][0], share_parts[1][0]]), axis=1)
-    kept_share = jnp.sum(jnp.concatenate([share_parts[0][1], share_parts[1][1]]), axis=1)
+    fitted = (kept + got[:half]) * room[None, :]
+    chip_sum, gate = lax.optimization_barrier((fitted.astype(jnp.float16), jnp.max(fitted, axis=0, keepdims=True)))
+    other_sum = swap(chip_sum, "cons", 2)
+    other_diagonal = swap(diagonal, "cons", 2)
+
+    own_shares = jnp.sum(share_sums(chars, tastes, row_values, gate), axis=1)
+    given_share, kept_share = jnp.sum(given_share, axis=1), jnp.sum(kept_share, axis=1)
     first_half = jnp.where(core == 0, kept_share, given_share)
     second_half = jnp.where(core == 0, given_share, kept_share)
-    own_shares = jnp.sum(share_sums(chars, tastes, row_values, gate), axis=1)
     sums = jnp.concatenate([own_shares, first_half, second_half])
     for mask in (1, 2):
         sums = sums + swap(sums, "cons", mask)
     sums = sums / count_consumers
     shares, firm_shares = sums[:products], sums[products:]
 
-    respond(0, *chip_sums[0])
-    respond(1, *chip_sums[1])
-    mine = [pair[0] for pair in responses]
-    theirs = [pair[1] for pair in responses]
-    response = jnp.where(core == 0, jnp.concatenate(mine + theirs, axis=0), jnp.concatenate(theirs + mine, axis=0))
+    firm_count, block_size = inverses.shape[0], inverses.shape[1]
+    own_inverses = lax.dynamic_slice_in_dim(inverses, core * (firm_count // 2), firm_count // 2, 0)
+    firm_ids = lax.dynamic_slice_in_dim(firm_map, core * half, half, 0)
+    other_room = 32768.0 / (count_products * jnp.maximum(other_diagonal, 1e-25))
+    unfit, other_unfit = 1.0 / (room * count_consumers), 1.0 / (other_room * count_consumers)
+    unfit = jnp.where(own_shares[0] >= 0.0, unfit, 0.0)
+    cross = chip_sum.astype(jnp.float32) * unfit[None, :] + other_sum.astype(jnp.float32) * other_unfit[None, :]
+    diagonal = (diagonal + other_diagonal) / count_consumers
+    jacobian = cross - jnp.where(firm_ids[:, None] == panel_cols[None, :], diagonal[None, :], 0.0)
+    mine = jnp.einsum(
+        "fab,fbc->fac",
+        own_inverses,
+        jacobian.reshape(firm_count // 2, block_size, cols),
+        precision=lax.Precision.HIGHEST,
+    ).reshape(half, cols)
+    theirs = swap(mine, "cons", 1)
+    response = jnp.where(core == 0, jnp.concatenate([mine, theirs]), jnp.concatenate([theirs, mine]))
     markup = jnp.sum(inverses * firm_shares.reshape(firm_count, 1, block_size), axis=2).reshape(products)
     return (shares, markup, response)
 

time: 130 us -> 118 us (0.908)
  local copies, waits for them, and re-layouts: 9.97 us -> 5.35 us
  other arithmetic: 16.5 us -> 13.8 us
  waiting for transfers between devices: 22.5 us -> 20.1 us
  starting transfers between devices: 42.3 us -> 40.1 us
    unnamed x23 -> x20, local copies, waits for them, and re-layouts: 8.13 us -> 2.6 us
    pallas_call x3 -> x1, Pallas kernels: 8.27 us -> 4.68 us  [panel(): pl.pallas_call(kernel, grid=(1,), in_specs=[pl.BlockSpec((rows, depth), l...]
    pallas_call x1, Pallas kernels: 4.63 us -> 7.09 us  [first_panel(): pl.pallas_call(kernel, grid=(consumers // block,), in_specs=[pl.BlockSpec...]
    ppermute x15 -> x11, waiting for transfers between devices: 22.5 us -> 20.1 us  [swap(): return lax.ppermute(value, axis, [(i, i ^ mask) for i in range(size)])]
    ppermute x15 -> x11, starting transfers between devices: 21.5 us -> 19.4 us  [swap(): return lax.ppermute(value, axis, [(i, i ^ mask) for i in range(size)])]
    reduce_max x2 -> x1, other arithmetic: 2.98 us -> 0.97 us  [body(): jnp.max(fitted, axis=0, keepdims=True)]
  transfers between devices with their start and end apart: 17 -> 13, of which waited for: 8 -> 8; matrix products, arithmetic and copies ran while one was open for 6% -> 3% of each run, Pallas kernels for 17% -> 18%
where the time goes in v5:
time: 118 us
  starting transfers between devices  40.1 us (34%)
  Pallas kernels  34.2 us (29%)
  waiting for transfers between devices  20.1 us (17%)
  other arithmetic  13.8 us (12%)
  local copies, waits for them, and re-layouts  5.35 us (5%)
  between operations  2.44 us (2%)
  matrix products  1.51 us (1%)
    ppermute x11, waiting for transfers between devices, swap(): return lax.ppermute(value, axis, [(i, i ^ mask) for i in range(size)])  20.1 us
    ppermute x11, starting transfers between devices, swap(): return lax.ppermute(value, axis, [(i, i ^ mask) for i in range(size)])  19.4 us
    all_to_all x1, starting transfers between devices, body(): lax.all_to_all(message, 'prod', split_axis=0, concat_axis=0, tiled=True)  11.3 us
    pallas_call x1, Pallas kernels, stats(): pl.pallas_call(kernel, grid=(consumers // block,), in_specs=[pl.BlockSpec...  9.49 us
    all_to_all x1, starting transfers between devices, body(): lax.all_to_all(sent.reshape(holders, each, depth), 'prod', split_axis=0,...  9.38 us
    pallas_call x1, Pallas kernels, share_sums(): pl.pallas_call(kernel, grid=(consumers // block,), in_specs=[pl.BlockSpec...  7.19 us
    pallas_call x1, Pallas kernels, first_panel(): pl.pallas_call(kernel, grid=(consumers // block,), in_specs=[pl.BlockSpec...  7.09 us
    pallas_call x1, Pallas kernels, panel(): pl.pallas_call(kernel, grid=(1,), in_specs=[pl.BlockSpec((rows, depth), l...  4.68 us
  transfers between devices with their start and end apart: 13, of which 8 were waited for; matrix products, arithmetic and copies ran while one was open for 3% of the time, Pallas kernels for 18%

profile of v5, /device:TPU:1, one launch (start us, length us, event | category | flops | bytes accessed | tf_op | source)
XLA Modules:
  0.0 117.7 jit_solution(3020051457050472024)
XLA Ops:
  0.6 0.7 reduce-precision_convert_fusion.1
  1.4 0.3 copy.43
  1.8 1.2 %fusion.9.chars_ref = bf16[2048,256]{1,0:T(8,128)(2,1)S(1)} fusion(bf16[2048,3]{1,0:T(8,128)(2,1)S(1)} %copy.43, bf16[2048,128]{1,0:T(8,128)(2,1)} %param.11), kind=kLoop, calls=%fused_computation.18 | loop fusion | flops 3145728 | bytes 1585152 | tf_op jit(solution)/shard_map/concatenate | solution.py:298
  3.0 0.5 fusion.6
  3.6 0.3 copy.56
  3.8 4.4 %sort.15 = (s32[2048]{0:T(1024)S(1)}, s32[2048]{0:T(1024)S(1)}) sort(s32[2048]{0:T(1024)S(1)} %copy-done.5, s32[2048]{0:T(1024)S(1)} %iota.8), dimensions={0}, to_apply=%region_0.1 | sort | flops 22528 | bytes 32768 | tf_op jit(solution)/shard_map/sort | solution.py:300
  8.3 0.1 reshape.103
  8.4 0.1 copy.44
  8.5 0.1 copy.49
  8.6 0.7 fusion.20.gate_ref
  9.3 11.3 %all-to-all-start = ((bf16[32,16,128]{2,1,0:T(8,128)(2,1)}), bf16[32,16,128]{2,1,0:T(8,128)(2,1)S(1)}, u32[]{:S(2)}, u32[]{:S(2)}) async-start(bf16[32,16,128]{2,1,0:T(8,128)(2,1)} %fusion.20.gate_ref), calls=%async_computation | async-start | bytes 262144 | tf_op jit(solution)/shard_map/all_to_all | solution.py:310
  20.7 0.1 pad.42.clone
  20.8 9.5 %stats.1.stat_ref = f32[2,4096]{1,0:T(2,128)S(1)} custom-call(bf16[2048,256]{1,0:T(8,128)(2,1)S(1)} %fusion.9.chars_ref, bf16[4096,128]{1,0:T(8,128)(2,1)S(1)} %copy-done, bf16[32,16,128]{2,1,0:T(8,128)(2,1)} %fusion.20.gate_ref), custom_call_target="tpu_custom_call" | custom-call | tf_op jit(solution)/shard_map/stats/pallas_call | solution.py:54
  30.3 0.0 copy-start.8
  30.4 0.1 copy.55
  30.6 0.1 pad_maximum_fusion.8.tail_ref
  30.6 3.3 %pick_rows.1 = (bf16[2560,128]{1,0:T(8,128)(2,1)}, f32[2,4096]{1,0:T(2,128)S(1)}) custom-call(s32[64,32]{1,0:T(8,128)S(1)} %fusion.25.ids_ref, bf16[2048,256]{1,0:T(8,128)(2,1)S(1)} %fusion.9.chars_ref, f32[16,128]{1,0:T(8,128)S(1)} %pad_maximum_fusion.8.tail_ref, f32[2,4096]{1,0:T(2,128)S(1)} %stats.1.stat_ref), custom_call_target="tpu_custom_call" | custom-call | tf_op jit(solution)/shard_map/pick_rows/pallas_call | solution.py:92
  33.9 9.4 %all-to-all-start.1 = ((bf16[32,80,128]{2,1,0:T(8,128)(2,1)}), bf16[32,80,128]{2,1,0:T(8,128)(2,1)S(1)}, u32[]{:S(2)}, u32[]{:S(2)}) async-start(bf16[32,80,128]{2,1,0:T(8,128)(2,1)} %bitcast.9), calls=%async_computation.1 | async-start | bytes 1310720 | tf_op jit(solution)/shard_map/all_to_all | solution.py:321
  43.3 0.5 slice.132
  44.5 14.7 %conditional.1 = (f32[2,4096]{1,0:T(2,128)S(1)}) conditional(s32[]{:T(128)} %bitcast.12, f32[2,4096]{1,0:T(2,128)S(1)} %get-tuple-element.24, f32[2,4096]{1,0:T(2,128)S(1)} %get-tuple-element.24), branch_computations={%region_2.3_spmd, %region_3.4_spmd} | conditional | flops 98304 | bytes 884864 | solution.py:341
  44.5 1.3 %collective-permute-start = (f32[2,4096]{1,0:T(2,128)S(1)}, f32[2,4096]{1,0:T(2,128)S(1)}, u32[]{:S(2)}, u32[]{:S(2)}) collective-permute-start(f32[2,4096]{1,0:T(2,128)S(1)} %param.1), channel_id=1, source_target_pairs={{0,1},{1,0},{2,3},{3,2},{4,5},{5,4},{6,7},{7,6},{8,9},{9,8},{10,11... | collective-permute-start | bytes 98312 | tf_op jit(solution)/shard_map/cond/branch_1_fun/ppermute | solution.py:273
  45.8 5.7 %collective-permute-done = f32[2,4096]{1,0:T(2,128)S(1)} collective-permute-done((f32[2,4096]{1,0:T(2,128)S(1)}, f32[2,4096]{1,0:T(2,128)S(1)}, u32[]{:S(2)}, u32[]{:S(2)}) %collective-permute-start) | collective-permute-done | bytes 32800 | tf_op jit(solution)/shard_map/cond/branch_1_fun/ppermute | solution.py:273
  51.6 0.1 fusion.2
  51.7 1.9 %collective-permute-start.1 = (f32[2,4096]{1,0:T(2,128)S(1)}, f32[2,4096]{1,0:T(2,128)S(1)}, u32[]{:S(2)}, u32[]{:S(2)}) collective-permute-start(f32[2,4096]{1,0:T(2,128)S(1)} %pad_maximum_fusion), channel_id=1, source_target_pairs={{0,3},{1,2},{2,1},{3,0},{4,7},{5,6},{6,5},{7,4},{8,11},{9,10},{10,... | collective-permute-start | bytes 98312 | tf_op jit(solution)/shard_map/cond/branch_1_fun/ppermute | solution.py:273
  53.5 2.5 %collective-permute-done.1 = f32[2,4096]{1,0:T(2,128)S(1)} collective-permute-done((f32[2,4096]{1,0:T(2,128)S(1)}, f32[2,4096]{1,0:T(2,128)S(1)}, u32[]{:S(2)}, u32[]{:S(2)}) %collective-permute-start.1) | collective-permute-done | bytes 32800 | tf_op jit(solution)/shard_map/cond/branch_1_fun/ppermute | solution.py:273
  56.0 0.1 fusion.1
  56.1 1.3 %collective-permute-start.2 = (f32[2,4096]{1,0:T(2,128)S(1)}, f32[2,4096]{1,0:T(2,128)S(1)}, u32[]{:S(2)}, u32[]{:S(2)}) collective-permute-start(f32[2,4096]{1,0:T(2,128)S(1)} %pad_maximum_fusion.1), channel_id=1, source_target_pairs={{0,4},{1,5},{2,6},{3,7},{4,0},{5,1},{6,2},{7,3},{8,12},{9,13},{10,... | collective-permute-start | bytes 98312 | tf_op jit(solution)/shard_map/cond/branch_1_fun/ppermute | solution.py:273
  57.4 1.6 %collective-permute-done.2 = f32[2,4096]{1,0:T(2,128)S(1)} collective-permute-done((f32[2,4096]{1,0:T(2,128)S(1)}, f32[2,4096]{1,0:T(2,128)S(1)}, u32[]{:S(2)}, u32[]{:S(2)}) %collective-permute-start.2) | collective-permute-done | bytes 32800 | tf_op jit(solution)/shard_map/cond/branch_1_fun/ppermute | solution.py:273
  59.0 0.1 slice_maximum_fusion
  59.3 0.1 fusion.22
  59.4 0.1 reshape.107.beside_ref
  59.5 2.4 %place_rows.1 = (bf16[2048,256]{1,0:T(8,128)(2,1)S(1)}, f32[2,4096]{1,0:T(2,128)S(1)}) custom-call(s32[1,2048]{1,0:T(1,128)S(1)} %bitcast.41, bf16[2560,128]{1,0:T(8,128)(2,1)S(1)} %bitcast.40, f32[8,2048]{1,0:T(8,128)S(1)} %reshape.107.beside_ref, f32[2,4096]{1,0:T(2,128)S(1)} %get-tuple-element.61.stat_ref), custom_call_target="tpu_custom_call" | custom-call | tf_op jit(solution)/shard_map/place_rows/pallas_call | solution.py:125
  62.0 1.0 copy-done.1
  63.0 2.4 %collective-permute-start.3 = (f32[2,4096]{1,0:T(2,128)S(1)}, f32[2,4096]{1,0:T(2,128)S(1)}, u32[]{:S(2)}, u32[]{:S(2)}) collective-permute-start(f32[2,4096]{1,0:T(2,128)S(1)} %get-tuple-element.25), channel_id=1, source_target_pairs={{0,12},{1,13},{2,14},{3,15},{4,8},{5,9},{6,10},{7,11},{8,4},{9,5},... | collective-permute-start | bytes 98312 | tf_op jit(solution)/shard_map/ppermute | solution.py:273
  65.4 0.3 copy.53
  65.7 1.3 %collective-permute-done.3 = f32[2,4096]{1,0:T(2,128)S(1)} collective-permute-done((f32[2,4096]{1,0:T(2,128)S(1)}, f32[2,4096]{1,0:T(2,128)S(1)}, u32[]{:S(2)}, u32[]{:S(2)}) %collective-permute-start.3) | collective-permute-done | bytes 32800 | tf_op jit(solution)/shard_map/ppermute | solution.py:273
  66.9 0.1 fusion.30
  67.1 2.8 %collective-permute-start.4 = (f32[2,4096]{1,0:T(2,128)S(1)}, f32[2,4096]{1,0:T(2,128)S(1)}, u32[]{:S(2)}, u32[]{:S(2)}) collective-permute-start(f32[2,4096]{1,0:T(2,128)S(1)} %pad_maximum_fusion.5), channel_id=1, source_target_pairs={{0,16},{1,17},{2,18},{3,19},{4,20},{5,21},{6,22},{7,23},{8,24},{9,... | collective-permute-start | bytes 98312 | tf_op jit(solution)/shard_map/ppermute | solution.py:273
  69.8 1.6 %collective-permute-done.4 = f32[2,4096]{1,0:T(2,128)S(1)} collective-permute-done((f32[2,4096]{1,0:T(2,128)S(1)}, f32[2,4096]{1,0:T(2,128)S(1)}, u32[]{:S(2)}, u32[]{:S(2)}) %collective-permute-start.4) | collective-permute-done | bytes 32800 | tf_op jit(solution)/shard_map/ppermute | solution.py:273
  71.4 0.1 maximum_maximum_fusion
  71.6 1.2 %copy-done.2 = bf16[2048,256]{1,0:T(8,128)(2,1)S(1)} copy-done((bf16[2048,256]{1,0:T(8,128)(2,1)S(1)}, bf16[2048,256]{1,0:T(8,128)(2,1)}, u32[]{:S(2)}) %copy-start.2) | copy-done | bytes 1048600
  72.8 7.1 %first_panel.1 = (f32[1032,256]{1,0:T(8,128)S(1)}, f32[1024,128]{1,0:T(8,128)S(1)}, bf16[256,4096]{1,0:T(8,128)(2,1)S(1)}) custom-call(bf16[2048,256]{1,0:T(8,128)(2,1)S(1)} %copy-done.2, bf16[4096,128]{1,0:T(8,128)(2,1)S(1)} %copy-done, f32[3,4096]{1,0:T(4,128)S(1)} %pad_maximum_fusion.3.rows_ref, bf16[256,256]{1,0:T(8,128)(2,1)S(1)} %fusion.19.cols_ref), custom_call_target="tpu_custom_call" | custom-call | flops 4294967296 | bytes 2097152 | tf_op jit(solution)/shard_map/first_panel/pallas_call | solution.py:171
  79.9 6.8 %collective-permute-start.5 = (f32[1032,256]{1,0:T(8,128)S(1)}, f32[1032,256]{1,0:T(8,128)S(1)}, u32[]{:S(2)}, u32[]{:S(2)}) collective-permute-start(f32[1032,256]{1,0:T(8,128)S(1)} %get-tuple-element.28.gate_ref), channel_id=1, source_target_pairs={{0,32},{32,0},{64,96},{96,64},{1,33},{33,1},{65,97},{97,65},{2,34}... | collective-permute-start | bytes 3170312 | tf_op jit(solution)/shard_map/ppermute | solution.py:273
  86.7 4.7 %panel.1 = (f32[1024,256]{1,0:T(8,128)S(1)}, f32[1024,128]{1,0:T(8,128)S(1)}) custom-call(bf16[2048,256]{1,0:T(8,128)(2,1)S(1)} %copy-done.3, bf16[4096,128]{1,0:T(8,128)(2,1)S(1)} %copy-done, f32[3,4096]{1,0:T(4,128)S(1)} %pad_maximum_fusion.3.rows_ref, bf16[256,4096]{1,0:T(8,128)(2,1)S(1)} %get-tuple-element.27.weight_ref, ...), custom_call_target="tpu_custom_call" | custom-call | flops 4294967296 | bytes 2097152 | tf_op jit(solution)/shard_map/panel/pallas_call | solution.py:213
  91.4 1.0 fusion.15
  92.4 0.4 collective-permute-start.8
  92.8 0.2 reduce_sum.47
  93.0 0.2 reduce_sum.48
  93.2 0.0 dynamic-slice-start
  93.3 7.2 %share_sums.1 = f32[2048,128]{1,0:T(8,128)S(1)} custom-call(bf16[2048,256]{1,0:T(8,128)(2,1)S(1)} %fusion.9.chars_ref, bf16[4096,128]{1,0:T(8,128)(2,1)S(1)} %copy-done, f32[3,4096]{1,0:T(4,128)S(1)} %pad_maximum_fusion.3.rows_ref, f32[1,256]{1,0:T(1,128)S(1)} %bitcast.42), custom_call_target="tpu_custom_call" | custom-call | tf_op jit(solution)/shard_map/share_sums/pallas_call | solution.py:255
  100.5 0.3 reduce_sum.46
  100.8 1.1 collective-permute-start.9
  102.0 0.5 slice.174
  103.1 3.1 %collective-permute-done.9 = f32[256]{0:T(256)S(1)} collective-permute-done((f32[256]{0:T(256)S(1)}, f32[256]{0:T(256)S(1)}, u32[]{:S(2)}, u32[]{:S(2)}) %collective-permute-start.9) | collective-permute-done | bytes 1056 | tf_op jit(solution)/shard_map/ppermute | solution.py:273
  106.3 1.5 %select_subtract_fusion = f32[1024,256]{1,0:T(8,128)S(1)} fusion(f16[1024,256]{1,0:T(8,128)(2,1)} %collective-permute-done.8, f16[1024,256]{1,0:T(8,128)(2,1)} %get-tuple-element.33, f32[256]{0:T(256)S(1)} %get-tuple-element.60, s32[256]{0:T(256)S(1)} %copy-done.7, f32[256]{0:T(256)S(1)} %get-tuple-element.59, f32[256]{0:T(256)S(1)} %bitcast.50, ...), kind=kLoop, calls=%fused_computation.21 | loop fusion | flops 2097152 | bytes 2105344 | tf_op jit(solution)/shard_map/sub | solution.py:379
  107.8 1.0 fusion.13
  108.8 0.9 collective-permute-start.10
  109.7 0.1 collective-permute-start.6
  109.8 2.2 %collective-permute-done.6 = f32[4096]{0:T(1024)S(1)} collective-permute-done((f32[4096]{0:T(1024)S(1)}, f32[4096]{0:T(1024)S(1)}, u32[]{:S(2)}, u32[]{:S(2)}) %collective-permute-start.6) | collective-permute-done | bytes 16416 | tf_op jit(solution)/shard_map/ppermute | solution.py:273
  112.0 0.4 collective-permute-start.7
  112.4 2.2 %collective-permute-done.7 = f32[4096]{0:T(1024)S(1)} collective-permute-done((f32[4096]{0:T(1024)S(1)}, f32[4096]{0:T(1024)S(1)}, u32[]{:S(2)}, u32[]{:S(2)}) %collective-permute-start.7) | collective-permute-done | bytes 16416 | tf_op jit(solution)/shard_map/ppermute | solution.py:273
  114.6 0.6 slice_bitcast_fusion.4
  115.2 0.9 multiply_reduce_fusion
  116.2 1.6 %maximum_select_fusion = f32[2048,256]{1,0:T(8,128)} fusion(f32[1024,256]{1,0:T(8,128)S(1)} %collective-permute-done.10, f32[1024,256]{1,0:T(8,128)S(1)} %bitcast.44, pred[]{:T(512)S(6)} %eq.54), kind=kLoop, calls=%fused_computation.13 | loop fusion | flops 1572864 | bytes 4194305 | tf_op jit(solution)/shard_map/jit(_where)/select_n | solution.py:387
  (58 shorter events, 0.6 us)
Async XLA Ops:
  0.6 2.4 %copy-start.7 = (s32[256]{0:T(256)S(1)}, s32[256]{0:T(256)}, u32[]{:S(2)}) copy-start(s32[256]{0:T(256)} %param.13) | copy-start | bytes 3076
  1.8 2.1 %copy-start.5 = (s32[2048]{0:T(1024)S(1)}, s32[2048]{0:T(1024)}, u32[]{:S(2)}) copy-start(s32[2048]{0:T(1024)} %param.14) | copy-start | bytes 24580
  3.0 17.8 %copy-start = (bf16[4096,128]{1,0:T(8,128)(2,1)S(1)}, bf16[4096,128]{1,0:T(8,128)(2,1)}, u32[]{:S(2)}) copy-start(bf16[4096,128]{1,0:T(8,128)(2,1)} %tastes_ref.7) | copy-start | bytes 3145732
  9.3 21.0 %all-to-all-start = ((bf16[32,16,128]{2,1,0:T(8,128)(2,1)}), bf16[32,16,128]{2,1,0:T(8,128)(2,1)S(1)}, u32[]{:S(2)}, u32[]{:S(2)}) async-start(bf16[32,16,128]{2,1,0:T(8,128)(2,1)} %fusion.20.gate_ref), calls=%async_computation | async-start | bytes 262144 | tf_op jit(solution)/shard_map/all_to_all | solution.py:310
  30.3 29.0 %copy-start.8 = (pred[8]{0:T(512)(128)(4,1)S(1)}, pred[8]{0:T(512)(128)(4,1)}, u32[]{:S(2)}) copy-start(pred[8]{0:T(512)(128)(4,1)} %constant.116.clone.1) | copy-start | bytes 28
  33.9 37.6 %copy-start.6 = (f32[4096]{0:T(1024)S(1)}, f32[4096]{0:T(1024)}, u32[]{:S(2)}) copy-start(f32[4096]{0:T(1024)} %param.10) | copy-start | bytes 49156
  33.9 25.3 %all-to-all-start.1 = ((bf16[32,80,128]{2,1,0:T(8,128)(2,1)}), bf16[32,80,128]{2,1,0:T(8,128)(2,1)S(1)}, u32[]{:S(2)}, u32[]{:S(2)}) async-start(bf16[32,80,128]{2,1,0:T(8,128)(2,1)} %bitcast.9), calls=%async_computation.1 | async-start | bytes 1310720 | tf_op jit(solution)/shard_map/all_to_all | solution.py:321
  44.5 7.0 %collective-permute-start = (f32[2,4096]{1,0:T(2,128)S(1)}, f32[2,4096]{1,0:T(2,128)S(1)}, u32[]{:S(2)}, u32[]{:S(2)}) collective-permute-start(f32[2,4096]{1,0:T(2,128)S(1)} %param.1), channel_id=1, source_target_pairs={{0,1},{1,0},{2,3},{3,2},{4,5},{5,4},{6,7},{7,6},{8,9},{9,8},{10,11... | collective-permute-start | bytes 98312 | tf_op jit(solution)/shard_map/cond/branch_1_fun/ppermute | solution.py:273
  51.7 4.3 %collective-permute-start.1 = (f32[2,4096]{1,0:T(2,128)S(1)}, f32[2,4096]{1,0:T(2,128)S(1)}, u32[]{:S(2)}, u32[]{:S(2)}) collective-permute-start(f32[2,4096]{1,0:T(2,128)S(1)} %pad_maximum_fusion), channel_id=1, source_target_pairs={{0,3},{1,2},{2,1},{3,0},{4,7},{5,6},{6,5},{7,4},{8,11},{9,10},{10,... | collective-permute-start | bytes 98312 | tf_op jit(solution)/shard_map/cond/branch_1_fun/ppermute | solution.py:273
  56.1 2.8 %collective-permute-start.2 = (f32[2,4096]{1,0:T(2,128)S(1)}, f32[2,4096]{1,0:T(2,128)S(1)}, u32[]{:S(2)}, u32[]{:S(2)}) collective-permute-start(f32[2,4096]{1,0:T(2,128)S(1)} %pad_maximum_fusion.1), channel_id=1, source_target_pairs={{0,4},{1,5},{2,6},{3,7},{4,0},{5,1},{6,2},{7,3},{8,12},{9,13},{10,... | collective-permute-start | bytes 98312 | tf_op jit(solution)/shard_map/cond/branch_1_fun/ppermute | solution.py:273
  62.0 1.0 copy-start.1
  63.0 4.0 %collective-permute-start.3 = (f32[2,4096]{1,0:T(2,128)S(1)}, f32[2,4096]{1,0:T(2,128)S(1)}, u32[]{:S(2)}, u32[]{:S(2)}) collective-permute-start(f32[2,4096]{1,0:T(2,128)S(1)} %get-tuple-element.25), channel_id=1, source_target_pairs={{0,12},{1,13},{2,14},{3,15},{4,8},{5,9},{6,10},{7,11},{8,4},{9,5},... | collective-permute-start | bytes 98312 | tf_op jit(solution)/shard_map/ppermute | solution.py:273
  67.1 4.3 %collective-permute-start.4 = (f32[2,4096]{1,0:T(2,128)S(1)}, f32[2,4096]{1,0:T(2,128)S(1)}, u32[]{:S(2)}, u32[]{:S(2)}) collective-permute-start(f32[2,4096]{1,0:T(2,128)S(1)} %pad_maximum_fusion.5), channel_id=1, source_target_pairs={{0,16},{1,17},{2,18},{3,19},{4,20},{5,21},{6,22},{7,23},{8,24},{9,... | collective-permute-start | bytes 98312 | tf_op jit(solution)/shard_map/ppermute | solution.py:273
  71.6 1.2 %copy-start.2 = (bf16[2048,256]{1,0:T(8,128)(2,1)S(1)}, bf16[2048,256]{1,0:T(8,128)(2,1)}, u32[]{:S(2)}) copy-start(bf16[2048,256]{1,0:T(8,128)(2,1)} %copy-done.1) | copy-start | bytes 3145732
  72.8 13.9 %copy-start.3 = (bf16[2048,256]{1,0:T(8,128)(2,1)S(1)}, bf16[2048,256]{1,0:T(8,128)(2,1)}, u32[]{:S(2)}) copy-start(bf16[2048,256]{1,0:T(8,128)(2,1)} %copy-done.1) | copy-start | bytes 3145732
  79.9 11.5 %collective-permute-start.5 = (f32[1032,256]{1,0:T(8,128)S(1)}, f32[1032,256]{1,0:T(8,128)S(1)}, u32[]{:S(2)}, u32[]{:S(2)}) collective-permute-start(f32[1032,256]{1,0:T(8,128)S(1)} %get-tuple-element.28.gate_ref), channel_id=1, source_target_pairs={{0,32},{32,0},{64,96},{96,64},{1,33},{33,1},{65,97},{97,65},{2,34}... | collective-permute-start | bytes 3170312 | tf_op jit(solution)/shard_map/ppermute | solution.py:273
  92.4 13.9 %collective-permute-start.8 = (f16[1024,256]{1,0:T(8,128)(2,1)}, f16[1024,256]{1,0:T(8,128)(2,1)}, u32[]{:S(2)}, u32[]{:S(2)}) collective-permute-start(f16[1024,256]{1,0:T(8,128)(2,1)} %get-tuple-element.33), channel_id=1, source_target_pairs={{0,64},{32,96},{64,0},{96,32},{1,65},{33,97},{65,1},{97,33},{2,66}... | collective-permute-start | bytes 1572872 | tf_op jit(solution)/shard_map/ppermute | solution.py:273
  93.2 13.1 %dynamic-slice-start = ((s32[2048]{0:T(1024)}, s32[]{:T(128)}), s32[1024]{0:T(1024)S(1)}, s32[]{:S(2)}) async-start(s32[2048]{0:T(1024)} %param.14, s32[]{:T(128)} %select_n.112), calls=%async_computation.2 | async-start | bytes 8704 | tf_op jit(solution)/shard_map/dynamic_slice | solution.py:373
  100.5 7.3 %copy-start.4 = (f32[16,128,128]{2,1,0:T(8,128)S(1)}, f32[16,128,128]{2,1,0:T(8,128)}, u32[]{:S(2)}) copy-start(f32[16,128,128]{2,1,0:T(8,128)} %param.15) | copy-start | bytes 3145732
  100.8 5.5 %collective-permute-start.9 = (f32[256]{0:T(256)S(1)}, f32[256]{0:T(256)S(1)}, u32[]{:S(2)}, u32[]{:S(2)}) collective-permute-start(f32[256]{0:T(256)S(1)} %bitcast.51), channel_id=1, source_target_pairs={{0,64},{32,96},{64,0},{96,32},{1,65},{33,97},{65,1},{97,33},{2,66}... | collective-permute-start | bytes 3080 | tf_op jit(solution)/shard_map/ppermute | solution.py:273
  108.8 7.3 %collective-permute-start.10 = (f32[1024,256]{1,0:T(8,128)S(1)}, f32[1024,256]{1,0:T(8,128)S(1)}, u32[]{:S(2)}, u32[]{:S(2)}) collective-permute-start(f32[1024,256]{1,0:T(8,128)S(1)} %bitcast.43), channel_id=1, source_target_pairs={{0,32},{32,0},{64,96},{96,64},{1,33},{33,1},{65,97},{97,65},{2,34}... | collective-permute-start | bytes 3145736 | tf_op jit(solution)/shard_map/ppermute | solution.py:273
  109.7 2.3 %collective-permute-start.6 = (f32[4096]{0:T(1024)S(1)}, f32[4096]{0:T(1024)S(1)}, u32[]{:S(2)}, u32[]{:S(2)}) collective-permute-start(f32[4096]{0:T(1024)S(1)} %pad_maximum_fusion.7), channel_id=1, source_target_pairs={{0,32},{32,0},{64,96},{96,64},{1,33},{33,1},{65,97},{97,65},{2,34}... | collective-permute-start | bytes 49160 | tf_op jit(solution)/shard_map/ppermute | solution.py:273
  112.0 2.6 %collective-permute-start.7 = (f32[4096]{0:T(1024)S(1)}, f32[4096]{0:T(1024)S(1)}, u32[]{:S(2)}, u32[]{:S(2)}) collective-permute-start(f32[4096]{0:T(1024)S(1)} %fusion.41), channel_id=1, source_target_pairs={{0,64},{32,96},{64,0},{96,32},{1,65},{33,97},{65,1},{97,33},{2,66}... | collective-permute-start | bytes 49160 | tf_op jit(solution)/shard_map/ppermute | solution.py:273

commit v6 on v5

--- a/solution.py
+++ b/solution.py
@@ -100,14 +100,13 @@
     )(ids_t, chars, tail, stat)
 
 
-def place_rows(order, received, beside, holders, stat):
+def place_rows(order, received, beside, holders, gate):
     rows = order.shape[1]
     total, depth = received.shape
     per_pair, each = rows // holders, total // holders
     chunk = 256
 
-    def kernel(order_ref, received_ref, beside_ref, stat_ref, out_ref, stat_out_ref):
-        stat_out_ref[...] = stat_ref[...]
+    def kernel(order_ref, received_ref, beside_ref, gate_ref, out_ref):
         order_row = order_ref[...]
         table = jnp.concatenate([received_ref[q * each : q * each + per_pair, :] for q in range(holders)], axis=0)
         blank = jnp.zeros((120, 128), jnp.float32)
@@ -124,10 +123,11 @@
 
     return pl.pallas_call(
         kernel,
-        out_shape=[jax.ShapeDtypeStruct((rows, 2 * depth), jnp.bfloat16), jax.ShapeDtypeStruct(stat.shape, stat.dtype)],
+        in_specs=[pl.BlockSpec(memory_space=pltpu.VMEM)] * 3 + [pl.BlockSpec(memory_space=pl.ANY)],
+        out_shape=jax.ShapeDtypeStruct((rows, 2 * depth), jnp.bfloat16),
         compiler_params=pltpu.CompilerParams(vmem_limit_bytes=VMEM_BYTES),
         name="place_rows",
-    )(order, received, beside, stat)
+    )(order, received, beside, gate)
 
 
 def lane_groups(values):
@@ -338,11 +338,10 @@
         return stat
 
     masks = butterfly_masks(holders)
-    stat = lax.cond(panel_cols[0] >= 0, lambda value: join(value, masks[:3]), lambda value: value, stat)
-    firm_chars, stat = place_rows(
+    stat = lax.cond(panel_cols[0] >= 0, lambda value: join(value, masks), lambda value: value, stat)
+    firm_chars = place_rows(
         place.reshape(1, products), second.reshape(holders * each, depth), mean_rows, holders, stat
     )
-    stat = join(stat, masks[3:])
     peak = jnp.maximum(stat[0], 0.0)
     denom = jnp.exp(-peak) + stat[1] * jnp.exp(stat[0] - peak)
     ratio = count_products / denom
@@ -356,24 +355,33 @@
     fitted = (kept + got[:half]) * room[None, :]
     chip_sum, gate = lax.optimization_barrier((fitted.astype(jnp.float16), jnp.max(fitted, axis=0, keepdims=True)))
     other_sum = swap(chip_sum, "cons", 2)
-    other_diagonal = swap(diagonal, "cons", 2)
-
-    own_shares = jnp.sum(share_sums(chars, tastes, row_values, gate), axis=1)
+
     given_share, kept_share = jnp.sum(given_share, axis=1), jnp.sum(kept_share, axis=1)
     first_half = jnp.where(core == 0, kept_share, given_share)
     second_half = jnp.where(core == 0, given_share, kept_share)
-    sums = jnp.concatenate([own_shares, first_half, second_half])
-    for mask in (1, 2):
-        sums = sums + swap(sums, "cons", mask)
-    sums = sums / count_consumers
-    shares, firm_shares = sums[:products], sums[products:]
+
+    def own_and_exchange(gate, others):
+        own_shares = jnp.sum(share_sums(chars, tastes, row_values, gate), axis=1)
+        sums = jnp.concatenate([own_shares, others])
+        sums = sums + swap(sums, "cons", 1)
+        return sums, swap(sums, "cons", 2)
+
+    sums, other_sums = lax.cond(
+        panel_cols[1] >= 0,
+        own_and_exchange,
+        lambda gate, others: (jnp.zeros(products + others.shape[0], jnp.float32),) * 2,
+        gate,
+        jnp.concatenate([first_half, second_half, given[half]]),
+    )
+    other_diagonal = other_sums[2 * products :]
+    sums = (sums + other_sums) / count_consumers
+    shares, firm_shares = sums[:products], sums[products : 2 * products]
 
     firm_count, block_size = inverses.shape[0], inverses.shape[1]
     own_inverses = lax.dynamic_slice_in_dim(inverses, core * (firm_count // 2), firm_count // 2, 0)
     firm_ids = lax.dynamic_slice_in_dim(firm_map, core * half, half, 0)
     other_room = 32768.0 / (count_products * jnp.maximum(other_diagonal, 1e-25))
     unfit, other_unfit = 1.0 / (room * count_consumers), 1.0 / (other_room * count_consumers)
-    unfit = jnp.where(own_shares[0] >= 0.0, unfit, 0.0)
     cross = chip_sum.astype(jnp.float32) * unfit[None, :] + other_sum.astype(jnp.float32) * other_unfit[None, :]
     diagonal = (diagonal + other_diagonal) / count_consumers
     jacobian = cross - jnp.where(firm_ids[:, None] == panel_cols[None, :], diagonal[None, :], 0.0)

time: 118 us -> 118 us (level)
  other arithmetic: 13.8 us -> 17.4 us
  waiting for transfers between devices: 20.1 us -> 17.4 us
  local copies, waits for them, and re-layouts: 5.35 us -> 3.4 us
    ppermute x11 -> x10, waiting for transfers between devices: 20.1 us -> 17.4 us  [swap(): return lax.ppermute(value, axis, [(i, i ^ mask) for i in range(size)])]
    unnamed x20 -> x14, local copies, waits for them, and re-layouts: 2.6 us -> 0.41 us
    ppermute x11 -> x10, starting transfers between devices: 19.4 us -> 19.4 us  [swap(): return lax.ppermute(value, axis, [(i, i ^ mask) for i in range(size)])]
  transfers between devices with their start and end apart: 13 -> 12, of which waited for: 8 -> 7; matrix products, arithmetic and copies ran while one was open for 3% -> 7% of each run, Pallas kernels for 18% -> 18%
where the time goes in v6:
time: 118 us; the launch traced here: 117 us
  starting transfers between devices  40 us (34%)
  Pallas kernels  34.7 us (29%)
  other arithmetic  17.4 us (15%)
  waiting for transfers between devices  17.4 us (15%)
  local copies, waits for them, and re-layouts  3.4 us (3%)
  between operations  2.37 us (2%)
  matrix products  1.51 us (1%)
    ppermute x10, starting transfers between devices, swap(): return lax.ppermute(value, axis, [(i, i ^ mask) for i in range(size)])  19.4 us
    ppermute x10, waiting for transfers between devices, swap(): return lax.ppermute(value, axis, [(i, i ^ mask) for i in range(size)])  17.4 us
    all_to_all x1, starting transfers between devices, body(): lax.all_to_all(message, 'prod', split_axis=0, concat_axis=0, tiled=True)  11.3 us
    pallas_call x1, Pallas kernels, stats(): pl.pallas_call(kernel, grid=(consumers // block,), in_specs=[pl.BlockSpec...  9.47 us
    all_to_all x1, starting transfers between devices, body(): lax.all_to_all(sent.reshape(holders, each, depth), 'prod', split_axis=0,...  9.27 us
    pallas_call x1, Pallas kernels, first_panel(): pl.pallas_call(kernel, grid=(consumers // block,), in_specs=[pl.BlockSpec...  7.42 us
    pallas_call x1, Pallas kernels, share_sums(): pl.pallas_call(kernel, grid=(consumers // block,), in_specs=[pl.BlockSpec...  7.19 us
    pallas_call x1, Pallas kernels, panel(): pl.pallas_call(kernel, grid=(1,), in_specs=[pl.BlockSpec((rows, depth), l...  4.88 us
  transfers between devices with their start and end apart: 12, of which 7 were waited for; matrix products, arithmetic and copies ran while one was open for 7% of the time, Pallas kernels for 18%

profile of v6, /device:TPU:1, one launch (start us, length us, event | category | flops | bytes accessed | tf_op | source)
XLA Modules:
  0.0 117.1 jit_solution(15286374863482081124)
XLA Ops:
  0.6 0.7 reduce-precision_convert_fusion.1
  1.4 0.3 copy.43
  1.8 1.2 %fusion.12.chars_ref = bf16[2048,256]{1,0:T(8,128)(2,1)S(1)} fusion(bf16[2048,3]{1,0:T(8,128)(2,1)S(1)} %copy.43, bf16[2048,128]{1,0:T(8,128)(2,1)} %param.13), kind=kLoop, calls=%fused_computation.30 | loop fusion | flops 3145728 | bytes 1585152 | tf_op jit(solution)/shard_map/concatenate | solution.py:298
  3.0 0.5 fusion.9
  3.6 0.3 copy.56
  3.8 4.4 %sort.15 = (s32[2048]{0:T(1024)S(1)}, s32[2048]{0:T(1024)S(1)}) sort(s32[2048]{0:T(1024)S(1)} %copy-done.2, s32[2048]{0:T(1024)S(1)} %iota.9), dimensions={0}, to_apply=%region_0.1 | sort | flops 22528 | bytes 32768 | tf_op jit(solution)/shard_map/sort | solution.py:300
  8.3 0.1 reshape.103
  8.4 0.1 copy.44
  8.5 0.1 copy.49
  8.6 0.7 fusion.23.gate_ref
  9.3 11.3 %all-to-all-start = ((bf16[32,16,128]{2,1,0:T(8,128)(2,1)}), bf16[32,16,128]{2,1,0:T(8,128)(2,1)S(1)}, u32[]{:S(2)}, u32[]{:S(2)}) async-start(bf16[32,16,128]{2,1,0:T(8,128)(2,1)} %fusion.23.gate_ref), calls=%async_computation | async-start | bytes 262144 | tf_op jit(solution)/shard_map/all_to_all | solution.py:310
  20.7 0.6 fusion.42
  21.3 0.1 pad.45.clone
  21.4 9.5 %stats.1.stat_ref = f32[2,4096]{1,0:T(2,128)S(1)} custom-call(bf16[2048,256]{1,0:T(8,128)(2,1)S(1)} %fusion.12.chars_ref, bf16[4096,128]{1,0:T(8,128)(2,1)S(1)} %copy-done, bf16[32,16,128]{2,1,0:T(8,128)(2,1)} %fusion.23.gate_ref), custom_call_target="tpu_custom_call" | custom-call | tf_op jit(solution)/shard_map/stats/pallas_call | solution.py:54
  31.6 0.1 copy.55
  31.8 0.1 pad_maximum_fusion.9.tail_ref
  31.9 3.3 %pick_rows.1 = (bf16[2560,128]{1,0:T(8,128)(2,1)}, f32[2,4096]{1,0:T(2,128)S(1)}) custom-call(s32[64,32]{1,0:T(8,128)S(1)} %fusion.28.ids_ref, bf16[2048,256]{1,0:T(8,128)(2,1)S(1)} %fusion.12.chars_ref, f32[16,128]{1,0:T(8,128)S(1)} %pad_maximum_fusion.9.tail_ref, f32[2,4096]{1,0:T(2,128)S(1)} %stats.1.stat_ref), custom_call_target="tpu_custom_call" | custom-call | tf_op jit(solution)/shard_map/pick_rows/pallas_call | solution.py:92
  35.2 9.3 %all-to-all-start.1 = ((bf16[32,80,128]{2,1,0:T(8,128)(2,1)}), bf16[32,80,128]{2,1,0:T(8,128)(2,1)S(1)}, u32[]{:S(2)}, u32[]{:S(2)}) async-start(bf16[32,80,128]{2,1,0:T(8,128)(2,1)} %bitcast.12), calls=%async_computation.1 | async-start | bytes 1310720 | tf_op jit(solution)/shard_map/all_to_all | solution.py:321
  44.5 25.9 %conditional.2 = (f32[2,4096]{1,0:T(2,128)S(1)}, f32[1,4096]{1,0:T(1,128)}, f32[1,4096]{1,0:T(1,128)}) conditional(s32[]{:T(128)} %bitcast.1, f32[2,4096]{1,0:T(2,128)S(1)} %get-tuple-element.62, f32[2,4096]{1,0:T(2,128)S(1)} %get-tuple-element.62), branch_computations={%region_2.3_spmd, %region_3.4_spmd} | conditional | flops 163840 | bytes 1474784 | solution.py:341
  44.5 1.3 %collective-permute-start.2 = (f32[2,4096]{1,0:T(2,128)S(1)}, f32[2,4096]{1,0:T(2,128)S(1)}, u32[]{:S(2)}, u32[]{:S(2)}) collective-permute-start(f32[2,4096]{1,0:T(2,128)S(1)} %param.1), channel_id=1, source_target_pairs={{0,1},{1,0},{2,3},{3,2},{4,5},{5,4},{6,7},{7,6},{8,9},{9,8},{10,11... | collective-permute-start | bytes 98312 | tf_op jit(solution)/shard_map/cond/branch_1_fun/ppermute | solution.py:273
  45.8 6.9 %collective-permute-done.2 = f32[2,4096]{1,0:T(2,128)S(1)} collective-permute-done((f32[2,4096]{1,0:T(2,128)S(1)}, f32[2,4096]{1,0:T(2,128)S(1)}, u32[]{:S(2)}, u32[]{:S(2)}) %collective-permute-start.2) | collective-permute-done | bytes 32800 | tf_op jit(solution)/shard_map/cond/branch_1_fun/ppermute | solution.py:273
  52.7 0.1 fusion.4
  52.8 1.9 %collective-permute-start.3 = (f32[2,4096]{1,0:T(2,128)S(1)}, f32[2,4096]{1,0:T(2,128)S(1)}, u32[]{:S(2)}, u32[]{:S(2)}) collective-permute-start(f32[2,4096]{1,0:T(2,128)S(1)} %pad_maximum_fusion), channel_id=1, source_target_pairs={{0,3},{1,2},{2,1},{3,0},{4,7},{5,6},{6,5},{7,4},{8,11},{9,10},{10,... | collective-permute-start | bytes 98312 | tf_op jit(solution)/shard_map/cond/branch_1_fun/ppermute | solution.py:273
  54.7 2.5 %collective-permute-done.3 = f32[2,4096]{1,0:T(2,128)S(1)} collective-permute-done((f32[2,4096]{1,0:T(2,128)S(1)}, f32[2,4096]{1,0:T(2,128)S(1)}, u32[]{:S(2)}, u32[]{:S(2)}) %collective-permute-start.3) | collective-permute-done | bytes 32800 | tf_op jit(solution)/shard_map/cond/branch_1_fun/ppermute | solution.py:273
  57.2 0.1 fusion.3
  57.3 1.3 %collective-permute-start.4 = (f32[2,4096]{1,0:T(2,128)S(1)}, f32[2,4096]{1,0:T(2,128)S(1)}, u32[]{:S(2)}, u32[]{:S(2)}) collective-permute-start(f32[2,4096]{1,0:T(2,128)S(1)} %pad_maximum_fusion.1), channel_id=1, source_target_pairs={{0,4},{1,5},{2,6},{3,7},{4,0},{5,1},{6,2},{7,3},{8,12},{9,13},{10,... | collective-permute-start | bytes 98312 | tf_op jit(solution)/shard_map/cond/branch_1_fun/ppermute | solution.py:273
  58.5 1.6 %collective-permute-done.4 = f32[2,4096]{1,0:T(2,128)S(1)} collective-permute-done((f32[2,4096]{1,0:T(2,128)S(1)}, f32[2,4096]{1,0:T(2,128)S(1)}, u32[]{:S(2)}, u32[]{:S(2)}) %collective-permute-start.4) | collective-permute-done | bytes 32800 | tf_op jit(solution)/shard_map/cond/branch_1_fun/ppermute | solution.py:273
  60.1 0.1 fusion.2
  60.2 2.5 %collective-permute-start.5 = (f32[2,4096]{1,0:T(2,128)S(1)}, f32[2,4096]{1,0:T(2,128)S(1)}, u32[]{:S(2)}, u32[]{:S(2)}) collective-permute-start(f32[2,4096]{1,0:T(2,128)S(1)} %pad_maximum_fusion.2), channel_id=1, source_target_pairs={{0,12},{1,13},{2,14},{3,15},{4,8},{5,9},{6,10},{7,11},{8,4},{9,5},... | collective-permute-start | bytes 98312 | tf_op jit(solution)/shard_map/cond/branch_1_fun/ppermute | solution.py:273
  62.7 1.6 %collective-permute-done.5 = f32[2,4096]{1,0:T(2,128)S(1)} collective-permute-done((f32[2,4096]{1,0:T(2,128)S(1)}, f32[2,4096]{1,0:T(2,128)S(1)}, u32[]{:S(2)}, u32[]{:S(2)}) %collective-permute-start.5) | collective-permute-done | bytes 32800 | tf_op jit(solution)/shard_map/cond/branch_1_fun/ppermute | solution.py:273
  64.3 0.1 fusion.1
  64.4 2.8 %collective-permute-start.6 = (f32[2,4096]{1,0:T(2,128)S(1)}, f32[2,4096]{1,0:T(2,128)S(1)}, u32[]{:S(2)}, u32[]{:S(2)}) collective-permute-start(f32[2,4096]{1,0:T(2,128)S(1)} %pad_maximum_fusion.3), channel_id=1, source_target_pairs={{0,16},{1,17},{2,18},{3,19},{4,20},{5,21},{6,22},{7,23},{8,24},{9,... | collective-permute-start | bytes 98312 | tf_op jit(solution)/shard_map/cond/branch_1_fun/ppermute | solution.py:273
  67.2 1.6 %collective-permute-done.6 = f32[2,4096]{1,0:T(2,128)S(1)} collective-permute-done((f32[2,4096]{1,0:T(2,128)S(1)}, f32[2,4096]{1,0:T(2,128)S(1)}, u32[]{:S(2)}, u32[]{:S(2)}) %collective-permute-start.6) | collective-permute-done | bytes 32800 | tf_op jit(solution)/shard_map/cond/branch_1_fun/ppermute | solution.py:273
  68.7 0.7 fusion
  69.4 0.8 pad_maximum_fusion.4
  70.4 0.8 broadcast_maximum_fusion
  71.3 0.3 copy.53
  71.6 0.1 fusion.25
  71.7 0.1 reshape.108.beside_ref
  71.8 2.4 %place_rows.1.chars_ref = bf16[2048,256]{1,0:T(8,128)(2,1)S(1)} custom-call(s32[1,2048]{1,0:T(1,128)S(1)} %bitcast.42, bf16[2560,128]{1,0:T(8,128)(2,1)S(1)} %bitcast.41, f32[8,2048]{1,0:T(8,128)S(1)} %reshape.108.beside_ref, f32[2,4096]{1,0:T(2,128)S(1)} %get-tuple-element.67.gate_ref), custom_call_target="tpu_custom_call" | custom-call | tf_op jit(solution)/shard_map/place_rows/pallas_call | solution.py:124
  74.3 7.4 %first_panel.1 = (f32[1032,256]{1,0:T(8,128)S(1)}, f32[1024,128]{1,0:T(8,128)S(1)}, bf16[256,4096]{1,0:T(8,128)(2,1)S(1)}) custom-call(bf16[2048,256]{1,0:T(8,128)(2,1)S(1)} %place_rows.1.chars_ref, bf16[4096,128]{1,0:T(8,128)(2,1)S(1)} %copy-done, f32[3,4096]{1,0:T(4,128)S(1)} %pad_maximum_fusion.6.rows_ref, bf16[256,256]{1,0:T(8,128)(2,1)S(1)} %fusion.22.cols_ref), custom_call_target="tpu_custom_call" | custom-call | flops 4294967296 | bytes 2097152 | tf_op jit(solution)/shard_map/first_panel/pallas_call | solution.py:171
  81.7 6.8 %collective-permute-start.7 = (f32[1032,256]{1,0:T(8,128)S(1)}, f32[1032,256]{1,0:T(8,128)S(1)}, u32[]{:S(2)}, u32[]{:S(2)}) collective-permute-start(f32[1032,256]{1,0:T(8,128)S(1)} %get-tuple-element.69.gate_ref), channel_id=1, source_target_pairs={{0,32},{32,0},{64,96},{96,64},{1,33},{33,1},{65,97},{97,65},{2,34}... | collective-permute-start | bytes 3170312 | tf_op jit(solution)/shard_map/ppermute | solution.py:273
  88.5 4.9 %panel.1 = (f32[1024,256]{1,0:T(8,128)S(1)}, f32[1024,128]{1,0:T(8,128)S(1)}) custom-call(bf16[2048,256]{1,0:T(8,128)(2,1)S(1)} %place_rows.1.chars_ref, bf16[4096,128]{1,0:T(8,128)(2,1)S(1)} %copy-done, f32[3,4096]{1,0:T(4,128)S(1)} %pad_maximum_fusion.6.rows_ref, bf16[256,4096]{1,0:T(8,128)(2,1)S(1)} %get-tuple-element.68.weight_ref, ...), custom_call_target="tpu_custom_call" | custom-call | flops 4294967296 | bytes 2097152 | tf_op jit(solution)/shard_map/panel/pallas_call | solution.py:213
  93.4 1.0 fusion.18
  94.4 0.4 collective-permute-start.8
  95.5 0.0 dynamic-slice-start
  95.5 14.0 %conditional.3 = (f32[4352]{0:T(1024)}, f32[4352]{0:T(1024)}, f32[256]{0:T(256)S(1)}) conditional(s32[]{:T(128)} %bitcast, () %tuple.30, (bf16[2048,256]{1,0:T(8,128)(2,1)S(1)}, bf16[4096,128]{1,0:T(8,128)(2,1)S(1)}, f32[3,4096]{1,0:T(4,128)S(1)}, f32[1,256]{1,0:T(1,128)S(1)}, pred[]{:T(512)}, /*index=5*/f32[1024,128]{1,0:T(8,128)S(1)}, ...), branch_computations={%region_5.6_spmd, %region_6.10_spmd} | conditional | flops 552704 | bytes 2358389 | solution.py:369
  95.5 0.2 reduce_sum.43
  95.7 0.2 reduce_sum.44
  95.9 7.2 %share_sums.1 = f32[2048,128]{1,0:T(8,128)S(1)} custom-call(bf16[2048,256]{1,0:T(8,128)(2,1)S(1)} %get-tuple-element.33.chars_ref, bf16[4096,128]{1,0:T(8,128)(2,1)S(1)} %get-tuple-element.34.tastes_ref, f32[3,4096]{1,0:T(4,128)S(1)} %get-tuple-element.35.rows_ref, f32[1,256]{1,0:T(1,128)S(1)} %get-tuple-element.36.gate_ref), custom_call_target="tpu_custom_call" | custom-call | tf_op jit(solution)/shard_map/cond/branch_1_fun/share_sums/pallas_call | solution.py:255
  103.1 0.3 reduce_sum.42
  103.5 0.4 collective-permute-start
  103.9 0.9 collective-permute-done
  104.8 0.6 fusion.5
  105.4 1.1 collective-permute-start.1
  106.5 2.4 %collective-permute-done.1 = f32[4352]{0:T(1024)} collective-permute-done((f32[4352]{0:T(1024)}, f32[4352]{0:T(1024)}, u32[]{:S(2)}, u32[]{:S(2)}) %collective-permute-start.1) | collective-permute-done | bytes 17440 | tf_op jit(solution)/shard_map/cond/branch_1_fun/ppermute | solution.py:273
  108.8 0.7 slice.164
  109.6 1.6 %select_subtract_fusion = f32[1024,256]{1,0:T(8,128)S(1)} fusion(f16[1024,256]{1,0:T(8,128)(2,1)} %collective-permute-done.8, f16[1024,256]{1,0:T(8,128)(2,1)} %get-tuple-element.76, f32[256]{0:T(256)S(1)} %get-tuple-element.110, s32[256]{0:T(256)S(1)} %copy-done.4, f32[256]{0:T(256)S(1)} %get-tuple-element.109, f32[256]{0:T(256)S(1)} %bitcast.52, ...), kind=kLoop, calls=%fused_computation.33 | loop fusion | flops 2097152 | bytes 2105344 | tf_op jit(solution)/shard_map/sub | solution.py:387
  111.1 1.0 fusion.16
  112.2 1.1 collective-permute-start.9
  113.2 0.7 add_multiply_fusion
  114.0 0.6 slice_bitcast_fusion.4
  114.6 0.9 multiply_reduce_fusion
  115.5 1.6 %maximum_select_fusion = f32[2048,256]{1,0:T(8,128)} fusion(f32[1024,256]{1,0:T(8,128)S(1)} %collective-permute-done.9, f32[1024,256]{1,0:T(8,128)S(1)} %bitcast.44, pred[]{:T(512)} %eq.54), kind=kLoop, calls=%fused_computation.25 | loop fusion | flops 1572864 | bytes 4194305 | tf_op jit(solution)/shard_map/jit(_where)/select_n | solution.py:395
  (52 shorter events, 0.6 us)
Async XLA Ops:
  0.6 2.4 %copy-start.4 = (s32[256]{0:T(256)S(1)}, s32[256]{0:T(256)}, u32[]{:S(2)}) copy-start(s32[256]{0:T(256)} %param.15) | copy-start | bytes 3076
  1.8 2.1 %copy-start.2 = (s32[2048]{0:T(1024)S(1)}, s32[2048]{0:T(1024)}, u32[]{:S(2)}) copy-start(s32[2048]{0:T(1024)} %param.16) | copy-start | bytes 24580
  3.0 18.3 %copy-start = (bf16[4096,128]{1,0:T(8,128)(2,1)S(1)}, bf16[4096,128]{1,0:T(8,128)(2,1)}, u32[]{:S(2)}) copy-start(bf16[4096,128]{1,0:T(8,128)(2,1)} %tastes_ref.5) | copy-start | bytes 3145732
  9.3 22.2 %all-to-all-start = ((bf16[32,16,128]{2,1,0:T(8,128)(2,1)}), bf16[32,16,128]{2,1,0:T(8,128)(2,1)S(1)}, u32[]{:S(2)}, u32[]{:S(2)}) async-start(bf16[32,16,128]{2,1,0:T(8,128)(2,1)} %fusion.23.gate_ref), calls=%async_computation | async-start | bytes 262144 | tf_op jit(solution)/shard_map/all_to_all | solution.py:310
  30.8 40.3 %copy-start.3 = (f32[4096]{0:T(1024)S(1)}, f32[4096]{0:T(1024)}, u32[]{:S(2)}) copy-start(f32[4096]{0:T(1024)} %param.12) | copy-start | bytes 49156
  31.8 39.8 %copy-start.5 = (pred[8]{0:T(512)(128)(4,1)S(1)}, pred[8]{0:T(512)(128)(4,1)}, u32[]{:S(2)}) copy-start(pred[8]{0:T(512)(128)(4,1)} %constant.123.clone.1) | copy-start | bytes 28
  35.2 36.0 %all-to-all-start.1 = ((bf16[32,80,128]{2,1,0:T(8,128)(2,1)}), bf16[32,80,128]{2,1,0:T(8,128)(2,1)S(1)}, u32[]{:S(2)}, u32[]{:S(2)}) async-start(bf16[32,80,128]{2,1,0:T(8,128)(2,1)} %bitcast.12), calls=%async_computation.1 | async-start | bytes 1310720 | tf_op jit(solution)/shard_map/all_to_all | solution.py:321
  44.5 8.2 %collective-permute-start.2 = (f32[2,4096]{1,0:T(2,128)S(1)}, f32[2,4096]{1,0:T(2,128)S(1)}, u32[]{:S(2)}, u32[]{:S(2)}) collective-permute-start(f32[2,4096]{1,0:T(2,128)S(1)} %param.1), channel_id=1, source_target_pairs={{0,1},{1,0},{2,3},{3,2},{4,5},{5,4},{6,7},{7,6},{8,9},{9,8},{10,11... | collective-permute-start | bytes 98312 | tf_op jit(solution)/shard_map/cond/branch_1_fun/ppermute | solution.py:273
  52.8 4.3 %collective-permute-start.3 = (f32[2,4096]{1,0:T(2,128)S(1)}, f32[2,4096]{1,0:T(2,128)S(1)}, u32[]{:S(2)}, u32[]{:S(2)}) collective-permute-start(f32[2,4096]{1,0:T(2,128)S(1)} %pad_maximum_fusion), channel_id=1, source_target_pairs={{0,3},{1,2},{2,1},{3,0},{4,7},{5,6},{6,5},{7,4},{8,11},{9,10},{10,... | collective-permute-start | bytes 98312 | tf_op jit(solution)/shard_map/cond/branch_1_fun/ppermute | solution.py:273
  57.3 2.8 %collective-permute-start.4 = (f32[2,4096]{1,0:T(2,128)S(1)}, f32[2,4096]{1,0:T(2,128)S(1)}, u32[]{:S(2)}, u32[]{:S(2)}) collective-permute-start(f32[2,4096]{1,0:T(2,128)S(1)} %pad_maximum_fusion.1), channel_id=1, source_target_pairs={{0,4},{1,5},{2,6},{3,7},{4,0},{5,1},{6,2},{7,3},{8,12},{9,13},{10,... | collective-permute-start | bytes 98312 | tf_op jit(solution)/shard_map/cond/branch_1_fun/ppermute | solution.py:273
  60.2 4.1 %collective-permute-start.5 = (f32[2,4096]{1,0:T(2,128)S(1)}, f32[2,4096]{1,0:T(2,128)S(1)}, u32[]{:S(2)}, u32[]{:S(2)}) collective-permute-start(f32[2,4096]{1,0:T(2,128)S(1)} %pad_maximum_fusion.2), channel_id=1, source_target_pairs={{0,12},{1,13},{2,14},{3,15},{4,8},{5,9},{6,10},{7,11},{8,4},{9,5},... | collective-permute-start | bytes 98312 | tf_op jit(solution)/shard_map/cond/branch_1_fun/ppermute | solution.py:273
  64.4 4.3 %collective-permute-start.6 = (f32[2,4096]{1,0:T(2,128)S(1)}, f32[2,4096]{1,0:T(2,128)S(1)}, u32[]{:S(2)}, u32[]{:S(2)}) collective-permute-start(f32[2,4096]{1,0:T(2,128)S(1)} %pad_maximum_fusion.3), channel_id=1, source_target_pairs={{0,16},{1,17},{2,18},{3,19},{4,20},{5,21},{6,22},{7,23},{8,24},{9,... | collective-permute-start | bytes 98312 | tf_op jit(solution)/shard_map/cond/branch_1_fun/ppermute | solution.py:273
  81.7 11.7 %collective-permute-start.7 = (f32[1032,256]{1,0:T(8,128)S(1)}, f32[1032,256]{1,0:T(8,128)S(1)}, u32[]{:S(2)}, u32[]{:S(2)}) collective-permute-start(f32[1032,256]{1,0:T(8,128)S(1)} %get-tuple-element.69.gate_ref), channel_id=1, source_target_pairs={{0,32},{32,0},{64,96},{96,64},{1,33},{33,1},{65,97},{97,65},{2,34}... | collective-permute-start | bytes 3170312 | tf_op jit(solution)/shard_map/ppermute | solution.py:273
  94.4 15.1 %collective-permute-start.8 = (f16[1024,256]{1,0:T(8,128)(2,1)}, f16[1024,256]{1,0:T(8,128)(2,1)}, u32[]{:S(2)}, u32[]{:S(2)}) collective-permute-start(f16[1024,256]{1,0:T(8,128)(2,1)} %get-tuple-element.76), channel_id=1, source_target_pairs={{0,64},{32,96},{64,0},{96,32},{1,65},{33,97},{65,1},{97,33},{2,66}... | collective-permute-start | bytes 1572872 | tf_op jit(solution)/shard_map/ppermute | solution.py:273
  95.5 14.1 %dynamic-slice-start = ((s32[2048]{0:T(1024)}, s32[]{:T(128)}), s32[1024]{0:T(1024)S(1)}, s32[]{:S(2)}) async-start(s32[2048]{0:T(1024)} %param.16, s32[]{:T(128)} %select_n.101), calls=%async_computation.2 | async-start | bytes 8704 | tf_op jit(solution)/shard_map/dynamic_slice | solution.py:382
  103.5 1.3 %collective-permute-start = (f32[4352]{0:T(1024)S(1)}, f32[4352]{0:T(1024)S(1)}, u32[]{:S(2)}, u32[]{:S(2)}) collective-permute-start(f32[4352]{0:T(1024)S(1)} %pad_maximum_fusion.5), channel_id=1, source_target_pairs={{0,32},{32,0},{64,96},{96,64},{1,33},{33,1},{65,97},{97,65},{2,34}... | collective-permute-start | bytes 52232 | tf_op jit(solution)/shard_map/cond/branch_1_fun/ppermute | solution.py:273
  105.4 3.4 %collective-permute-start.1 = (f32[4352]{0:T(1024)}, f32[4352]{0:T(1024)}, u32[]{:S(2)}, u32[]{:S(2)}) collective-permute-start(f32[4352]{0:T(1024)} %fusion.5), channel_id=1, source_target_pairs={{0,64},{32,96},{64,0},{96,32},{1,65},{33,97},{65,1},{97,33},{2,66}... | collective-permute-start | bytes 52232 | tf_op jit(solution)/shard_map/cond/branch_1_fun/ppermute | solution.py:273
  109.5 1.6 %copy-start.1 = (f32[16,128,128]{2,1,0:T(8,128)S(1)}, f32[16,128,128]{2,1,0:T(8,128)}, u32[]{:S(2)}) copy-start(f32[16,128,128]{2,1,0:T(8,128)} %param.17) | copy-start | bytes 3145732
  112.2 3.4 %collective-permute-start.9 = (f32[1024,256]{1,0:T(8,128)S(1)}, f32[1024,256]{1,0:T(8,128)S(1)}, u32[]{:S(2)}, u32[]{:S(2)}) collective-permute-start(f32[1024,256]{1,0:T(8,128)S(1)} %bitcast.43), channel_id=1, source_target_pairs={{0,32},{32,0},{64,96},{96,64},{1,33},{33,1},{65,97},{97,65},{2,34}... | collective-permute-start | bytes 3145736 | tf_op jit(solution)/shard_map/ppermute | solution.py:273

commit v7 on v6

--- a/solution.py
+++ b/solution.py
@@ -326,8 +326,9 @@
     odd = lax.axis_index("prod") % 2 == 1
     mean_rows = jnp.where(odd, mean_rows[:, :, per_pair:], mean_rows[:, :, :per_pair])
     mean_rows = jnp.pad(mean_rows[:, :3], ((0, 0), (0, 5), (0, 0))).transpose(1, 0, 2).reshape(8, products)
-    half = products // 2
-    place = (order // half == core).astype(jnp.int32) * half + order % half
+    half, quarter = products // 2, products // 4
+    kept_row = (order // half == core).astype(jnp.int32)
+    place = (order // quarter % 2) * half + kept_row * quarter + order % quarter
 
     def join(stat, masks):
         for mask in masks:
@@ -347,31 +348,53 @@
     ratio = count_products / denom
 
     row_values = jnp.stack([peak, ratio, price_coef])
-    given, given_share, weighted = first_panel(firm_chars, 2, tastes, row_values, col_chars)
+    given, given_share, weighted = first_panel(firm_chars, 4, tastes, row_values, col_chars)
+    own_diagonal = given[quarter]
     got = swap(given, "cons", 1)
-    kept, kept_share = panel(firm_chars, 1, 2, tastes, row_values, weighted, given)
-    diagonal = given[half] + got[half]
+    kept, kept_share = panel(firm_chars, 1, 4, tastes, row_values, weighted, given)
+    diagonal = own_diagonal + got[quarter]
     room = 32768.0 / (count_products * jnp.maximum(diagonal, 1e-25))
-    fitted = (kept + got[:half]) * room[None, :]
-    chip_sum, gate = lax.optimization_barrier((fitted.astype(jnp.float16), jnp.max(fitted, axis=0, keepdims=True)))
+
+    def fit(values):
+        fitted = values * room[None, :]
+        return lax.optimization_barrier((fitted.astype(jnp.float16), jnp.max(fitted, axis=0, keepdims=True)))
+
+    def second_quarters(gate):
+        given, given_share = panel(firm_chars, 2, 4, tastes, row_values, weighted, gate)
+        got = swap(given, "cons", 1)
+        kept, kept_share = panel(firm_chars, 3, 4, tastes, row_values, weighted, given)
+        return *fit(kept + got), given_share, kept_share
+
+    chip_sum, gate = fit(kept + got[:quarter])
+    shapes = jax.eval_shape(second_quarters, gate)
+    last_sum, last_gate, given_last, kept_last = lax.cond(
+        panel_cols[2] >= 0,
+        second_quarters,
+        lambda gate: tuple(jnp.zeros(shape.shape, shape.dtype) for shape in shapes),
+        gate,
+    )
     other_sum = swap(chip_sum, "cons", 2)
-
-    given_share, kept_share = jnp.sum(given_share, axis=1), jnp.sum(kept_share, axis=1)
-    first_half = jnp.where(core == 0, kept_share, given_share)
-    second_half = jnp.where(core == 0, given_share, kept_share)
-
-    def own_and_exchange(gate, others):
+    chip_sums = [(chip_sum, other_sum), (last_sum, swap(last_sum, "cons", 2))]
+    shares_of = [given_share, kept_share, given_last, kept_last]
+    gate = jnp.maximum(last_gate, jnp.max(other_sum.astype(jnp.float32), axis=0, keepdims=True))
+
+    def own_and_exchange(gate, parts, own_diagonal):
+        given_0, kept_0, given_1, kept_1 = (jnp.sum(part, axis=1) for part in parts)
+        kept_share, given_share = jnp.concatenate([kept_0, kept_1]), jnp.concatenate([given_0, given_1])
+        first_half = jnp.where(core == 0, kept_share, given_share)
+        second_half = jnp.where(core == 0, given_share, kept_share)
         own_shares = jnp.sum(share_sums(chars, tastes, row_values, gate), axis=1)
-        sums = jnp.concatenate([own_shares, others])
+        sums = jnp.concatenate([own_shares, first_half, second_half, own_diagonal])
         sums = sums + swap(sums, "cons", 1)
         return sums, swap(sums, "cons", 2)
 
     sums, other_sums = lax.cond(
         panel_cols[1] >= 0,
         own_and_exchange,
-        lambda gate, others: (jnp.zeros(products + others.shape[0], jnp.float32),) * 2,
+        lambda gate, parts, own_diagonal: (jnp.zeros(2 * products + cols, jnp.float32),) * 2,
         gate,
-        jnp.concatenate([first_half, second_half, given[half]]),
+        shares_of,
+        own_diagonal,
     )
     other_diagonal = other_sums[2 * products :]
     sums = (sums + other_sums) / count_consumers
@@ -382,13 +405,16 @@
     firm_ids = lax.dynamic_slice_in_dim(firm_map, core * half, half, 0)
     other_room = 32768.0 / (count_products * jnp.maximum(other_diagonal, 1e-25))
     unfit, other_unfit = 1.0 / (room * count_consumers), 1.0 / (other_room * count_consumers)
-    cross = chip_sum.astype(jnp.float32) * unfit[None, :] + other_sum.astype(jnp.float32) * other_unfit[None, :]
     diagonal = (diagonal + other_diagonal) / count_consumers
-    jacobian = cross - jnp.where(firm_ids[:, None] == panel_cols[None, :], diagonal[None, :], 0.0)
+    jacobians = []
+    for part, (chip_sum, other_sum) in enumerate(chip_sums):
+        cross = chip_sum.astype(jnp.float32) * unfit[None, :] + other_sum.astype(jnp.float32) * other_unfit[None, :]
+        marks = firm_ids[part * quarter : (part + 1) * quarter, None] == panel_cols[None, :]
+        jacobians.append(cross - jnp.where(marks, diagonal[None, :], 0.0))
     mine = jnp.einsum(
         "fab,fbc->fac",
         own_inverses,
-        jacobian.reshape(firm_count // 2, block_size, cols),
+        jnp.concatenate(jacobians).reshape(firm_count // 2, block_size, cols),
         precision=lax.Precision.HIGHEST,
     ).reshape(half, cols)
     theirs = swap(mine, "cons", 1)

time: 118 us -> 130 us (1.10)
  other arithmetic: 17.4 us -> 22.3 us
  Pallas kernels: 34.7 us -> 38.4 us
  starting transfers between devices: 40 us -> 41.7 us
    pallas_call x1 -> x3, Pallas kernels: 4.88 us -> 10.5 us  [panel(): pl.pallas_call(kernel, grid=(1,), in_specs=[pl.BlockSpec((rows, depth), l...]
    reduce_sum x2 -> x4, other arithmetic: 0.41 us -> 3.43 us  [own_and_exchange(): given_0, kept_0, given_1, kept_1 = (jnp.sum(part, axis=1) for part in parts)]
    pallas_call x1, Pallas kernels: 7.42 us -> 5.48 us  [first_panel(): pl.pallas_call(kernel, grid=(consumers // block,), in_specs=[pl.BlockSpec...]
    convert_element_type x0 -> x2, other arithmetic: none -> 1.84 us  [the longest x1 1.8 us: body(): chip_sum.astype(jnp.float32) * unfit[None, :]]
    ppermute x10 -> x12, starting transfers between devices: 19.4 us -> 21.1 us  [swap(): return lax.ppermute(value, axis, [(i, i ^ mask) for i in range(size)])]
    ppermute x10 -> x12, waiting for transfers between devices: 17.4 us -> 17.5 us  [swap(): return lax.ppermute(value, axis, [(i, i ^ mask) for i in range(size)])]
  transfers between devices with their start and end apart: 12 -> 14, of which waited for: 7 -> 7; matrix products, arithmetic and copies ran while one was open for 7% -> 10% of each run, Pallas kernels for 18% -> 21%
where the time goes in v7:
time: 130 us; the launch traced here: 129 us
  starting transfers between devices  41.7 us (32%)
  Pallas kernels  38.4 us (30%)
  other arithmetic  22.3 us (17%)
  waiting for transfers between devices  17.5 us (13%)
  local copies, waits for them, and re-layouts  4.09 us (3%)
  between operations  3.05 us (2%)
  matrix products  1.51 us (1%)
    ppermute x12, starting transfers between devices, swap(): return lax.ppermute(value, axis, [(i, i ^ mask) for i in range(size)])  21.1 us
    ppermute x12, waiting for transfers between devices, swap(): return lax.ppermute(value, axis, [(i, i ^ mask) for i in range(size)])  17.5 us
    all_to_all x1, starting transfers between devices, body(): lax.all_to_all(message, 'prod', split_axis=0, concat_axis=0, tiled=True)  11.3 us
    pallas_call x3, Pallas kernels, panel(): pl.pallas_call(kernel, grid=(1,), in_specs=[pl.BlockSpec((rows, depth), l...  10.5 us
    pallas_call x1, Pallas kernels, stats(): pl.pallas_call(kernel, grid=(consumers // block,), in_specs=[pl.BlockSpec...  9.47 us
    all_to_all x1, starting transfers between devices, body(): lax.all_to_all(sent.reshape(holders, each, depth), 'prod', split_axis=0,...  9.27 us
    pallas_call x1, Pallas kernels, share_sums(): pl.pallas_call(kernel, grid=(consumers // block,), in_specs=[pl.BlockSpec...  7.2 us
    pallas_call x1, Pallas kernels, first_panel(): pl.pallas_call(kernel, grid=(consumers // block,), in_specs=[pl.BlockSpec...  5.48 us
  transfers between devices with their start and end apart: 14, of which 7 were waited for; matrix products, arithmetic and copies ran while one was open for 10% of the time, Pallas kernels for 21%

profile of v7, /device:TPU:1, one launch (start us, length us, event | category | flops | bytes accessed | tf_op | source)
XLA Modules:
  0.0 128.9 jit_solution(8480047556314006225)
XLA Ops:
  0.6 0.7 reduce-precision_convert_fusion.1
  1.4 0.3 copy.43
  1.8 1.2 fusion.16.chars_ref
  3.0 0.5 fusion.13
  3.6 0.3 copy.56
  3.8 4.4 %sort.15 = (s32[2048]{0:T(1024)S(1)}, s32[2048]{0:T(1024)S(1)}) sort(s32[2048]{0:T(1024)S(1)} %copy-done.5, s32[2048]{0:T(1024)S(1)} %iota.8), dimensions={0}, to_apply=%region_0.1 | sort | flops 22528 | bytes 32768 | tf_op jit(solution)/shard_map/sort | solution.py:300
  8.6 0.7 fusion.27.gate_ref
  9.3 11.3 %all-to-all-start = ((bf16[32,16,128]{2,1,0:T(8,128)(2,1)}), bf16[32,16,128]{2,1,0:T(8,128)(2,1)S(1)}, u32[]{:S(2)}, u32[]{:S(2)}) async-start(bf16[32,16,128]{2,1,0:T(8,128)(2,1)} %fusion.27.gate_ref), calls=%async_computation | async-start | bytes 262144 | tf_op jit(solution)/shard_map/all_to_all | solution.py:310
  20.7 0.6 fusion.51
  21.4 9.5 %stats.1.stat_ref = f32[2,4096]{1,0:T(2,128)S(1)} custom-call(bf16[2048,256]{1,0:T(8,128)(2,1)S(1)} %fusion.16.chars_ref, bf16[4096,128]{1,0:T(8,128)(2,1)S(1)} %copy-done, bf16[32,16,128]{2,1,0:T(8,128)(2,1)} %fusion.27.gate_ref), custom_call_target="tpu_custom_call" | custom-call | tf_op jit(solution)/shard_map/stats/pallas_call | solution.py:54
  31.7 0.1 copy.55
  31.9 3.3 %pick_rows.1 = (bf16[2560,128]{1,0:T(8,128)(2,1)}, f32[2,4096]{1,0:T(2,128)S(1)}) custom-call(s32[64,32]{1,0:T(8,128)S(1)} %fusion.32.ids_ref, bf16[2048,256]{1,0:T(8,128)(2,1)S(1)} %fusion.16.chars_ref, f32[16,128]{1,0:T(8,128)S(1)} %pad_maximum_fusion.12.tail_ref, f32[2,4096]{1,0:T(2,128)S(1)} %stats.1.stat_ref), custom_call_target="tpu_custom_call" | custom-call | tf_op jit(solution)/shard_map/pick_rows/pallas_call | solution.py:92
  35.2 9.3 %all-to-all-start.1 = ((bf16[32,80,128]{2,1,0:T(8,128)(2,1)}), bf16[32,80,128]{2,1,0:T(8,128)(2,1)S(1)}, u32[]{:S(2)}, u32[]{:S(2)}) async-start(bf16[32,80,128]{2,1,0:T(8,128)(2,1)} %bitcast.12), calls=%async_computation.1 | async-start | bytes 1310720 | tf_op jit(solution)/shard_map/all_to_all | solution.py:321
  44.5 25.9 %conditional.3 = (f32[2,4096]{1,0:T(2,128)S(1)}, f32[1,4096]{1,0:T(1,128)}, f32[1,4096]{1,0:T(1,128)}) conditional(s32[]{:T(128)} %bitcast.15, f32[2,4096]{1,0:T(2,128)S(1)} %get-tuple-element.107, f32[2,4096]{1,0:T(2,128)S(1)} %get-tuple-element.107), branch_computations={%region_2.3_spmd, %region_3.4_spmd} | conditional | flops 163840 | bytes 1474784 | solution.py:342
  44.5 1.3 %collective-permute-start.3 = (f32[2,4096]{1,0:T(2,128)S(1)}, f32[2,4096]{1,0:T(2,128)S(1)}, u32[]{:S(2)}, u32[]{:S(2)}) collective-permute-start(f32[2,4096]{1,0:T(2,128)S(1)} %param.1), channel_id=1, source_target_pairs={{0,1},{1,0},{2,3},{3,2},{4,5},{5,4},{6,7},{7,6},{8,9},{9,8},{10,11... | collective-permute-start | bytes 98312 | tf_op jit(solution)/shard_map/cond/branch_1_fun/ppermute | solution.py:273
  45.8 6.9 %collective-permute-done.3 = f32[2,4096]{1,0:T(2,128)S(1)} collective-permute-done((f32[2,4096]{1,0:T(2,128)S(1)}, f32[2,4096]{1,0:T(2,128)S(1)}, u32[]{:S(2)}, u32[]{:S(2)}) %collective-permute-start.3) | collective-permute-done | bytes 32800 | tf_op jit(solution)/shard_map/cond/branch_1_fun/ppermute | solution.py:273
  52.9 1.9 %collective-permute-start.4 = (f32[2,4096]{1,0:T(2,128)S(1)}, f32[2,4096]{1,0:T(2,128)S(1)}, u32[]{:S(2)}, u32[]{:S(2)}) collective-permute-start(f32[2,4096]{1,0:T(2,128)S(1)} %pad_maximum_fusion), channel_id=1, source_target_pairs={{0,3},{1,2},{2,1},{3,0},{4,7},{5,6},{6,5},{7,4},{8,11},{9,10},{10,... | collective-permute-start | bytes 98312 | tf_op jit(solution)/shard_map/cond/branch_1_fun/ppermute | solution.py:273
  54.7 2.5 %collective-permute-done.4 = f32[2,4096]{1,0:T(2,128)S(1)} collective-permute-done((f32[2,4096]{1,0:T(2,128)S(1)}, f32[2,4096]{1,0:T(2,128)S(1)}, u32[]{:S(2)}, u32[]{:S(2)}) %collective-permute-start.4) | collective-permute-done | bytes 32800 | tf_op jit(solution)/shard_map/cond/branch_1_fun/ppermute | solution.py:273
  57.3 1.3 collective-permute-start.5
  58.6 1.6 %collective-permute-done.5 = f32[2,4096]{1,0:T(2,128)S(1)} collective-permute-done((f32[2,4096]{1,0:T(2,128)S(1)}, f32[2,4096]{1,0:T(2,128)S(1)}, u32[]{:S(2)}, u32[]{:S(2)}) %collective-permute-start.5) | collective-permute-done | bytes 32800 | tf_op jit(solution)/shard_map/cond/branch_1_fun/ppermute | solution.py:273
  60.3 2.5 %collective-permute-start.6 = (f32[2,4096]{1,0:T(2,128)S(1)}, f32[2,4096]{1,0:T(2,128)S(1)}, u32[]{:S(2)}, u32[]{:S(2)}) collective-permute-start(f32[2,4096]{1,0:T(2,128)S(1)} %pad_maximum_fusion.2), channel_id=1, source_target_pairs={{0,12},{1,13},{2,14},{3,15},{4,8},{5,9},{6,10},{7,11},{8,4},{9,5},... | collective-permute-start | bytes 98312 | tf_op jit(solution)/shard_map/cond/branch_1_fun/ppermute | solution.py:273
  62.8 1.6 %collective-permute-done.6 = f32[2,4096]{1,0:T(2,128)S(1)} collective-permute-done((f32[2,4096]{1,0:T(2,128)S(1)}, f32[2,4096]{1,0:T(2,128)S(1)}, u32[]{:S(2)}, u32[]{:S(2)}) %collective-permute-start.6) | collective-permute-done | bytes 32800 | tf_op jit(solution)/shard_map/cond/branch_1_fun/ppermute | solution.py:273
  64.4 2.8 %collective-permute-start.7 = (f32[2,4096]{1,0:T(2,128)S(1)}, f32[2,4096]{1,0:T(2,128)S(1)}, u32[]{:S(2)}, u32[]{:S(2)}) collective-permute-start(f32[2,4096]{1,0:T(2,128)S(1)} %pad_maximum_fusion.3), channel_id=1, source_target_pairs={{0,16},{1,17},{2,18},{3,19},{4,20},{5,21},{6,22},{7,23},{8,24},{9,... | collective-permute-start | bytes 98312 | tf_op jit(solution)/shard_map/cond/branch_1_fun/ppermute | solution.py:273
  67.2 1.6 %collective-permute-done.7 = f32[2,4096]{1,0:T(2,128)S(1)} collective-permute-done((f32[2,4096]{1,0:T(2,128)S(1)}, f32[2,4096]{1,0:T(2,128)S(1)}, u32[]{:S(2)}, u32[]{:S(2)}) %collective-permute-start.7) | collective-permute-done | bytes 32800 | tf_op jit(solution)/shard_map/cond/branch_1_fun/ppermute | solution.py:273
  68.8 0.7 fusion
  69.4 0.8 pad_maximum_fusion.4
  70.4 0.8 broadcast_maximum_fusion
  71.3 0.3 copy.53
  71.6 0.1 fusion.29
  71.8 0.1 reshape.114.beside_ref
  71.9 2.4 %place_rows.1.chars_ref = bf16[2048,256]{1,0:T(8,128)(2,1)S(1)} custom-call(s32[1,2048]{1,0:T(1,128)S(1)} %bitcast.45, bf16[2560,128]{1,0:T(8,128)(2,1)S(1)} %bitcast.44, f32[8,2048]{1,0:T(8,128)S(1)} %reshape.114.beside_ref, f32[2,4096]{1,0:T(2,128)S(1)} %get-tuple-element.108.gate_ref), custom_call_target="tpu_custom_call" | custom-call | tf_op jit(solution)/shard_map/place_rows/pallas_call | solution.py:124
  74.3 5.5 %first_panel.1 = (f32[520,256]{1,0:T(8,128)S(1)}, f32[512,128]{1,0:T(8,128)}, bf16[256,4096]{1,0:T(8,128)(2,1)S(1)}) custom-call(bf16[2048,256]{1,0:T(8,128)(2,1)S(1)} %place_rows.1.chars_ref, bf16[4096,128]{1,0:T(8,128)(2,1)S(1)} %copy-done, f32[3,4096]{1,0:T(4,128)S(1)} %pad_maximum_fusion.9.rows_ref, bf16[256,256]{1,0:T(8,128)(2,1)S(1)} %fusion.26.cols_ref), custom_call_target="tpu_custom_call" | custom-call | flops 2147483648 | bytes 1048576 | tf_op jit(solution)/shard_map/first_panel/pallas_call | solution.py:171
  79.8 6.7 %collective-permute-start.8 = (f32[520,256]{1,0:T(8,128)S(1)}, f32[520,256]{1,0:T(8,128)S(1)}, u32[]{:S(2)}, u32[]{:S(2)}) collective-permute-start(f32[520,256]{1,0:T(8,128)S(1)} %get-tuple-element.112.gate_ref), channel_id=1, source_target_pairs={{0,32},{32,0},{64,96},{96,64},{1,33},{33,1},{65,97},{97,65},{2,34}... | collective-permute-start | bytes 1597448 | tf_op jit(solution)/shard_map/ppermute | solution.py:273
  86.6 3.1 %panel.5 = (f32[512,256]{1,0:T(8,128)S(1)}, f32[512,128]{1,0:T(8,128)}) custom-call(bf16[2048,256]{1,0:T(8,128)(2,1)S(1)} %place_rows.1.chars_ref, bf16[4096,128]{1,0:T(8,128)(2,1)S(1)} %copy-done, f32[3,4096]{1,0:T(4,128)S(1)} %pad_maximum_fusion.9.rows_ref, bf16[256,4096]{1,0:T(8,128)(2,1)S(1)} %get-tuple-element.111.weight_ref, ...), custom_call_target="tpu_custom_call" | custom-call | flops 2147483648 | bytes 1048576 | tf_op jit(solution)/shard_map/panel/pallas_call | solution.py:213
  89.7 0.1 fusion.24
  89.8 0.5 collective-permute-start.9
  91.0 10.6 %conditional.4 = (f16[512,256]{1,0:T(8,128)(2,1)}, f32[1,256]{1,0:T(1,128)S(1)}, f32[512,128]{1,0:T(8,128)S(1)}, f32[512,128]{1,0:T(8,128)}, f32[512,256]{1,0:T(8,128)}) conditional(s32[]{:T(128)} %bitcast.22, () %tuple.42, (bf16[2048,256]{1,0:T(8,128)(2,1)}, bf16[4096,128]{1,0:T(8,128)(2,1)S(1)}, f32[3,4096]{1,0:T(4,128)S(1)}, ...), branch_computations={%region_5.6_spmd, %region_6.8_spmd} | conditional | flops 4295623680 | bytes 18879624 | solution.py:370
  91.0 4.3 %panel.3 = (f32[512,256]{1,0:T(8,128)S(1)}, f32[512,128]{1,0:T(8,128)S(1)}) custom-call(bf16[2048,256]{1,0:T(8,128)(2,1)} %get-tuple-element.55.chars_ref, bf16[4096,128]{1,0:T(8,128)(2,1)S(1)} %get-tuple-element.56.tastes_ref, f32[3,4096]{1,0:T(4,128)S(1)} %get-tuple-element.57.rows_ref, bf16[256,4096]{1,0:T(8,128)(2,1)} %get-tuple-element.58.weight_ref, ...), custom_call_target="tpu_custom_call" | custom-call | flops 2147483648 | bytes 1048576 | tf_op jit(solution)/shard_map/cond/branch_1_fun/panel/pallas_call | solution.py:213
  95.3 0.6 collective-permute-start
  95.9 3.1 %panel.4 = (f32[512,256]{1,0:T(8,128)S(1)}, f32[512,128]{1,0:T(8,128)}) custom-call(bf16[2048,256]{1,0:T(8,128)(2,1)S(1)} %copy-done.4, bf16[4096,128]{1,0:T(8,128)(2,1)S(1)} %get-tuple-element.56.tastes_ref, f32[3,4096]{1,0:T(4,128)S(1)} %get-tuple-element.57.rows_ref, bf16[256,4096]{1,0:T(8,128)(2,1)S(1)} %copy-done.10, ...), custom_call_target="tpu_custom_call" | custom-call | flops 2147483648 | bytes 1048576 | tf_op jit(solution)/shard_map/cond/branch_1_fun/panel/pallas_call | solution.py:213
  99.0 0.8 fusion.5
  99.8 1.8 %convert_element_type.63 = f32[512,256]{1,0:T(8,128)} convert(f16[512,256]{1,0:T(8,128)(2,1)} %get-tuple-element.179) | non-fusion elementwise | flops 131072 | bytes 786432 | tf_op jit(solution)/shard_map/convert_element_type | solution.py:411
  101.6 1.1 collective-permute-start.10
  103.4 0.6 copy-done.2
  104.0 16.8 %conditional.5 = (f32[4352]{0:T(1024)}, f32[4352]{0:T(1024)}, f32[256]{0:T(256)S(1)}) conditional(s32[]{:T(128)} %bitcast.2, () %tuple.40, (f32[512,256]{1,0:T(8,128)S(1)}, f32[1,256]{1,0:T(1,128)S(1)}, bf16[2048,256]{1,0:T(8,128)(2,1)S(1)}, bf16[4096,128]{1,0:T(8,128)(2,1)S(1)}, f32[3,4096]{1,0:T(4,128)S(1)}, /*index=5*/s32[]{:T(128)}, ...), branch_computations={%region_8.9_spmd, %region_9.16_spmd} | conditional | flops 685825 | bytes 2886794 | solution.py:391
  104.0 1.1 reduce_sum.57
  105.1 1.1 reduce_sum.58
  106.2 1.1 reduce_sum.59
  107.3 0.1 reduce_sum.60
  107.6 7.2 %share_sums.1 = f32[2048,128]{1,0:T(8,128)S(1)} custom-call(bf16[2048,256]{1,0:T(8,128)(2,1)S(1)} %get-tuple-element.68.chars_ref, bf16[4096,128]{1,0:T(8,128)(2,1)S(1)} %get-tuple-element.69.tastes_ref, f32[3,4096]{1,0:T(4,128)S(1)} %get-tuple-element.70.rows_ref, f32[1,256]{1,0:T(1,128)S(1)} %max.63.gate_ref), custom_call_target="tpu_custom_call" | custom-call | tf_op jit(solution)/shard_map/cond/branch_1_fun/share_sums/pallas_call | solution.py:255
  114.8 0.3 reduce_sum.56
  115.2 0.6 collective-permute-start.1
  115.7 0.8 collective-permute-done.1
  116.6 0.6 fusion.9
  117.2 0.4 collective-permute-start.2
  117.6 2.5 %collective-permute-done.2 = f32[4352]{0:T(1024)} collective-permute-done((f32[4352]{0:T(1024)}, f32[4352]{0:T(1024)}, u32[]{:S(2)}, u32[]{:S(2)}) %collective-permute-start.2) | collective-permute-done | bytes 17440 | tf_op jit(solution)/shard_map/cond/branch_1_fun/ppermute | solution.py:273
  120.1 0.7 slice.175
  120.8 1.6 %select_subtract_fusion.1 = (f32[512,256]{1,0:T(8,128)S(1)}, f32[512,256]{1,0:T(8,128)S(1)}) fusion(f16[512,256]{1,0:T(8,128)(2,1)S(1)} %get-tuple-element.114, f32[256]{0:T(256)S(1)} %get-tuple-element.164, s32[256]{0:T(256)S(1)} %copy-done.7, f32[256]{0:T(256)S(1)} %get-tuple-element.163, f32[256]{0:T(256)S(1)} %bitcast.55, s32[512]{0:T(512)S(1)} %get-tuple-element.161, ...), kind=kLoop, calls=%fused_computation.44 | loop fusion | flops 1966080 | bytes 2367488 | tf_op jit(solution)/shard_map/sub | solution.py:413
  122.5 1.0 fusion.20
  123.5 1.6 %collective-permute-start.11 = (f32[1024,256]{1,0:T(8,128)S(1)}, f32[1024,256]{1,0:T(8,128)S(1)}, u32[]{:S(2)}, u32[]{:S(2)}) collective-permute-start(f32[1024,256]{1,0:T(8,128)S(1)} %bitcast.46), channel_id=1, source_target_pairs={{0,32},{32,0},{64,96},{96,64},{1,33},{33,1},{65,97},{97,65},{2,34}... | collective-permute-start | bytes 3145736 | tf_op jit(solution)/shard_map/ppermute | solution.py:273
  125.1 0.7 add_multiply_fusion.1
  125.8 0.6 slice_bitcast_fusion.4
  126.4 0.9 multiply_reduce_fusion
  127.4 1.6 %maximum_select_fusion = f32[2048,256]{1,0:T(8,128)} fusion(f32[1024,256]{1,0:T(8,128)S(1)} %collective-permute-done.11, f32[1024,256]{1,0:T(8,128)S(1)} %bitcast.47, pred[]{:T(512)S(6)} %eq.68), kind=kLoop, calls=%fused_computation.31 | loop fusion | flops 1572864 | bytes 4194305 | tf_op jit(solution)/shard_map/jit(_where)/select_n | solution.py:421
  (81 shorter events, 1.5 us)
Async XLA Ops:
  0.6 2.4 %copy-start.7 = (s32[256]{0:T(256)S(1)}, s32[256]{0:T(256)}, u32[]{:S(2)}) copy-start(s32[256]{0:T(256)} %param.17) | copy-start | bytes 3076
  1.8 2.1 %copy-start.5 = (s32[2048]{0:T(1024)S(1)}, s32[2048]{0:T(1024)}, u32[]{:S(2)}) copy-start(s32[2048]{0:T(1024)} %param.18) | copy-start | bytes 24580
  3.0 18.4 %copy-start = (bf16[4096,128]{1,0:T(8,128)(2,1)S(1)}, bf16[4096,128]{1,0:T(8,128)(2,1)}, u32[]{:S(2)}) copy-start(bf16[4096,128]{1,0:T(8,128)(2,1)} %tastes_ref.5) | copy-start | bytes 3145732
  9.3 22.3 %all-to-all-start = ((bf16[32,16,128]{2,1,0:T(8,128)(2,1)}), bf16[32,16,128]{2,1,0:T(8,128)(2,1)S(1)}, u32[]{:S(2)}, u32[]{:S(2)}) async-start(bf16[32,16,128]{2,1,0:T(8,128)(2,1)} %fusion.27.gate_ref), calls=%async_computation | async-start | bytes 262144 | tf_op jit(solution)/shard_map/all_to_all | solution.py:310
  30.9 40.3 %copy-start.6 = (f32[4096]{0:T(1024)S(1)}, f32[4096]{0:T(1024)}, u32[]{:S(2)}) copy-start(f32[4096]{0:T(1024)} %param.14) | copy-start | bytes 49156
  31.8 39.8 %copy-start.8 = (pred[8]{0:T(512)(128)(4,1)S(1)}, pred[8]{0:T(512)(128)(4,1)}, u32[]{:S(2)}) copy-start(pred[8]{0:T(512)(128)(4,1)} %constant.153.clone.1) | copy-start | bytes 28
  35.2 36.0 %all-to-all-start.1 = ((bf16[32,80,128]{2,1,0:T(8,128)(2,1)}), bf16[32,80,128]{2,1,0:T(8,128)(2,1)S(1)}, u32[]{:S(2)}, u32[]{:S(2)}) async-start(bf16[32,80,128]{2,1,0:T(8,128)(2,1)} %bitcast.12), calls=%async_computation.1 | async-start | bytes 1310720 | tf_op jit(solution)/shard_map/all_to_all | solution.py:321
  44.5 8.2 %collective-permute-start.3 = (f32[2,4096]{1,0:T(2,128)S(1)}, f32[2,4096]{1,0:T(2,128)S(1)}, u32[]{:S(2)}, u32[]{:S(2)}) collective-permute-start(f32[2,4096]{1,0:T(2,128)S(1)} %param.1), channel_id=1, source_target_pairs={{0,1},{1,0},{2,3},{3,2},{4,5},{5,4},{6,7},{7,6},{8,9},{9,8},{10,11... | collective-permute-start | bytes 98312 | tf_op jit(solution)/shard_map/cond/branch_1_fun/ppermute | solution.py:273
  52.9 4.3 %collective-permute-start.4 = (f32[2,4096]{1,0:T(2,128)S(1)}, f32[2,4096]{1,0:T(2,128)S(1)}, u32[]{:S(2)}, u32[]{:S(2)}) collective-permute-start(f32[2,4096]{1,0:T(2,128)S(1)} %pad_maximum_fusion), channel_id=1, source_target_pairs={{0,3},{1,2},{2,1},{3,0},{4,7},{5,6},{6,5},{7,4},{8,11},{9,10},{10,... | collective-permute-start | bytes 98312 | tf_op jit(solution)/shard_map/cond/branch_1_fun/ppermute | solution.py:273
  57.3 2.8 %collective-permute-start.5 = (f32[2,4096]{1,0:T(2,128)S(1)}, f32[2,4096]{1,0:T(2,128)S(1)}, u32[]{:S(2)}, u32[]{:S(2)}) collective-permute-start(f32[2,4096]{1,0:T(2,128)S(1)} %pad_maximum_fusion.1), channel_id=1, source_target_pairs={{0,4},{1,5},{2,6},{3,7},{4,0},{5,1},{6,2},{7,3},{8,12},{9,13},{10,... | collective-permute-start | bytes 98312 | tf_op jit(solution)/shard_map/cond/branch_1_fun/ppermute | solution.py:273
  60.3 4.1 %collective-permute-start.6 = (f32[2,4096]{1,0:T(2,128)S(1)}, f32[2,4096]{1,0:T(2,128)S(1)}, u32[]{:S(2)}, u32[]{:S(2)}) collective-permute-start(f32[2,4096]{1,0:T(2,128)S(1)} %pad_maximum_fusion.2), channel_id=1, source_target_pairs={{0,12},{1,13},{2,14},{3,15},{4,8},{5,9},{6,10},{7,11},{8,4},{9,5},... | collective-permute-start | bytes 98312 | tf_op jit(solution)/shard_map/cond/branch_1_fun/ppermute | solution.py:273
  64.4 4.3 %collective-permute-start.7 = (f32[2,4096]{1,0:T(2,128)S(1)}, f32[2,4096]{1,0:T(2,128)S(1)}, u32[]{:S(2)}, u32[]{:S(2)}) collective-permute-start(f32[2,4096]{1,0:T(2,128)S(1)} %pad_maximum_fusion.3), channel_id=1, source_target_pairs={{0,16},{1,17},{2,18},{3,19},{4,20},{5,21},{6,22},{7,23},{8,24},{9,... | collective-permute-start | bytes 98312 | tf_op jit(solution)/shard_map/cond/branch_1_fun/ppermute | solution.py:273
  74.3 12.2 %copy-start.3 = (bf16[2048,256]{1,0:T(8,128)(2,1)}, bf16[2048,256]{1,0:T(8,128)(2,1)S(1)}, u32[]{:S(2)}) copy-start(bf16[2048,256]{1,0:T(8,128)(2,1)S(1)} %place_rows.1.chars_ref) | copy-start | bytes 3145732
  79.8 9.8 %copy-start.9 = (bf16[256,4096]{1,0:T(8,128)(2,1)}, bf16[256,4096]{1,0:T(8,128)(2,1)S(1)}, u32[]{:S(2)}) copy-start(bf16[256,4096]{1,0:T(8,128)(2,1)S(1)} %get-tuple-element.111.weight_ref) | copy-start | bytes 6291460
  79.8 9.8 %collective-permute-start.8 = (f32[520,256]{1,0:T(8,128)S(1)}, f32[520,256]{1,0:T(8,128)S(1)}, u32[]{:S(2)}, u32[]{:S(2)}) collective-permute-start(f32[520,256]{1,0:T(8,128)S(1)} %get-tuple-element.112.gate_ref), channel_id=1, source_target_pairs={{0,32},{32,0},{64,96},{96,64},{1,33},{33,1},{65,97},{97,65},{2,34}... | collective-permute-start | bytes 1597448 | tf_op jit(solution)/shard_map/ppermute | solution.py:273
  89.8 13.5 %collective-permute-start.9 = (f16[512,256]{1,0:T(8,128)(2,1)S(1)}, f16[512,256]{1,0:T(8,128)(2,1)S(1)}, u32[]{:S(2)}, u32[]{:S(2)}) collective-permute-start(f16[512,256]{1,0:T(8,128)(2,1)S(1)} %get-tuple-element.114), channel_id=1, source_target_pairs={{0,64},{32,96},{64,0},{96,32},{1,65},{33,97},{65,1},{97,33},{2,66}... | collective-permute-start | bytes 786440 | tf_op jit(solution)/shard_map/ppermute | solution.py:273
  91.0 11.7 %dynamic-slice-start = ((s32[2048]{0:T(1024)}, s32[]{:T(128)}), s32[1024]{0:T(1024)S(1)}, s32[]{:S(2)}) async-start(s32[2048]{0:T(1024)} %param.18, s32[]{:T(128)} %select_n.110), calls=%async_computation.2 | async-start | bytes 8704 | tf_op jit(solution)/shard_map/dynamic_slice | solution.py:405
  91.0 4.9 %copy-start.4 = (bf16[2048,256]{1,0:T(8,128)(2,1)S(1)}, bf16[2048,256]{1,0:T(8,128)(2,1)}, u32[]{:S(2)}) copy-start(bf16[2048,256]{1,0:T(8,128)(2,1)} %get-tuple-element.55.chars_ref) | copy-start | bytes 3145732 | tf_op jit(solution)/shard_map/cond
  91.0 4.9 %copy-start.10 = (bf16[256,4096]{1,0:T(8,128)(2,1)S(1)}, bf16[256,4096]{1,0:T(8,128)(2,1)}, u32[]{:S(2)}) copy-start(bf16[256,4096]{1,0:T(8,128)(2,1)} %get-tuple-element.58.weight_ref) | copy-start | bytes 6291460 | tf_op jit(solution)/shard_map/cond
  95.3 3.7 %collective-permute-start = (f32[512,256]{1,0:T(8,128)S(1)}, f32[512,256]{1,0:T(8,128)S(1)}, u32[]{:S(2)}, u32[]{:S(2)}) collective-permute-start(f32[512,256]{1,0:T(8,128)S(1)} %get-tuple-element.60.gate_ref), channel_id=1, source_target_pairs={{0,32},{32,0},{64,96},{96,64},{1,33},{33,1},{65,97},{97,65},{2,34}... | collective-permute-start | bytes 1572872 | tf_op jit(solution)/shard_map/cond/branch_1_fun/ppermute | solution.py:273
  101.6 19.2 %collective-permute-start.10 = (f16[512,256]{1,0:T(8,128)(2,1)}, f16[512,256]{1,0:T(8,128)(2,1)}, u32[]{:S(2)}, u32[]{:S(2)}) collective-permute-start(f16[512,256]{1,0:T(8,128)(2,1)} %get-tuple-element.125), channel_id=1, source_target_pairs={{0,64},{32,96},{64,0},{96,32},{1,65},{33,97},{65,1},{97,33},{2,66}... | collective-permute-start | bytes 786440 | tf_op jit(solution)/shard_map/ppermute | solution.py:273
  103.3 0.7 copy-start.2
  115.2 1.4 %collective-permute-start.1 = (f32[4352]{0:T(1024)S(1)}, f32[4352]{0:T(1024)S(1)}, u32[]{:S(2)}, u32[]{:S(2)}) collective-permute-start(f32[4352]{0:T(1024)S(1)} %pad_maximum_fusion.5), channel_id=1, source_target_pairs={{0,32},{32,0},{64,96},{96,64},{1,33},{33,1},{65,97},{97,65},{2,34}... | collective-permute-start | bytes 52232 | tf_op jit(solution)/shard_map/cond/branch_1_fun/ppermute | solution.py:273
  117.2 2.9 %collective-permute-start.2 = (f32[4352]{0:T(1024)}, f32[4352]{0:T(1024)}, u32[]{:S(2)}, u32[]{:S(2)}) collective-permute-start(f32[4352]{0:T(1024)} %fusion.9), channel_id=1, source_target_pairs={{0,64},{32,96},{64,0},{96,32},{1,65},{33,97},{65,1},{97,33},{2,66}... | collective-permute-start | bytes 52232 | tf_op jit(solution)/shard_map/cond/branch_1_fun/ppermute | solution.py:273
  120.8 1.7 %copy-start.1 = (f32[16,128,128]{2,1,0:T(8,128)S(1)}, f32[16,128,128]{2,1,0:T(8,128)}, u32[]{:S(2)}) copy-start(f32[16,128,128]{2,1,0:T(8,128)} %param.19) | copy-start | bytes 3145732
  123.5 3.9 %collective-permute-start.11 = (f32[1024,256]{1,0:T(8,128)S(1)}, f32[1024,256]{1,0:T(8,128)S(1)}, u32[]{:S(2)}, u32[]{:S(2)}) collective-permute-start(f32[1024,256]{1,0:T(8,128)S(1)} %bitcast.46), channel_id=1, source_target_pairs={{0,32},{32,0},{64,96},{96,64},{1,33},{33,1},{65,97},{97,65},{2,34}... | collective-permute-start | bytes 3145736 | tf_op jit(solution)/shard_map/ppermute | solution.py:273

commit v8 on v6

--- a/solution.py
+++ b/solution.py
@@ -13,17 +13,95 @@
     return lax.dot_general(left, right, NT, preferred_element_type=jnp.float32)
 
 
-def split3(values):
-    high = lax.reduce_precision(values, 8, 7)
-    middle = lax.reduce_precision(values - high, 8, 7)
-    low = lax.reduce_precision(values - high - middle, 8, 7)
-    high, middle, low = (piece.astype(jnp.bfloat16) for piece in (high, middle, low))
-    return high, middle, low
+def rounded(values):
+    return values.astype(jnp.bfloat16).astype(jnp.float32)
+
+
+def prepare(characteristics, means, firm_row, panel_rows, holders):
+    rows, depth = characteristics.shape
+    per_pair = rows // holders
+    cols = panel_rows.shape[0] * 128
+    share_cols = cols // holders
+    chunk = 256
+
+    def kernel(chars_ref, means_ref, firm_ref, panel_ref, both_ref, message_ref, order_ref):
+        lane = lax.broadcasted_iota(jnp.int32, (128, 128), 1)
+        values = means_ref[...]
+        high = rounded(values)
+        middle = rounded(values - high)
+        low = values - high - middle
+        pieces = jnp.concatenate([high, middle, low, jnp.zeros((128 - 3 * values.shape[0], 128), jnp.float32)], axis=0).T
+        count = values.shape[0]
+        both_ref[:, :depth] = chars_ref[...]
+        for k in range(count):
+            beside = jnp.zeros((128, 128), jnp.float32)
+            for piece in range(3):
+                place = piece * count + k
+                beside = jnp.where(lane == piece + 1, pieces[:, place : place + 1], beside)
+            both_ref[k * 128 : (k + 1) * 128, depth:] = beside.astype(jnp.bfloat16)
+
+        firm = firm_ref[...]
+        holder, wanted = firm // rows, firm % rows
+        holder_id = lax.broadcasted_iota(jnp.int32, (holders, rows), 0)
+        named = jnp.where(holder_id == holder, 1.0, 0.0)
+        blocks = [named[:, start : start + 128] for start in range(0, rows, 128)]
+        before = (lax.broadcasted_iota(jnp.int32, (128, 128), 0) < lane).astype(jnp.float32).astype(jnp.bfloat16)
+        counts = jnp.dot(
+            jnp.concatenate(blocks, axis=0).astype(jnp.bfloat16), before, preferred_element_type=jnp.float32
+        )
+        seen = jnp.zeros((holders, 1), jnp.float32)
+        ranks = []
+        for k, block in enumerate(blocks):
+            rank = counts[k * holders : (k + 1) * holders, :] + seen
+            ranks.append(jnp.sum(block * rank, axis=0, keepdims=True))
+            seen = seen + jnp.sum(block, axis=1, keepdims=True)
+        slot = holder * per_pair + jnp.concatenate(ranks, axis=1).astype(jnp.int32)
+
+        row = lax.broadcasted_iota(jnp.int32, (8, rows), 0)
+        firm_place = lax.broadcasted_iota(jnp.int32, (8, rows), 1)
+        digits = jnp.where(row == 0, wanted // 256, jnp.where(row == 1, wanted % 256, 0))
+        digits = jnp.where(row == 2, firm_place // 256, jnp.where(row == 3, firm_place % 256, digits))
+        digits = jnp.concatenate([digits, jnp.zeros_like(digits)], axis=0).astype(jnp.float32).astype(jnp.bfloat16)
+        asked = []
+        for start in range(0, rows, chunk):
+            slots = start + lax.broadcasted_iota(jnp.int32, (chunk, rows), 0)
+            hot = jnp.where(slots == slot, 1.0, 0.0).astype(jnp.bfloat16)
+            found = dot_nt(digits, hot)
+            order_ref[:, start : start + chunk] = (found[2:3, :] * 256.0 + found[3:4, :]).astype(jnp.int32)
+            asked.append(found)
+
+        products = lax.broadcasted_iota(jnp.int32, (128, rows), 1).astype(jnp.float32)
+        both = both_ref[...]
+        wide = jnp.concatenate([panel_ref[...], jnp.zeros((128 - panel_ref.shape[0], 128), jnp.float32)], axis=0).T
+        part_row = lax.broadcasted_iota(jnp.int32, (8, 128), 0)
+        for k in range(cols // 128):
+            hot = jnp.where(wide[:, k : k + 1] == products, 1.0, 0.0).astype(jnp.bfloat16)
+            part = jnp.dot(hot, both, preferred_element_type=jnp.float32)
+            part_pieces = part[:, depth:].T[:8, :]
+            for place in range(128 // share_cols):
+                q = k * (128 // share_cols) + place
+                start = q * per_pair // 128 * 128 % chunk
+                found = asked[q * per_pair // chunk][:, start : start + 128]
+                extra = jnp.where(part_row == 0, found[0:1, :], jnp.where(part_row == 4, found[1:2, :], part_pieces))
+                mine = part[place * share_cols : (place + 1) * share_cols, :depth]
+                message_ref[q * 16 : (q + 1) * 16, :] = jnp.concatenate([mine, extra], axis=0).astype(jnp.bfloat16)
+
+    return pl.pallas_call(
+        kernel,
+        out_shape=[
+            jax.ShapeDtypeStruct((rows, 2 * depth), jnp.bfloat16),
+            jax.ShapeDtypeStruct((16 * holders, depth), jnp.bfloat16),
+            jax.ShapeDtypeStruct((1, rows), jnp.int32),
+        ],
+        compiler_params=pltpu.CompilerParams(vmem_limit_bytes=VMEM_BYTES),
+        name="prepare",
+    )(characteristics, means, firm_row, panel_rows)
 
 
 def beside_ones(tastes):
-    ones = lax.broadcasted_iota(jnp.int32, tastes.shape, 1) < 3
-    return jnp.concatenate([tastes, jnp.where(ones, 1.0, 0.0).astype(tastes.dtype)], axis=1)
+    lane = lax.broadcasted_iota(jnp.int32, tastes.shape, 1)
+    ones = jnp.where((lane >= 1) & (lane <= 3), 1.0, 0.0)
+    return jnp.concatenate([tastes, ones.astype(tastes.dtype)], axis=1)
 
 
 def stats(chars, tastes, gate):
@@ -294,38 +372,35 @@
     base = lax.axis_index("prod") * products
     core = lax.axis_index("cons") % 2
 
-    pieces = jnp.stack(split3(mean_utility), axis=1)
-    chars = jnp.concatenate([characteristics, jnp.pad(pieces, ((0, 0), (0, depth - 3)))], axis=1)
-
-    wanted, order = lax.sort((firm_map, lax.iota(jnp.int32, products)), num_keys=1)
-    wanted = (wanted % products).reshape(holders, per_pair)
-    digits = jnp.concatenate([wanted // 256, wanted % 256], axis=1).astype(jnp.bfloat16)[:, None, :]
-    product_ids = base + lax.iota(jnp.int32, products)
-    hits = (panel_cols[:, None] == product_ids[None, :]).astype(jnp.bfloat16)
-    col_part = jnp.dot(hits, chars, preferred_element_type=jnp.float32).astype(jnp.bfloat16)
     share_cols = cols // holders
-    col_pieces = col_part[:, depth : depth + 3].reshape(holders, share_cols, 3).transpose(0, 2, 1)
-    col_pieces = jnp.pad(col_pieces, ((0, 0), (0, 4), (0, depth - share_cols)))
-    message = jnp.concatenate([col_part[:, :depth].reshape(holders, share_cols, depth), digits, col_pieces], axis=1)
-    first = lax.all_to_all(message, "prod", split_axis=0, concat_axis=0, tiled=True)
+    chars, message, order = prepare(
+        characteristics,
+        mean_utility.reshape(products // 128, 128),
+        firm_map.reshape(1, products),
+        (panel_cols - base).astype(jnp.float32).reshape(cols // 128, 128),
+        holders,
+    )
+    first = lax.all_to_all(message.reshape(holders, 16, depth), "prod", split_axis=0, concat_axis=0, tiled=True)
 
     stat = stats(chars, tastes, message)
 
-    asked = first[:, share_cols, :].astype(jnp.int32)
-    ids = asked[:, :per_pair] * 256 + asked[:, per_pair:]
+    odd = lax.axis_index("prod") % 2 == 1
+
+    def own_lanes(values):
+        return jnp.where(odd, values[..., per_pair:], values[..., :per_pair])
+
+    high, low = own_lanes(first[:, 8, :]), own_lanes(first[:, 12, :])
+    ids = high.astype(jnp.int32) * 256 + low.astype(jnp.int32)
     summed = jnp.sum(first.astype(jnp.float32), axis=0)
-    zeros = jnp.zeros((3, depth), jnp.float32)
-    tail = jnp.concatenate([zeros, summed[share_cols + 1 : share_cols + 4], zeros[:2], summed[:share_cols]], axis=0)
+    tail = jnp.concatenate([jnp.zeros((5, depth), jnp.float32), summed[9:12], summed[:8]], axis=0)
     each = per_pair + 16
     sent, stat = pick_rows(ids.T, chars, tail, stat)
     second = lax.all_to_all(sent.reshape(holders, each, depth), "prod", split_axis=0, concat_axis=0, tiled=True)
-    col_pieces = second[:, per_pair + 3 : per_pair + 6, :share_cols].transpose(0, 2, 1).reshape(cols, 3)
+    col_pieces = second[:: 128 // share_cols, per_pair + 5 : per_pair + 8, :].transpose(0, 2, 1).reshape(cols, 3)
     col_chars = second[:, per_pair + 8 :, :].reshape(cols, depth)
-    col_chars = jnp.concatenate([col_chars, jnp.pad(col_pieces, ((0, 0), (0, depth - 3)))], axis=1)
-    mean_rows = second[:, per_pair : per_pair + 8, :].astype(jnp.float32)
-    odd = lax.axis_index("prod") % 2 == 1
-    mean_rows = jnp.where(odd, mean_rows[:, :, per_pair:], mean_rows[:, :, :per_pair])
-    mean_rows = jnp.pad(mean_rows[:, :3], ((0, 0), (0, 5), (0, 0))).transpose(1, 0, 2).reshape(8, products)
+    col_chars = jnp.concatenate([col_chars, jnp.pad(col_pieces, ((0, 0), (1, depth - 4)))], axis=1)
+    mean_rows = own_lanes(second[:, per_pair : per_pair + 4, :].astype(jnp.float32))
+    mean_rows = jnp.pad(mean_rows, ((0, 0), (0, 4), (0, 0))).transpose(1, 0, 2).reshape(8, products)
     half = products // 2
     place = (order // half == core).astype(jnp.int32) * half + order % half
 

time: 118 us -> 117 us (level)
  other arithmetic: 17.4 us -> 10.9 us
  Pallas kernels: 34.7 us -> 38.8 us
  local copies, waits for them, and re-layouts: 3.4 us -> 5.66 us
    sort x1 -> x0, other arithmetic: 4.44 us -> none  [body(): lax.sort((firm_map, lax.iota(jnp.int32, products)), num_keys=1)]
    pallas_call x0 -> x1, Pallas kernels: none -> 3.64 us  [prepare(): pl.pallas_call(kernel, out_shape=[jax.ShapeDtypeStruct((rows, 2 * depth),...]
    unnamed x14 -> x18, local copies, waits for them, and re-layouts: 0.41 us -> 2.7 us
    concatenate x6 -> x2, other arithmetic: 2.12 us -> 0.16 us  [the longest x1 0.09 us: body(): jnp.concatenate([col_chars, jnp.pad(col_pieces, ((0, 0), (1, depth - 4)))...]
  transfers between devices with their start and end apart: 12 -> 12, of which waited for: 7 -> 7; matrix products, arithmetic and copies ran while one was open for 7% -> 7% of each run, Pallas kernels for 18% -> 19%
where the time goes in v8:
time: 117 us; the launch traced here: 116 us
  starting transfers between devices  39.9 us (34%)
  Pallas kernels  38.8 us (33%)
  waiting for transfers between devices  17.5 us (15%)
  other arithmetic  10.9 us (9%)
  local copies, waits for them, and re-layouts  5.66 us (5%)
  between operations  2.28 us (2%)
    ppermute x10, starting transfers between devices, swap(): return lax.ppermute(value, axis, [(i, i ^ mask) for i in range(size)])  19.3 us
    ppermute x10, waiting for transfers between devices, swap(): return lax.ppermute(value, axis, [(i, i ^ mask) for i in range(size)])  17.5 us
    all_to_all x1, starting transfers between devices, body(): lax.all_to_all(message.reshape(holders, 16, depth), 'prod', split_axis=0,...  11.3 us
    pallas_call x1, Pallas kernels, stats(): pl.pallas_call(kernel, grid=(consumers // block,), in_specs=[pl.BlockSpec...  10.6 us
    all_to_all x1, starting transfers between devices, body(): lax.all_to_all(sent.reshape(holders, each, depth), 'prod', split_axis=0,...  9.27 us
    pallas_call x1, Pallas kernels, first_panel(): pl.pallas_call(kernel, grid=(consumers // block,), in_specs=[pl.BlockSpec...  7.16 us
    pallas_call x1, Pallas kernels, share_sums(): pl.pallas_call(kernel, grid=(consumers // block,), in_specs=[pl.BlockSpec...  7.01 us
    pallas_call x1, Pallas kernels, panel(): pl.pallas_call(kernel, grid=(1,), in_specs=[pl.BlockSpec((rows, depth), l...  4.69 us
  transfers between devices with their start and end apart: 12, of which 7 were waited for; matrix products, arithmetic and copies ran while one was open for 7% of the time, Pallas kernels for 19%

profile of v8, /device:TPU:1, one launch (start us, length us, event | category | flops | bytes accessed | tf_op | source)
XLA Modules:
  0.0 116.4 jit_solution(6746223742340126498)
XLA Ops:
  0.6 0.7 convert_bitcast_fusion.panel_ref
  1.3 1.0 copy-done
  2.4 0.7 copy-done.1
  3.1 0.7 copy-done.3
  3.8 3.6 %prepare.1 = (bf16[2048,256]{1,0:T(8,128)(2,1)S(1)}, bf16[512,128]{1,0:T(8,128)(2,1)}, s32[1,2048]{1,0:T(1,128)S(1)}) custom-call(bf16[2048,128]{1,0:T(8,128)(2,1)S(1)} %copy-done, f32[16,128]{1,0:T(8,128)S(1)} %bitcast.34, s32[1,2048]{1,0:T(1,128)S(1)} %bitcast.33, f32[2,128]{1,0:T(2,128)S(1)} %convert_bitcast_fusion.panel_ref), custom_call_target="tpu_custom_call" | custom-call | tf_op jit(solution)/shard_map/prepare/pallas_call | solution.py:89
  7.4 11.3 %all-to-all-start = ((bf16[32,16,128]{2,1,0:T(8,128)(2,1)}), bf16[32,16,128]{2,1,0:T(8,128)(2,1)S(1)}, u32[]{:S(2)}, u32[]{:S(2)}) async-start(bf16[32,16,128]{2,1,0:T(8,128)(2,1)} %bitcast.5), calls=%async_computation | async-start | bytes 262144 | tf_op jit(solution)/shard_map/all_to_all | solution.py:383
  18.8 0.1 fusion.13.order_ref
  18.8 1.3 %fusion.17 = (s32[1]{0:T(128)}, s32[1]{0:T(128)}) fusion(s32[256]{0:T(256)} %param.15), kind=kLoop, calls=%fused_computation.66 | loop fusion | bytes 16 | tf_op jit(solution)/shard_map/slice | solution.py:416
  20.9 10.6 %stats.1.stat_ref = f32[2,4096]{1,0:T(2,128)S(1)} custom-call(bf16[2048,256]{1,0:T(8,128)(2,1)S(1)} %get-tuple-element.62.chars_ref, bf16[4096,128]{1,0:T(8,128)(2,1)} %tastes_ref.5, bf16[512,128]{1,0:T(8,128)(2,1)} %get-tuple-element.63.gate_ref), custom_call_target="tpu_custom_call" | custom-call | tf_op jit(solution)/shard_map/stats/pallas_call | solution.py:132
  31.5 0.0 copy-start.6
  31.6 0.1 copy.23
  31.7 0.1 copy.24
  31.9 0.1 pad_maximum_fusion.7.tail_ref
  31.9 3.3 %pick_rows.1 = (bf16[2560,128]{1,0:T(8,128)(2,1)}, f32[2,4096]{1,0:T(2,128)S(1)}) custom-call(s32[64,32]{1,0:T(8,128)S(1)} %add_bitcast_fusion.ids_ref, bf16[2048,256]{1,0:T(8,128)(2,1)S(1)} %get-tuple-element.62.chars_ref, f32[16,128]{1,0:T(8,128)S(1)} %pad_maximum_fusion.7.tail_ref, f32[2,4096]{1,0:T(2,128)S(1)} %stats.1.stat_ref), custom_call_target="tpu_custom_call" | custom-call | tf_op jit(solution)/shard_map/pick_rows/pallas_call | solution.py:170
  35.2 9.3 %all-to-all-start.1 = ((bf16[32,80,128]{2,1,0:T(8,128)(2,1)}), bf16[32,80,128]{2,1,0:T(8,128)(2,1)S(1)}, u32[]{:S(2)}, u32[]{:S(2)}) async-start(bf16[32,80,128]{2,1,0:T(8,128)(2,1)} %bitcast.10), calls=%async_computation.1 | async-start | bytes 1310720 | tf_op jit(solution)/shard_map/all_to_all | solution.py:398
  44.5 0.0 copy-start.4
  44.5 25.9 %conditional.2 = (f32[2,4096]{1,0:T(2,128)S(1)}, f32[1,4096]{1,0:T(1,128)}, f32[1,4096]{1,0:T(1,128)}) conditional(s32[]{:T(128)} %bitcast.4, f32[2,4096]{1,0:T(2,128)S(1)} %get-tuple-element.64, f32[2,4096]{1,0:T(2,128)S(1)} %get-tuple-element.64), branch_computations={%region_1.2_spmd, %region_2.3_spmd} | conditional | flops 163840 | bytes 1474784 | solution.py:416
  44.5 1.3 %collective-permute-start.2 = (f32[2,4096]{1,0:T(2,128)S(1)}, f32[2,4096]{1,0:T(2,128)S(1)}, u32[]{:S(2)}, u32[]{:S(2)}) collective-permute-start(f32[2,4096]{1,0:T(2,128)S(1)} %param.1), channel_id=1, source_target_pairs={{0,1},{1,0},{2,3},{3,2},{4,5},{5,4},{6,7},{7,6},{8,9},{9,8},{10,11... | collective-permute-start | bytes 98312 | tf_op jit(solution)/shard_map/cond/branch_1_fun/ppermute | solution.py:351
  45.8 6.9 %collective-permute-done.2 = f32[2,4096]{1,0:T(2,128)S(1)} collective-permute-done((f32[2,4096]{1,0:T(2,128)S(1)}, f32[2,4096]{1,0:T(2,128)S(1)}, u32[]{:S(2)}, u32[]{:S(2)}) %collective-permute-start.2) | collective-permute-done | bytes 32800 | tf_op jit(solution)/shard_map/cond/branch_1_fun/ppermute | solution.py:351
  52.7 0.1 fusion.4
  52.9 1.9 %collective-permute-start.3 = (f32[2,4096]{1,0:T(2,128)S(1)}, f32[2,4096]{1,0:T(2,128)S(1)}, u32[]{:S(2)}, u32[]{:S(2)}) collective-permute-start(f32[2,4096]{1,0:T(2,128)S(1)} %pad_maximum_fusion), channel_id=1, source_target_pairs={{0,3},{1,2},{2,1},{3,0},{4,7},{5,6},{6,5},{7,4},{8,11},{9,10},{10,... | collective-permute-start | bytes 98312 | tf_op jit(solution)/shard_map/cond/branch_1_fun/ppermute | solution.py:351
  54.7 2.5 %collective-permute-done.3 = f32[2,4096]{1,0:T(2,128)S(1)} collective-permute-done((f32[2,4096]{1,0:T(2,128)S(1)}, f32[2,4096]{1,0:T(2,128)S(1)}, u32[]{:S(2)}, u32[]{:S(2)}) %collective-permute-start.3) | collective-permute-done | bytes 32800 | tf_op jit(solution)/shard_map/cond/branch_1_fun/ppermute | solution.py:351
  57.2 0.1 fusion.3
  57.3 1.3 %collective-permute-start.4 = (f32[2,4096]{1,0:T(2,128)S(1)}, f32[2,4096]{1,0:T(2,128)S(1)}, u32[]{:S(2)}, u32[]{:S(2)}) collective-permute-start(f32[2,4096]{1,0:T(2,128)S(1)} %pad_maximum_fusion.1), channel_id=1, source_target_pairs={{0,4},{1,5},{2,6},{3,7},{4,0},{5,1},{6,2},{7,3},{8,12},{9,13},{10,... | collective-permute-start | bytes 98312 | tf_op jit(solution)/shard_map/cond/branch_1_fun/ppermute | solution.py:351
  58.6 1.6 %collective-permute-done.4 = f32[2,4096]{1,0:T(2,128)S(1)} collective-permute-done((f32[2,4096]{1,0:T(2,128)S(1)}, f32[2,4096]{1,0:T(2,128)S(1)}, u32[]{:S(2)}, u32[]{:S(2)}) %collective-permute-start.4) | collective-permute-done | bytes 32800 | tf_op jit(solution)/shard_map/cond/branch_1_fun/ppermute | solution.py:351
  60.2 0.1 fusion.2
  60.3 2.5 %collective-permute-start.5 = (f32[2,4096]{1,0:T(2,128)S(1)}, f32[2,4096]{1,0:T(2,128)S(1)}, u32[]{:S(2)}, u32[]{:S(2)}) collective-permute-start(f32[2,4096]{1,0:T(2,128)S(1)} %pad_maximum_fusion.2), channel_id=1, source_target_pairs={{0,12},{1,13},{2,14},{3,15},{4,8},{5,9},{6,10},{7,11},{8,4},{9,5},... | collective-permute-start | bytes 98312 | tf_op jit(solution)/shard_map/cond/branch_1_fun/ppermute | solution.py:351
  62.7 1.6 %collective-permute-done.5 = f32[2,4096]{1,0:T(2,128)S(1)} collective-permute-done((f32[2,4096]{1,0:T(2,128)S(1)}, f32[2,4096]{1,0:T(2,128)S(1)}, u32[]{:S(2)}, u32[]{:S(2)}) %collective-permute-start.5) | collective-permute-done | bytes 32800 | tf_op jit(solution)/shard_map/cond/branch_1_fun/ppermute | solution.py:351
  64.3 0.1 fusion.1
  64.4 2.8 %collective-permute-start.6 = (f32[2,4096]{1,0:T(2,128)S(1)}, f32[2,4096]{1,0:T(2,128)S(1)}, u32[]{:S(2)}, u32[]{:S(2)}) collective-permute-start(f32[2,4096]{1,0:T(2,128)S(1)} %pad_maximum_fusion.3), channel_id=1, source_target_pairs={{0,16},{1,17},{2,18},{3,19},{4,20},{5,21},{6,22},{7,23},{8,24},{9,... | collective-permute-start | bytes 98312 | tf_op jit(solution)/shard_map/cond/branch_1_fun/ppermute | solution.py:351
  67.2 1.6 %collective-permute-done.6 = f32[2,4096]{1,0:T(2,128)S(1)} collective-permute-done((f32[2,4096]{1,0:T(2,128)S(1)}, f32[2,4096]{1,0:T(2,128)S(1)}, u32[]{:S(2)}, u32[]{:S(2)}) %collective-permute-start.6) | collective-permute-done | bytes 32800 | tf_op jit(solution)/shard_map/cond/branch_1_fun/ppermute | solution.py:351
  68.8 0.7 fusion
  69.4 0.8 pad_maximum_fusion.4
  70.4 0.8 broadcast_maximum_fusion
  71.3 0.1 copy.22
  71.4 0.1 slice_select_fusion
  71.6 0.1 reshape.70.beside_ref
  71.7 0.1 fusion.12.cols_ref
  71.8 2.4 %place_rows.1.chars_ref = bf16[2048,256]{1,0:T(8,128)(2,1)S(1)} custom-call(s32[1,2048]{1,0:T(1,128)S(1)} %fusion.13.order_ref, bf16[2560,128]{1,0:T(8,128)(2,1)S(1)} %bitcast.32, f32[8,2048]{1,0:T(8,128)S(1)} %reshape.70.beside_ref, f32[2,4096]{1,0:T(2,128)S(1)} %get-tuple-element.69.gate_ref), custom_call_target="tpu_custom_call" | custom-call | tf_op jit(solution)/shard_map/place_rows/pallas_call | solution.py:202
  74.3 7.2 %first_panel.1 = (f32[1032,256]{1,0:T(8,128)S(1)}, f32[1024,128]{1,0:T(8,128)S(1)}, bf16[256,4096]{1,0:T(8,128)(2,1)S(1)}) custom-call(bf16[2048,256]{1,0:T(8,128)(2,1)S(1)} %place_rows.1.chars_ref, bf16[4096,128]{1,0:T(8,128)(2,1)S(1)} %copy-done.4, f32[3,4096]{1,0:T(4,128)S(1)} %pad_maximum_fusion.6.rows_ref, bf16[256,256]{1,0:T(8,128)(2,1)S(1)} %fusion.12.cols_ref), custom_call_target="tpu_custom_call" | custom-call | flops 4294967296 | bytes 2097152 | tf_op jit(solution)/shard_map/first_panel/pallas_call | solution.py:249
  81.4 6.8 %collective-permute-start.7 = (f32[1032,256]{1,0:T(8,128)S(1)}, f32[1032,256]{1,0:T(8,128)S(1)}, u32[]{:S(2)}, u32[]{:S(2)}) collective-permute-start(f32[1032,256]{1,0:T(8,128)S(1)} %get-tuple-element.71.gate_ref), channel_id=1, source_target_pairs={{0,32},{32,0},{64,96},{96,64},{1,33},{33,1},{65,97},{97,65},{2,34}... | collective-permute-start | bytes 3170312 | tf_op jit(solution)/shard_map/ppermute | solution.py:351
  88.2 4.7 %panel.1 = (f32[1024,256]{1,0:T(8,128)S(1)}, f32[1024,128]{1,0:T(8,128)S(1)}) custom-call(bf16[2048,256]{1,0:T(8,128)(2,1)S(1)} %place_rows.1.chars_ref, bf16[4096,128]{1,0:T(8,128)(2,1)S(1)} %copy-done.4, f32[3,4096]{1,0:T(4,128)S(1)} %pad_maximum_fusion.6.rows_ref, bf16[256,4096]{1,0:T(8,128)(2,1)S(1)} %get-tuple-element.70.weight_ref, ...), custom_call_target="tpu_custom_call" | custom-call | flops 4294967296 | bytes 2097152 | tf_op jit(solution)/shard_map/panel/pallas_call | solution.py:291
  92.9 0.0 copy-start.2
  93.0 1.0 fusion.9
  93.9 0.4 collective-permute-start.8
  95.1 0.0 copy-start.7
  95.1 13.9 %conditional.3 = (f32[4352]{0:T(1024)}, f32[4352]{0:T(1024)}, f32[256]{0:T(256)S(1)}) conditional(s32[]{:T(128)} %bitcast, () %tuple.30, (bf16[2048,256]{1,0:T(8,128)(2,1)S(1)}, bf16[4096,128]{1,0:T(8,128)(2,1)S(1)}, f32[3,4096]{1,0:T(4,128)S(1)}, f32[1,256]{1,0:T(1,128)S(1)}, pred[]{:T(512)}, /*index=5*/f32[1024,128]{1,0:T(8,128)S(1)}, ...), branch_computations={%region_4.5_spmd, %region_5.9_spmd} | conditional | flops 552704 | bytes 2358389 | solution.py:444
  95.1 0.2 reduce_sum.43
  95.3 0.2 reduce_sum.44
  95.5 7.0 %share_sums.1 = f32[2048,128]{1,0:T(8,128)S(1)} custom-call(bf16[2048,256]{1,0:T(8,128)(2,1)S(1)} %get-tuple-element.33.chars_ref, bf16[4096,128]{1,0:T(8,128)(2,1)S(1)} %get-tuple-element.34.tastes_ref, f32[3,4096]{1,0:T(4,128)S(1)} %get-tuple-element.35.rows_ref, f32[1,256]{1,0:T(1,128)S(1)} %get-tuple-element.36.gate_ref), custom_call_target="tpu_custom_call" | custom-call | tf_op jit(solution)/shard_map/cond/branch_1_fun/share_sums/pallas_call | solution.py:333
  102.5 0.3 reduce_sum.42
  102.9 0.4 collective-permute-start
  103.3 0.9 collective-permute-done
  104.2 0.6 fusion.5
  104.8 1.0 collective-permute-start.1
  105.8 2.5 %collective-permute-done.1 = f32[4352]{0:T(1024)} collective-permute-done((f32[4352]{0:T(1024)}, f32[4352]{0:T(1024)}, u32[]{:S(2)}, u32[]{:S(2)}) %collective-permute-start.1) | collective-permute-done | bytes 17440 | tf_op jit(solution)/shard_map/cond/branch_1_fun/ppermute | solution.py:351
  108.3 0.7 slice.162
  109.0 1.6 %select_subtract_fusion = f32[1024,256]{1,0:T(8,128)S(1)} fusion(f16[1024,256]{1,0:T(8,128)(2,1)} %collective-permute-done.8, f16[1024,256]{1,0:T(8,128)(2,1)} %get-tuple-element.78, f32[256]{0:T(256)S(1)} %get-tuple-element.107, s32[256]{0:T(256)S(1)} %copy-done.7, f32[256]{0:T(256)S(1)} %get-tuple-element.106, f32[256]{0:T(256)S(1)} %bitcast.46, ...), kind=kLoop, calls=%fused_computation.27 | loop fusion | flops 2097152 | bytes 2105344 | tf_op jit(solution)/shard_map/sub | solution.py:462
  110.6 1.0 fusion.7
  111.6 0.9 collective-permute-start.9
  112.6 0.7 add_multiply_fusion
  113.3 0.6 slice_bitcast_fusion.1
  113.9 0.9 multiply_reduce_fusion
  114.9 1.6 %maximum_select_fusion = f32[2048,256]{1,0:T(8,128)} fusion(f32[1024,256]{1,0:T(8,128)S(1)} %collective-permute-done.9, f32[1024,256]{1,0:T(8,128)S(1)} %bitcast.36, pred[]{:T(512)} %eq.35), kind=kLoop, calls=%fused_computation.24 | loop fusion | flops 1572864 | bytes 4194305 | tf_op jit(solution)/shard_map/jit(_where)/select_n | solution.py:470
  (36 shorter events, 0.4 us)
Async XLA Ops:
  1.3 1.0 copy-start
  2.4 0.7 copy-start.1
  3.1 0.7 copy-start.3
  7.4 24.1 %all-to-all-start = ((bf16[32,16,128]{2,1,0:T(8,128)(2,1)}), bf16[32,16,128]{2,1,0:T(8,128)(2,1)S(1)}, u32[]{:S(2)}, u32[]{:S(2)}) async-start(bf16[32,16,128]{2,1,0:T(8,128)(2,1)} %bitcast.5), calls=%async_computation | async-start | bytes 262144 | tf_op jit(solution)/shard_map/all_to_all | solution.py:383
  31.5 39.7 %copy-start.6 = (f32[4096]{0:T(1024)S(1)}, f32[4096]{0:T(1024)}, u32[]{:S(2)}) copy-start(f32[4096]{0:T(1024)} %param.12) | copy-start | bytes 49156
  35.2 36.0 %all-to-all-start.1 = ((bf16[32,80,128]{2,1,0:T(8,128)(2,1)}), bf16[32,80,128]{2,1,0:T(8,128)(2,1)S(1)}, u32[]{:S(2)}, u32[]{:S(2)}) async-start(bf16[32,80,128]{2,1,0:T(8,128)(2,1)} %bitcast.10), calls=%async_computation.1 | async-start | bytes 1310720 | tf_op jit(solution)/shard_map/all_to_all | solution.py:398
  44.5 29.8 %copy-start.4 = (bf16[4096,128]{1,0:T(8,128)(2,1)S(1)}, bf16[4096,128]{1,0:T(8,128)(2,1)}, u32[]{:S(2)}) copy-start(bf16[4096,128]{1,0:T(8,128)(2,1)} %tastes_ref.5) | copy-start | bytes 3145732
  44.5 8.2 %collective-permute-start.2 = (f32[2,4096]{1,0:T(2,128)S(1)}, f32[2,4096]{1,0:T(2,128)S(1)}, u32[]{:S(2)}, u32[]{:S(2)}) collective-permute-start(f32[2,4096]{1,0:T(2,128)S(1)} %param.1), channel_id=1, source_target_pairs={{0,1},{1,0},{2,3},{3,2},{4,5},{5,4},{6,7},{7,6},{8,9},{9,8},{10,11... | collective-permute-start | bytes 98312 | tf_op jit(solution)/shard_map/cond/branch_1_fun/ppermute | solution.py:351
  52.9 4.3 %collective-permute-start.3 = (f32[2,4096]{1,0:T(2,128)S(1)}, f32[2,4096]{1,0:T(2,128)S(1)}, u32[]{:S(2)}, u32[]{:S(2)}) collective-permute-start(f32[2,4096]{1,0:T(2,128)S(1)} %pad_maximum_fusion), channel_id=1, source_target_pairs={{0,3},{1,2},{2,1},{3,0},{4,7},{5,6},{6,5},{7,4},{8,11},{9,10},{10,... | collective-permute-start | bytes 98312 | tf_op jit(solution)/shard_map/cond/branch_1_fun/ppermute | solution.py:351
  57.3 2.8 %collective-permute-start.4 = (f32[2,4096]{1,0:T(2,128)S(1)}, f32[2,4096]{1,0:T(2,128)S(1)}, u32[]{:S(2)}, u32[]{:S(2)}) collective-permute-start(f32[2,4096]{1,0:T(2,128)S(1)} %pad_maximum_fusion.1), channel_id=1, source_target_pairs={{0,4},{1,5},{2,6},{3,7},{4,0},{5,1},{6,2},{7,3},{8,12},{9,13},{10,... | collective-permute-start | bytes 98312 | tf_op jit(solution)/shard_map/cond/branch_1_fun/ppermute | solution.py:351
  60.3 4.1 %collective-permute-start.5 = (f32[2,4096]{1,0:T(2,128)S(1)}, f32[2,4096]{1,0:T(2,128)S(1)}, u32[]{:S(2)}, u32[]{:S(2)}) collective-permute-start(f32[2,4096]{1,0:T(2,128)S(1)} %pad_maximum_fusion.2), channel_id=1, source_target_pairs={{0,12},{1,13},{2,14},{3,15},{4,8},{5,9},{6,10},{7,11},{8,4},{9,5},... | collective-permute-start | bytes 98312 | tf_op jit(solution)/shard_map/cond/branch_1_fun/ppermute | solution.py:351
  64.4 4.3 %collective-permute-start.6 = (f32[2,4096]{1,0:T(2,128)S(1)}, f32[2,4096]{1,0:T(2,128)S(1)}, u32[]{:S(2)}, u32[]{:S(2)}) collective-permute-start(f32[2,4096]{1,0:T(2,128)S(1)} %pad_maximum_fusion.3), channel_id=1, source_target_pairs={{0,16},{1,17},{2,18},{3,19},{4,20},{5,21},{6,22},{7,23},{8,24},{9,... | collective-permute-start | bytes 98312 | tf_op jit(solution)/shard_map/cond/branch_1_fun/ppermute | solution.py:351
  81.4 11.5 %collective-permute-start.7 = (f32[1032,256]{1,0:T(8,128)S(1)}, f32[1032,256]{1,0:T(8,128)S(1)}, u32[]{:S(2)}, u32[]{:S(2)}) collective-permute-start(f32[1032,256]{1,0:T(8,128)S(1)} %get-tuple-element.71.gate_ref), channel_id=1, source_target_pairs={{0,32},{32,0},{64,96},{96,64},{1,33},{33,1},{65,97},{97,65},{2,34}... | collective-permute-start | bytes 3170312 | tf_op jit(solution)/shard_map/ppermute | solution.py:351
  92.9 2.1 %copy-start.2 = (s32[2048]{0:T(1024)S(1)}, s32[2048]{0:T(1024)}, u32[]{:S(2)}) copy-start(s32[2048]{0:T(1024)} %param.16) | copy-start | bytes 24580
  93.9 15.1 %collective-permute-start.8 = (f16[1024,256]{1,0:T(8,128)(2,1)}, f16[1024,256]{1,0:T(8,128)(2,1)}, u32[]{:S(2)}, u32[]{:S(2)}) collective-permute-start(f16[1024,256]{1,0:T(8,128)(2,1)} %get-tuple-element.78), channel_id=1, source_target_pairs={{0,64},{32,96},{64,0},{96,32},{1,65},{33,97},{65,1},{97,33},{2,66}... | collective-permute-start | bytes 1572872 | tf_op jit(solution)/shard_map/ppermute | solution.py:351
  95.1 14.0 %copy-start.7 = (s32[256]{0:T(256)S(1)}, s32[256]{0:T(256)}, u32[]{:S(2)}) copy-start(s32[256]{0:T(256)} %param.15) | copy-start | bytes 3076
  102.9 1.3 %collective-permute-start = (f32[4352]{0:T(1024)S(1)}, f32[4352]{0:T(1024)S(1)}, u32[]{:S(2)}, u32[]{:S(2)}) collective-permute-start(f32[4352]{0:T(1024)S(1)} %pad_maximum_fusion.5), channel_id=1, source_target_pairs={{0,32},{32,0},{64,96},{96,64},{1,33},{33,1},{65,97},{97,65},{2,34}... | collective-permute-start | bytes 52232 | tf_op jit(solution)/shard_map/cond/branch_1_fun/ppermute | solution.py:351
  104.8 3.5 %collective-permute-start.1 = (f32[4352]{0:T(1024)}, f32[4352]{0:T(1024)}, u32[]{:S(2)}, u32[]{:S(2)}) collective-permute-start(f32[4352]{0:T(1024)} %fusion.5), channel_id=1, source_target_pairs={{0,64},{32,96},{64,0},{96,32},{1,65},{33,97},{65,1},{97,33},{2,66}... | collective-permute-start | bytes 52232 | tf_op jit(solution)/shard_map/cond/branch_1_fun/ppermute | solution.py:351
  109.0 1.6 %copy-start.5 = (f32[16,128,128]{2,1,0:T(8,128)S(1)}, f32[16,128,128]{2,1,0:T(8,128)}, u32[]{:S(2)}) copy-start(f32[16,128,128]{2,1,0:T(8,128)} %param.17) | copy-start | bytes 3145732
  111.6 3.2 %collective-permute-start.9 = (f32[1024,256]{1,0:T(8,128)S(1)}, f32[1024,256]{1,0:T(8,128)S(1)}, u32[]{:S(2)}, u32[]{:S(2)}) collective-permute-start(f32[1024,256]{1,0:T(8,128)S(1)} %bitcast.35), channel_id=1, source_target_pairs={{0,32},{32,0},{64,96},{96,64},{1,33},{33,1},{65,97},{97,65},{2,34}... | collective-permute-start | bytes 3145736 | tf_op jit(solution)/shard_map/ppermute | solution.py:351

commit v9 on v8

--- a/solution.py
+++ b/solution.py
@@ -86,14 +86,20 @@
                 mine = part[place * share_cols : (place + 1) * share_cols, :depth]
                 message_ref[q * 16 : (q + 1) * 16, :] = jnp.concatenate([mine, extra], axis=0).astype(jnp.bfloat16)
 
-    return pl.pallas_call(
-        kernel,
+    def whole(shape):
+        return pl.BlockSpec(shape, lambda i: (0, 0))
+
+    return pl.pallas_call(
+        kernel,
+        grid=(1,),
+        in_specs=[whole(value.shape) for value in (characteristics, means, firm_row, panel_rows)],
+        out_specs=[whole((rows, 2 * depth)), whole((16 * holders, depth)), whole((1, rows))],
         out_shape=[
             jax.ShapeDtypeStruct((rows, 2 * depth), jnp.bfloat16),
             jax.ShapeDtypeStruct((16 * holders, depth), jnp.bfloat16),
             jax.ShapeDtypeStruct((1, rows), jnp.int32),
         ],
-        compiler_params=pltpu.CompilerParams(vmem_limit_bytes=VMEM_BYTES),
+        compiler_params=pltpu.CompilerParams(vmem_limit_bytes=60 * 1024 * 1024),
         name="prepare",
     )(characteristics, means, firm_row, panel_rows)
 
@@ -104,30 +110,24 @@
     return jnp.concatenate([tastes, ones.astype(tastes.dtype)], axis=1)
 
 
-def stats(chars, tastes, gate):
+def stats(chars, tastes):
     rows, depth = chars.shape
     consumers = tastes.shape[0]
-    block, sub, chunk = 2048, 256, 256
-    count = block // sub
-
-    def kernel(chars_ref, tastes_ref, gate_ref, stat_ref, util_ref):
-        people = [beside_ones(tastes_ref[k * sub : (k + 1) * sub, :]) for k in range(count)]
-        before = None
-        for k in range(count + 1):
-            peak = jnp.full((8, sub), -jnp.inf, jnp.float32)
-            total = jnp.zeros((8, sub), jnp.float32)
-            for start in range(0, rows, chunk):
-                if k < count:
-                    util = dot_nt(chars_ref[start : start + chunk, :], people[k])
-                    util_ref[k % 2, start : start + chunk, :] = util
-                    peak = jnp.maximum(peak, jnp.max(util.reshape(chunk // 8, 8, sub), axis=0))
-                if k > 0:
-                    expo = jnp.exp(util_ref[(k - 1) % 2, start : start + chunk, :] - before)
-                    total = total + jnp.sum(expo.reshape(chunk // 8, 8, sub), axis=0)
-            if k > 0:
-                stat_ref[0:1, (k - 1) * sub : k * sub] = before
-                stat_ref[1:2, (k - 1) * sub : k * sub] = jnp.sum(total, axis=0, keepdims=True)
-            before = jnp.max(peak, axis=0, keepdims=True)
+    block, chunk = 2048, 256
+
+    def kernel(chars_ref, tastes_ref, stat_ref):
+        people = beside_ones(tastes_ref[...])
+        peak = jnp.full((1, block), -jnp.inf, jnp.float32)
+        total = jnp.zeros((8, block), jnp.float32)
+        for start in range(0, rows, chunk):
+            util = dot_nt(chars_ref[start : start + chunk, :], people)
+            highest = jnp.max(util.reshape(chunk // 8, 8, block), axis=0)
+            joint = jnp.maximum(peak, jnp.max(highest, axis=0, keepdims=True))
+            expo = jnp.exp(util - joint)
+            total = total * jnp.exp(peak - joint) + jnp.sum(expo.reshape(chunk // 8, 8, block), axis=0)
+            peak = joint
+        stat_ref[0:1, :] = peak
+        stat_ref[1:2, :] = jnp.sum(total, axis=0, keepdims=True)
 
     return pl.pallas_call(
         kernel,
@@ -135,14 +135,12 @@
         in_specs=[
             pl.BlockSpec((rows, depth), lambda i: (0, 0)),
             pl.BlockSpec((block, tastes.shape[1]), lambda i: (i, 0)),
-            pl.BlockSpec(memory_space=pl.ANY),
         ],
         out_specs=pl.BlockSpec((2, block), lambda i: (0, i)),
         out_shape=jax.ShapeDtypeStruct((2, consumers), jnp.float32),
-        scratch_shapes=[pltpu.VMEM((2, rows, sub), jnp.float32)],
         compiler_params=pltpu.CompilerParams(vmem_limit_bytes=VMEM_BYTES),
         name="stats",
-    )(chars, tastes, gate)
+    )(chars, tastes)
 
 
 def pick_rows(ids_t, chars, tail, stat):
@@ -382,7 +380,7 @@
     )
     first = lax.all_to_all(message.reshape(holders, 16, depth), "prod", split_axis=0, concat_axis=0, tiled=True)
 
-    stat = stats(chars, tastes, message)
+    stat = stats(chars, tastes)
 
     odd = lax.axis_index("prod") % 2 == 1
 
@@ -413,7 +411,8 @@
         return stat
 
     masks = butterfly_masks(holders)
-    stat = lax.cond(panel_cols[0] >= 0, lambda value: join(value, masks), lambda value: value, stat)
+    taken = panel_cols[0] >= 0
+    stat = lax.cond(taken, lambda value: join(value, masks), lambda value: value, stat)
     firm_chars = place_rows(
         place.reshape(1, products), second.reshape(holders * each, depth), mean_rows, holders, stat
     )
@@ -442,7 +441,7 @@
         return sums, swap(sums, "cons", 2)
 
     sums, other_sums = lax.cond(
-        panel_cols[1] >= 0,
+        taken,
         own_and_exchange,
         lambda gate, others: (jnp.zeros(products + others.shape[0], jnp.float32),) * 2,
         gate,

time: 117 us -> 116 us (level)
  local copies, waits for them, and re-layouts: 5.66 us -> 3.07 us
  other arithmetic: 10.9 us -> 12.2 us
    unnamed x18 -> x12, local copies, waits for them, and re-layouts: 2.7 us -> 0.27 us
  transfers between devices with their start and end apart: 12 -> 12, of which waited for: 7 -> 7; matrix products, arithmetic and copies ran while one was open for 7% -> 8% of each run, Pallas kernels for 19% -> 19%
where the time goes in v9:
time: 116 us; the launch traced here: 115 us
  starting transfers between devices  39.8 us (34%)
  Pallas kernels  39.2 us (34%)
  waiting for transfers between devices  18.1 us (16%)
  other arithmetic  12.2 us (11%)
  local copies, waits for them, and re-layouts  3.07 us (3%)
  between operations  1.59 us (1%)
    ppermute x10, starting transfers between devices, swap(): return lax.ppermute(value, axis, [(i, i ^ mask) for i in range(size)])  19.2 us
    ppermute x10, waiting for transfers between devices, swap(): return lax.ppermute(value, axis, [(i, i ^ mask) for i in range(size)])  18.1 us
    all_to_all x1, starting transfers between devices, body(): lax.all_to_all(message.reshape(holders, 16, depth), 'prod', split_axis=0,...  11.3 us
    pallas_call x1, Pallas kernels, stats(): pl.pallas_call(kernel, grid=(consumers // block,), in_specs=[pl.BlockSpec...  9.78 us
    all_to_all x1, starting transfers between devices, body(): lax.all_to_all(sent.reshape(holders, each, depth), 'prod', split_axis=0,...  9.26 us
    pallas_call x1, Pallas kernels, first_panel(): pl.pallas_call(kernel, grid=(consumers // block,), in_specs=[pl.BlockSpec...  7.24 us
    pallas_call x1, Pallas kernels, share_sums(): pl.pallas_call(kernel, grid=(consumers // block,), in_specs=[pl.BlockSpec...  7.1 us
    pallas_call x1, Pallas kernels, prepare(): pl.pallas_call(kernel, grid=(1,), in_specs=[whole(value.shape) for value...  4.69 us
  transfers between devices with their start and end apart: 12, of which 7 were waited for; matrix products, arithmetic and copies ran while one was open for 8% of the time, Pallas kernels for 19%

profile of v9, /device:TPU:1, one launch (start us, length us, event | category | flops | bytes accessed | tf_op | source)
XLA Modules:
  0.0 115.3 jit_solution(17048382669067353821)
XLA Ops:
  0.6 1.2 %convert_bitcast_fusion.panel_ref = f32[2,128]{1,0:T(2,128)} fusion(s32[256]{0:T(256)} %param.15, s32[]{:T(128)S(6)} %mul.134), kind=kLoop, calls=%fused_computation.62 | loop fusion | flops 512 | bytes 2052 | tf_op jit(solution)/shard_map/reshape | solution.py:378
  1.9 4.7 %prepare.1 = (bf16[2048,256]{1,0:T(8,128)(2,1)S(1)}, bf16[512,128]{1,0:T(8,128)(2,1)}, s32[1,2048]{1,0:T(1,128)}) custom-call(bf16[2048,128]{1,0:T(8,128)(2,1)} %chars_ref.1, f32[16,128]{1,0:T(8,128)} %bitcast.43, s32[1,2048]{1,0:T(1,128)} %bitcast.39, f32[2,128]{1,0:T(2,128)} %convert_bitcast_fusion.panel_ref), custom_call_target="tpu_custom_call" | custom-call | tf_op jit(solution)/shard_map/prepare/pallas_call | solution.py:92
  6.6 11.3 %all-to-all-start = ((bf16[32,16,128]{2,1,0:T(8,128)(2,1)}), bf16[32,16,128]{2,1,0:T(8,128)(2,1)S(1)}, u32[]{:S(2)}, u32[]{:S(2)}) async-start(bf16[32,16,128]{2,1,0:T(8,128)(2,1)} %bitcast.38), calls=%async_computation | async-start | bytes 262144 | tf_op jit(solution)/shard_map/all_to_all | solution.py:381
  17.9 0.8 fusion.13.order_ref
  18.7 1.2 %slice.128 = s32[1]{0:T(128)} slice(s32[256]{0:T(256)} %param.15), slice={[0:1]} | slice | bytes 8 | tf_op jit(solution)/shard_map/slice | solution.py:414
  20.6 9.8 %stats.1.stat_ref = f32[2,4096]{1,0:T(2,128)S(1)} custom-call(bf16[2048,256]{1,0:T(8,128)(2,1)S(1)} %get-tuple-element.62.chars_ref, bf16[4096,128]{1,0:T(8,128)(2,1)} %tastes_ref.5), custom_call_target="tpu_custom_call" | custom-call | tf_op jit(solution)/shard_map/stats/pallas_call | solution.py:132
  30.4 0.0 copy-start.3
  30.4 0.0 all-to-all-done
  30.5 0.1 copy.23
  30.6 0.1 copy.24
  30.8 0.1 pad_maximum_fusion.7.tail_ref
  30.8 3.3 %pick_rows.1 = (bf16[2560,128]{1,0:T(8,128)(2,1)}, f32[2,4096]{1,0:T(2,128)S(1)}) custom-call(s32[64,32]{1,0:T(8,128)S(1)} %add_bitcast_fusion.ids_ref, bf16[2048,256]{1,0:T(8,128)(2,1)S(1)} %get-tuple-element.62.chars_ref, f32[16,128]{1,0:T(8,128)S(1)} %pad_maximum_fusion.7.tail_ref, f32[2,4096]{1,0:T(2,128)S(1)} %stats.1.stat_ref), custom_call_target="tpu_custom_call" | custom-call | tf_op jit(solution)/shard_map/pick_rows/pallas_call | solution.py:168
  34.1 9.3 %all-to-all-start.1 = ((bf16[32,80,128]{2,1,0:T(8,128)(2,1)}), bf16[32,80,128]{2,1,0:T(8,128)(2,1)S(1)}, u32[]{:S(2)}, u32[]{:S(2)}) async-start(bf16[32,80,128]{2,1,0:T(8,128)(2,1)} %bitcast.9), calls=%async_computation.1 | async-start | bytes 1310720 | tf_op jit(solution)/shard_map/all_to_all | solution.py:396
  43.4 0.0 copy-start
  43.4 25.9 %conditional.2 = (f32[2,4096]{1,0:T(2,128)S(1)}, f32[1,4096]{1,0:T(1,128)}, f32[1,4096]{1,0:T(1,128)}) conditional(s32[]{:T(128)} %bitcast, f32[2,4096]{1,0:T(2,128)S(1)} %get-tuple-element.64, f32[2,4096]{1,0:T(2,128)S(1)} %get-tuple-element.64), branch_computations={%region_1.2_spmd, %region_2.3_spmd} | conditional | flops 163840 | bytes 1474784 | solution.py:415
  43.4 1.3 %collective-permute-start.2 = (f32[2,4096]{1,0:T(2,128)S(1)}, f32[2,4096]{1,0:T(2,128)S(1)}, u32[]{:S(2)}, u32[]{:S(2)}) collective-permute-start(f32[2,4096]{1,0:T(2,128)S(1)} %param.1), channel_id=1, source_target_pairs={{0,1},{1,0},{2,3},{3,2},{4,5},{5,4},{6,7},{7,6},{8,9},{9,8},{10,11... | collective-permute-start | bytes 98312 | tf_op jit(solution)/shard_map/cond/branch_1_fun/ppermute | solution.py:349
  44.7 6.9 %collective-permute-done.2 = f32[2,4096]{1,0:T(2,128)S(1)} collective-permute-done((f32[2,4096]{1,0:T(2,128)S(1)}, f32[2,4096]{1,0:T(2,128)S(1)}, u32[]{:S(2)}, u32[]{:S(2)}) %collective-permute-start.2) | collective-permute-done | bytes 32800 | tf_op jit(solution)/shard_map/cond/branch_1_fun/ppermute | solution.py:349
  51.6 0.1 fusion.4
  51.7 1.9 %collective-permute-start.3 = (f32[2,4096]{1,0:T(2,128)S(1)}, f32[2,4096]{1,0:T(2,128)S(1)}, u32[]{:S(2)}, u32[]{:S(2)}) collective-permute-start(f32[2,4096]{1,0:T(2,128)S(1)} %pad_maximum_fusion), channel_id=1, source_target_pairs={{0,3},{1,2},{2,1},{3,0},{4,7},{5,6},{6,5},{7,4},{8,11},{9,10},{10,... | collective-permute-start | bytes 98312 | tf_op jit(solution)/shard_map/cond/branch_1_fun/ppermute | solution.py:349
  53.6 2.5 %collective-permute-done.3 = f32[2,4096]{1,0:T(2,128)S(1)} collective-permute-done((f32[2,4096]{1,0:T(2,128)S(1)}, f32[2,4096]{1,0:T(2,128)S(1)}, u32[]{:S(2)}, u32[]{:S(2)}) %collective-permute-start.3) | collective-permute-done | bytes 32800 | tf_op jit(solution)/shard_map/cond/branch_1_fun/ppermute | solution.py:349
  56.1 0.1 fusion.3
  56.2 1.3 %collective-permute-start.4 = (f32[2,4096]{1,0:T(2,128)S(1)}, f32[2,4096]{1,0:T(2,128)S(1)}, u32[]{:S(2)}, u32[]{:S(2)}) collective-permute-start(f32[2,4096]{1,0:T(2,128)S(1)} %pad_maximum_fusion.1), channel_id=1, source_target_pairs={{0,4},{1,5},{2,6},{3,7},{4,0},{5,1},{6,2},{7,3},{8,12},{9,13},{10,... | collective-permute-start | bytes 98312 | tf_op jit(solution)/shard_map/cond/branch_1_fun/ppermute | solution.py:349
  57.5 1.6 %collective-permute-done.4 = f32[2,4096]{1,0:T(2,128)S(1)} collective-permute-done((f32[2,4096]{1,0:T(2,128)S(1)}, f32[2,4096]{1,0:T(2,128)S(1)}, u32[]{:S(2)}, u32[]{:S(2)}) %collective-permute-start.4) | collective-permute-done | bytes 32800 | tf_op jit(solution)/shard_map/cond/branch_1_fun/ppermute | solution.py:349
  59.0 0.1 fusion.2
  59.1 2.5 %collective-permute-start.5 = (f32[2,4096]{1,0:T(2,128)S(1)}, f32[2,4096]{1,0:T(2,128)S(1)}, u32[]{:S(2)}, u32[]{:S(2)}) collective-permute-start(f32[2,4096]{1,0:T(2,128)S(1)} %pad_maximum_fusion.2), channel_id=1, source_target_pairs={{0,12},{1,13},{2,14},{3,15},{4,8},{5,9},{6,10},{7,11},{8,4},{9,5},... | collective-permute-start | bytes 98312 | tf_op jit(solution)/shard_map/cond/branch_1_fun/ppermute | solution.py:349
  61.6 1.6 %collective-permute-done.5 = f32[2,4096]{1,0:T(2,128)S(1)} collective-permute-done((f32[2,4096]{1,0:T(2,128)S(1)}, f32[2,4096]{1,0:T(2,128)S(1)}, u32[]{:S(2)}, u32[]{:S(2)}) %collective-permute-start.5) | collective-permute-done | bytes 32800 | tf_op jit(solution)/shard_map/cond/branch_1_fun/ppermute | solution.py:349
  63.2 0.1 fusion.1
  63.3 2.8 %collective-permute-start.6 = (f32[2,4096]{1,0:T(2,128)S(1)}, f32[2,4096]{1,0:T(2,128)S(1)}, u32[]{:S(2)}, u32[]{:S(2)}) collective-permute-start(f32[2,4096]{1,0:T(2,128)S(1)} %pad_maximum_fusion.3), channel_id=1, source_target_pairs={{0,16},{1,17},{2,18},{3,19},{4,20},{5,21},{6,22},{7,23},{8,24},{9,... | collective-permute-start | bytes 98312 | tf_op jit(solution)/shard_map/cond/branch_1_fun/ppermute | solution.py:349
  66.1 1.6 %collective-permute-done.6 = f32[2,4096]{1,0:T(2,128)S(1)} collective-permute-done((f32[2,4096]{1,0:T(2,128)S(1)}, f32[2,4096]{1,0:T(2,128)S(1)}, u32[]{:S(2)}, u32[]{:S(2)}) %collective-permute-start.6) | collective-permute-done | bytes 32800 | tf_op jit(solution)/shard_map/cond/branch_1_fun/ppermute | solution.py:349
  67.6 0.7 fusion
  68.3 0.8 pad_maximum_fusion.4
  69.3 0.8 broadcast_maximum_fusion
  70.1 0.0 all-to-all-done.1
  70.2 0.1 copy.22
  70.3 0.1 slice_select_fusion
  70.5 0.1 reshape.66.beside_ref
  70.6 0.1 fusion.12.cols_ref
  70.7 2.5 %place_rows.1.chars_ref = bf16[2048,256]{1,0:T(8,128)(2,1)S(1)} custom-call(s32[1,2048]{1,0:T(1,128)S(1)} %fusion.13.order_ref, bf16[2560,128]{1,0:T(8,128)(2,1)S(1)} %bitcast.31, f32[8,2048]{1,0:T(8,128)S(1)} %reshape.66.beside_ref, f32[2,4096]{1,0:T(2,128)S(1)} %get-tuple-element.69.gate_ref), custom_call_target="tpu_custom_call" | custom-call | tf_op jit(solution)/shard_map/place_rows/pallas_call | solution.py:200
  73.2 7.2 %first_panel.1 = (f32[1032,256]{1,0:T(8,128)S(1)}, f32[1024,128]{1,0:T(8,128)S(1)}, bf16[256,4096]{1,0:T(8,128)(2,1)S(1)}) custom-call(bf16[2048,256]{1,0:T(8,128)(2,1)S(1)} %place_rows.1.chars_ref, bf16[4096,128]{1,0:T(8,128)(2,1)S(1)} %copy-done, f32[3,4096]{1,0:T(4,128)S(1)} %pad_maximum_fusion.6.rows_ref, bf16[256,256]{1,0:T(8,128)(2,1)S(1)} %fusion.12.cols_ref), custom_call_target="tpu_custom_call" | custom-call | flops 4294967296 | bytes 2097152 | tf_op jit(solution)/shard_map/first_panel/pallas_call | solution.py:247
  80.4 6.8 %collective-permute-start.7 = (f32[1032,256]{1,0:T(8,128)S(1)}, f32[1032,256]{1,0:T(8,128)S(1)}, u32[]{:S(2)}, u32[]{:S(2)}) collective-permute-start(f32[1032,256]{1,0:T(8,128)S(1)} %get-tuple-element.71.gate_ref), channel_id=1, source_target_pairs={{0,32},{32,0},{64,96},{96,64},{1,33},{33,1},{65,97},{97,65},{2,34}... | collective-permute-start | bytes 3170312 | tf_op jit(solution)/shard_map/ppermute | solution.py:349
  87.2 4.7 %panel.1 = (f32[1024,256]{1,0:T(8,128)S(1)}, f32[1024,128]{1,0:T(8,128)S(1)}) custom-call(bf16[2048,256]{1,0:T(8,128)(2,1)S(1)} %place_rows.1.chars_ref, bf16[4096,128]{1,0:T(8,128)(2,1)S(1)} %copy-done, f32[3,4096]{1,0:T(4,128)S(1)} %pad_maximum_fusion.6.rows_ref, bf16[256,4096]{1,0:T(8,128)(2,1)S(1)} %get-tuple-element.70.weight_ref, ...), custom_call_target="tpu_custom_call" | custom-call | flops 4294967296 | bytes 2097152 | tf_op jit(solution)/shard_map/panel/pallas_call | solution.py:289
  91.9 0.0 copy-start.2
  91.9 0.0 collective-permute-done.7
  92.0 1.0 fusion.9
  92.9 0.4 collective-permute-start.8
  93.3 14.6 %conditional.3 = (f32[4352]{0:T(1024)}, f32[4352]{0:T(1024)}, f32[256]{0:T(256)S(1)}) conditional(s32[]{:T(128)} %bitcast, () %tuple.30, (bf16[2048,256]{1,0:T(8,128)(2,1)S(1)}, bf16[4096,128]{1,0:T(8,128)(2,1)S(1)}, f32[3,4096]{1,0:T(4,128)S(1)}, f32[1,256]{1,0:T(1,128)S(1)}, pred[]{:T(512)}, /*index=5*/f32[1024,128]{1,0:T(8,128)S(1)}, ...), branch_computations={%region_4.5_spmd, %region_5.9_spmd} | conditional | flops 552704 | bytes 2358389 | solution.py:443
  93.3 0.2 reduce_sum.43
  93.5 0.2 reduce_sum.44
  93.8 7.1 %share_sums.1 = f32[2048,128]{1,0:T(8,128)S(1)} custom-call(bf16[2048,256]{1,0:T(8,128)(2,1)S(1)} %get-tuple-element.33.chars_ref, bf16[4096,128]{1,0:T(8,128)(2,1)S(1)} %get-tuple-element.34.tastes_ref, f32[3,4096]{1,0:T(4,128)S(1)} %get-tuple-element.35.rows_ref, f32[1,256]{1,0:T(1,128)S(1)} %get-tuple-element.36.gate_ref), custom_call_target="tpu_custom_call" | custom-call | tf_op jit(solution)/shard_map/cond/branch_1_fun/share_sums/pallas_call | solution.py:331
  100.9 0.3 reduce_sum.42
  101.2 0.4 collective-permute-start
  101.6 0.9 collective-permute-done
  102.5 0.6 fusion.5
  103.1 1.1 collective-permute-start.1
  104.2 3.0 %collective-permute-done.1 = f32[4352]{0:T(1024)} collective-permute-done((f32[4352]{0:T(1024)}, f32[4352]{0:T(1024)}, u32[]{:S(2)}, u32[]{:S(2)}) %collective-permute-start.1) | collective-permute-done | bytes 17440 | tf_op jit(solution)/shard_map/cond/branch_1_fun/ppermute | solution.py:349
  107.2 0.7 slice.158
  107.9 0.0 collective-permute-done.8
  107.9 1.6 %select_subtract_fusion = f32[1024,256]{1,0:T(8,128)S(1)} fusion(f16[1024,256]{1,0:T(8,128)(2,1)} %collective-permute-done.8, f16[1024,256]{1,0:T(8,128)(2,1)} %get-tuple-element.78, f32[256]{0:T(256)S(1)} %get-tuple-element.107, s32[256]{0:T(256)S(1)} %copy-done.4, f32[256]{0:T(256)S(1)} %get-tuple-element.106, f32[256]{0:T(256)S(1)} %bitcast.46, ...), kind=kLoop, calls=%fused_computation.27 | loop fusion | flops 2097152 | bytes 2105344 | tf_op jit(solution)/shard_map/sub | solution.py:461
  109.5 1.0 fusion.7
  110.5 0.9 collective-permute-start.9
  111.4 0.7 add_multiply_fusion
  112.2 0.6 slice_bitcast_fusion.1
  112.8 0.9 multiply_reduce_fusion
  113.7 1.6 %maximum_select_fusion = f32[2048,256]{1,0:T(8,128)} fusion(f32[1024,256]{1,0:T(8,128)S(1)} %collective-permute-done.9, f32[1024,256]{1,0:T(8,128)S(1)} %bitcast.33, pred[]{:T(512)} %eq.35), kind=kLoop, calls=%fused_computation.24 | loop fusion | flops 1572864 | bytes 4194305 | tf_op jit(solution)/shard_map/jit(_where)/select_n | solution.py:469
  (30 shorter events, 0.4 us)
Async XLA Ops:
  6.6 23.8 %all-to-all-start = ((bf16[32,16,128]{2,1,0:T(8,128)(2,1)}), bf16[32,16,128]{2,1,0:T(8,128)(2,1)S(1)}, u32[]{:S(2)}, u32[]{:S(2)}) async-start(bf16[32,16,128]{2,1,0:T(8,128)(2,1)} %bitcast.38), calls=%async_computation | async-start | bytes 262144 | tf_op jit(solution)/shard_map/all_to_all | solution.py:381
  30.4 39.7 %copy-start.3 = (f32[4096]{0:T(1024)S(1)}, f32[4096]{0:T(1024)}, u32[]{:S(2)}) copy-start(f32[4096]{0:T(1024)} %param.12) | copy-start | bytes 49156
  34.1 36.0 %all-to-all-start.1 = ((bf16[32,80,128]{2,1,0:T(8,128)(2,1)}), bf16[32,80,128]{2,1,0:T(8,128)(2,1)S(1)}, u32[]{:S(2)}, u32[]{:S(2)}) async-start(bf16[32,80,128]{2,1,0:T(8,128)(2,1)} %bitcast.9), calls=%async_computation.1 | async-start | bytes 1310720 | tf_op jit(solution)/shard_map/all_to_all | solution.py:396
  43.4 29.8 %copy-start = (bf16[4096,128]{1,0:T(8,128)(2,1)S(1)}, bf16[4096,128]{1,0:T(8,128)(2,1)}, u32[]{:S(2)}) copy-start(bf16[4096,128]{1,0:T(8,128)(2,1)} %tastes_ref.5) | copy-start | bytes 3145732
  43.4 8.2 %collective-permute-start.2 = (f32[2,4096]{1,0:T(2,128)S(1)}, f32[2,4096]{1,0:T(2,128)S(1)}, u32[]{:S(2)}, u32[]{:S(2)}) collective-permute-start(f32[2,4096]{1,0:T(2,128)S(1)} %param.1), channel_id=1, source_target_pairs={{0,1},{1,0},{2,3},{3,2},{4,5},{5,4},{6,7},{7,6},{8,9},{9,8},{10,11... | collective-permute-start | bytes 98312 | tf_op jit(solution)/shard_map/cond/branch_1_fun/ppermute | solution.py:349
  51.7 4.3 %collective-permute-start.3 = (f32[2,4096]{1,0:T(2,128)S(1)}, f32[2,4096]{1,0:T(2,128)S(1)}, u32[]{:S(2)}, u32[]{:S(2)}) collective-permute-start(f32[2,4096]{1,0:T(2,128)S(1)} %pad_maximum_fusion), channel_id=1, source_target_pairs={{0,3},{1,2},{2,1},{3,0},{4,7},{5,6},{6,5},{7,4},{8,11},{9,10},{10,... | collective-permute-start | bytes 98312 | tf_op jit(solution)/shard_map/cond/branch_1_fun/ppermute | solution.py:349
  56.2 2.8 %collective-permute-start.4 = (f32[2,4096]{1,0:T(2,128)S(1)}, f32[2,4096]{1,0:T(2,128)S(1)}, u32[]{:S(2)}, u32[]{:S(2)}) collective-permute-start(f32[2,4096]{1,0:T(2,128)S(1)} %pad_maximum_fusion.1), channel_id=1, source_target_pairs={{0,4},{1,5},{2,6},{3,7},{4,0},{5,1},{6,2},{7,3},{8,12},{9,13},{10,... | collective-permute-start | bytes 98312 | tf_op jit(solution)/shard_map/cond/branch_1_fun/ppermute | solution.py:349
  59.1 4.1 %collective-permute-start.5 = (f32[2,4096]{1,0:T(2,128)S(1)}, f32[2,4096]{1,0:T(2,128)S(1)}, u32[]{:S(2)}, u32[]{:S(2)}) collective-permute-start(f32[2,4096]{1,0:T(2,128)S(1)} %pad_maximum_fusion.2), channel_id=1, source_target_pairs={{0,12},{1,13},{2,14},{3,15},{4,8},{5,9},{6,10},{7,11},{8,4},{9,5},... | collective-permute-start | bytes 98312 | tf_op jit(solution)/shard_map/cond/branch_1_fun/ppermute | solution.py:349
  63.3 4.3 %collective-permute-start.6 = (f32[2,4096]{1,0:T(2,128)S(1)}, f32[2,4096]{1,0:T(2,128)S(1)}, u32[]{:S(2)}, u32[]{:S(2)}) collective-permute-start(f32[2,4096]{1,0:T(2,128)S(1)} %pad_maximum_fusion.3), channel_id=1, source_target_pairs={{0,16},{1,17},{2,18},{3,19},{4,20},{5,21},{6,22},{7,23},{8,24},{9,... | collective-permute-start | bytes 98312 | tf_op jit(solution)/shard_map/cond/branch_1_fun/ppermute | solution.py:349
  80.4 11.5 %collective-permute-start.7 = (f32[1032,256]{1,0:T(8,128)S(1)}, f32[1032,256]{1,0:T(8,128)S(1)}, u32[]{:S(2)}, u32[]{:S(2)}) collective-permute-start(f32[1032,256]{1,0:T(8,128)S(1)} %get-tuple-element.71.gate_ref), channel_id=1, source_target_pairs={{0,32},{32,0},{64,96},{96,64},{1,33},{33,1},{65,97},{97,65},{2,34}... | collective-permute-start | bytes 3170312 | tf_op jit(solution)/shard_map/ppermute | solution.py:349
  91.9 1.4 %copy-start.2 = (s32[2048]{0:T(1024)S(1)}, s32[2048]{0:T(1024)}, u32[]{:S(2)}) copy-start(s32[2048]{0:T(1024)} %param.16) | copy-start | bytes 24580
  92.9 15.0 %collective-permute-start.8 = (f16[1024,256]{1,0:T(8,128)(2,1)}, f16[1024,256]{1,0:T(8,128)(2,1)}, u32[]{:S(2)}, u32[]{:S(2)}) collective-permute-start(f16[1024,256]{1,0:T(8,128)(2,1)} %get-tuple-element.78), channel_id=1, source_target_pairs={{0,64},{32,96},{64,0},{96,32},{1,65},{33,97},{65,1},{97,33},{2,66}... | collective-permute-start | bytes 1572872 | tf_op jit(solution)/shard_map/ppermute | solution.py:349
  93.3 14.6 %copy-start.4 = (s32[256]{0:T(256)S(1)}, s32[256]{0:T(256)}, u32[]{:S(2)}) copy-start(s32[256]{0:T(256)} %param.15) | copy-start | bytes 3076
  101.2 1.3 %collective-permute-start = (f32[4352]{0:T(1024)S(1)}, f32[4352]{0:T(1024)S(1)}, u32[]{:S(2)}, u32[]{:S(2)}) collective-permute-start(f32[4352]{0:T(1024)S(1)} %pad_maximum_fusion.5), channel_id=1, source_target_pairs={{0,32},{32,0},{64,96},{96,64},{1,33},{33,1},{65,97},{97,65},{2,34}... | collective-permute-start | bytes 52232 | tf_op jit(solution)/shard_map/cond/branch_1_fun/ppermute | solution.py:349
  103.1 4.1 %collective-permute-start.1 = (f32[4352]{0:T(1024)}, f32[4352]{0:T(1024)}, u32[]{:S(2)}, u32[]{:S(2)}) collective-permute-start(f32[4352]{0:T(1024)} %fusion.5), channel_id=1, source_target_pairs={{0,64},{32,96},{64,0},{96,32},{1,65},{33,97},{65,1},{97,33},{2,66}... | collective-permute-start | bytes 52232 | tf_op jit(solution)/shard_map/cond/branch_1_fun/ppermute | solution.py:349
  107.9 1.6 %copy-start.1 = (f32[16,128,128]{2,1,0:T(8,128)S(1)}, f32[16,128,128]{2,1,0:T(8,128)}, u32[]{:S(2)}) copy-start(f32[16,128,128]{2,1,0:T(8,128)} %param.17) | copy-start | bytes 3145732
  110.5 3.2 %collective-permute-start.9 = (f32[1024,256]{1,0:T(8,128)S(1)}, f32[1024,256]{1,0:T(8,128)S(1)}, u32[]{:S(2)}, u32[]{:S(2)}) collective-permute-start(f32[1024,256]{1,0:T(8,128)S(1)} %bitcast.32), channel_id=1, source_target_pairs={{0,32},{32,0},{64,96},{96,64},{1,33},{33,1},{65,97},{97,65},{2,34}... | collective-permute-start | bytes 3145736 | tf_op jit(solution)/shard_map/ppermute | solution.py:349

commit v10 on v9

--- a/solution.py
+++ b/solution.py
@@ -403,24 +403,25 @@
     place = (order // half == core).astype(jnp.int32) * half + order % half
 
     def join(stat, masks):
+        peak, total = stat[0], stat[1]
         for mask in masks:
-            other = swap(stat, "prod", mask)
-            joint = jnp.maximum(stat[0], other[0])
-            total = stat[1] * jnp.exp(stat[0] - joint) + other[1] * jnp.exp(other[0] - joint)
-            stat = jnp.stack([joint, total])
-        return stat
+            other = swap(jnp.concatenate([peak, total]), "prod", mask)
+            other_peak, other_total = other[:consumers], other[consumers:]
+            joint = jnp.maximum(peak, other_peak)
+            total = total * jnp.exp(peak - joint) + other_total * jnp.exp(other_peak - joint)
+            peak = joint
+        return peak, total
 
     masks = butterfly_masks(holders)
     taken = panel_cols[0] >= 0
-    stat = lax.cond(taken, lambda value: join(value, masks), lambda value: value, stat)
+    high, total = lax.cond(taken, lambda value: join(value, masks), lambda value: (value[0], value[1]), stat)
+    peak = jnp.maximum(high, 0.0)
+    denom = jnp.exp(-peak) + total * jnp.exp(high - peak)
+    ratio = count_products / denom
+    row_values = jnp.stack([peak, ratio, price_coef])
     firm_chars = place_rows(
-        place.reshape(1, products), second.reshape(holders * each, depth), mean_rows, holders, stat
+        place.reshape(1, products), second.reshape(holders * each, depth), mean_rows, holders, row_values
     )
-    peak = jnp.maximum(stat[0], 0.0)
-    denom = jnp.exp(-peak) + stat[1] * jnp.exp(stat[0] - peak)
-    ratio = count_products / denom
-
-    row_values = jnp.stack([peak, ratio, price_coef])
     given, given_share, weighted = first_panel(firm_chars, 2, tastes, row_values, col_chars)
     got = swap(given, "cons", 1)
     kept, kept_share = panel(firm_chars, 1, 2, tastes, row_values, weighted, given)

time: 116 us -> 114 us (0.983)
  other arithmetic: 12.2 us -> 9.72 us
  transfers between devices with their start and end apart: 12 -> 12, of which waited for: 7 -> 7; matrix products, arithmetic and copies ran while one was open for 8% -> 6% of each run, Pallas kernels for 19% -> 19%
where the time goes in v10:
time: 114 us; the launch traced here: 113 us
  starting transfers between devices  39.8 us (35%)
  Pallas kernels  39.6 us (35%)
  waiting for transfers between devices  17.9 us (16%)
  other arithmetic  9.72 us (9%)
  local copies, waits for them, and re-layouts  3.1 us (3%)
  between operations  1.59 us (1%)
    ppermute x10, starting transfers between devices, swap(): return lax.ppermute(value, axis, [(i, i ^ mask) for i in range(size)])  19.2 us
    ppermute x10, waiting for transfers between devices, swap(): return lax.ppermute(value, axis, [(i, i ^ mask) for i in range(size)])  17.9 us
    all_to_all x1, starting transfers between devices, body(): lax.all_to_all(message.reshape(holders, 16, depth), 'prod', split_axis=0,...  11.3 us
    pallas_call x1, Pallas kernels, stats(): pl.pallas_call(kernel, grid=(consumers // block,), in_specs=[pl.BlockSpec...  9.77 us
    all_to_all x1, starting transfers between devices, body(): lax.all_to_all(sent.reshape(holders, each, depth), 'prod', split_axis=0,...  9.26 us
    pallas_call x1, Pallas kernels, first_panel(): pl.pallas_call(kernel, grid=(consumers // block,), in_specs=[pl.BlockSpec...  7.4 us
    pallas_call x1, Pallas kernels, share_sums(): pl.pallas_call(kernel, grid=(consumers // block,), in_specs=[pl.BlockSpec...  7.18 us
    pallas_call x1, Pallas kernels, panel(): pl.pallas_call(kernel, grid=(1,), in_specs=[pl.BlockSpec((rows, depth), l...  4.88 us
  transfers between devices with their start and end apart: 12, of which 7 were waited for; matrix products, arithmetic and copies ran while one was open for 6% of the time, Pallas kernels for 19%

profile of v10, /device:TPU:1, one launch (start us, length us, event | category | flops | bytes accessed | tf_op | source)
XLA Modules:
  0.0 113.2 jit_solution(14486781735452948474)
XLA Ops:
  0.6 1.2 %convert_bitcast_fusion.panel_ref = f32[2,128]{1,0:T(2,128)} fusion(s32[256]{0:T(256)} %param.15, s32[]{:T(128)S(6)} %mul.103), kind=kLoop, calls=%fused_computation.62 | loop fusion | flops 512 | bytes 2052 | tf_op jit(solution)/shard_map/reshape | solution.py:378
  1.9 4.7 %prepare.1 = (bf16[2048,256]{1,0:T(8,128)(2,1)S(1)}, bf16[512,128]{1,0:T(8,128)(2,1)}, s32[1,2048]{1,0:T(1,128)}) custom-call(bf16[2048,128]{1,0:T(8,128)(2,1)} %chars_ref.1, f32[16,128]{1,0:T(8,128)} %bitcast.57, s32[1,2048]{1,0:T(1,128)} %bitcast.53, f32[2,128]{1,0:T(2,128)} %convert_bitcast_fusion.panel_ref), custom_call_target="tpu_custom_call" | custom-call | tf_op jit(solution)/shard_map/prepare/pallas_call | solution.py:92
  6.6 11.3 %all-to-all-start = ((bf16[32,16,128]{2,1,0:T(8,128)(2,1)}), bf16[32,16,128]{2,1,0:T(8,128)(2,1)S(1)}, u32[]{:S(2)}, u32[]{:S(2)}) async-start(bf16[32,16,128]{2,1,0:T(8,128)(2,1)} %bitcast.48), calls=%async_computation | async-start | bytes 262144 | tf_op jit(solution)/shard_map/all_to_all | solution.py:381
  17.9 0.8 fusion.13.order_ref
  18.7 1.2 %slice.117 = s32[1]{0:T(128)} slice(s32[256]{0:T(256)} %param.15), slice={[0:1]} | slice | bytes 8 | tf_op jit(solution)/shard_map/slice | solution.py:416
  20.6 9.8 %stats.1.stat_ref = f32[2,4096]{1,0:T(2,128)S(1)} custom-call(bf16[2048,256]{1,0:T(8,128)(2,1)S(1)} %get-tuple-element.57.chars_ref, bf16[4096,128]{1,0:T(8,128)(2,1)} %tastes_ref.5), custom_call_target="tpu_custom_call" | custom-call | tf_op jit(solution)/shard_map/stats/pallas_call | solution.py:132
  30.4 0.0 copy-start.3
  30.4 0.0 all-to-all-done
  30.5 0.1 copy.24
  30.6 0.1 copy.23
  30.7 0.1 pad_maximum_fusion.7.tail_ref
  30.8 3.3 %pick_rows.1 = (bf16[2560,128]{1,0:T(8,128)(2,1)}, f32[2,4096]{1,0:T(2,128)S(1)}) custom-call(s32[64,32]{1,0:T(8,128)S(1)} %add_bitcast_fusion.ids_ref, bf16[2048,256]{1,0:T(8,128)(2,1)S(1)} %get-tuple-element.57.chars_ref, f32[16,128]{1,0:T(8,128)S(1)} %pad_maximum_fusion.7.tail_ref, f32[2,4096]{1,0:T(2,128)S(1)} %stats.1.stat_ref), custom_call_target="tpu_custom_call" | custom-call | tf_op jit(solution)/shard_map/pick_rows/pallas_call | solution.py:168
  34.1 9.3 %all-to-all-start.1 = ((bf16[32,80,128]{2,1,0:T(8,128)(2,1)}), bf16[32,80,128]{2,1,0:T(8,128)(2,1)S(1)}, u32[]{:S(2)}, u32[]{:S(2)}) async-start(bf16[32,80,128]{2,1,0:T(8,128)(2,1)} %bitcast.15), calls=%async_computation.1 | async-start | bytes 1310720 | tf_op jit(solution)/shard_map/all_to_all | solution.py:396
  43.4 0.0 copy-start
  43.4 24.2 %conditional.2 = (f32[4096]{0:T(1024)S(1)}, f32[4096]{0:T(1024)S(1)}) conditional(s32[]{:T(128)} %bitcast.4, f32[2,4096]{1,0:T(2,128)S(1)} %get-tuple-element.59, f32[2,4096]{1,0:T(2,128)S(1)} %get-tuple-element.59), branch_computations={%region_1.2_spmd, %region_2.3_spmd} | conditional | flops 163840 | bytes 1540312 | solution.py:417
  43.5 1.3 %collective-permute-start.2 = (f32[8192]{0:T(1024)S(1)}, f32[8192]{0:T(1024)S(1)}, u32[]{:S(2)}, u32[]{:S(2)}) collective-permute-start(f32[8192]{0:T(1024)S(1)} %pad_maximum_fusion), channel_id=1, source_target_pairs={{0,1},{1,0},{2,3},{3,2},{4,5},{5,4},{6,7},{7,6},{8,9},{9,8},{10,11... | collective-permute-start | bytes 98312 | tf_op jit(solution)/shard_map/cond/branch_1_fun/ppermute | solution.py:349
  44.8 6.8 %collective-permute-done.2 = f32[8192]{0:T(1024)S(1)} collective-permute-done((f32[8192]{0:T(1024)S(1)}, f32[8192]{0:T(1024)S(1)}, u32[]{:S(2)}, u32[]{:S(2)}) %collective-permute-start.2) | collective-permute-done | bytes 32800 | tf_op jit(solution)/shard_map/cond/branch_1_fun/ppermute | solution.py:349
  51.6 1.9 %collective-permute-start.3 = (f32[8192]{0:T(1024)S(1)}, f32[8192]{0:T(1024)S(1)}, u32[]{:S(2)}, u32[]{:S(2)}) collective-permute-start(f32[8192]{0:T(1024)S(1)} %pad_maximum_fusion.1), channel_id=1, source_target_pairs={{0,3},{1,2},{2,1},{3,0},{4,7},{5,6},{6,5},{7,4},{8,11},{9,10},{10,... | collective-permute-start | bytes 98312 | tf_op jit(solution)/shard_map/cond/branch_1_fun/ppermute | solution.py:349
  53.5 2.5 %collective-permute-done.3 = f32[8192]{0:T(1024)S(1)} collective-permute-done((f32[8192]{0:T(1024)S(1)}, f32[8192]{0:T(1024)S(1)}, u32[]{:S(2)}, u32[]{:S(2)}) %collective-permute-start.3) | collective-permute-done | bytes 32800 | tf_op jit(solution)/shard_map/cond/branch_1_fun/ppermute | solution.py:349
  56.0 1.3 %collective-permute-start.4 = (f32[8192]{0:T(1024)S(1)}, f32[8192]{0:T(1024)S(1)}, u32[]{:S(2)}, u32[]{:S(2)}) collective-permute-start(f32[8192]{0:T(1024)S(1)} %pad_maximum_fusion.2), channel_id=1, source_target_pairs={{0,4},{1,5},{2,6},{3,7},{4,0},{5,1},{6,2},{7,3},{8,12},{9,13},{10,... | collective-permute-start | bytes 98312 | tf_op jit(solution)/shard_map/cond/branch_1_fun/ppermute | solution.py:349
  57.3 1.6 %collective-permute-done.4 = f32[8192]{0:T(1024)S(1)} collective-permute-done((f32[8192]{0:T(1024)S(1)}, f32[8192]{0:T(1024)S(1)}, u32[]{:S(2)}, u32[]{:S(2)}) %collective-permute-start.4) | collective-permute-done | bytes 32800 | tf_op jit(solution)/shard_map/cond/branch_1_fun/ppermute | solution.py:349
  58.9 2.5 %collective-permute-start.5 = (f32[8192]{0:T(1024)S(1)}, f32[8192]{0:T(1024)S(1)}, u32[]{:S(2)}, u32[]{:S(2)}) collective-permute-start(f32[8192]{0:T(1024)S(1)} %pad_maximum_fusion.3), channel_id=1, source_target_pairs={{0,12},{1,13},{2,14},{3,15},{4,8},{5,9},{6,10},{7,11},{8,4},{9,5},... | collective-permute-start | bytes 98312 | tf_op jit(solution)/shard_map/cond/branch_1_fun/ppermute | solution.py:349
  61.4 1.6 %collective-permute-done.5 = f32[8192]{0:T(1024)S(1)} collective-permute-done((f32[8192]{0:T(1024)S(1)}, f32[8192]{0:T(1024)S(1)}, u32[]{:S(2)}, u32[]{:S(2)}) %collective-permute-start.5) | collective-permute-done | bytes 32800 | tf_op jit(solution)/shard_map/cond/branch_1_fun/ppermute | solution.py:349
  63.0 2.8 %collective-permute-start.6 = (f32[8192]{0:T(1024)S(1)}, f32[8192]{0:T(1024)S(1)}, u32[]{:S(2)}, u32[]{:S(2)}) collective-permute-start(f32[8192]{0:T(1024)S(1)} %pad_maximum_fusion.4), channel_id=1, source_target_pairs={{0,16},{1,17},{2,18},{3,19},{4,20},{5,21},{6,22},{7,23},{8,24},{9,... | collective-permute-start | bytes 98312 | tf_op jit(solution)/shard_map/cond/branch_1_fun/ppermute | solution.py:349
  65.8 1.6 %collective-permute-done.6 = f32[8192]{0:T(1024)S(1)} collective-permute-done((f32[8192]{0:T(1024)S(1)}, f32[8192]{0:T(1024)S(1)}, u32[]{:S(2)}, u32[]{:S(2)}) %collective-permute-start.6) | collective-permute-done | bytes 32800 | tf_op jit(solution)/shard_map/cond/branch_1_fun/ppermute | solution.py:349
  67.6 0.0 copy-done.3
  67.7 0.0 all-to-all-done.1
  67.7 0.1 copy.22
  67.9 0.1 slice_select_fusion
  68.0 0.1 reshape.66.beside_ref
  68.1 0.1 fusion.12.cols_ref
  68.2 2.4 %place_rows.1.chars_ref = bf16[2048,256]{1,0:T(8,128)(2,1)S(1)} custom-call(s32[1,2048]{1,0:T(1,128)S(1)} %fusion.13.order_ref, bf16[2560,128]{1,0:T(8,128)(2,1)S(1)} %bitcast.37, f32[8,2048]{1,0:T(8,128)S(1)} %reshape.66.beside_ref, f32[3,4096]{1,0:T(4,128)S(1)} %pad_maximum_fusion.6.gate_ref.rows_ref), custom_call_target="tpu_custom_call" | custom-call | tf_op jit(solution)/shard_map/place_rows/pallas_call | solution.py:200
  70.7 0.0 copy-done
  70.7 7.4 %first_panel.1 = (f32[1032,256]{1,0:T(8,128)S(1)}, f32[1024,128]{1,0:T(8,128)S(1)}, bf16[256,4096]{1,0:T(8,128)(2,1)S(1)}) custom-call(bf16[2048,256]{1,0:T(8,128)(2,1)S(1)} %place_rows.1.chars_ref, bf16[4096,128]{1,0:T(8,128)(2,1)S(1)} %copy-done, f32[3,4096]{1,0:T(4,128)S(1)} %pad_maximum_fusion.6.gate_ref.rows_ref, bf16[256,256]{1,0:T(8,128)(2,1)S(1)} %fusion.12.cols_ref), custom_call_target="tpu_custom_call" | custom-call | flops 4294967296 | bytes 2097152 | tf_op jit(solution)/shard_map/first_panel/pallas_call | solution.py:247
  78.1 6.8 %collective-permute-start.7 = (f32[1032,256]{1,0:T(8,128)S(1)}, f32[1032,256]{1,0:T(8,128)S(1)}, u32[]{:S(2)}, u32[]{:S(2)}) collective-permute-start(f32[1032,256]{1,0:T(8,128)S(1)} %get-tuple-element.65.gate_ref), channel_id=1, source_target_pairs={{0,32},{32,0},{64,96},{96,64},{1,33},{33,1},{65,97},{97,65},{2,34}... | collective-permute-start | bytes 3170312 | tf_op jit(solution)/shard_map/ppermute | solution.py:349
  84.9 4.9 %panel.1 = (f32[1024,256]{1,0:T(8,128)S(1)}, f32[1024,128]{1,0:T(8,128)S(1)}) custom-call(bf16[2048,256]{1,0:T(8,128)(2,1)S(1)} %place_rows.1.chars_ref, bf16[4096,128]{1,0:T(8,128)(2,1)S(1)} %copy-done, f32[3,4096]{1,0:T(4,128)S(1)} %pad_maximum_fusion.6.gate_ref.rows_ref, bf16[256,4096]{1,0:T(8,128)(2,1)S(1)} %get-tuple-element.64.weight_ref, ...), custom_call_target="tpu_custom_call" | custom-call | flops 4294967296 | bytes 2097152 | tf_op jit(solution)/shard_map/panel/pallas_call | solution.py:289
  89.8 0.0 copy-start.2
  89.8 0.0 collective-permute-done.7
  89.8 1.0 fusion.9
  90.8 0.4 collective-permute-start.8
  91.2 0.0 copy-done.2
  91.2 0.0 copy-start.4
  91.2 14.6 %conditional.3 = (f32[4352]{0:T(1024)}, f32[4352]{0:T(1024)}, f32[256]{0:T(256)S(1)}) conditional(s32[]{:T(128)} %bitcast.4, () %tuple.28, (bf16[2048,256]{1,0:T(8,128)(2,1)S(1)}, bf16[4096,128]{1,0:T(8,128)(2,1)S(1)}, f32[3,4096]{1,0:T(4,128)S(1)}, f32[1,256]{1,0:T(1,128)S(1)}, pred[]{:T(512)}, /*index=5*/f32[1024,128]{1,0:T(8,128)S(1)}, ...), branch_computations={%region_4.5_spmd, %region_5.9_spmd} | conditional | flops 552704 | bytes 2358389 | solution.py:444
  91.2 0.2 reduce_sum.43
  91.4 0.2 reduce_sum.44
  91.6 7.2 %share_sums.1 = f32[2048,128]{1,0:T(8,128)S(1)} custom-call(bf16[2048,256]{1,0:T(8,128)(2,1)S(1)} %get-tuple-element.29.chars_ref, bf16[4096,128]{1,0:T(8,128)(2,1)S(1)} %get-tuple-element.30.tastes_ref, f32[3,4096]{1,0:T(4,128)S(1)} %get-tuple-element.31.rows_ref, f32[1,256]{1,0:T(1,128)S(1)} %get-tuple-element.32.gate_ref), custom_call_target="tpu_custom_call" | custom-call | tf_op jit(solution)/shard_map/cond/branch_1_fun/share_sums/pallas_call | solution.py:331
  98.8 0.3 reduce_sum.42
  99.2 0.4 collective-permute-start
  99.6 0.9 collective-permute-done
  100.5 0.6 fusion.5
  101.1 1.1 collective-permute-start.1
  102.2 2.9 %collective-permute-done.1 = f32[4352]{0:T(1024)} collective-permute-done((f32[4352]{0:T(1024)}, f32[4352]{0:T(1024)}, u32[]{:S(2)}, u32[]{:S(2)}) %collective-permute-start.1) | collective-permute-done | bytes 17440 | tf_op jit(solution)/shard_map/cond/branch_1_fun/ppermute | solution.py:349
  105.1 0.7 slice.147
  105.8 0.0 collective-permute-done.8
  105.8 0.0 copy-done.4
  105.8 1.6 %select_subtract_fusion = f32[1024,256]{1,0:T(8,128)S(1)} fusion(f16[1024,256]{1,0:T(8,128)(2,1)} %collective-permute-done.8, f16[1024,256]{1,0:T(8,128)(2,1)} %get-tuple-element.72, f32[256]{0:T(256)S(1)} %get-tuple-element.103, s32[256]{0:T(256)S(1)} %copy-done.4, f32[256]{0:T(256)S(1)} %get-tuple-element.102, f32[256]{0:T(256)S(1)} %bitcast.60, ...), kind=kLoop, calls=%fused_computation.27 | loop fusion | flops 2097152 | bytes 2105344 | tf_op jit(solution)/shard_map/sub | solution.py:462
  107.4 0.0 copy-done.1
  107.4 1.0 fusion.7
  108.4 0.9 collective-permute-start.9
  109.3 0.7 add_multiply_fusion
  110.0 0.6 slice_bitcast_fusion.1
  110.6 0.9 multiply_reduce_fusion
  111.6 0.0 collective-permute-done.9
  111.6 1.6 %maximum_select_fusion = f32[2048,256]{1,0:T(8,128)} fusion(f32[1024,256]{1,0:T(8,128)S(1)} %collective-permute-done.9, f32[1024,256]{1,0:T(8,128)S(1)} %bitcast.39, pred[]{:T(512)} %eq.35), kind=kLoop, calls=%fused_computation.24 | loop fusion | flops 1572864 | bytes 4194305 | tf_op jit(solution)/shard_map/jit(_where)/select_n | solution.py:470
  (31 shorter events, 0.4 us)
Async XLA Ops:
  6.6 23.8 %all-to-all-start = ((bf16[32,16,128]{2,1,0:T(8,128)(2,1)}), bf16[32,16,128]{2,1,0:T(8,128)(2,1)S(1)}, u32[]{:S(2)}, u32[]{:S(2)}) async-start(bf16[32,16,128]{2,1,0:T(8,128)(2,1)} %bitcast.48), calls=%async_computation | async-start | bytes 262144 | tf_op jit(solution)/shard_map/all_to_all | solution.py:381
  30.4 37.3 %copy-start.3 = (f32[4096]{0:T(1024)S(1)}, f32[4096]{0:T(1024)}, u32[]{:S(2)}) copy-start(f32[4096]{0:T(1024)} %param.12) | copy-start | bytes 49156
  34.1 33.6 %all-to-all-start.1 = ((bf16[32,80,128]{2,1,0:T(8,128)(2,1)}), bf16[32,80,128]{2,1,0:T(8,128)(2,1)S(1)}, u32[]{:S(2)}, u32[]{:S(2)}) async-start(bf16[32,80,128]{2,1,0:T(8,128)(2,1)} %bitcast.15), calls=%async_computation.1 | async-start | bytes 1310720 | tf_op jit(solution)/shard_map/all_to_all | solution.py:396
  43.4 27.3 %copy-start = (bf16[4096,128]{1,0:T(8,128)(2,1)S(1)}, bf16[4096,128]{1,0:T(8,128)(2,1)}, u32[]{:S(2)}) copy-start(bf16[4096,128]{1,0:T(8,128)(2,1)} %tastes_ref.5) | copy-start | bytes 3145732
  43.5 8.1 %collective-permute-start.2 = (f32[8192]{0:T(1024)S(1)}, f32[8192]{0:T(1024)S(1)}, u32[]{:S(2)}, u32[]{:S(2)}) collective-permute-start(f32[8192]{0:T(1024)S(1)} %pad_maximum_fusion), channel_id=1, source_target_pairs={{0,1},{1,0},{2,3},{3,2},{4,5},{5,4},{6,7},{7,6},{8,9},{9,8},{10,11... | collective-permute-start | bytes 98312 | tf_op jit(solution)/shard_map/cond/branch_1_fun/ppermute | solution.py:349
  51.6 4.3 %collective-permute-start.3 = (f32[8192]{0:T(1024)S(1)}, f32[8192]{0:T(1024)S(1)}, u32[]{:S(2)}, u32[]{:S(2)}) collective-permute-start(f32[8192]{0:T(1024)S(1)} %pad_maximum_fusion.1), channel_id=1, source_target_pairs={{0,3},{1,2},{2,1},{3,0},{4,7},{5,6},{6,5},{7,4},{8,11},{9,10},{10,... | collective-permute-start | bytes 98312 | tf_op jit(solution)/shard_map/cond/branch_1_fun/ppermute | solution.py:349
  56.0 2.9 %collective-permute-start.4 = (f32[8192]{0:T(1024)S(1)}, f32[8192]{0:T(1024)S(1)}, u32[]{:S(2)}, u32[]{:S(2)}) collective-permute-start(f32[8192]{0:T(1024)S(1)} %pad_maximum_fusion.2), channel_id=1, source_target_pairs={{0,4},{1,5},{2,6},{3,7},{4,0},{5,1},{6,2},{7,3},{8,12},{9,13},{10,... | collective-permute-start | bytes 98312 | tf_op jit(solution)/shard_map/cond/branch_1_fun/ppermute | solution.py:349
  58.9 4.1 %collective-permute-start.5 = (f32[8192]{0:T(1024)S(1)}, f32[8192]{0:T(1024)S(1)}, u32[]{:S(2)}, u32[]{:S(2)}) collective-permute-start(f32[8192]{0:T(1024)S(1)} %pad_maximum_fusion.3), channel_id=1, source_target_pairs={{0,12},{1,13},{2,14},{3,15},{4,8},{5,9},{6,10},{7,11},{8,4},{9,5},... | collective-permute-start | bytes 98312 | tf_op jit(solution)/shard_map/cond/branch_1_fun/ppermute | solution.py:349
  63.0 4.3 %collective-permute-start.6 = (f32[8192]{0:T(1024)S(1)}, f32[8192]{0:T(1024)S(1)}, u32[]{:S(2)}, u32[]{:S(2)}) collective-permute-start(f32[8192]{0:T(1024)S(1)} %pad_maximum_fusion.4), channel_id=1, source_target_pairs={{0,16},{1,17},{2,18},{3,19},{4,20},{5,21},{6,22},{7,23},{8,24},{9,... | collective-permute-start | bytes 98312 | tf_op jit(solution)/shard_map/cond/branch_1_fun/ppermute | solution.py:349
  78.1 11.7 %collective-permute-start.7 = (f32[1032,256]{1,0:T(8,128)S(1)}, f32[1032,256]{1,0:T(8,128)S(1)}, u32[]{:S(2)}, u32[]{:S(2)}) collective-permute-start(f32[1032,256]{1,0:T(8,128)S(1)} %get-tuple-element.65.gate_ref), channel_id=1, source_target_pairs={{0,32},{32,0},{64,96},{96,64},{1,33},{33,1},{65,97},{97,65},{2,34}... | collective-permute-start | bytes 3170312 | tf_op jit(solution)/shard_map/ppermute | solution.py:349
  89.8 1.4 %copy-start.2 = (s32[2048]{0:T(1024)S(1)}, s32[2048]{0:T(1024)}, u32[]{:S(2)}) copy-start(s32[2048]{0:T(1024)} %param.16) | copy-start | bytes 24580
  90.8 15.0 %collective-permute-start.8 = (f16[1024,256]{1,0:T(8,128)(2,1)}, f16[1024,256]{1,0:T(8,128)(2,1)}, u32[]{:S(2)}, u32[]{:S(2)}) collective-permute-start(f16[1024,256]{1,0:T(8,128)(2,1)} %get-tuple-element.72), channel_id=1, source_target_pairs={{0,64},{32,96},{64,0},{96,32},{1,65},{33,97},{65,1},{97,33},{2,66}... | collective-permute-start | bytes 1572872 | tf_op jit(solution)/shard_map/ppermute | solution.py:349
  91.2 14.6 %copy-start.4 = (s32[256]{0:T(256)S(1)}, s32[256]{0:T(256)}, u32[]{:S(2)}) copy-start(s32[256]{0:T(256)} %param.15) | copy-start | bytes 3076
  99.2 1.3 %collective-permute-start = (f32[4352]{0:T(1024)S(1)}, f32[4352]{0:T(1024)S(1)}, u32[]{:S(2)}, u32[]{:S(2)}) collective-permute-start(f32[4352]{0:T(1024)S(1)} %pad_maximum_fusion.5), channel_id=1, source_target_pairs={{0,32},{32,0},{64,96},{96,64},{1,33},{33,1},{65,97},{97,65},{2,34}... | collective-permute-start | bytes 52232 | tf_op jit(solution)/shard_map/cond/branch_1_fun/ppermute | solution.py:349
  101.1 4.0 %collective-permute-start.1 = (f32[4352]{0:T(1024)}, f32[4352]{0:T(1024)}, u32[]{:S(2)}, u32[]{:S(2)}) collective-permute-start(f32[4352]{0:T(1024)} %fusion.5), channel_id=1, source_target_pairs={{0,64},{32,96},{64,0},{96,32},{1,65},{33,97},{65,1},{97,33},{2,66}... | collective-permute-start | bytes 52232 | tf_op jit(solution)/shard_map/cond/branch_1_fun/ppermute | solution.py:349
  105.8 1.6 %copy-start.1 = (f32[16,128,128]{2,1,0:T(8,128)S(1)}, f32[16,128,128]{2,1,0:T(8,128)}, u32[]{:S(2)}) copy-start(f32[16,128,128]{2,1,0:T(8,128)} %param.17) | copy-start | bytes 3145732
  108.4 3.2 %collective-permute-start.9 = (f32[1024,256]{1,0:T(8,128)S(1)}, f32[1024,256]{1,0:T(8,128)S(1)}, u32[]{:S(2)}, u32[]{:S(2)}) collective-permute-start(f32[1024,256]{1,0:T(8,128)S(1)} %bitcast.38), channel_id=1, source_target_pairs={{0,32},{32,0},{64,96},{96,64},{1,33},{33,1},{65,97},{97,65},{2,34}... | collective-permute-start | bytes 3145736 | tf_op jit(solution)/shard_map/ppermute | solution.py:349

commit v11 on v10

--- a/solution.py
+++ b/solution.py
@@ -126,8 +126,7 @@
             expo = jnp.exp(util - joint)
             total = total * jnp.exp(peak - joint) + jnp.sum(expo.reshape(chunk // 8, 8, block), axis=0)
             peak = joint
-        stat_ref[0:1, :] = peak
-        stat_ref[1:2, :] = jnp.sum(total, axis=0, keepdims=True)
+        stat_ref[...] = peak + jnp.log(jnp.sum(total, axis=0, keepdims=True))
 
     return pl.pallas_call(
         kernel,
@@ -136,8 +135,8 @@
             pl.BlockSpec((rows, depth), lambda i: (0, 0)),
             pl.BlockSpec((block, tastes.shape[1]), lambda i: (i, 0)),
         ],
-        out_specs=pl.BlockSpec((2, block), lambda i: (0, i)),
-        out_shape=jax.ShapeDtypeStruct((2, consumers), jnp.float32),
+        out_specs=pl.BlockSpec((1, block), lambda i: (0, i)),
+        out_shape=jax.ShapeDtypeStruct((1, consumers), jnp.float32),
         compiler_params=pltpu.CompilerParams(vmem_limit_bytes=VMEM_BYTES),
         name="stats",
     )(chars, tastes)
@@ -403,20 +402,17 @@
     place = (order // half == core).astype(jnp.int32) * half + order % half
 
     def join(stat, masks):
-        peak, total = stat[0], stat[1]
         for mask in masks:
-            other = swap(jnp.concatenate([peak, total]), "prod", mask)
-            other_peak, other_total = other[:consumers], other[consumers:]
-            joint = jnp.maximum(peak, other_peak)
-            total = total * jnp.exp(peak - joint) + other_total * jnp.exp(other_peak - joint)
-            peak = joint
-        return peak, total
+            other = swap(stat, "prod", mask)
+            joint = jnp.maximum(stat, other)
+            stat = joint + jnp.log(jnp.exp(stat - joint) + jnp.exp(other - joint))
+        return stat
 
     masks = butterfly_masks(holders)
     taken = panel_cols[0] >= 0
-    high, total = lax.cond(taken, lambda value: join(value, masks), lambda value: (value[0], value[1]), stat)
-    peak = jnp.maximum(high, 0.0)
-    denom = jnp.exp(-peak) + total * jnp.exp(high - peak)
+    total = lax.cond(taken, lambda value: join(value, masks), lambda value: value, stat[0])
+    peak = jnp.maximum(total, 0.0)
+    denom = jnp.exp(-peak) + jnp.exp(total - peak)
     ratio = count_products / denom
     row_values = jnp.stack([peak, ratio, price_coef])
     firm_chars = place_rows(

time: 114 us -> 112 us (0.982)
  no operation moved by 1% of the time
where the time goes in v11:
time: 112 us
  starting transfers between devices  39.6 us (35%)
  Pallas kernels  39.2 us (35%)
  waiting for transfers between devices  17.2 us (15%)
  other arithmetic  9.71 us (9%)
  local copies, waits for them, and re-layouts  3.07 us (3%)
  between operations  1.59 us (1%)
    ppermute x10, starting transfers between devices, swap(): return lax.ppermute(value, axis, [(i, i ^ mask) for i in range(size)])  19 us
    ppermute x10, waiting for transfers between devices, swap(): return lax.ppermute(value, axis, [(i, i ^ mask) for i in range(size)])  17.2 us
    all_to_all x1, starting transfers between devices, body(): lax.all_to_all(message.reshape(holders, 16, depth), 'prod', split_axis=0,...  11.3 us
    pallas_call x1, Pallas kernels, stats(): pl.pallas_call(kernel, grid=(consumers // block,), in_specs=[pl.BlockSpec...  9.78 us
    all_to_all x1, starting transfers between devices, body(): lax.all_to_all(sent.reshape(holders, each, depth), 'prod', split_axis=0,...  9.26 us
    pallas_call x1, Pallas kernels, first_panel(): pl.pallas_call(kernel, grid=(consumers // block,), in_specs=[pl.BlockSpec...  7.24 us
    pallas_call x1, Pallas kernels, share_sums(): pl.pallas_call(kernel, grid=(consumers // block,), in_specs=[pl.BlockSpec...  7.09 us
    pallas_call x1, Pallas kernels, prepare(): pl.pallas_call(kernel, grid=(1,), in_specs=[whole(value.shape) for value...  4.69 us
  transfers between devices with their start and end apart: 12, of which 7 were waited for; matrix products, arithmetic and copies ran while one was open for 6% of the time, Pallas kernels for 19%

profile of v11, /device:TPU:1, one launch (start us, length us, event | category | flops | bytes accessed | tf_op | source)
XLA Modules:
  0.0 111.7 jit_solution(14027977877940920050)
XLA Ops:
  0.6 1.2 %convert_bitcast_fusion.panel_ref = f32[2,128]{1,0:T(2,128)} fusion(s32[256]{0:T(256)} %param.15, s32[]{:T(128)S(6)} %mul.70), kind=kLoop, calls=%fused_computation.57 | loop fusion | flops 512 | bytes 2052 | tf_op jit(solution)/shard_map/reshape | solution.py:377
  1.9 4.7 %prepare.1 = (bf16[2048,256]{1,0:T(8,128)(2,1)S(1)}, bf16[512,128]{1,0:T(8,128)(2,1)}, s32[1,2048]{1,0:T(1,128)}) custom-call(bf16[2048,128]{1,0:T(8,128)(2,1)} %chars_ref.1, f32[16,128]{1,0:T(8,128)} %bitcast.50, s32[1,2048]{1,0:T(1,128)} %bitcast.46, f32[2,128]{1,0:T(2,128)} %convert_bitcast_fusion.panel_ref), custom_call_target="tpu_custom_call" | custom-call | tf_op jit(solution)/shard_map/prepare/pallas_call | solution.py:92
  6.6 11.3 %all-to-all-start = ((bf16[32,16,128]{2,1,0:T(8,128)(2,1)}), bf16[32,16,128]{2,1,0:T(8,128)(2,1)S(1)}, u32[]{:S(2)}, u32[]{:S(2)}) async-start(bf16[32,16,128]{2,1,0:T(8,128)(2,1)} %bitcast.41), calls=%async_computation | async-start | bytes 262144 | tf_op jit(solution)/shard_map/all_to_all | solution.py:380
  17.9 0.8 fusion.13.order_ref
  18.7 1.2 %slice.75 = s32[1]{0:T(128)} slice(s32[256]{0:T(256)} %param.15), slice={[0:1]} | slice | bytes 8 | tf_op jit(solution)/shard_map/slice | solution.py:412
  20.6 9.8 %stats.1.stat_ref = f32[1,4096]{1,0:T(1,128)S(1)} custom-call(bf16[2048,256]{1,0:T(8,128)(2,1)S(1)} %get-tuple-element.58.chars_ref, bf16[4096,128]{1,0:T(8,128)(2,1)} %tastes_ref.5), custom_call_target="tpu_custom_call" | custom-call | tf_op jit(solution)/shard_map/stats/pallas_call | solution.py:131
  30.4 0.0 copy-start.3
  30.4 0.0 all-to-all-done
  30.5 0.1 copy.23
  30.6 0.1 copy.24
  30.8 0.1 pad_maximum_fusion.2.tail_ref
  30.8 3.3 %pick_rows.1 = (bf16[2560,128]{1,0:T(8,128)(2,1)}, f32[1,4096]{1,0:T(1,128)S(1)}) custom-call(s32[64,32]{1,0:T(8,128)S(1)} %add_bitcast_fusion.ids_ref, bf16[2048,256]{1,0:T(8,128)(2,1)S(1)} %get-tuple-element.58.chars_ref, f32[16,128]{1,0:T(8,128)S(1)} %pad_maximum_fusion.2.tail_ref, f32[1,4096]{1,0:T(1,128)S(1)} %stats.1.stat_ref), custom_call_target="tpu_custom_call" | custom-call | tf_op jit(solution)/shard_map/pick_rows/pallas_call | solution.py:167
  34.1 9.3 %all-to-all-start.1 = ((bf16[32,80,128]{2,1,0:T(8,128)(2,1)}), bf16[32,80,128]{2,1,0:T(8,128)(2,1)S(1)}, u32[]{:S(2)}, u32[]{:S(2)}) async-start(bf16[32,80,128]{2,1,0:T(8,128)(2,1)} %bitcast.12), calls=%async_computation.1 | async-start | bytes 1310720 | tf_op jit(solution)/shard_map/all_to_all | solution.py:395
  43.4 0.0 copy-start
  43.4 23.3 %conditional.2 = (f32[4096]{0:T(1024)S(1)}) conditional(s32[]{:T(128)} %bitcast, f32[4096]{0:T(1024)S(1)} %bitcast.42, f32[4096]{0:T(1024)S(1)} %bitcast.43), branch_computations={%region_1.2_spmd, %region_2.3_spmd} | conditional | flops 102400 | bytes 573648 | solution.py:413
  43.4 1.3 %collective-permute-start = (f32[4096]{0:T(1024)S(1)}, f32[4096]{0:T(1024)S(1)}, u32[]{:S(2)}, u32[]{:S(2)}) collective-permute-start(f32[4096]{0:T(1024)S(1)} %param.1), channel_id=1, source_target_pairs={{0,1},{1,0},{2,3},{3,2},{4,5},{5,4},{6,7},{7,6},{8,9},{9,8},{10,11... | collective-permute-start | bytes 49160 | tf_op jit(solution)/shard_map/cond/branch_1_fun/ppermute | solution.py:348
  44.7 6.5 %collective-permute-done = f32[4096]{0:T(1024)S(1)} collective-permute-done((f32[4096]{0:T(1024)S(1)}, f32[4096]{0:T(1024)S(1)}, u32[]{:S(2)}, u32[]{:S(2)}) %collective-permute-start) | collective-permute-done | bytes 16416 | tf_op jit(solution)/shard_map/cond/branch_1_fun/ppermute | solution.py:348
  51.3 1.9 %collective-permute-start.1 = (f32[4096]{0:T(1024)S(1)}, f32[4096]{0:T(1024)S(1)}, u32[]{:S(2)}, u32[]{:S(2)}) collective-permute-start(f32[4096]{0:T(1024)S(1)} %log_add_fusion.4), channel_id=1, source_target_pairs={{0,3},{1,2},{2,1},{3,0},{4,7},{5,6},{6,5},{7,4},{8,11},{9,10},{10,... | collective-permute-start | bytes 49160 | tf_op jit(solution)/shard_map/cond/branch_1_fun/ppermute | solution.py:348
  53.2 2.3 %collective-permute-done.1 = f32[4096]{0:T(1024)S(1)} collective-permute-done((f32[4096]{0:T(1024)S(1)}, f32[4096]{0:T(1024)S(1)}, u32[]{:S(2)}, u32[]{:S(2)}) %collective-permute-start.1) | collective-permute-done | bytes 16416 | tf_op jit(solution)/shard_map/cond/branch_1_fun/ppermute | solution.py:348
  55.5 1.3 %collective-permute-start.2 = (f32[4096]{0:T(1024)S(1)}, f32[4096]{0:T(1024)S(1)}, u32[]{:S(2)}, u32[]{:S(2)}) collective-permute-start(f32[4096]{0:T(1024)S(1)} %log_add_fusion.3), channel_id=1, source_target_pairs={{0,4},{1,5},{2,6},{3,7},{4,0},{5,1},{6,2},{7,3},{8,12},{9,13},{10,... | collective-permute-start | bytes 49160 | tf_op jit(solution)/shard_map/cond/branch_1_fun/ppermute | solution.py:348
  56.8 1.6 %collective-permute-done.2 = f32[4096]{0:T(1024)S(1)} collective-permute-done((f32[4096]{0:T(1024)S(1)}, f32[4096]{0:T(1024)S(1)}, u32[]{:S(2)}, u32[]{:S(2)}) %collective-permute-start.2) | collective-permute-done | bytes 16416 | tf_op jit(solution)/shard_map/cond/branch_1_fun/ppermute | solution.py:348
  58.4 2.5 %collective-permute-start.3 = (f32[4096]{0:T(1024)S(1)}, f32[4096]{0:T(1024)S(1)}, u32[]{:S(2)}, u32[]{:S(2)}) collective-permute-start(f32[4096]{0:T(1024)S(1)} %log_add_fusion.2), channel_id=1, source_target_pairs={{0,12},{1,13},{2,14},{3,15},{4,8},{5,9},{6,10},{7,11},{8,4},{9,5},... | collective-permute-start | bytes 49160 | tf_op jit(solution)/shard_map/cond/branch_1_fun/ppermute | solution.py:348
  60.9 1.4 %collective-permute-done.3 = f32[4096]{0:T(1024)S(1)} collective-permute-done((f32[4096]{0:T(1024)S(1)}, f32[4096]{0:T(1024)S(1)}, u32[]{:S(2)}, u32[]{:S(2)}) %collective-permute-start.3) | collective-permute-done | bytes 16416 | tf_op jit(solution)/shard_map/cond/branch_1_fun/ppermute | solution.py:348
  62.3 2.8 %collective-permute-start.4 = (f32[4096]{0:T(1024)S(1)}, f32[4096]{0:T(1024)S(1)}, u32[]{:S(2)}, u32[]{:S(2)}) collective-permute-start(f32[4096]{0:T(1024)S(1)} %log_add_fusion.1), channel_id=1, source_target_pairs={{0,16},{1,17},{2,18},{3,19},{4,20},{5,21},{6,22},{7,23},{8,24},{9,... | collective-permute-start | bytes 49160 | tf_op jit(solution)/shard_map/cond/branch_1_fun/ppermute | solution.py:348
  65.1 1.4 %collective-permute-done.4 = f32[4096]{0:T(1024)S(1)} collective-permute-done((f32[4096]{0:T(1024)S(1)}, f32[4096]{0:T(1024)S(1)}, u32[]{:S(2)}, u32[]{:S(2)}) %collective-permute-start.4) | collective-permute-done | bytes 16416 | tf_op jit(solution)/shard_map/cond/branch_1_fun/ppermute | solution.py:348
  66.7 0.0 copy-done.3
  66.8 0.0 all-to-all-done.1
  66.8 0.1 copy.22
  67.0 0.1 slice_select_fusion
  67.1 0.1 reshape.66.beside_ref
  67.2 0.1 fusion.12.cols_ref
  67.3 2.4 %place_rows.1.chars_ref = bf16[2048,256]{1,0:T(8,128)(2,1)S(1)} custom-call(s32[1,2048]{1,0:T(1,128)S(1)} %fusion.13.order_ref, bf16[2560,128]{1,0:T(8,128)(2,1)S(1)} %bitcast.34, f32[8,2048]{1,0:T(8,128)S(1)} %reshape.66.beside_ref, f32[3,4096]{1,0:T(4,128)S(1)} %pad_maximum_fusion.1.gate_ref.rows_ref), custom_call_target="tpu_custom_call" | custom-call | tf_op jit(solution)/shard_map/place_rows/pallas_call | solution.py:199
  69.8 0.0 copy-done
  69.8 7.2 %first_panel.1 = (f32[1032,256]{1,0:T(8,128)S(1)}, f32[1024,128]{1,0:T(8,128)S(1)}, bf16[256,4096]{1,0:T(8,128)(2,1)S(1)}) custom-call(bf16[2048,256]{1,0:T(8,128)(2,1)S(1)} %place_rows.1.chars_ref, bf16[4096,128]{1,0:T(8,128)(2,1)S(1)} %copy-done, f32[3,4096]{1,0:T(4,128)S(1)} %pad_maximum_fusion.1.gate_ref.rows_ref, bf16[256,256]{1,0:T(8,128)(2,1)S(1)} %fusion.12.cols_ref), custom_call_target="tpu_custom_call" | custom-call | flops 4294967296 | bytes 2097152 | tf_op jit(solution)/shard_map/first_panel/pallas_call | solution.py:246
  77.1 6.6 %collective-permute-start.7 = (f32[1032,256]{1,0:T(8,128)S(1)}, f32[1032,256]{1,0:T(8,128)S(1)}, u32[]{:S(2)}, u32[]{:S(2)}) collective-permute-start(f32[1032,256]{1,0:T(8,128)S(1)} %get-tuple-element.64.gate_ref), channel_id=1, source_target_pairs={{0,32},{32,0},{64,96},{96,64},{1,33},{33,1},{65,97},{97,65},{2,34}... | collective-permute-start | bytes 3170312 | tf_op jit(solution)/shard_map/ppermute | solution.py:348
  83.7 4.7 %panel.1 = (f32[1024,256]{1,0:T(8,128)S(1)}, f32[1024,128]{1,0:T(8,128)S(1)}) custom-call(bf16[2048,256]{1,0:T(8,128)(2,1)S(1)} %place_rows.1.chars_ref, bf16[4096,128]{1,0:T(8,128)(2,1)S(1)} %copy-done, f32[3,4096]{1,0:T(4,128)S(1)} %pad_maximum_fusion.1.gate_ref.rows_ref, bf16[256,4096]{1,0:T(8,128)(2,1)S(1)} %get-tuple-element.63.weight_ref, ...), custom_call_target="tpu_custom_call" | custom-call | flops 4294967296 | bytes 2097152 | tf_op jit(solution)/shard_map/panel/pallas_call | solution.py:288
  88.4 0.0 copy-start.2
  88.4 0.0 collective-permute-done.7
  88.4 1.0 fusion.9
  89.4 0.4 collective-permute-start.8
  89.8 0.0 copy-done.2
  89.8 0.0 copy-start.4
  89.8 14.6 %conditional.3 = (f32[4352]{0:T(1024)}, f32[4352]{0:T(1024)}, f32[256]{0:T(256)S(1)}) conditional(s32[]{:T(128)} %bitcast, () %tuple.26, (bf16[2048,256]{1,0:T(8,128)(2,1)S(1)}, bf16[4096,128]{1,0:T(8,128)(2,1)S(1)}, f32[3,4096]{1,0:T(4,128)S(1)}, f32[1,256]{1,0:T(1,128)S(1)}, pred[]{:T(512)}, /*index=5*/f32[1024,128]{1,0:T(8,128)S(1)}, ...), branch_computations={%region_4.5_spmd, %region_5.9_spmd} | conditional | flops 552704 | bytes 2358389 | solution.py:440
  89.8 0.2 reduce_sum.43
  90.0 0.2 reduce_sum.44
  90.2 7.1 %share_sums.1 = f32[2048,128]{1,0:T(8,128)S(1)} custom-call(bf16[2048,256]{1,0:T(8,128)(2,1)S(1)} %get-tuple-element.32.chars_ref, bf16[4096,128]{1,0:T(8,128)(2,1)S(1)} %get-tuple-element.33.tastes_ref, f32[3,4096]{1,0:T(4,128)S(1)} %get-tuple-element.34.rows_ref, f32[1,256]{1,0:T(1,128)S(1)} %get-tuple-element.35.gate_ref), custom_call_target="tpu_custom_call" | custom-call | tf_op jit(solution)/shard_map/cond/branch_1_fun/share_sums/pallas_call | solution.py:330
  97.3 0.3 reduce_sum.42
  97.7 0.4 collective-permute-start.5
  98.0 0.9 collective-permute-done.5
  98.9 0.6 fusion.5
  99.5 1.1 collective-permute-start.6
  100.6 3.0 %collective-permute-done.6 = f32[4352]{0:T(1024)} collective-permute-done((f32[4352]{0:T(1024)}, f32[4352]{0:T(1024)}, u32[]{:S(2)}, u32[]{:S(2)}) %collective-permute-start.6) | collective-permute-done | bytes 17440 | tf_op jit(solution)/shard_map/cond/branch_1_fun/ppermute | solution.py:348
  103.7 0.7 slice.95
  104.4 0.0 collective-permute-done.8
  104.4 0.0 copy-done.4
  104.4 1.6 %select_subtract_fusion = f32[1024,256]{1,0:T(8,128)S(1)} fusion(f16[1024,256]{1,0:T(8,128)(2,1)} %collective-permute-done.8, f16[1024,256]{1,0:T(8,128)(2,1)} %get-tuple-element.71, f32[256]{0:T(256)S(1)} %get-tuple-element.88, s32[256]{0:T(256)S(1)} %copy-done.4, f32[256]{0:T(256)S(1)} %get-tuple-element.87, f32[256]{0:T(256)S(1)} %bitcast.53, ...), kind=kLoop, calls=%fused_computation.22 | loop fusion | flops 2097152 | bytes 2105344 | tf_op jit(solution)/shard_map/sub | solution.py:458
  105.9 0.0 copy-done.1
  106.0 1.0 fusion.7
  107.0 0.9 collective-permute-start.9
  107.9 0.7 add_multiply_fusion
  108.6 0.6 slice_bitcast_fusion.1
  109.2 0.9 multiply_reduce_fusion
  110.2 0.0 collective-permute-done.9
  110.2 1.6 %maximum_select_fusion = f32[2048,256]{1,0:T(8,128)} fusion(f32[1024,256]{1,0:T(8,128)S(1)} %collective-permute-done.9, f32[1024,256]{1,0:T(8,128)S(1)} %bitcast.36, pred[]{:T(512)} %eq.35), kind=kLoop, calls=%fused_computation.19 | loop fusion | flops 1572864 | bytes 4194305 | tf_op jit(solution)/shard_map/jit(_where)/select_n | solution.py:466
  (25 shorter events, 0.4 us)
Async XLA Ops:
  6.6 23.8 %all-to-all-start = ((bf16[32,16,128]{2,1,0:T(8,128)(2,1)}), bf16[32,16,128]{2,1,0:T(8,128)(2,1)S(1)}, u32[]{:S(2)}, u32[]{:S(2)}) async-start(bf16[32,16,128]{2,1,0:T(8,128)(2,1)} %bitcast.41), calls=%async_computation | async-start | bytes 262144 | tf_op jit(solution)/shard_map/all_to_all | solution.py:380
  30.4 36.4 %copy-start.3 = (f32[4096]{0:T(1024)S(1)}, f32[4096]{0:T(1024)}, u32[]{:S(2)}) copy-start(f32[4096]{0:T(1024)} %param.12) | copy-start | bytes 49156
  34.1 32.7 %all-to-all-start.1 = ((bf16[32,80,128]{2,1,0:T(8,128)(2,1)}), bf16[32,80,128]{2,1,0:T(8,128)(2,1)S(1)}, u32[]{:S(2)}, u32[]{:S(2)}) async-start(bf16[32,80,128]{2,1,0:T(8,128)(2,1)} %bitcast.12), calls=%async_computation.1 | async-start | bytes 1310720 | tf_op jit(solution)/shard_map/all_to_all | solution.py:395
  43.4 26.4 %copy-start = (bf16[4096,128]{1,0:T(8,128)(2,1)S(1)}, bf16[4096,128]{1,0:T(8,128)(2,1)}, u32[]{:S(2)}) copy-start(bf16[4096,128]{1,0:T(8,128)(2,1)} %tastes_ref.5) | copy-start | bytes 3145732
  43.4 7.9 %collective-permute-start = (f32[4096]{0:T(1024)S(1)}, f32[4096]{0:T(1024)S(1)}, u32[]{:S(2)}, u32[]{:S(2)}) collective-permute-start(f32[4096]{0:T(1024)S(1)} %param.1), channel_id=1, source_target_pairs={{0,1},{1,0},{2,3},{3,2},{4,5},{5,4},{6,7},{7,6},{8,9},{9,8},{10,11... | collective-permute-start | bytes 49160 | tf_op jit(solution)/shard_map/cond/branch_1_fun/ppermute | solution.py:348
  51.3 4.2 %collective-permute-start.1 = (f32[4096]{0:T(1024)S(1)}, f32[4096]{0:T(1024)S(1)}, u32[]{:S(2)}, u32[]{:S(2)}) collective-permute-start(f32[4096]{0:T(1024)S(1)} %log_add_fusion.4), channel_id=1, source_target_pairs={{0,3},{1,2},{2,1},{3,0},{4,7},{5,6},{6,5},{7,4},{8,11},{9,10},{10,... | collective-permute-start | bytes 49160 | tf_op jit(solution)/shard_map/cond/branch_1_fun/ppermute | solution.py:348
  55.5 2.9 %collective-permute-start.2 = (f32[4096]{0:T(1024)S(1)}, f32[4096]{0:T(1024)S(1)}, u32[]{:S(2)}, u32[]{:S(2)}) collective-permute-start(f32[4096]{0:T(1024)S(1)} %log_add_fusion.3), channel_id=1, source_target_pairs={{0,4},{1,5},{2,6},{3,7},{4,0},{5,1},{6,2},{7,3},{8,12},{9,13},{10,... | collective-permute-start | bytes 49160 | tf_op jit(solution)/shard_map/cond/branch_1_fun/ppermute | solution.py:348
  58.4 3.9 %collective-permute-start.3 = (f32[4096]{0:T(1024)S(1)}, f32[4096]{0:T(1024)S(1)}, u32[]{:S(2)}, u32[]{:S(2)}) collective-permute-start(f32[4096]{0:T(1024)S(1)} %log_add_fusion.2), channel_id=1, source_target_pairs={{0,12},{1,13},{2,14},{3,15},{4,8},{5,9},{6,10},{7,11},{8,4},{9,5},... | collective-permute-start | bytes 49160 | tf_op jit(solution)/shard_map/cond/branch_1_fun/ppermute | solution.py:348
  62.3 4.2 %collective-permute-start.4 = (f32[4096]{0:T(1024)S(1)}, f32[4096]{0:T(1024)S(1)}, u32[]{:S(2)}, u32[]{:S(2)}) collective-permute-start(f32[4096]{0:T(1024)S(1)} %log_add_fusion.1), channel_id=1, source_target_pairs={{0,16},{1,17},{2,18},{3,19},{4,20},{5,21},{6,22},{7,23},{8,24},{9,... | collective-permute-start | bytes 49160 | tf_op jit(solution)/shard_map/cond/branch_1_fun/ppermute | solution.py:348
  77.1 11.3 %collective-permute-start.7 = (f32[1032,256]{1,0:T(8,128)S(1)}, f32[1032,256]{1,0:T(8,128)S(1)}, u32[]{:S(2)}, u32[]{:S(2)}) collective-permute-start(f32[1032,256]{1,0:T(8,128)S(1)} %get-tuple-element.64.gate_ref), channel_id=1, source_target_pairs={{0,32},{32,0},{64,96},{96,64},{1,33},{33,1},{65,97},{97,65},{2,34}... | collective-permute-start | bytes 3170312 | tf_op jit(solution)/shard_map/ppermute | solution.py:348
  88.4 1.4 %copy-start.2 = (s32[2048]{0:T(1024)S(1)}, s32[2048]{0:T(1024)}, u32[]{:S(2)}) copy-start(s32[2048]{0:T(1024)} %param.16) | copy-start | bytes 24580
  89.4 15.0 %collective-permute-start.8 = (f16[1024,256]{1,0:T(8,128)(2,1)}, f16[1024,256]{1,0:T(8,128)(2,1)}, u32[]{:S(2)}, u32[]{:S(2)}) collective-permute-start(f16[1024,256]{1,0:T(8,128)(2,1)} %get-tuple-element.71), channel_id=1, source_target_pairs={{0,64},{32,96},{64,0},{96,32},{1,65},{33,97},{65,1},{97,33},{2,66}... | collective-permute-start | bytes 1572872 | tf_op jit(solution)/shard_map/ppermute | solution.py:348
  89.8 14.6 %copy-start.4 = (s32[256]{0:T(256)S(1)}, s32[256]{0:T(256)}, u32[]{:S(2)}) copy-start(s32[256]{0:T(256)} %param.15) | copy-start | bytes 3076
  97.7 1.3 %collective-permute-start.5 = (f32[4352]{0:T(1024)S(1)}, f32[4352]{0:T(1024)S(1)}, u32[]{:S(2)}, u32[]{:S(2)}) collective-permute-start(f32[4352]{0:T(1024)S(1)} %pad_maximum_fusion), channel_id=1, source_target_pairs={{0,32},{32,0},{64,96},{96,64},{1,33},{33,1},{65,97},{97,65},{2,34}... | collective-permute-start | bytes 52232 | tf_op jit(solution)/shard_map/cond/branch_1_fun/ppermute | solution.py:348
  99.5 4.1 %collective-permute-start.6 = (f32[4352]{0:T(1024)}, f32[4352]{0:T(1024)}, u32[]{:S(2)}, u32[]{:S(2)}) collective-permute-start(f32[4352]{0:T(1024)} %fusion.5), channel_id=1, source_target_pairs={{0,64},{32,96},{64,0},{96,32},{1,65},{33,97},{65,1},{97,33},{2,66}... | collective-permute-start | bytes 52232 | tf_op jit(solution)/shard_map/cond/branch_1_fun/ppermute | solution.py:348
  104.3 1.6 %copy-start.1 = (f32[16,128,128]{2,1,0:T(8,128)S(1)}, f32[16,128,128]{2,1,0:T(8,128)}, u32[]{:S(2)}) copy-start(f32[16,128,128]{2,1,0:T(8,128)} %param.17) | copy-start | bytes 3145732
  107.0 3.2 %collective-permute-start.9 = (f32[1024,256]{1,0:T(8,128)S(1)}, f32[1024,256]{1,0:T(8,128)S(1)}, u32[]{:S(2)}, u32[]{:S(2)}) collective-permute-start(f32[1024,256]{1,0:T(8,128)S(1)} %bitcast.35), channel_id=1, source_target_pairs={{0,32},{32,0},{64,96},{96,64},{1,33},{33,1},{65,97},{97,65},{2,34}... | collective-permute-start | bytes 3145736 | tf_op jit(solution)/shard_map/ppermute | solution.py:348

commit v12 on v11

--- a/solution.py
+++ b/solution.py
@@ -24,7 +24,9 @@
     share_cols = cols // holders
     chunk = 256
 
-    def kernel(chars_ref, means_ref, firm_ref, panel_ref, both_ref, message_ref, order_ref):
+    def kernel(chars_ref, means_ref, firm_ref, panel_ref, both_ref, message_ref, place_ref):
+        core, half = lax.axis_index("cons") % 2, rows // 2
+        base = lax.axis_index("prod") * rows
         lane = lax.broadcasted_iota(jnp.int32, (128, 128), 1)
         values = means_ref[...]
         high = rounded(values)
@@ -67,12 +69,14 @@
             slots = start + lax.broadcasted_iota(jnp.int32, (chunk, rows), 0)
             hot = jnp.where(slots == slot, 1.0, 0.0).astype(jnp.bfloat16)
             found = dot_nt(digits, hot)
-            order_ref[:, start : start + chunk] = (found[2:3, :] * 256.0 + found[3:4, :]).astype(jnp.int32)
+            order = (found[2:3, :] * 256.0 + found[3:4, :]).astype(jnp.int32)
+            place_ref[:, start : start + chunk] = jnp.where(order // half == core, half, 0) + order % half
             asked.append(found)
 
         products = lax.broadcasted_iota(jnp.int32, (128, rows), 1).astype(jnp.float32)
         both = both_ref[...]
-        wide = jnp.concatenate([panel_ref[...], jnp.zeros((128 - panel_ref.shape[0], 128), jnp.float32)], axis=0).T
+        local = (panel_ref[...] - base).astype(jnp.float32)
+        wide = jnp.concatenate([local, jnp.zeros((128 - panel_ref.shape[0], 128), jnp.float32)], axis=0).T
         part_row = lax.broadcasted_iota(jnp.int32, (8, 128), 0)
         for k in range(cols // 128):
             hot = jnp.where(wide[:, k : k + 1] == products, 1.0, 0.0).astype(jnp.bfloat16)
@@ -366,15 +370,14 @@
     per_pair = products // holders
     count_products = products * holders
     count_consumers = consumers * lax.axis_size("cons")
-    base = lax.axis_index("prod") * products
     core = lax.axis_index("cons") % 2
 
     share_cols = cols // holders
-    chars, message, order = prepare(
+    chars, message, place = prepare(
         characteristics,
         mean_utility.reshape(products // 128, 128),
         firm_map.reshape(1, products),
-        (panel_cols - base).astype(jnp.float32).reshape(cols // 128, 128),
+        panel_cols.reshape(cols // 128, 128),
         holders,
     )
     first = lax.all_to_all(message.reshape(holders, 16, depth), "prod", split_axis=0, concat_axis=0, tiled=True)
@@ -399,7 +402,6 @@
     mean_rows = own_lanes(second[:, per_pair : per_pair + 4, :].astype(jnp.float32))
     mean_rows = jnp.pad(mean_rows, ((0, 0), (0, 4), (0, 0))).transpose(1, 0, 2).reshape(8, products)
     half = products // 2
-    place = (order // half == core).astype(jnp.int32) * half + order % half
 
     def join(stat, masks):
         for mask in masks:
@@ -416,7 +418,7 @@
     ratio = count_products / denom
     row_values = jnp.stack([peak, ratio, price_coef])
     firm_chars = place_rows(
-        place.reshape(1, products), second.reshape(holders * each, depth), mean_rows, holders, row_values
+        place, second.reshape(holders * each, depth), mean_rows, holders, row_values
     )
     given, given_share, weighted = first_panel(firm_chars, 2, tastes, row_values, col_chars)
     got = swap(given, "cons", 1)
@@ -435,17 +437,16 @@
         own_shares = jnp.sum(share_sums(chars, tastes, row_values, gate), axis=1)
         sums = jnp.concatenate([own_shares, others])
         sums = sums + swap(sums, "cons", 1)
-        return sums, swap(sums, "cons", 2)
-
-    sums, other_sums = lax.cond(
+        other_sums = swap(sums, "cons", 2)
+        return (sums + other_sums) / count_consumers, other_sums[2 * products :]
+
+    sums, other_diagonal = lax.cond(
         taken,
         own_and_exchange,
-        lambda gate, others: (jnp.zeros(products + others.shape[0], jnp.float32),) * 2,
+        lambda gate, others: (jnp.zeros(2 * products + cols, jnp.float32), jnp.zeros(cols, jnp.float32)),
         gate,
         jnp.concatenate([first_half, second_half, given[half]]),
     )
-    other_diagonal = other_sums[2 * products :]
-    sums = (sums + other_sums) / count_consumers
     shares, firm_shares = sums[:products], sums[products : 2 * products]
 
     firm_count, block_size = inverses.shape[0], inverses.shape[1]

time: 112 us -> 109 us (0.973)
  other arithmetic: 9.71 us -> 6.36 us
  waiting for transfers between devices: 17.2 us -> 18.5 us
    reshape x1 -> x0, other arithmetic: 1.25 us -> none  [body(): (panel_cols - base).astype(jnp.float32).reshape(cols // 128, 128)]
    ppermute x10, waiting for transfers between devices: 17.2 us -> 18.5 us  [swap(): return lax.ppermute(value, axis, [(i, i ^ mask) for i in range(size)])]
  transfers between devices with their start and end apart: 12 -> 12, of which waited for: 7 -> 8; matrix products, arithmetic and copies ran while one was open for 6% -> 3% of each run, Pallas kernels for 19% -> 20%
where the time goes in v12:
time: 109 us
  starting transfers between devices  39.5 us (36%)
  Pallas kernels  39.2 us (36%)
  waiting for transfers between devices  18.5 us (17%)
  other arithmetic  6.36 us (6%)
  local copies, waits for them, and re-layouts  2.4 us (2%)
  between operations  1.6 us (1%)
    ppermute x10, starting transfers between devices, swap(): return lax.ppermute(value, axis, [(i, i ^ mask) for i in range(size)])  18.9 us
    ppermute x10, waiting for transfers between devices, swap(): return lax.ppermute(value, axis, [(i, i ^ mask) for i in range(size)])  18.5 us
    all_to_all x1, starting transfers between devices, body(): lax.all_to_all(message.reshape(holders, 16, depth), 'prod', split_axis=0,...  11.3 us
    pallas_call x1, Pallas kernels, stats(): pl.pallas_call(kernel, grid=(consumers // block,), in_specs=[pl.BlockSpec...  9.77 us
    all_to_all x1, starting transfers between devices, body(): lax.all_to_all(sent.reshape(holders, each, depth), 'prod', split_axis=0,...  9.27 us
    pallas_call x1, Pallas kernels, share_sums(): pl.pallas_call(kernel, grid=(consumers // block,), in_specs=[pl.BlockSpec...  7.19 us
    pallas_call x1, Pallas kernels, first_panel(): pl.pallas_call(kernel, grid=(consumers // block,), in_specs=[pl.BlockSpec...  7.1 us
    pallas_call x1, Pallas kernels, prepare(): pl.pallas_call(kernel, grid=(1,), in_specs=[whole(value.shape) for value...  4.69 us
  transfers between devices with their start and end apart: 12, of which 8 were waited for; matrix products, arithmetic and copies ran while one was open for 3% of the time, Pallas kernels for 20%

profile of v12, /device:TPU:1, one launch (start us, length us, event | category | flops | bytes accessed | tf_op | source)
XLA Modules:
  0.0 108.8 jit_solution(5488048363606840884)
XLA Ops:
  0.6 4.7 %prepare.1 = (bf16[2048,256]{1,0:T(8,128)(2,1)S(1)}, bf16[512,128]{1,0:T(8,128)(2,1)}, s32[1,2048]{1,0:T(1,128)}) custom-call(bf16[2048,128]{1,0:T(8,128)(2,1)} %chars_ref.1, f32[16,128]{1,0:T(8,128)} %bitcast.49, s32[1,2048]{1,0:T(1,128)} %bitcast.45, s32[2,128]{1,0:T(2,128)} %bitcast.51), custom_call_target="tpu_custom_call" | custom-call | tf_op jit(solution)/shard_map/prepare/pallas_call | solution.py:96
  5.3 11.3 %all-to-all-start = ((bf16[32,16,128]{2,1,0:T(8,128)(2,1)}), bf16[32,16,128]{2,1,0:T(8,128)(2,1)S(1)}, u32[]{:S(2)}, u32[]{:S(2)}) async-start(bf16[32,16,128]{2,1,0:T(8,128)(2,1)} %bitcast.40), calls=%async_computation | async-start | bytes 262144 | tf_op jit(solution)/shard_map/all_to_all | solution.py:383
  16.7 1.2 %slice.71 = s32[1]{0:T(128)} slice(s32[256]{0:T(256)} %param.15), slice={[0:1]} | slice | bytes 8 | tf_op jit(solution)/shard_map/slice | solution.py:414
  18.5 9.8 %stats.1.stat_ref = f32[1,4096]{1,0:T(1,128)S(1)} custom-call(bf16[2048,256]{1,0:T(8,128)(2,1)S(1)} %get-tuple-element.56.chars_ref, bf16[4096,128]{1,0:T(8,128)(2,1)} %tastes_ref.5), custom_call_target="tpu_custom_call" | custom-call | tf_op jit(solution)/shard_map/stats/pallas_call | solution.py:135
  28.3 0.0 copy-start.4
  28.3 0.0 all-to-all-done
  28.4 0.1 copy.23
  28.6 0.1 copy.24
  28.7 0.1 pad_maximum_fusion.2.tail_ref
  28.8 0.0 copy-start
  28.8 3.3 %pick_rows.1 = (bf16[2560,128]{1,0:T(8,128)(2,1)}, f32[1,4096]{1,0:T(1,128)S(1)}) custom-call(s32[64,32]{1,0:T(8,128)S(1)} %add_bitcast_fusion.ids_ref, bf16[2048,256]{1,0:T(8,128)(2,1)S(1)} %get-tuple-element.56.chars_ref, f32[16,128]{1,0:T(8,128)S(1)} %pad_maximum_fusion.2.tail_ref, f32[1,4096]{1,0:T(1,128)S(1)} %stats.1.stat_ref), custom_call_target="tpu_custom_call" | custom-call | tf_op jit(solution)/shard_map/pick_rows/pallas_call | solution.py:171
  32.1 9.3 %all-to-all-start.1 = ((bf16[32,80,128]{2,1,0:T(8,128)(2,1)}), bf16[32,80,128]{2,1,0:T(8,128)(2,1)S(1)}, u32[]{:S(2)}, u32[]{:S(2)}) async-start(bf16[32,80,128]{2,1,0:T(8,128)(2,1)} %bitcast.12), calls=%async_computation.1 | async-start | bytes 1310720 | tf_op jit(solution)/shard_map/all_to_all | solution.py:398
  41.4 0.0 copy-start.1
  41.4 23.3 %conditional.2 = (f32[4096]{0:T(1024)S(1)}) conditional(s32[]{:T(128)} %bitcast, f32[4096]{0:T(1024)S(1)} %bitcast.41, f32[4096]{0:T(1024)S(1)} %bitcast.42), branch_computations={%region_1.2_spmd, %region_2.3_spmd} | conditional | flops 102400 | bytes 573648 | solution.py:415
  41.4 1.3 %collective-permute-start = (f32[4096]{0:T(1024)S(1)}, f32[4096]{0:T(1024)S(1)}, u32[]{:S(2)}, u32[]{:S(2)}) collective-permute-start(f32[4096]{0:T(1024)S(1)} %param.1), channel_id=1, source_target_pairs={{0,1},{1,0},{2,3},{3,2},{4,5},{5,4},{6,7},{7,6},{8,9},{9,8},{10,11... | collective-permute-start | bytes 49160 | tf_op jit(solution)/shard_map/cond/branch_1_fun/ppermute | solution.py:352
  42.7 6.6 %collective-permute-done = f32[4096]{0:T(1024)S(1)} collective-permute-done((f32[4096]{0:T(1024)S(1)}, f32[4096]{0:T(1024)S(1)}, u32[]{:S(2)}, u32[]{:S(2)}) %collective-permute-start) | collective-permute-done | bytes 16416 | tf_op jit(solution)/shard_map/cond/branch_1_fun/ppermute | solution.py:352
  49.3 1.9 %collective-permute-start.1 = (f32[4096]{0:T(1024)S(1)}, f32[4096]{0:T(1024)S(1)}, u32[]{:S(2)}, u32[]{:S(2)}) collective-permute-start(f32[4096]{0:T(1024)S(1)} %log_add_fusion.4), channel_id=1, source_target_pairs={{0,3},{1,2},{2,1},{3,0},{4,7},{5,6},{6,5},{7,4},{8,11},{9,10},{10,... | collective-permute-start | bytes 49160 | tf_op jit(solution)/shard_map/cond/branch_1_fun/ppermute | solution.py:352
  51.2 2.3 %collective-permute-done.1 = f32[4096]{0:T(1024)S(1)} collective-permute-done((f32[4096]{0:T(1024)S(1)}, f32[4096]{0:T(1024)S(1)}, u32[]{:S(2)}, u32[]{:S(2)}) %collective-permute-start.1) | collective-permute-done | bytes 16416 | tf_op jit(solution)/shard_map/cond/branch_1_fun/ppermute | solution.py:352
  53.5 1.3 %collective-permute-start.2 = (f32[4096]{0:T(1024)S(1)}, f32[4096]{0:T(1024)S(1)}, u32[]{:S(2)}, u32[]{:S(2)}) collective-permute-start(f32[4096]{0:T(1024)S(1)} %log_add_fusion.3), channel_id=1, source_target_pairs={{0,4},{1,5},{2,6},{3,7},{4,0},{5,1},{6,2},{7,3},{8,12},{9,13},{10,... | collective-permute-start | bytes 49160 | tf_op jit(solution)/shard_map/cond/branch_1_fun/ppermute | solution.py:352
  54.8 1.6 %collective-permute-done.2 = f32[4096]{0:T(1024)S(1)} collective-permute-done((f32[4096]{0:T(1024)S(1)}, f32[4096]{0:T(1024)S(1)}, u32[]{:S(2)}, u32[]{:S(2)}) %collective-permute-start.2) | collective-permute-done | bytes 16416 | tf_op jit(solution)/shard_map/cond/branch_1_fun/ppermute | solution.py:352
  56.4 2.5 %collective-permute-start.3 = (f32[4096]{0:T(1024)S(1)}, f32[4096]{0:T(1024)S(1)}, u32[]{:S(2)}, u32[]{:S(2)}) collective-permute-start(f32[4096]{0:T(1024)S(1)} %log_add_fusion.2), channel_id=1, source_target_pairs={{0,12},{1,13},{2,14},{3,15},{4,8},{5,9},{6,10},{7,11},{8,4},{9,5},... | collective-permute-start | bytes 49160 | tf_op jit(solution)/shard_map/cond/branch_1_fun/ppermute | solution.py:352
  58.9 1.4 %collective-permute-done.3 = f32[4096]{0:T(1024)S(1)} collective-permute-done((f32[4096]{0:T(1024)S(1)}, f32[4096]{0:T(1024)S(1)}, u32[]{:S(2)}, u32[]{:S(2)}) %collective-permute-start.3) | collective-permute-done | bytes 16416 | tf_op jit(solution)/shard_map/cond/branch_1_fun/ppermute | solution.py:352
  60.3 2.8 %collective-permute-start.4 = (f32[4096]{0:T(1024)S(1)}, f32[4096]{0:T(1024)S(1)}, u32[]{:S(2)}, u32[]{:S(2)}) collective-permute-start(f32[4096]{0:T(1024)S(1)} %log_add_fusion.1), channel_id=1, source_target_pairs={{0,16},{1,17},{2,18},{3,19},{4,20},{5,21},{6,22},{7,23},{8,24},{9,... | collective-permute-start | bytes 49160 | tf_op jit(solution)/shard_map/cond/branch_1_fun/ppermute | solution.py:352
  63.1 1.4 %collective-permute-done.4 = f32[4096]{0:T(1024)S(1)} collective-permute-done((f32[4096]{0:T(1024)S(1)}, f32[4096]{0:T(1024)S(1)}, u32[]{:S(2)}, u32[]{:S(2)}) %collective-permute-start.4) | collective-permute-done | bytes 16416 | tf_op jit(solution)/shard_map/cond/branch_1_fun/ppermute | solution.py:352
  64.7 0.0 copy-done.4
  64.8 0.0 all-to-all-done.1
  64.8 0.1 copy.22
  65.0 0.1 slice_select_fusion
  65.1 0.1 reshape.66.beside_ref
  65.2 0.1 fusion.12.cols_ref
  65.3 0.0 copy-done
  65.3 2.4 %place_rows.1.chars_ref = bf16[2048,256]{1,0:T(8,128)(2,1)S(1)} custom-call(s32[1,2048]{1,0:T(1,128)S(1)} %copy-done, bf16[2560,128]{1,0:T(8,128)(2,1)S(1)} %bitcast.33, f32[8,2048]{1,0:T(8,128)S(1)} %reshape.66.beside_ref, f32[3,4096]{1,0:T(4,128)S(1)} %pad_maximum_fusion.1.gate_ref.rows_ref), custom_call_target="tpu_custom_call" | custom-call | tf_op jit(solution)/shard_map/place_rows/pallas_call | solution.py:203
  67.8 0.0 copy-done.1
  67.8 7.1 %first_panel.1 = (f32[1032,256]{1,0:T(8,128)S(1)}, f32[1024,128]{1,0:T(8,128)S(1)}, bf16[256,4096]{1,0:T(8,128)(2,1)S(1)}) custom-call(bf16[2048,256]{1,0:T(8,128)(2,1)S(1)} %place_rows.1.chars_ref, bf16[4096,128]{1,0:T(8,128)(2,1)S(1)} %copy-done.1, f32[3,4096]{1,0:T(4,128)S(1)} %pad_maximum_fusion.1.gate_ref.rows_ref, bf16[256,256]{1,0:T(8,128)(2,1)S(1)} %fusion.12.cols_ref), custom_call_target="tpu_custom_call" | custom-call | flops 4294967296 | bytes 2097152 | tf_op jit(solution)/shard_map/first_panel/pallas_call | solution.py:250
  74.9 6.6 %collective-permute-start.7 = (f32[1032,256]{1,0:T(8,128)S(1)}, f32[1032,256]{1,0:T(8,128)S(1)}, u32[]{:S(2)}, u32[]{:S(2)}) collective-permute-start(f32[1032,256]{1,0:T(8,128)S(1)} %get-tuple-element.62.gate_ref), channel_id=1, source_target_pairs={{0,32},{32,0},{64,96},{96,64},{1,33},{33,1},{65,97},{97,65},{2,34}... | collective-permute-start | bytes 3170312 | tf_op jit(solution)/shard_map/ppermute | solution.py:352
  81.5 4.7 %panel.1 = (f32[1024,256]{1,0:T(8,128)S(1)}, f32[1024,128]{1,0:T(8,128)S(1)}) custom-call(bf16[2048,256]{1,0:T(8,128)(2,1)S(1)} %place_rows.1.chars_ref, bf16[4096,128]{1,0:T(8,128)(2,1)S(1)} %copy-done.1, f32[3,4096]{1,0:T(4,128)S(1)} %pad_maximum_fusion.1.gate_ref.rows_ref, bf16[256,4096]{1,0:T(8,128)(2,1)S(1)} %get-tuple-element.61.weight_ref, ...), custom_call_target="tpu_custom_call" | custom-call | flops 4294967296 | bytes 2097152 | tf_op jit(solution)/shard_map/panel/pallas_call | solution.py:292
  86.2 0.0 copy-start.3
  86.2 0.0 collective-permute-done.7
  86.2 1.0 fusion.9
  87.2 0.4 collective-permute-start.8
  87.6 0.0 copy-done.3
  87.6 0.0 copy-start.5
  87.6 13.9 %conditional.3 = (f32[4352]{0:T(1024)S(1)}, f32[256]{0:T(256)S(1)}) conditional(s32[]{:T(128)} %bitcast, () %tuple.24, (bf16[2048,256]{1,0:T(8,128)(2,1)S(1)}, bf16[4096,128]{1,0:T(8,128)(2,1)S(1)}, f32[3,4096]{1,0:T(4,128)S(1)}, f32[1,256]{1,0:T(1,128)S(1)}, pred[]{:T(512)}, /*index=5*/f32[1024,128]{1,0:T(8,128)S(1)}, f32[1024,128]{1,0:T(8,128)S(1)}, ...), branch_computations={%region_4.5_spmd, %region_5.9_spmd} | conditional | flops 561408 | bytes 2410605 | solution.py:443
  87.6 0.2 reduce_sum.43
  87.8 0.2 reduce_sum.44
  88.1 7.2 %share_sums.1 = f32[2048,128]{1,0:T(8,128)S(1)} custom-call(bf16[2048,256]{1,0:T(8,128)(2,1)S(1)} %get-tuple-element.31.chars_ref, bf16[4096,128]{1,0:T(8,128)(2,1)S(1)} %get-tuple-element.32.tastes_ref, f32[3,4096]{1,0:T(4,128)S(1)} %get-tuple-element.33.rows_ref, f32[1,256]{1,0:T(1,128)S(1)} %get-tuple-element.34.gate_ref), custom_call_target="tpu_custom_call" | custom-call | tf_op jit(solution)/shard_map/cond/branch_1_fun/share_sums/pallas_call | solution.py:334
  95.3 0.3 reduce_sum.42
  95.6 0.4 collective-permute-start.5
  96.0 0.9 collective-permute-done.5
  96.9 1.1 collective-permute-start.6
  98.0 3.5 %collective-permute-done.6 = f32[4352]{0:T(1024)S(1)} collective-permute-done((f32[4352]{0:T(1024)S(1)}, f32[4352]{0:T(1024)S(1)}, u32[]{:S(2)}, u32[]{:S(2)}) %collective-permute-start.6) | collective-permute-done | bytes 17440 | tf_op jit(solution)/shard_map/cond/branch_1_fun/ppermute | solution.py:352
  101.5 0.0 copy-start.2
  101.6 0.0 collective-permute-done.8
  101.6 0.0 copy-done.5
  101.6 1.6 %select_subtract_fusion = f32[1024,256]{1,0:T(8,128)S(1)} fusion(f16[1024,256]{1,0:T(8,128)(2,1)} %collective-permute-done.8, f16[1024,256]{1,0:T(8,128)(2,1)} %get-tuple-element.68, f32[256]{0:T(256)S(1)} %get-tuple-element.85, s32[256]{0:T(256)S(1)} %copy-done.5, f32[256]{0:T(256)S(1)} %get-tuple-element.84, f32[256]{0:T(256)S(1)} %bitcast.53, ...), kind=kLoop, calls=%fused_computation.23 | loop fusion | flops 2097152 | bytes 2105344 | tf_op jit(solution)/shard_map/sub | solution.py:459
  103.1 0.0 copy-done.2
  103.1 1.0 fusion.7
  104.2 0.8 collective-permute-start.9
  104.9 0.6 slice_bitcast_fusion.1
  105.5 0.9 multiply_reduce_fusion
  106.5 0.7 collective-permute-done.9
  107.2 1.6 %maximum_select_fusion = f32[2048,256]{1,0:T(8,128)} fusion(f32[1024,256]{1,0:T(8,128)S(1)} %collective-permute-done.9, f32[1024,256]{1,0:T(8,128)S(1)} %bitcast.35, pred[]{:T(512)} %eq.25), kind=kLoop, calls=%fused_computation.20 | loop fusion | flops 1572864 | bytes 4194305 | tf_op jit(solution)/shard_map/jit(_where)/select_n | solution.py:467
  (27 shorter events, 0.4 us)
Async XLA Ops:
  5.3 23.0 %all-to-all-start = ((bf16[32,16,128]{2,1,0:T(8,128)(2,1)}), bf16[32,16,128]{2,1,0:T(8,128)(2,1)S(1)}, u32[]{:S(2)}, u32[]{:S(2)}) async-start(bf16[32,16,128]{2,1,0:T(8,128)(2,1)} %bitcast.40), calls=%async_computation | async-start | bytes 262144 | tf_op jit(solution)/shard_map/all_to_all | solution.py:383
  28.3 36.4 %copy-start.4 = (f32[4096]{0:T(1024)S(1)}, f32[4096]{0:T(1024)}, u32[]{:S(2)}) copy-start(f32[4096]{0:T(1024)} %param.12) | copy-start | bytes 49156
  28.8 36.5 %copy-start = (s32[1,2048]{1,0:T(1,128)S(1)}, s32[1,2048]{1,0:T(1,128)}, u32[]{:S(2)}) copy-start(s32[1,2048]{1,0:T(1,128)} %get-tuple-element.59.order_ref) | copy-start | bytes 24580
  32.1 32.7 %all-to-all-start.1 = ((bf16[32,80,128]{2,1,0:T(8,128)(2,1)}), bf16[32,80,128]{2,1,0:T(8,128)(2,1)S(1)}, u32[]{:S(2)}, u32[]{:S(2)}) async-start(bf16[32,80,128]{2,1,0:T(8,128)(2,1)} %bitcast.12), calls=%async_computation.1 | async-start | bytes 1310720 | tf_op jit(solution)/shard_map/all_to_all | solution.py:398
  41.4 26.4 %copy-start.1 = (bf16[4096,128]{1,0:T(8,128)(2,1)S(1)}, bf16[4096,128]{1,0:T(8,128)(2,1)}, u32[]{:S(2)}) copy-start(bf16[4096,128]{1,0:T(8,128)(2,1)} %tastes_ref.5) | copy-start | bytes 3145732
  41.4 7.9 %collective-permute-start = (f32[4096]{0:T(1024)S(1)}, f32[4096]{0:T(1024)S(1)}, u32[]{:S(2)}, u32[]{:S(2)}) collective-permute-start(f32[4096]{0:T(1024)S(1)} %param.1), channel_id=1, source_target_pairs={{0,1},{1,0},{2,3},{3,2},{4,5},{5,4},{6,7},{7,6},{8,9},{9,8},{10,11... | collective-permute-start | bytes 49160 | tf_op jit(solution)/shard_map/cond/branch_1_fun/ppermute | solution.py:352
  49.3 4.2 %collective-permute-start.1 = (f32[4096]{0:T(1024)S(1)}, f32[4096]{0:T(1024)S(1)}, u32[]{:S(2)}, u32[]{:S(2)}) collective-permute-start(f32[4096]{0:T(1024)S(1)} %log_add_fusion.4), channel_id=1, source_target_pairs={{0,3},{1,2},{2,1},{3,0},{4,7},{5,6},{6,5},{7,4},{8,11},{9,10},{10,... | collective-permute-start | bytes 49160 | tf_op jit(solution)/shard_map/cond/branch_1_fun/ppermute | solution.py:352
  53.5 2.9 %collective-permute-start.2 = (f32[4096]{0:T(1024)S(1)}, f32[4096]{0:T(1024)S(1)}, u32[]{:S(2)}, u32[]{:S(2)}) collective-permute-start(f32[4096]{0:T(1024)S(1)} %log_add_fusion.3), channel_id=1, source_target_pairs={{0,4},{1,5},{2,6},{3,7},{4,0},{5,1},{6,2},{7,3},{8,12},{9,13},{10,... | collective-permute-start | bytes 49160 | tf_op jit(solution)/shard_map/cond/branch_1_fun/ppermute | solution.py:352
  56.4 3.9 %collective-permute-start.3 = (f32[4096]{0:T(1024)S(1)}, f32[4096]{0:T(1024)S(1)}, u32[]{:S(2)}, u32[]{:S(2)}) collective-permute-start(f32[4096]{0:T(1024)S(1)} %log_add_fusion.2), channel_id=1, source_target_pairs={{0,12},{1,13},{2,14},{3,15},{4,8},{5,9},{6,10},{7,11},{8,4},{9,5},... | collective-permute-start | bytes 49160 | tf_op jit(solution)/shard_map/cond/branch_1_fun/ppermute | solution.py:352
  60.3 4.2 %collective-permute-start.4 = (f32[4096]{0:T(1024)S(1)}, f32[4096]{0:T(1024)S(1)}, u32[]{:S(2)}, u32[]{:S(2)}) collective-permute-start(f32[4096]{0:T(1024)S(1)} %log_add_fusion.1), channel_id=1, source_target_pairs={{0,16},{1,17},{2,18},{3,19},{4,20},{5,21},{6,22},{7,23},{8,24},{9,... | collective-permute-start | bytes 49160 | tf_op jit(solution)/shard_map/cond/branch_1_fun/ppermute | solution.py:352
  74.9 11.3 %collective-permute-start.7 = (f32[1032,256]{1,0:T(8,128)S(1)}, f32[1032,256]{1,0:T(8,128)S(1)}, u32[]{:S(2)}, u32[]{:S(2)}) collective-permute-start(f32[1032,256]{1,0:T(8,128)S(1)} %get-tuple-element.62.gate_ref), channel_id=1, source_target_pairs={{0,32},{32,0},{64,96},{96,64},{1,33},{33,1},{65,97},{97,65},{2,34}... | collective-permute-start | bytes 3170312 | tf_op jit(solution)/shard_map/ppermute | solution.py:352
  86.2 1.4 %copy-start.3 = (s32[2048]{0:T(1024)S(1)}, s32[2048]{0:T(1024)}, u32[]{:S(2)}) copy-start(s32[2048]{0:T(1024)} %param.16) | copy-start | bytes 24580
  87.2 14.3 %collective-permute-start.8 = (f16[1024,256]{1,0:T(8,128)(2,1)}, f16[1024,256]{1,0:T(8,128)(2,1)}, u32[]{:S(2)}, u32[]{:S(2)}) collective-permute-start(f16[1024,256]{1,0:T(8,128)(2,1)} %get-tuple-element.68), channel_id=1, source_target_pairs={{0,64},{32,96},{64,0},{96,32},{1,65},{33,97},{65,1},{97,33},{2,66}... | collective-permute-start | bytes 1572872 | tf_op jit(solution)/shard_map/ppermute | solution.py:352
  87.6 13.9 %copy-start.5 = (s32[256]{0:T(256)S(1)}, s32[256]{0:T(256)}, u32[]{:S(2)}) copy-start(s32[256]{0:T(256)} %param.15) | copy-start | bytes 3076
  95.6 1.3 %collective-permute-start.5 = (f32[4352]{0:T(1024)S(1)}, f32[4352]{0:T(1024)S(1)}, u32[]{:S(2)}, u32[]{:S(2)}) collective-permute-start(f32[4352]{0:T(1024)S(1)} %pad_maximum_fusion), channel_id=1, source_target_pairs={{0,32},{32,0},{64,96},{96,64},{1,33},{33,1},{65,97},{97,65},{2,34}... | collective-permute-start | bytes 52232 | tf_op jit(solution)/shard_map/cond/branch_1_fun/ppermute | solution.py:352
  96.9 4.6 %collective-permute-start.6 = (f32[4352]{0:T(1024)S(1)}, f32[4352]{0:T(1024)S(1)}, u32[]{:S(2)}, u32[]{:S(2)}) collective-permute-start(f32[4352]{0:T(1024)S(1)} %fusion.5), channel_id=1, source_target_pairs={{0,64},{32,96},{64,0},{96,32},{1,65},{33,97},{65,1},{97,33},{2,66}... | collective-permute-start | bytes 52232 | tf_op jit(solution)/shard_map/cond/branch_1_fun/ppermute | solution.py:352
  101.5 1.6 %copy-start.2 = (f32[16,128,128]{2,1,0:T(8,128)S(1)}, f32[16,128,128]{2,1,0:T(8,128)}, u32[]{:S(2)}) copy-start(f32[16,128,128]{2,1,0:T(8,128)} %param.17) | copy-start | bytes 3145732
  104.2 3.1 %collective-permute-start.9 = (f32[1024,256]{1,0:T(8,128)S(1)}, f32[1024,256]{1,0:T(8,128)S(1)}, u32[]{:S(2)}, u32[]{:S(2)}) collective-permute-start(f32[1024,256]{1,0:T(8,128)S(1)} %bitcast.34), channel_id=1, source_target_pairs={{0,32},{32,0},{64,96},{96,64},{1,33},{33,1},{65,97},{97,65},{2,34}... | collective-permute-start | bytes 3145736 | tf_op jit(solution)/shard_map/ppermute | solution.py:352

commit v13 on v12

--- a/solution.py
+++ b/solution.py
@@ -82,6 +82,7 @@
             hot = jnp.where(wide[:, k : k + 1] == products, 1.0, 0.0).astype(jnp.bfloat16)
             part = jnp.dot(hot, both, preferred_element_type=jnp.float32)
             part_pieces = part[:, depth:].T[:8, :]
+            part_pieces = jnp.concatenate([part_pieces[4:8, :], part_pieces[0:4, :]], axis=0)
             for place in range(128 // share_cols):
                 q = k * (128 // share_cols) + place
                 start = q * per_pair // 128 * 128 % chunk
@@ -156,6 +157,7 @@
         stat_out_ref[...] = stat_ref[...]
         lanes = lax.broadcasted_iota(jnp.int32, (per_pair, rows), 1)
         table = chars_ref[...]
+        pieces = jnp.where(lax.broadcasted_iota(jnp.int32, (8, 128), 0) >= 5, tail_ref[8:16, :], 0.0)
         for start in range(0, holders, group):
             span = range(start, start + group)
             marks = [jnp.where(ids_ref[:, q : q + 1] == lanes, 1.0, 0.0).astype(jnp.bfloat16) for q in span]
@@ -163,7 +165,7 @@
             for place, q in enumerate(span):
                 if place % pair == 0:
                     beside = picked[place * per_pair : (place + pair) * per_pair, 128:].T[:8, :]
-                    block = jnp.concatenate([beside + tail_ref[0:8, :], tail_ref[8:16, :]], axis=0).astype(jnp.bfloat16)
+                    block = jnp.concatenate([beside + pieces, tail_ref[0:8, :]], axis=0).astype(jnp.bfloat16)
                 mine = picked[place * per_pair : (place + 1) * per_pair, :128]
                 out_ref[q * each : q * each + per_pair, :] = mine.astype(jnp.bfloat16)
                 out_ref[q * each + per_pair : (q + 1) * each, :] = block
@@ -392,9 +394,8 @@
     high, low = own_lanes(first[:, 8, :]), own_lanes(first[:, 12, :])
     ids = high.astype(jnp.int32) * 256 + low.astype(jnp.int32)
     summed = jnp.sum(first.astype(jnp.float32), axis=0)
-    tail = jnp.concatenate([jnp.zeros((5, depth), jnp.float32), summed[9:12], summed[:8]], axis=0)
     each = per_pair + 16
-    sent, stat = pick_rows(ids.T, chars, tail, stat)
+    sent, stat = pick_rows(ids.T, chars, summed, stat)
     second = lax.all_to_all(sent.reshape(holders, each, depth), "prod", split_axis=0, concat_axis=0, tiled=True)
     col_pieces = second[:: 128 // share_cols, per_pair + 5 : per_pair + 8, :].transpose(0, 2, 1).reshape(cols, 3)
     col_chars = second[:, per_pair + 8 :, :].reshape(cols, depth)
@@ -411,7 +412,7 @@
         return stat
 
     masks = butterfly_masks(holders)
-    taken = panel_cols[0] >= 0
+    taken = ids[0, 0] >= 0
     total = lax.cond(taken, lambda value: join(value, masks), lambda value: value, stat[0])
     peak = jnp.maximum(total, 0.0)
     denom = jnp.exp(-peak) + jnp.exp(total - peak)

time: 109 us -> 108 us (level)
  transfers between devices with their start and end apart: 12 -> 12, of which waited for: 8 -> 8; matrix products, arithmetic and copies ran while one was open for 3% -> 2% of each run, Pallas kernels for 20% -> 20%
where the time goes in v13:
time: 108 us; the launch traced here: 107 us
  starting transfers between devices  39.6 us (37%)
  Pallas kernels  39.2 us (36%)
  waiting for transfers between devices  17.7 us (16%)
  other arithmetic  6.28 us (6%)
  local copies, waits for them, and re-layouts  1.71 us (2%)
  between operations  1.66 us (2%)
    ppermute x10, starting transfers between devices, swap(): return lax.ppermute(value, axis, [(i, i ^ mask) for i in range(size)])  18.9 us
    ppermute x10, waiting for transfers between devices, swap(): return lax.ppermute(value, axis, [(i, i ^ mask) for i in range(size)])  17.7 us
    all_to_all x1, starting transfers between devices, body(): lax.all_to_all(message.reshape(holders, 16, depth), 'prod', split_axis=0,...  11.3 us
    pallas_call x1, Pallas kernels, stats(): pl.pallas_call(kernel, grid=(consumers // block,), in_specs=[pl.BlockSpec...  9.78 us
    all_to_all x1, starting transfers between devices, body(): lax.all_to_all(sent.reshape(holders, each, depth), 'prod', split_axis=0,...  9.27 us
    pallas_call x1, Pallas kernels, share_sums(): pl.pallas_call(kernel, grid=(consumers // block,), in_specs=[pl.BlockSpec...  7.19 us
    pallas_call x1, Pallas kernels, first_panel(): pl.pallas_call(kernel, grid=(consumers // block,), in_specs=[pl.BlockSpec...  7.08 us
    pallas_call x1, Pallas kernels, prepare(): pl.pallas_call(kernel, grid=(1,), in_specs=[whole(value.shape) for value...  4.69 us
  transfers between devices with their start and end apart: 12, of which 8 were waited for; matrix products, arithmetic and copies ran while one was open for 2% of the time, Pallas kernels for 20%

profile of v13, /device:TPU:1, one launch (start us, length us, event | category | flops | bytes accessed | tf_op | source)
XLA Modules:
  0.0 107.4 jit_solution(13759152309545417661)
XLA Ops:
  0.6 4.7 %prepare.1 = (bf16[2048,256]{1,0:T(8,128)(2,1)S(1)}, bf16[512,128]{1,0:T(8,128)(2,1)}, s32[1,2048]{1,0:T(1,128)}) custom-call(bf16[2048,128]{1,0:T(8,128)(2,1)} %chars_ref.1, f32[16,128]{1,0:T(8,128)} %bitcast.49, s32[1,2048]{1,0:T(1,128)} %bitcast.45, s32[2,128]{1,0:T(2,128)} %bitcast.51), custom_call_target="tpu_custom_call" | custom-call | tf_op jit(solution)/shard_map/prepare/pallas_call | solution.py:97
  5.3 11.3 %all-to-all-start = ((bf16[32,16,128]{2,1,0:T(8,128)(2,1)}), bf16[32,16,128]{2,1,0:T(8,128)(2,1)S(1)}, u32[]{:S(2)}, u32[]{:S(2)}) async-start(bf16[32,16,128]{2,1,0:T(8,128)(2,1)} %bitcast.40), calls=%async_computation | async-start | bytes 262144 | tf_op jit(solution)/shard_map/all_to_all | solution.py:385
  16.7 9.8 %stats.1.stat_ref = f32[1,4096]{1,0:T(1,128)S(1)} custom-call(bf16[2048,256]{1,0:T(8,128)(2,1)S(1)} %get-tuple-element.57.chars_ref, bf16[4096,128]{1,0:T(8,128)(2,1)} %tastes_ref.5), custom_call_target="tpu_custom_call" | custom-call | tf_op jit(solution)/shard_map/stats/pallas_call | solution.py:136
  26.5 0.0 copy-start.4
  26.5 0.0 all-to-all-done
  26.5 0.1 copy.23
  26.6 0.1 copy.24
  26.8 0.5 slice.90
  27.4 0.0 copy-start
  27.4 3.3 %pick_rows.1 = (bf16[2560,128]{1,0:T(8,128)(2,1)}, f32[1,4096]{1,0:T(1,128)S(1)}) custom-call(s32[64,32]{1,0:T(8,128)S(1)} %bitcast.33, bf16[2048,256]{1,0:T(8,128)(2,1)S(1)} %get-tuple-element.57.chars_ref, f32[16,128]{1,0:T(8,128)S(1)} %convert_reduce_fusion.tail_ref, f32[1,4096]{1,0:T(1,128)S(1)} %stats.1.stat_ref), custom_call_target="tpu_custom_call" | custom-call | tf_op jit(solution)/shard_map/pick_rows/pallas_call | solution.py:173
  30.7 9.3 %all-to-all-start.1 = ((bf16[32,80,128]{2,1,0:T(8,128)(2,1)}), bf16[32,80,128]{2,1,0:T(8,128)(2,1)S(1)}, u32[]{:S(2)}, u32[]{:S(2)}) async-start(bf16[32,80,128]{2,1,0:T(8,128)(2,1)} %bitcast.12), calls=%async_computation.1 | async-start | bytes 1310720 | tf_op jit(solution)/shard_map/all_to_all | solution.py:399
  39.9 0.0 copy-start.1
  40.7 22.5 %conditional.2 = (f32[4096]{0:T(1024)S(1)}) conditional(s32[]{:T(128)} %bitcast.6, f32[4096]{0:T(1024)S(1)} %bitcast.41, f32[4096]{0:T(1024)S(1)} %bitcast.42), branch_computations={%region_1.2_spmd, %region_2.3_spmd} | conditional | flops 102400 | bytes 573648 | solution.py:416
  40.7 1.3 %collective-permute-start = (f32[4096]{0:T(1024)S(1)}, f32[4096]{0:T(1024)S(1)}, u32[]{:S(2)}, u32[]{:S(2)}) collective-permute-start(f32[4096]{0:T(1024)S(1)} %param.1), channel_id=1, source_target_pairs={{0,1},{1,0},{2,3},{3,2},{4,5},{5,4},{6,7},{7,6},{8,9},{9,8},{10,11... | collective-permute-start | bytes 49160 | tf_op jit(solution)/shard_map/cond/branch_1_fun/ppermute | solution.py:354
  42.0 5.8 %collective-permute-done = f32[4096]{0:T(1024)S(1)} collective-permute-done((f32[4096]{0:T(1024)S(1)}, f32[4096]{0:T(1024)S(1)}, u32[]{:S(2)}, u32[]{:S(2)}) %collective-permute-start) | collective-permute-done | bytes 16416 | tf_op jit(solution)/shard_map/cond/branch_1_fun/ppermute | solution.py:354
  47.9 1.9 %collective-permute-start.1 = (f32[4096]{0:T(1024)S(1)}, f32[4096]{0:T(1024)S(1)}, u32[]{:S(2)}, u32[]{:S(2)}) collective-permute-start(f32[4096]{0:T(1024)S(1)} %log_add_fusion.4), channel_id=1, source_target_pairs={{0,3},{1,2},{2,1},{3,0},{4,7},{5,6},{6,5},{7,4},{8,11},{9,10},{10,... | collective-permute-start | bytes 49160 | tf_op jit(solution)/shard_map/cond/branch_1_fun/ppermute | solution.py:354
  49.7 2.3 %collective-permute-done.1 = f32[4096]{0:T(1024)S(1)} collective-permute-done((f32[4096]{0:T(1024)S(1)}, f32[4096]{0:T(1024)S(1)}, u32[]{:S(2)}, u32[]{:S(2)}) %collective-permute-start.1) | collective-permute-done | bytes 16416 | tf_op jit(solution)/shard_map/cond/branch_1_fun/ppermute | solution.py:354
  52.1 1.3 %collective-permute-start.2 = (f32[4096]{0:T(1024)S(1)}, f32[4096]{0:T(1024)S(1)}, u32[]{:S(2)}, u32[]{:S(2)}) collective-permute-start(f32[4096]{0:T(1024)S(1)} %log_add_fusion.3), channel_id=1, source_target_pairs={{0,4},{1,5},{2,6},{3,7},{4,0},{5,1},{6,2},{7,3},{8,12},{9,13},{10,... | collective-permute-start | bytes 49160 | tf_op jit(solution)/shard_map/cond/branch_1_fun/ppermute | solution.py:354
  53.3 1.6 %collective-permute-done.2 = f32[4096]{0:T(1024)S(1)} collective-permute-done((f32[4096]{0:T(1024)S(1)}, f32[4096]{0:T(1024)S(1)}, u32[]{:S(2)}, u32[]{:S(2)}) %collective-permute-start.2) | collective-permute-done | bytes 16416 | tf_op jit(solution)/shard_map/cond/branch_1_fun/ppermute | solution.py:354
  55.0 2.5 %collective-permute-start.3 = (f32[4096]{0:T(1024)S(1)}, f32[4096]{0:T(1024)S(1)}, u32[]{:S(2)}, u32[]{:S(2)}) collective-permute-start(f32[4096]{0:T(1024)S(1)} %log_add_fusion.2), channel_id=1, source_target_pairs={{0,12},{1,13},{2,14},{3,15},{4,8},{5,9},{6,10},{7,11},{8,4},{9,5},... | collective-permute-start | bytes 49160 | tf_op jit(solution)/shard_map/cond/branch_1_fun/ppermute | solution.py:354
  57.4 1.4 %collective-permute-done.3 = f32[4096]{0:T(1024)S(1)} collective-permute-done((f32[4096]{0:T(1024)S(1)}, f32[4096]{0:T(1024)S(1)}, u32[]{:S(2)}, u32[]{:S(2)}) %collective-permute-start.3) | collective-permute-done | bytes 16416 | tf_op jit(solution)/shard_map/cond/branch_1_fun/ppermute | solution.py:354
  58.9 2.8 %collective-permute-start.4 = (f32[4096]{0:T(1024)S(1)}, f32[4096]{0:T(1024)S(1)}, u32[]{:S(2)}, u32[]{:S(2)}) collective-permute-start(f32[4096]{0:T(1024)S(1)} %log_add_fusion.1), channel_id=1, source_target_pairs={{0,16},{1,17},{2,18},{3,19},{4,20},{5,21},{6,22},{7,23},{8,24},{9,... | collective-permute-start | bytes 49160 | tf_op jit(solution)/shard_map/cond/branch_1_fun/ppermute | solution.py:354
  61.6 1.4 %collective-permute-done.4 = f32[4096]{0:T(1024)S(1)} collective-permute-done((f32[4096]{0:T(1024)S(1)}, f32[4096]{0:T(1024)S(1)}, u32[]{:S(2)}, u32[]{:S(2)}) %collective-permute-start.4) | collective-permute-done | bytes 16416 | tf_op jit(solution)/shard_map/cond/branch_1_fun/ppermute | solution.py:354
  63.3 0.0 copy-done.4
  63.3 0.0 all-to-all-done.1
  63.4 0.1 copy.22
  63.5 0.1 slice_select_fusion
  63.7 0.1 reshape.66.beside_ref
  63.8 0.1 fusion.12.cols_ref
  63.9 0.0 copy-done
  63.9 2.4 %place_rows.1.chars_ref = bf16[2048,256]{1,0:T(8,128)(2,1)S(1)} custom-call(s32[1,2048]{1,0:T(1,128)S(1)} %copy-done, bf16[2560,128]{1,0:T(8,128)(2,1)S(1)} %bitcast.32, f32[8,2048]{1,0:T(8,128)S(1)} %reshape.66.beside_ref, f32[3,4096]{1,0:T(4,128)S(1)} %pad_maximum_fusion.1.gate_ref.rows_ref), custom_call_target="tpu_custom_call" | custom-call | tf_op jit(solution)/shard_map/place_rows/pallas_call | solution.py:205
  66.3 0.0 copy-done.1
  66.4 7.1 %first_panel.1 = (f32[1032,256]{1,0:T(8,128)S(1)}, f32[1024,128]{1,0:T(8,128)S(1)}, bf16[256,4096]{1,0:T(8,128)(2,1)S(1)}) custom-call(bf16[2048,256]{1,0:T(8,128)(2,1)S(1)} %place_rows.1.chars_ref, bf16[4096,128]{1,0:T(8,128)(2,1)S(1)} %copy-done.1, f32[3,4096]{1,0:T(4,128)S(1)} %pad_maximum_fusion.1.gate_ref.rows_ref, bf16[256,256]{1,0:T(8,128)(2,1)S(1)} %fusion.12.cols_ref), custom_call_target="tpu_custom_call" | custom-call | flops 4294967296 | bytes 2097152 | tf_op jit(solution)/shard_map/first_panel/pallas_call | solution.py:252
  73.4 6.6 %collective-permute-start.7 = (f32[1032,256]{1,0:T(8,128)S(1)}, f32[1032,256]{1,0:T(8,128)S(1)}, u32[]{:S(2)}, u32[]{:S(2)}) collective-permute-start(f32[1032,256]{1,0:T(8,128)S(1)} %get-tuple-element.62.gate_ref), channel_id=1, source_target_pairs={{0,32},{32,0},{64,96},{96,64},{1,33},{33,1},{65,97},{97,65},{2,34}... | collective-permute-start | bytes 3170312 | tf_op jit(solution)/shard_map/ppermute | solution.py:354
  80.1 4.7 %panel.1 = (f32[1024,256]{1,0:T(8,128)S(1)}, f32[1024,128]{1,0:T(8,128)S(1)}) custom-call(bf16[2048,256]{1,0:T(8,128)(2,1)S(1)} %place_rows.1.chars_ref, bf16[4096,128]{1,0:T(8,128)(2,1)S(1)} %copy-done.1, f32[3,4096]{1,0:T(4,128)S(1)} %pad_maximum_fusion.1.gate_ref.rows_ref, bf16[256,4096]{1,0:T(8,128)(2,1)S(1)} %get-tuple-element.61.weight_ref, ...), custom_call_target="tpu_custom_call" | custom-call | flops 4294967296 | bytes 2097152 | tf_op jit(solution)/shard_map/panel/pallas_call | solution.py:294
  84.8 0.0 copy-start.3
  84.8 0.0 collective-permute-done.7
  84.8 1.0 fusion.9
  85.8 0.4 collective-permute-start.8
  86.2 0.0 copy-done.3
  86.2 0.0 copy-start.5
  86.2 13.9 %conditional.3 = (f32[4352]{0:T(1024)S(1)}, f32[256]{0:T(256)S(1)}) conditional(s32[]{:T(128)} %bitcast.6, () %tuple.24, (bf16[2048,256]{1,0:T(8,128)(2,1)S(1)}, bf16[4096,128]{1,0:T(8,128)(2,1)S(1)}, f32[3,4096]{1,0:T(4,128)S(1)}, f32[1,256]{1,0:T(1,128)S(1)}, pred[]{:T(512)}, /*index=5*/f32[1024,128]{1,0:T(8,128)S(1)}, f32[1024,128]{1,0:T(8,128)S(1)}, ...), branch_computations={%region_4.5_spmd, %region_5.9_spmd} | conditional | flops 561408 | bytes 2410605 | solution.py:444
  86.2 0.2 reduce_sum.43
  86.4 0.2 reduce_sum.44
  86.6 7.2 %share_sums.1 = f32[2048,128]{1,0:T(8,128)S(1)} custom-call(bf16[2048,256]{1,0:T(8,128)(2,1)S(1)} %get-tuple-element.31.chars_ref, bf16[4096,128]{1,0:T(8,128)(2,1)S(1)} %get-tuple-element.32.tastes_ref, f32[3,4096]{1,0:T(4,128)S(1)} %get-tuple-element.33.rows_ref, f32[1,256]{1,0:T(1,128)S(1)} %get-tuple-element.34.gate_ref), custom_call_target="tpu_custom_call" | custom-call | tf_op jit(solution)/shard_map/cond/branch_1_fun/share_sums/pallas_call | solution.py:336
  93.8 0.3 reduce_sum.42
  94.2 0.4 collective-permute-start.5
  94.6 0.9 collective-permute-done.5
  95.5 1.1 collective-permute-start.6
  96.5 3.5 %collective-permute-done.6 = f32[4352]{0:T(1024)S(1)} collective-permute-done((f32[4352]{0:T(1024)S(1)}, f32[4352]{0:T(1024)S(1)}, u32[]{:S(2)}, u32[]{:S(2)}) %collective-permute-start.6) | collective-permute-done | bytes 17440 | tf_op jit(solution)/shard_map/cond/branch_1_fun/ppermute | solution.py:354
  100.1 0.0 copy-start.2
  100.1 0.0 collective-permute-done.8
  100.1 0.0 copy-done.5
  100.1 1.6 %select_subtract_fusion = f32[1024,256]{1,0:T(8,128)S(1)} fusion(f16[1024,256]{1,0:T(8,128)(2,1)} %collective-permute-done.8, f16[1024,256]{1,0:T(8,128)(2,1)} %get-tuple-element.68, f32[256]{0:T(256)S(1)} %get-tuple-element.85, s32[256]{0:T(256)S(1)} %copy-done.5, f32[256]{0:T(256)S(1)} %get-tuple-element.84, f32[256]{0:T(256)S(1)} %bitcast.53, ...), kind=kLoop, calls=%fused_computation.23 | loop fusion | flops 2097152 | bytes 2105344 | tf_op jit(solution)/shard_map/sub | solution.py:460
  101.7 0.0 copy-done.2
  101.7 1.0 fusion.7
  102.7 0.8 collective-permute-start.9
  103.5 0.6 slice_bitcast_fusion.1
  104.1 0.9 multiply_reduce_fusion
  105.1 0.7 collective-permute-done.9
  105.8 1.6 %maximum_select_fusion = f32[2048,256]{1,0:T(8,128)} fusion(f32[1024,256]{1,0:T(8,128)S(1)} %collective-permute-done.9, f32[1024,256]{1,0:T(8,128)S(1)} %bitcast.35, pred[]{:T(512)} %eq.25), kind=kLoop, calls=%fused_computation.20 | loop fusion | flops 1572864 | bytes 4194305 | tf_op jit(solution)/shard_map/jit(_where)/select_n | solution.py:468
  (23 shorter events, 0.4 us)
Async XLA Ops:
  5.3 21.2 %all-to-all-start = ((bf16[32,16,128]{2,1,0:T(8,128)(2,1)}), bf16[32,16,128]{2,1,0:T(8,128)(2,1)S(1)}, u32[]{:S(2)}, u32[]{:S(2)}) async-start(bf16[32,16,128]{2,1,0:T(8,128)(2,1)} %bitcast.40), calls=%async_computation | async-start | bytes 262144 | tf_op jit(solution)/shard_map/all_to_all | solution.py:385
  26.5 36.8 %copy-start.4 = (f32[4096]{0:T(1024)S(1)}, f32[4096]{0:T(1024)}, u32[]{:S(2)}) copy-start(f32[4096]{0:T(1024)} %param.12) | copy-start | bytes 49156
  27.4 36.5 %copy-start = (s32[1,2048]{1,0:T(1,128)S(1)}, s32[1,2048]{1,0:T(1,128)}, u32[]{:S(2)}) copy-start(s32[1,2048]{1,0:T(1,128)} %get-tuple-element.59.order_ref) | copy-start | bytes 24580
  30.7 32.7 %all-to-all-start.1 = ((bf16[32,80,128]{2,1,0:T(8,128)(2,1)}), bf16[32,80,128]{2,1,0:T(8,128)(2,1)S(1)}, u32[]{:S(2)}, u32[]{:S(2)}) async-start(bf16[32,80,128]{2,1,0:T(8,128)(2,1)} %bitcast.12), calls=%async_computation.1 | async-start | bytes 1310720 | tf_op jit(solution)/shard_map/all_to_all | solution.py:399
  39.9 26.4 %copy-start.1 = (bf16[4096,128]{1,0:T(8,128)(2,1)S(1)}, bf16[4096,128]{1,0:T(8,128)(2,1)}, u32[]{:S(2)}) copy-start(bf16[4096,128]{1,0:T(8,128)(2,1)} %tastes_ref.5) | copy-start | bytes 3145732
  40.7 7.1 %collective-permute-start = (f32[4096]{0:T(1024)S(1)}, f32[4096]{0:T(1024)S(1)}, u32[]{:S(2)}, u32[]{:S(2)}) collective-permute-start(f32[4096]{0:T(1024)S(1)} %param.1), channel_id=1, source_target_pairs={{0,1},{1,0},{2,3},{3,2},{4,5},{5,4},{6,7},{7,6},{8,9},{9,8},{10,11... | collective-permute-start | bytes 49160 | tf_op jit(solution)/shard_map/cond/branch_1_fun/ppermute | solution.py:354
  47.9 4.2 %collective-permute-start.1 = (f32[4096]{0:T(1024)S(1)}, f32[4096]{0:T(1024)S(1)}, u32[]{:S(2)}, u32[]{:S(2)}) collective-permute-start(f32[4096]{0:T(1024)S(1)} %log_add_fusion.4), channel_id=1, source_target_pairs={{0,3},{1,2},{2,1},{3,0},{4,7},{5,6},{6,5},{7,4},{8,11},{9,10},{10,... | collective-permute-start | bytes 49160 | tf_op jit(solution)/shard_map/cond/branch_1_fun/ppermute | solution.py:354
  52.1 2.9 %collective-permute-start.2 = (f32[4096]{0:T(1024)S(1)}, f32[4096]{0:T(1024)S(1)}, u32[]{:S(2)}, u32[]{:S(2)}) collective-permute-start(f32[4096]{0:T(1024)S(1)} %log_add_fusion.3), channel_id=1, source_target_pairs={{0,4},{1,5},{2,6},{3,7},{4,0},{5,1},{6,2},{7,3},{8,12},{9,13},{10,... | collective-permute-start | bytes 49160 | tf_op jit(solution)/shard_map/cond/branch_1_fun/ppermute | solution.py:354
  55.0 3.9 %collective-permute-start.3 = (f32[4096]{0:T(1024)S(1)}, f32[4096]{0:T(1024)S(1)}, u32[]{:S(2)}, u32[]{:S(2)}) collective-permute-start(f32[4096]{0:T(1024)S(1)} %log_add_fusion.2), channel_id=1, source_target_pairs={{0,12},{1,13},{2,14},{3,15},{4,8},{5,9},{6,10},{7,11},{8,4},{9,5},... | collective-permute-start | bytes 49160 | tf_op jit(solution)/shard_map/cond/branch_1_fun/ppermute | solution.py:354
  58.9 4.2 %collective-permute-start.4 = (f32[4096]{0:T(1024)S(1)}, f32[4096]{0:T(1024)S(1)}, u32[]{:S(2)}, u32[]{:S(2)}) collective-permute-start(f32[4096]{0:T(1024)S(1)} %log_add_fusion.1), channel_id=1, source_target_pairs={{0,16},{1,17},{2,18},{3,19},{4,20},{5,21},{6,22},{7,23},{8,24},{9,... | collective-permute-start | bytes 49160 | tf_op jit(solution)/shard_map/cond/branch_1_fun/ppermute | solution.py:354
  73.4 11.3 %collective-permute-start.7 = (f32[1032,256]{1,0:T(8,128)S(1)}, f32[1032,256]{1,0:T(8,128)S(1)}, u32[]{:S(2)}, u32[]{:S(2)}) collective-permute-start(f32[1032,256]{1,0:T(8,128)S(1)} %get-tuple-element.62.gate_ref), channel_id=1, source_target_pairs={{0,32},{32,0},{64,96},{96,64},{1,33},{33,1},{65,97},{97,65},{2,34}... | collective-permute-start | bytes 3170312 | tf_op jit(solution)/shard_map/ppermute | solution.py:354
  84.8 1.4 %copy-start.3 = (s32[2048]{0:T(1024)S(1)}, s32[2048]{0:T(1024)}, u32[]{:S(2)}) copy-start(s32[2048]{0:T(1024)} %param.16) | copy-start | bytes 24580
  85.8 14.3 %collective-permute-start.8 = (f16[1024,256]{1,0:T(8,128)(2,1)}, f16[1024,256]{1,0:T(8,128)(2,1)}, u32[]{:S(2)}, u32[]{:S(2)}) collective-permute-start(f16[1024,256]{1,0:T(8,128)(2,1)} %get-tuple-element.68), channel_id=1, source_target_pairs={{0,64},{32,96},{64,0},{96,32},{1,65},{33,97},{65,1},{97,33},{2,66}... | collective-permute-start | bytes 1572872 | tf_op jit(solution)/shard_map/ppermute | solution.py:354
  86.2 13.9 %copy-start.5 = (s32[256]{0:T(256)S(1)}, s32[256]{0:T(256)}, u32[]{:S(2)}) copy-start(s32[256]{0:T(256)} %param.15) | copy-start | bytes 3076
  94.2 1.3 %collective-permute-start.5 = (f32[4352]{0:T(1024)S(1)}, f32[4352]{0:T(1024)S(1)}, u32[]{:S(2)}, u32[]{:S(2)}) collective-permute-start(f32[4352]{0:T(1024)S(1)} %pad_maximum_fusion), channel_id=1, source_target_pairs={{0,32},{32,0},{64,96},{96,64},{1,33},{33,1},{65,97},{97,65},{2,34}... | collective-permute-start | bytes 52232 | tf_op jit(solution)/shard_map/cond/branch_1_fun/ppermute | solution.py:354
  95.5 4.6 %collective-permute-start.6 = (f32[4352]{0:T(1024)S(1)}, f32[4352]{0:T(1024)S(1)}, u32[]{:S(2)}, u32[]{:S(2)}) collective-permute-start(f32[4352]{0:T(1024)S(1)} %fusion.5), channel_id=1, source_target_pairs={{0,64},{32,96},{64,0},{96,32},{1,65},{33,97},{65,1},{97,33},{2,66}... | collective-permute-start | bytes 52232 | tf_op jit(solution)/shard_map/cond/branch_1_fun/ppermute | solution.py:354
  100.1 1.6 %copy-start.2 = (f32[16,128,128]{2,1,0:T(8,128)S(1)}, f32[16,128,128]{2,1,0:T(8,128)}, u32[]{:S(2)}) copy-start(f32[16,128,128]{2,1,0:T(8,128)} %param.17) | copy-start | bytes 3145732
  102.7 3.1 %collective-permute-start.9 = (f32[1024,256]{1,0:T(8,128)S(1)}, f32[1024,256]{1,0:T(8,128)S(1)}, u32[]{:S(2)}, u32[]{:S(2)}) collective-permute-start(f32[1024,256]{1,0:T(8,128)S(1)} %bitcast.34), channel_id=1, source_target_pairs={{0,32},{32,0},{64,96},{96,64},{1,33},{33,1},{65,97},{97,65},{2,34}... | collective-permute-start | bytes 3145736 | tf_op jit(solution)/shard_map/ppermute | solution.py:354

commit v14 on v13

--- a/solution.py
+++ b/solution.py
@@ -222,7 +222,7 @@
     rows, depth = chars.shape[0] // parts, chars.shape[1]
     consumers = tastes.shape[0]
     cols = col_chars.shape[0]
-    block, chunk = 1024, 256
+    block, chunk = 2048, 256
 
     def kernel(chars_ref, tastes_ref, rows_ref, cols_ref, panel_ref, share_ref, weight_ref, diag_ref):
         step = pl.program_id(0)

time: 108 us -> 107 us (level)
  no operation moved by 1% of the time
where the time goes in v14:
time: 107 us
  starting transfers between devices  39.5 us (37%)
  Pallas kernels  38.7 us (36%)
  waiting for transfers between devices  17.7 us (17%)
  other arithmetic  6.28 us (6%)
  local copies, waits for them, and re-layouts  1.71 us (2%)
  between operations  1.66 us (2%)
    ppermute x10, starting transfers between devices, swap(): return lax.ppermute(value, axis, [(i, i ^ mask) for i in range(size)])  18.9 us
    ppermute x10, waiting for transfers between devices, swap(): return lax.ppermute(value, axis, [(i, i ^ mask) for i in range(size)])  17.7 us
    all_to_all x1, starting transfers between devices, body(): lax.all_to_all(message.reshape(holders, 16, depth), 'prod', split_axis=0,...  11.3 us
    pallas_call x1, Pallas kernels, stats(): pl.pallas_call(kernel, grid=(consumers // block,), in_specs=[pl.BlockSpec...  9.78 us
    all_to_all x1, starting transfers between devices, body(): lax.all_to_all(sent.reshape(holders, each, depth), 'prod', split_axis=0,...  9.27 us
    pallas_call x1, Pallas kernels, share_sums(): pl.pallas_call(kernel, grid=(consumers // block,), in_specs=[pl.BlockSpec...  7.19 us
    pallas_call x1, Pallas kernels, first_panel(): pl.pallas_call(kernel, grid=(consumers // block,), in_specs=[pl.BlockSpec...  6.63 us
    pallas_call x1, Pallas kernels, prepare(): pl.pallas_call(kernel, grid=(1,), in_specs=[whole(value.shape) for value...  4.69 us
  transfers between devices with their start and end apart: 12, of which 8 were waited for; matrix products, arithmetic and copies ran while one was open for 2% of the time, Pallas kernels for 20%

profile of v14, /device:TPU:1, one launch (start us, length us, event | category | flops | bytes accessed | tf_op | source)
XLA Modules:
  0.0 106.9 jit_solution(9456818208069697466)
XLA Ops:
  0.6 4.7 %prepare.1 = (bf16[2048,256]{1,0:T(8,128)(2,1)S(1)}, bf16[512,128]{1,0:T(8,128)(2,1)}, s32[1,2048]{1,0:T(1,128)}) custom-call(bf16[2048,128]{1,0:T(8,128)(2,1)} %chars_ref.1, f32[16,128]{1,0:T(8,128)} %bitcast.49, s32[1,2048]{1,0:T(1,128)} %bitcast.45, s32[2,128]{1,0:T(2,128)} %bitcast.51), custom_call_target="tpu_custom_call" | custom-call | tf_op jit(solution)/shard_map/prepare/pallas_call | solution.py:97
  5.3 11.3 %all-to-all-start = ((bf16[32,16,128]{2,1,0:T(8,128)(2,1)}), bf16[32,16,128]{2,1,0:T(8,128)(2,1)S(1)}, u32[]{:S(2)}, u32[]{:S(2)}) async-start(bf16[32,16,128]{2,1,0:T(8,128)(2,1)} %bitcast.40), calls=%async_computation | async-start | bytes 262144 | tf_op jit(solution)/shard_map/all_to_all | solution.py:385
  16.7 9.8 %stats.1.stat_ref = f32[1,4096]{1,0:T(1,128)S(1)} custom-call(bf16[2048,256]{1,0:T(8,128)(2,1)S(1)} %get-tuple-element.57.chars_ref, bf16[4096,128]{1,0:T(8,128)(2,1)} %tastes_ref.5), custom_call_target="tpu_custom_call" | custom-call | tf_op jit(solution)/shard_map/stats/pallas_call | solution.py:136
  26.5 0.0 copy-start.4
  26.5 0.0 all-to-all-done
  26.5 0.1 copy.23
  26.6 0.1 copy.24
  26.8 0.5 slice.90
  27.4 0.0 copy-start
  27.4 3.3 %pick_rows.1 = (bf16[2560,128]{1,0:T(8,128)(2,1)}, f32[1,4096]{1,0:T(1,128)S(1)}) custom-call(s32[64,32]{1,0:T(8,128)S(1)} %bitcast.33, bf16[2048,256]{1,0:T(8,128)(2,1)S(1)} %get-tuple-element.57.chars_ref, f32[16,128]{1,0:T(8,128)S(1)} %convert_reduce_fusion.tail_ref, f32[1,4096]{1,0:T(1,128)S(1)} %stats.1.stat_ref), custom_call_target="tpu_custom_call" | custom-call | tf_op jit(solution)/shard_map/pick_rows/pallas_call | solution.py:173
  30.7 9.3 %all-to-all-start.1 = ((bf16[32,80,128]{2,1,0:T(8,128)(2,1)}), bf16[32,80,128]{2,1,0:T(8,128)(2,1)S(1)}, u32[]{:S(2)}, u32[]{:S(2)}) async-start(bf16[32,80,128]{2,1,0:T(8,128)(2,1)} %bitcast.12), calls=%async_computation.1 | async-start | bytes 1310720 | tf_op jit(solution)/shard_map/all_to_all | solution.py:399
  39.9 0.0 copy-start.1
  40.7 22.5 %conditional.2 = (f32[4096]{0:T(1024)S(1)}) conditional(s32[]{:T(128)} %bitcast.6, f32[4096]{0:T(1024)S(1)} %bitcast.41, f32[4096]{0:T(1024)S(1)} %bitcast.42), branch_computations={%region_1.2_spmd, %region_2.3_spmd} | conditional | flops 102400 | bytes 573648 | solution.py:416
  40.7 1.3 %collective-permute-start = (f32[4096]{0:T(1024)S(1)}, f32[4096]{0:T(1024)S(1)}, u32[]{:S(2)}, u32[]{:S(2)}) collective-permute-start(f32[4096]{0:T(1024)S(1)} %param.1), channel_id=1, source_target_pairs={{0,1},{1,0},{2,3},{3,2},{4,5},{5,4},{6,7},{7,6},{8,9},{9,8},{10,11... | collective-permute-start | bytes 49160 | tf_op jit(solution)/shard_map/cond/branch_1_fun/ppermute | solution.py:354
  42.0 5.8 %collective-permute-done = f32[4096]{0:T(1024)S(1)} collective-permute-done((f32[4096]{0:T(1024)S(1)}, f32[4096]{0:T(1024)S(1)}, u32[]{:S(2)}, u32[]{:S(2)}) %collective-permute-start) | collective-permute-done | bytes 16416 | tf_op jit(solution)/shard_map/cond/branch_1_fun/ppermute | solution.py:354
  47.9 1.9 %collective-permute-start.1 = (f32[4096]{0:T(1024)S(1)}, f32[4096]{0:T(1024)S(1)}, u32[]{:S(2)}, u32[]{:S(2)}) collective-permute-start(f32[4096]{0:T(1024)S(1)} %log_add_fusion.4), channel_id=1, source_target_pairs={{0,3},{1,2},{2,1},{3,0},{4,7},{5,6},{6,5},{7,4},{8,11},{9,10},{10,... | collective-permute-start | bytes 49160 | tf_op jit(solution)/shard_map/cond/branch_1_fun/ppermute | solution.py:354
  49.7 2.3 %collective-permute-done.1 = f32[4096]{0:T(1024)S(1)} collective-permute-done((f32[4096]{0:T(1024)S(1)}, f32[4096]{0:T(1024)S(1)}, u32[]{:S(2)}, u32[]{:S(2)}) %collective-permute-start.1) | collective-permute-done | bytes 16416 | tf_op jit(solution)/shard_map/cond/branch_1_fun/ppermute | solution.py:354
  52.1 1.3 %collective-permute-start.2 = (f32[4096]{0:T(1024)S(1)}, f32[4096]{0:T(1024)S(1)}, u32[]{:S(2)}, u32[]{:S(2)}) collective-permute-start(f32[4096]{0:T(1024)S(1)} %log_add_fusion.3), channel_id=1, source_target_pairs={{0,4},{1,5},{2,6},{3,7},{4,0},{5,1},{6,2},{7,3},{8,12},{9,13},{10,... | collective-permute-start | bytes 49160 | tf_op jit(solution)/shard_map/cond/branch_1_fun/ppermute | solution.py:354
  53.3 1.6 %collective-permute-done.2 = f32[4096]{0:T(1024)S(1)} collective-permute-done((f32[4096]{0:T(1024)S(1)}, f32[4096]{0:T(1024)S(1)}, u32[]{:S(2)}, u32[]{:S(2)}) %collective-permute-start.2) | collective-permute-done | bytes 16416 | tf_op jit(solution)/shard_map/cond/branch_1_fun/ppermute | solution.py:354
  55.0 2.5 %collective-permute-start.3 = (f32[4096]{0:T(1024)S(1)}, f32[4096]{0:T(1024)S(1)}, u32[]{:S(2)}, u32[]{:S(2)}) collective-permute-start(f32[4096]{0:T(1024)S(1)} %log_add_fusion.2), channel_id=1, source_target_pairs={{0,12},{1,13},{2,14},{3,15},{4,8},{5,9},{6,10},{7,11},{8,4},{9,5},... | collective-permute-start | bytes 49160 | tf_op jit(solution)/shard_map/cond/branch_1_fun/ppermute | solution.py:354
  57.4 1.4 %collective-permute-done.3 = f32[4096]{0:T(1024)S(1)} collective-permute-done((f32[4096]{0:T(1024)S(1)}, f32[4096]{0:T(1024)S(1)}, u32[]{:S(2)}, u32[]{:S(2)}) %collective-permute-start.3) | collective-permute-done | bytes 16416 | tf_op jit(solution)/shard_map/cond/branch_1_fun/ppermute | solution.py:354
  58.9 2.8 %collective-permute-start.4 = (f32[4096]{0:T(1024)S(1)}, f32[4096]{0:T(1024)S(1)}, u32[]{:S(2)}, u32[]{:S(2)}) collective-permute-start(f32[4096]{0:T(1024)S(1)} %log_add_fusion.1), channel_id=1, source_target_pairs={{0,16},{1,17},{2,18},{3,19},{4,20},{5,21},{6,22},{7,23},{8,24},{9,... | collective-permute-start | bytes 49160 | tf_op jit(solution)/shard_map/cond/branch_1_fun/ppermute | solution.py:354
  61.6 1.4 %collective-permute-done.4 = f32[4096]{0:T(1024)S(1)} collective-permute-done((f32[4096]{0:T(1024)S(1)}, f32[4096]{0:T(1024)S(1)}, u32[]{:S(2)}, u32[]{:S(2)}) %collective-permute-start.4) | collective-permute-done | bytes 16416 | tf_op jit(solution)/shard_map/cond/branch_1_fun/ppermute | solution.py:354
  63.3 0.0 copy-done.4
  63.3 0.0 all-to-all-done.1
  63.4 0.1 copy.22
  63.5 0.1 slice_select_fusion
  63.7 0.1 reshape.66.beside_ref
  63.8 0.1 fusion.12.cols_ref
  63.9 0.0 copy-done
  63.9 2.4 %place_rows.1.chars_ref = bf16[2048,256]{1,0:T(8,128)(2,1)S(1)} custom-call(s32[1,2048]{1,0:T(1,128)S(1)} %copy-done, bf16[2560,128]{1,0:T(8,128)(2,1)S(1)} %bitcast.32, f32[8,2048]{1,0:T(8,128)S(1)} %reshape.66.beside_ref, f32[3,4096]{1,0:T(4,128)S(1)} %pad_maximum_fusion.1.gate_ref.rows_ref), custom_call_target="tpu_custom_call" | custom-call | tf_op jit(solution)/shard_map/place_rows/pallas_call | solution.py:205
  66.3 0.0 copy-done.1
  66.4 6.6 %first_panel.1 = (f32[1032,256]{1,0:T(8,128)S(1)}, f32[1024,128]{1,0:T(8,128)S(1)}, bf16[256,4096]{1,0:T(8,128)(2,1)S(1)}) custom-call(bf16[2048,256]{1,0:T(8,128)(2,1)S(1)} %place_rows.1.chars_ref, bf16[4096,128]{1,0:T(8,128)(2,1)S(1)} %copy-done.1, f32[3,4096]{1,0:T(4,128)S(1)} %pad_maximum_fusion.1.gate_ref.rows_ref, bf16[256,256]{1,0:T(8,128)(2,1)S(1)} %fusion.12.cols_ref), custom_call_target="tpu_custom_call" | custom-call | flops 4294967296 | bytes 2097152 | tf_op jit(solution)/shard_map/first_panel/pallas_call | solution.py:252
  73.0 6.6 %collective-permute-start.7 = (f32[1032,256]{1,0:T(8,128)S(1)}, f32[1032,256]{1,0:T(8,128)S(1)}, u32[]{:S(2)}, u32[]{:S(2)}) collective-permute-start(f32[1032,256]{1,0:T(8,128)S(1)} %get-tuple-element.62.gate_ref), channel_id=1, source_target_pairs={{0,32},{32,0},{64,96},{96,64},{1,33},{33,1},{65,97},{97,65},{2,34}... | collective-permute-start | bytes 3170312 | tf_op jit(solution)/shard_map/ppermute | solution.py:354
  79.6 4.7 %panel.1 = (f32[1024,256]{1,0:T(8,128)S(1)}, f32[1024,128]{1,0:T(8,128)S(1)}) custom-call(bf16[2048,256]{1,0:T(8,128)(2,1)S(1)} %place_rows.1.chars_ref, bf16[4096,128]{1,0:T(8,128)(2,1)S(1)} %copy-done.1, f32[3,4096]{1,0:T(4,128)S(1)} %pad_maximum_fusion.1.gate_ref.rows_ref, bf16[256,4096]{1,0:T(8,128)(2,1)S(1)} %get-tuple-element.61.weight_ref, ...), custom_call_target="tpu_custom_call" | custom-call | flops 4294967296 | bytes 2097152 | tf_op jit(solution)/shard_map/panel/pallas_call | solution.py:294
  84.3 0.0 copy-start.3
  84.3 0.0 collective-permute-done.7
  84.3 1.0 fusion.9
  85.3 0.4 collective-permute-start.8
  85.7 0.0 copy-done.3
  85.7 0.0 copy-start.5
  85.7 13.9 %conditional.3 = (f32[4352]{0:T(1024)S(1)}, f32[256]{0:T(256)S(1)}) conditional(s32[]{:T(128)} %bitcast.6, () %tuple.24, (bf16[2048,256]{1,0:T(8,128)(2,1)S(1)}, bf16[4096,128]{1,0:T(8,128)(2,1)S(1)}, f32[3,4096]{1,0:T(4,128)S(1)}, f32[1,256]{1,0:T(1,128)S(1)}, pred[]{:T(512)}, /*index=5*/f32[1024,128]{1,0:T(8,128)S(1)}, f32[1024,128]{1,0:T(8,128)S(1)}, ...), branch_computations={%region_4.5_spmd, %region_5.9_spmd} | conditional | flops 561408 | bytes 2410605 | solution.py:444
  85.7 0.2 reduce_sum.43
  85.9 0.2 reduce_sum.44
  86.2 7.2 %share_sums.1 = f32[2048,128]{1,0:T(8,128)S(1)} custom-call(bf16[2048,256]{1,0:T(8,128)(2,1)S(1)} %get-tuple-element.31.chars_ref, bf16[4096,128]{1,0:T(8,128)(2,1)S(1)} %get-tuple-element.32.tastes_ref, f32[3,4096]{1,0:T(4,128)S(1)} %get-tuple-element.33.rows_ref, f32[1,256]{1,0:T(1,128)S(1)} %get-tuple-element.34.gate_ref), custom_call_target="tpu_custom_call" | custom-call | tf_op jit(solution)/shard_map/cond/branch_1_fun/share_sums/pallas_call | solution.py:336
  93.4 0.3 reduce_sum.42
  93.7 0.4 collective-permute-start.5
  94.1 0.9 collective-permute-done.5
  95.0 1.1 %collective-permute-start.6 = (f32[4352]{0:T(1024)S(1)}, f32[4352]{0:T(1024)S(1)}, u32[]{:S(2)}, u32[]{:S(2)}) collective-permute-start(f32[4352]{0:T(1024)S(1)} %fusion.5), channel_id=1, source_target_pairs={{0,64},{32,96},{64,0},{96,32},{1,65},{33,97},{65,1},{97,33},{2,66}... | collective-permute-start | bytes 52232 | tf_op jit(solution)/shard_map/cond/branch_1_fun/ppermute | solution.py:354
  96.1 3.5 %collective-permute-done.6 = f32[4352]{0:T(1024)S(1)} collective-permute-done((f32[4352]{0:T(1024)S(1)}, f32[4352]{0:T(1024)S(1)}, u32[]{:S(2)}, u32[]{:S(2)}) %collective-permute-start.6) | collective-permute-done | bytes 17440 | tf_op jit(solution)/shard_map/cond/branch_1_fun/ppermute | solution.py:354
  99.6 0.0 copy-start.2
  99.7 0.0 collective-permute-done.8
  99.7 0.0 copy-done.5
  99.7 1.6 %select_subtract_fusion = f32[1024,256]{1,0:T(8,128)S(1)} fusion(f16[1024,256]{1,0:T(8,128)(2,1)} %collective-permute-done.8, f16[1024,256]{1,0:T(8,128)(2,1)} %get-tuple-element.68, f32[256]{0:T(256)S(1)} %get-tuple-element.85, s32[256]{0:T(256)S(1)} %copy-done.5, f32[256]{0:T(256)S(1)} %get-tuple-element.84, f32[256]{0:T(256)S(1)} %bitcast.53, ...), kind=kLoop, calls=%fused_computation.23 | loop fusion | flops 2097152 | bytes 2105344 | tf_op jit(solution)/shard_map/sub | solution.py:460
  101.2 0.0 copy-done.2
  101.3 1.0 fusion.7
  102.3 0.8 collective-permute-start.9
  103.1 0.6 slice_bitcast_fusion.1
  103.7 0.9 multiply_reduce_fusion
  104.6 0.7 collective-permute-done.9
  105.3 1.6 %maximum_select_fusion = f32[2048,256]{1,0:T(8,128)} fusion(f32[1024,256]{1,0:T(8,128)S(1)} %collective-permute-done.9, f32[1024,256]{1,0:T(8,128)S(1)} %bitcast.35, pred[]{:T(512)} %eq.25), kind=kLoop, calls=%fused_computation.20 | loop fusion | flops 1572864 | bytes 4194305 | tf_op jit(solution)/shard_map/jit(_where)/select_n | solution.py:468
  (23 shorter events, 0.4 us)
Async XLA Ops:
  5.3 21.2 %all-to-all-start = ((bf16[32,16,128]{2,1,0:T(8,128)(2,1)}), bf16[32,16,128]{2,1,0:T(8,128)(2,1)S(1)}, u32[]{:S(2)}, u32[]{:S(2)}) async-start(bf16[32,16,128]{2,1,0:T(8,128)(2,1)} %bitcast.40), calls=%async_computation | async-start | bytes 262144 | tf_op jit(solution)/shard_map/all_to_all | solution.py:385
  26.5 36.8 %copy-start.4 = (f32[4096]{0:T(1024)S(1)}, f32[4096]{0:T(1024)}, u32[]{:S(2)}) copy-start(f32[4096]{0:T(1024)} %param.12) | copy-start | bytes 49156
  27.4 36.5 %copy-start = (s32[1,2048]{1,0:T(1,128)S(1)}, s32[1,2048]{1,0:T(1,128)}, u32[]{:S(2)}) copy-start(s32[1,2048]{1,0:T(1,128)} %get-tuple-element.59.order_ref) | copy-start | bytes 24580
  30.7 32.7 %all-to-all-start.1 = ((bf16[32,80,128]{2,1,0:T(8,128)(2,1)}), bf16[32,80,128]{2,1,0:T(8,128)(2,1)S(1)}, u32[]{:S(2)}, u32[]{:S(2)}) async-start(bf16[32,80,128]{2,1,0:T(8,128)(2,1)} %bitcast.12), calls=%async_computation.1 | async-start | bytes 1310720 | tf_op jit(solution)/shard_map/all_to_all | solution.py:399
  39.9 26.4 %copy-start.1 = (bf16[4096,128]{1,0:T(8,128)(2,1)S(1)}, bf16[4096,128]{1,0:T(8,128)(2,1)}, u32[]{:S(2)}) copy-start(bf16[4096,128]{1,0:T(8,128)(2,1)} %tastes_ref.5) | copy-start | bytes 3145732
  40.7 7.1 %collective-permute-start = (f32[4096]{0:T(1024)S(1)}, f32[4096]{0:T(1024)S(1)}, u32[]{:S(2)}, u32[]{:S(2)}) collective-permute-start(f32[4096]{0:T(1024)S(1)} %param.1), channel_id=1, source_target_pairs={{0,1},{1,0},{2,3},{3,2},{4,5},{5,4},{6,7},{7,6},{8,9},{9,8},{10,11... | collective-permute-start | bytes 49160 | tf_op jit(solution)/shard_map/cond/branch_1_fun/ppermute | solution.py:354
  47.9 4.2 %collective-permute-start.1 = (f32[4096]{0:T(1024)S(1)}, f32[4096]{0:T(1024)S(1)}, u32[]{:S(2)}, u32[]{:S(2)}) collective-permute-start(f32[4096]{0:T(1024)S(1)} %log_add_fusion.4), channel_id=1, source_target_pairs={{0,3},{1,2},{2,1},{3,0},{4,7},{5,6},{6,5},{7,4},{8,11},{9,10},{10,... | collective-permute-start | bytes 49160 | tf_op jit(solution)/shard_map/cond/branch_1_fun/ppermute | solution.py:354
  52.1 2.9 %collective-permute-start.2 = (f32[4096]{0:T(1024)S(1)}, f32[4096]{0:T(1024)S(1)}, u32[]{:S(2)}, u32[]{:S(2)}) collective-permute-start(f32[4096]{0:T(1024)S(1)} %log_add_fusion.3), channel_id=1, source_target_pairs={{0,4},{1,5},{2,6},{3,7},{4,0},{5,1},{6,2},{7,3},{8,12},{9,13},{10,... | collective-permute-start | bytes 49160 | tf_op jit(solution)/shard_map/cond/branch_1_fun/ppermute | solution.py:354
  55.0 3.9 %collective-permute-start.3 = (f32[4096]{0:T(1024)S(1)}, f32[4096]{0:T(1024)S(1)}, u32[]{:S(2)}, u32[]{:S(2)}) collective-permute-start(f32[4096]{0:T(1024)S(1)} %log_add_fusion.2), channel_id=1, source_target_pairs={{0,12},{1,13},{2,14},{3,15},{4,8},{5,9},{6,10},{7,11},{8,4},{9,5},... | collective-permute-start | bytes 49160 | tf_op jit(solution)/shard_map/cond/branch_1_fun/ppermute | solution.py:354
  58.9 4.2 %collective-permute-start.4 = (f32[4096]{0:T(1024)S(1)}, f32[4096]{0:T(1024)S(1)}, u32[]{:S(2)}, u32[]{:S(2)}) collective-permute-start(f32[4096]{0:T(1024)S(1)} %log_add_fusion.1), channel_id=1, source_target_pairs={{0,16},{1,17},{2,18},{3,19},{4,20},{5,21},{6,22},{7,23},{8,24},{9,... | collective-permute-start | bytes 49160 | tf_op jit(solution)/shard_map/cond/branch_1_fun/ppermute | solution.py:354
  73.0 11.3 %collective-permute-start.7 = (f32[1032,256]{1,0:T(8,128)S(1)}, f32[1032,256]{1,0:T(8,128)S(1)}, u32[]{:S(2)}, u32[]{:S(2)}) collective-permute-start(f32[1032,256]{1,0:T(8,128)S(1)} %get-tuple-element.62.gate_ref), channel_id=1, source_target_pairs={{0,32},{32,0},{64,96},{96,64},{1,33},{33,1},{65,97},{97,65},{2,34}... | collective-permute-start | bytes 3170312 | tf_op jit(solution)/shard_map/ppermute | solution.py:354
  84.3 1.4 %copy-start.3 = (s32[2048]{0:T(1024)S(1)}, s32[2048]{0:T(1024)}, u32[]{:S(2)}) copy-start(s32[2048]{0:T(1024)} %param.16) | copy-start | bytes 24580
  85.3 14.3 %collective-permute-start.8 = (f16[1024,256]{1,0:T(8,128)(2,1)}, f16[1024,256]{1,0:T(8,128)(2,1)}, u32[]{:S(2)}, u32[]{:S(2)}) collective-permute-start(f16[1024,256]{1,0:T(8,128)(2,1)} %get-tuple-element.68), channel_id=1, source_target_pairs={{0,64},{32,96},{64,0},{96,32},{1,65},{33,97},{65,1},{97,33},{2,66}... | collective-permute-start | bytes 1572872 | tf_op jit(solution)/shard_map/ppermute | solution.py:354
  85.7 14.0 %copy-start.5 = (s32[256]{0:T(256)S(1)}, s32[256]{0:T(256)}, u32[]{:S(2)}) copy-start(s32[256]{0:T(256)} %param.15) | copy-start | bytes 3076
  93.7 1.3 %collective-permute-start.5 = (f32[4352]{0:T(1024)S(1)}, f32[4352]{0:T(1024)S(1)}, u32[]{:S(2)}, u32[]{:S(2)}) collective-permute-start(f32[4352]{0:T(1024)S(1)} %pad_maximum_fusion), channel_id=1, source_target_pairs={{0,32},{32,0},{64,96},{96,64},{1,33},{33,1},{65,97},{97,65},{2,34}... | collective-permute-start | bytes 52232 | tf_op jit(solution)/shard_map/cond/branch_1_fun/ppermute | solution.py:354
  95.0 4.6 %collective-permute-start.6 = (f32[4352]{0:T(1024)S(1)}, f32[4352]{0:T(1024)S(1)}, u32[]{:S(2)}, u32[]{:S(2)}) collective-permute-start(f32[4352]{0:T(1024)S(1)} %fusion.5), channel_id=1, source_target_pairs={{0,64},{32,96},{64,0},{96,32},{1,65},{33,97},{65,1},{97,33},{2,66}... | collective-permute-start | bytes 52232 | tf_op jit(solution)/shard_map/cond/branch_1_fun/ppermute | solution.py:354
  99.6 1.6 %copy-start.2 = (f32[16,128,128]{2,1,0:T(8,128)S(1)}, f32[16,128,128]{2,1,0:T(8,128)}, u32[]{:S(2)}) copy-start(f32[16,128,128]{2,1,0:T(8,128)} %param.17) | copy-start | bytes 3145732
  102.3 3.1 %collective-permute-start.9 = (f32[1024,256]{1,0:T(8,128)S(1)}, f32[1024,256]{1,0:T(8,128)S(1)}, u32[]{:S(2)}, u32[]{:S(2)}) collective-permute-start(f32[1024,256]{1,0:T(8,128)S(1)} %bitcast.34), channel_id=1, source_target_pairs={{0,32},{32,0},{64,96},{96,64},{1,33},{33,1},{65,97},{97,65},{2,34}... | collective-permute-start | bytes 3145736 | tf_op jit(solution)/shard_map/ppermute | solution.py:354
